TPU v7x, 32 devices: a whole 2x2x4 slice. The times are simulated.
32 devices in a mesh: dp: 8 (over y, x, core), seq: 4 (over z).
Axes of the slice: x: 2, y: 2, z: 4, core: 2. Of those that a mesh axis runs over, the one named last changes fastest.
Arguments:
- queries: bfloat16 [8, 512, 1536], P('dp', 'seq'), may hold values from -120 to 120
- keys: bfloat16 [8, 512, 1536], P('dp', 'seq'), may hold values from -4.5 to 4.5
- values: bfloat16 [8, 512, 1536], P('dp', 'seq'), may hold values from -6 to 6
- grad_out: bfloat16 [8, 512, 1536], P('dp', 'seq'), may hold values from -6 to 6
- conv_weight: float32 [31, 1536], replicated, may hold values from -2 to 2
- conv_bias: float32 [1536], replicated, may hold values from -4 to 4
- lengths: int32 [8], P('dp'), may hold values from 128 to 512, as said below
Outputs:
- query_grad: bfloat16 [8, 512, 1536], P('dp', 'seq')
- key_grad: bfloat16 [8, 512, 1536], P('dp', 'seq')
- value_grad: bfloat16 [8, 512, 1536], P('dp', 'seq')
- weight_grad: float32 [31, 1536], P(None, 'seq')
- bias_grad: float32 [1536], P('seq')
Inputs may be any that keep to these rules, and one draw needn't show every extreme that they name: `lengths`: each utterance's valid frames are its first ones; in every draw some utterance has all 512 frames valid.
All inputs are finite; a program needn't handle non-finite values.
Results may differ from a plain program's by a relative error of at most 0.024.
Values may be sent and summed in bfloat16 or wider, within the bound.
No kernel may reach another device: no remote copies, remote signals or barrier semaphores. Data moves between devices by JAX's collectives and lax.ppermute only.
A program may use at most 64 MiB of HBM per device.

v0:
```python
import functools
import math

import jax
import jax.numpy as jnp
from jax import lax
from jax.experimental import pallas as pl
from jax.experimental.pallas import tpu as pltpu
from jax.sharding import PartitionSpec as P

HEADS = 16
KERNEL = 31
PAD = 16
CUTS = 4
masked_score = -1e30
VMEM = pl.BlockSpec(memory_space=pltpu.VMEM)
SMEM = pl.BlockSpec(memory_space=pltpu.SMEM)
LIMIT = 16 * 1024 * 1024
bf16, f32 = jnp.bfloat16, jnp.float32


def pack_kernel(count, chunks, rank_ref, *refs):
    arrays, outs, (plain, turned, sems) = refs[:4], refs[4:-3], refs[-3:]
    rank = rank_ref[0]
    high = outs[0].shape[1]
    share = high * chunks
    frames = plain.shape[1]
    cut = frames // CUTS

    def copy(which, part):
        at = pl.ds(part * cut, cut)
        return pltpu.make_async_copy(
            arrays[which].at[0, at, :], plain.at[which, at, :], sems.at[which, part]
        )

    for which in range(4):
        for part in range(CUTS):
            copy(which, part).start()
    for which in range(4):
        for part in range(CUTS):
            copy(which, part).wait()
        turned[which] = plain[which].T
        for distance in range(count):
            for chunk in range(chunks):
                first = pl.multiple_of((rank ^ distance) * share + chunk * high, 16)
                outs[chunk * count + distance][which] = turned[which, pl.ds(first, high), :]


def pack(rank, arrays, count, chunks):
    _, frames, width = arrays[0].shape
    high = width // count // chunks
    piece = jax.ShapeDtypeStruct((4, high, frames), bf16)
    outs = pl.pallas_call(
        functools.partial(pack_kernel, count, chunks),
        out_shape=(piece,) * (count * chunks),
        in_specs=[SMEM] + [pl.BlockSpec(memory_space=pltpu.HBM)] * 4,
        out_specs=(VMEM,) * (count * chunks),
        scratch_shapes=[
            pltpu.VMEM((4, frames, width), bf16),
            pltpu.VMEM((4, width, frames), bf16),
            pltpu.SemaphoreType.DMA((4, CUTS)),
        ],
        compiler_params=pltpu.CompilerParams(vmem_limit_bytes=LIMIT),
        cost_estimate=pl.CostEstimate(
            flops=0, bytes_accessed=16 * frames * width, transcendentals=0
        ),
    )(rank, *[pltpu.with_memory_space_constraint(array, pltpu.HBM) for array in arrays])
    return [outs[chunk * count : (chunk + 1) * count] for chunk in range(chunks)]


def unpack_kernel(count, chunks, rank_ref, taps_ref, *refs):
    pieces, outs, turned = refs[: count * chunks], refs[-6:-3], refs[-1]
    weight_ref, bias_ref = refs[-3:-1]
    taps = jnp.sum(taps_ref[...], axis=0)
    heads, _, depth = taps.shape
    for head in range(heads):
        at = slice(head * depth, (head + 1) * depth)
        weight_ref[:, at] = taps[head, :KERNEL]
        bias_ref[:, at] = taps[head, KERNEL:]
    rank = rank_ref[0]
    high = pieces[0].shape[1]
    share = high * chunks
    for which, out in enumerate(outs):
        for distance in range(count):
            for chunk in range(chunks):
                first = pl.multiple_of((rank ^ distance) * share + chunk * high, 16)
                turned[which, pl.ds(first, high), :] = pieces[chunk * count + distance][which]
        out[0] = turned[which].T


def unpack(rank, taps, pieces, count, chunks):
    _, high, frames = pieces[0][0].shape
    width = high * count * chunks
    whole = jax.ShapeDtypeStruct((1, frames, width), bf16)
    return pl.pallas_call(
        functools.partial(unpack_kernel, count, chunks),
        out_shape=(whole,) * 3
        + (
            jax.ShapeDtypeStruct((KERNEL, width // count), f32),
            jax.ShapeDtypeStruct((1, width // count), f32),
        ),
        in_specs=[SMEM] + [VMEM] * (1 + count * chunks),
        out_specs=(VMEM,) * 5,
        scratch_shapes=[pltpu.VMEM((3, width, frames), bf16)],
        compiler_params=pltpu.CompilerParams(vmem_limit_bytes=LIMIT),
        cost_estimate=pl.CostEstimate(
            flops=0, bytes_accessed=12 * frames * width, transcendentals=0
        ),
    )(rank, taps, *[piece for part in pieces for piece in part])


def core_kernel(count, block, scalars, weight_ref, bias_ref, *refs):
    pieces, outs, taps_ref = refs[:count], refs[count : 2 * count], refs[2 * count]
    q_t, k_t, v_t, a_t, q_n, k_n, v_n, g_n, a_n, probs, shifted, pre_grad = refs[2 * count + 1 :]
    heads, rows, depth = q_n.shape
    frames = pieces[0].shape[2]
    blocks = rows // block
    scale = 1.0 / math.sqrt(depth)
    log_scale = scale * math.log2(math.e)
    length, rank = scalars[0], scalars[1]

    def span(head):
        return slice(head * depth, (head + 1) * depth)

    for distance, piece in enumerate(pieces):
        at = pl.ds(pl.multiple_of((rank ^ distance) * frames, 128), frames)
        q_t[:, at] = piece[0]
        k_t[:, at] = piece[1]
        v_t[:, at] = piece[2]
        for head in range(heads):
            q_n[head, at, :] = piece[0, span(head), :].T
            k_n[head, at, :] = piece[1, span(head), :].T
            v_n[head, at, :] = piece[2, span(head), :].T
            g_n[head, at, :] = piece[3, span(head), :].T

    def forward(index, head):
        cols = pl.ds(pl.multiple_of(index * block, block), block)
        scores = jnp.dot(k_n[head], q_t[span(head), cols], preferred_element_type=f32)
        key_at = lax.broadcasted_iota(jnp.int32, scores.shape, 0)
        scores = jnp.where(key_at < length, scores, masked_score)
        exped = jnp.exp2((scores - jnp.max(scores, axis=0, keepdims=True)) * log_scale)
        found = exped * (1.0 / jnp.sum(exped, axis=0, keepdims=True))
        probs[head, :, cols] = found
        out = jnp.dot(v_t[span(head), :], found.astype(bf16), preferred_element_type=f32)
        frame_at = index * block + lax.broadcasted_iota(jnp.int32, out.shape, 1)
        a_t[span(head), cols] = jnp.where(frame_at < length, out, 0.0).astype(bf16)

    def each_block(body):
        if blocks == 1:
            for head in range(heads):
                body(0, head)
        else:

            def step(index, carry):
                for head in range(heads):
                    body(index, head)
                return carry

            lax.fori_loop(0, blocks, step, 0)

    each_block(forward)

    tall = shifted.shape[1]

    def shift_all(source_rows):
        shifted[0, 0:PAD, :] = jnp.zeros((PAD, depth), f32)
        shifted[0, PAD + rows : tall, :] = jnp.zeros((tall - PAD - rows, depth), f32)
        for first in range(0, rows, frames):
            shifted[0, PAD + first : PAD + first + frames, :] = source_rows(first)
        for s in range(1, 8):
            shifted[s, 0 : tall - 8, :] = shifted[0, s : tall - 8 + s, :]

    step_rows = 64

    def filtered(head, row, reverse):
        total = None
        for offset in range(1, KERNEL + 1):
            s, a = offset % 8, offset // 8 * 8
            tap = KERNEL - offset if reverse else offset - 1
            term = weight_ref[head, tap : tap + 1, :] * shifted[s, pl.ds(row + a, step_rows), :]
            total = term if total is None else total + term
        return total

    def eights(array):
        return jnp.sum(array.reshape(step_rows // 8, 8, depth), axis=0)

    for head in range(heads):
        shift_all(lambda first: a_t[span(head), first : first + frames].T.astype(f32))

        def conv_step(index, carry, head=head):
            row = pl.multiple_of(index * step_rows, step_rows)
            conv_pre = filtered(head, row, False) + bias_ref[head]
            sig = 1.0 / (1.0 + jnp.exp(-conv_pre))
            grad = g_n[head, pl.ds(row, step_rows), :].astype(f32)
            pre = grad * (sig * (1.0 + conv_pre * (1.0 - sig)))
            pre = pre.astype(bf16).astype(f32)
            pre_grad[pl.ds(row, step_rows), :] = pre
            new = []
            for offset in range(1, KERNEL + 1):
                s, a = offset % 8, offset // 8 * 8
                term = pre * shifted[s, pl.ds(row + a, step_rows), :]
                new.append(carry[offset - 1] + eights(term))
            new.append(carry[KERNEL] + eights(pre))
            return tuple(new)

        zero = jnp.zeros((8, depth), f32)
        sums = lax.fori_loop(0, rows // step_rows, conv_step, (zero,) * (KERNEL + 1))
        for tap in range(KERNEL + 1):
            taps_ref[head, tap : tap + 1, :] = jnp.sum(sums[tap], axis=0, keepdims=True)

        shift_all(lambda first: pre_grad[first : first + frames, :])

        def back_step(index, carry, head=head):
            row = pl.multiple_of(index * step_rows, step_rows)
            total = g_n[head, pl.ds(row, step_rows), :].astype(f32) + filtered(head, row, True)
            frame_at = row + lax.broadcasted_iota(jnp.int32, total.shape, 0)
            total = jnp.where(frame_at < length, total, 0.0)
            a_n[head, pl.ds(row, step_rows), :] = total.astype(bf16)
            return carry

        lax.fori_loop(0, rows // step_rows, back_step, 0)
        for first in range(0, rows, frames):
            a_t[span(head), first : first + frames] = a_n[head, first : first + frames, :].T

    def backward(index, head):
        cols = pl.ds(pl.multiple_of(index * block, block), block)
        score_grad = jnp.dot(v_n[head], a_t[span(head), cols], preferred_element_type=f32)
        found = probs[head, :, cols]
        delta = jnp.sum(found * score_grad, axis=0, keepdims=True)
        diff = (found * (score_grad - delta)).astype(bf16)
        value = jnp.dot(found.astype(bf16), a_n[head, cols, :], preferred_element_type=f32)
        key = jnp.dot(diff, q_n[head, cols, :], preferred_element_type=f32)
        query = jnp.dot(k_t[span(head), :], diff, preferred_element_type=f32)
        q_t[span(head), cols] = (query * scale).astype(bf16)
        return key, value

    def finish(head, key, value):
        for first in range(0, rows, frames):
            at = slice(first, first + frames)
            k_t[span(head), at] = (key[at, :] * scale).astype(bf16).T
            v_t[span(head), at] = value[at, :].astype(bf16).T

    for head in range(heads):
        if blocks == 1:
            finish(head, *backward(0, head))
        else:
            zeros = jnp.zeros((rows, depth), f32)

            def step(index, carry, head=head):
                key, value = backward(index, head)
                return carry[0] + key, carry[1] + value

            finish(head, *lax.fori_loop(0, blocks, step, (zeros, zeros)))

    for distance, out in enumerate(outs):
        at = pl.ds(pl.multiple_of((rank ^ distance) * frames, 128), frames)
        out[0] = q_t[:, at]
        out[1] = k_t[:, at]
        out[2] = v_t[:, at]


def core(scalars, weight, bias, pieces):
    count = len(pieces)
    _, high, frames = pieces[0].shape
    heads, _, depth = weight.shape
    rows = count * frames
    block = math.gcd(rows, 512)
    tall = rows + 2 * PAD + 8
    piece = jax.ShapeDtypeStruct((3, high, frames), bf16)
    turned = pltpu.VMEM((high, rows), bf16)
    plain = pltpu.VMEM((heads, rows, depth), bf16)
    outs = pl.pallas_call(
        functools.partial(core_kernel, count, block),
        out_shape=(piece,) * count + (jax.ShapeDtypeStruct((heads, KERNEL + 1, depth), f32),),
        in_specs=[SMEM] + [VMEM] * (2 + count),
        out_specs=(VMEM,) * (count + 1),
        scratch_shapes=[turned] * 4
        + [plain] * 5
        + [
            pltpu.VMEM((heads, rows, rows), f32),
            pltpu.VMEM((8, tall, depth), f32),
            pltpu.VMEM((rows, depth), f32),
        ],
        compiler_params=pltpu.CompilerParams(
            vmem_limit_bytes=12 * 2**20 + 8 * heads * rows * rows + 4096 * tall
        ),
        cost_estimate=pl.CostEstimate(
            flops=24 * rows * rows * high,
            bytes_accessed=14 * rows * high,
            transcendentals=heads * rows * rows,
        ),
    )(scalars, weight, bias, *pieces)
    return outs[:count], outs[count]


def exchanged(parts):
    done = []
    for pieces in parts:
        moved = [pieces[0]]
        for distance in range(1, len(pieces)):
            piece = pieces[distance]
            if done:
                piece, done[-1][distance] = lax.optimization_barrier((piece, done[-1][distance]))
            pairs = [(i, i ^ distance) for i in range(len(pieces))]
            moved.append(lax.ppermute(piece, "seq", pairs))
        done.append(moved)
    return done


def on_device(queries, keys, values, grad_out, conv_weight, conv_bias, lengths):
    count = lax.axis_size("seq")
    rank = lax.axis_index("seq").astype(jnp.int32)
    width = queries.shape[2]
    depth = width // HEADS
    heads = HEADS // count
    chunks = math.gcd(heads, 2)
    step = heads // chunks
    by_head = conv_weight.reshape(KERNEL, HEADS, depth).transpose(1, 0, 2)
    weight = lax.dynamic_slice_in_dim(by_head, rank * heads, heads, axis=0)
    bias = lax.dynamic_slice_in_dim(conv_bias.reshape(HEADS, 1, depth), rank * heads, heads, axis=0)
    scalars = jnp.stack([lengths[0], rank])
    sent = pack(rank[None], (queries, keys, values, grad_out), count, chunks)
    arrived = exchanged(sent)
    kept, taps = [], []
    for chunk, pieces in enumerate(arrived):
        at = slice(chunk * step, (chunk + 1) * step)
        grads, part = core(scalars, weight[at], bias[at], pieces)
        kept.append(grads)
        taps.append(part)
    returned = exchanged(kept)
    taps, returned[0] = lax.optimization_barrier((jnp.concatenate(taps, axis=0), returned[0]))
    taps = lax.all_gather(taps, "dp")
    query_grad, key_grad, value_grad, weight_grad, bias_grad = unpack(
        rank[None], taps, returned, count, chunks
    )
    return query_grad, key_grad, value_grad, weight_grad, bias_grad[0]


def solution(mesh):
    return jax.shard_map(
        on_device,
        mesh=mesh,
        in_specs=(
            P("dp", "seq", None),
            P("dp", "seq", None),
            P("dp", "seq", None),
            P("dp", "seq", None),
            P(),
            P(),
            P("dp"),
        ),
        out_specs=(
            P("dp", "seq", None),
            P("dp", "seq", None),
            P("dp", "seq", None),
            P(None, "seq"),
            P("seq"),
        ),
        check_vma=False,
    )
```

profile of v0, /device:TPU:0, one launch (start us, length us, event | category | flops | bytes accessed | tf_op | source)
XLA Modules:
  0.0 78.6 jit_solution(10806112040652476332)
XLA Ops:
  0.6 2.0 %shard_map.110 = (bf16[4,192,128]{2,1,0:T(8,128)(2,1)S(1)}, bf16[4,192,128]{2,1,0:T(8,128)(2,1)S(1)}, bf16[4,192,128]{2,1,0:T(8,128)(2,1)S(1)}, bf16[4,192,128]{...) custom-call(s32[1]{0:T(128)} %bitcast.rank_ref, ...), custom_call_target="tpu_custom_call" | custom-call | bytes 3145728 | tf_op jit(solution)/shard_map/pallas_call | solution.py:53
  2.6 0.0 copy-start.1
  2.6 3.1 %collective-permute-start = (bf16[4,192,128]{2,1,0:T(8,128)(2,1)S(1)}, bf16[4,192,128]{2,1,0:T(8,128)(2,1)S(1)}, u32[]{:S(2)}, u32[]{:S(2)}) collective-permute-start(bf16[4,192,128]{2,1,0:T(8,128)(2,1)S(1)} %get-tuple-element.47), channel_id=1, source_target_pairs={{0,1},{1,0},{2,3},{3,2},{4,5},{5,4},{6,7},{7,6},{8,9},{9,8},{10,11... | collective-permute-start | bytes 589832 | tf_op jit(solution)/shard_map/ppermute | solution.py:305
  5.7 2.6 %collective-permute-start.1 = (bf16[4,192,128]{2,1,0:T(8,128)(2,1)S(1)}, bf16[4,192,128]{2,1,0:T(8,128)(2,1)S(1)}, u32[]{:S(2)}, u32[]{:S(2)}) collective-permute-start(bf16[4,192,128]{2,1,0:T(8,128)(2,1)S(1)} %get-tuple-element.50), channel_id=1, source_target_pairs={{0,2},{1,3},{2,0},{3,1},{4,6},{5,7},{6,4},{7,5},{8,10},{9,11},{10,... | collective-permute-start | bytes 589832 | tf_op jit(solution)/shard_map/ppermute | solution.py:305
  8.3 0.0 collective-permute-start.2
  9.0 0.1 reshape.17
  9.1 0.1 reshape.16
  9.3 4.8 %collective-permute-done.refs_1_ = bf16[4,192,128]{2,1,0:T(8,128)(2,1)S(1)} collective-permute-done((bf16[4,192,128]{2,1,0:T(8,128)(2,1)S(1)}, bf16[4,192,128]{2,1,0:T(8,128)(2,1)S(1)}, u32[]{:S(2)}, u32[]{:S(2)}) %collective-permute-start) | collective-permute-done | bytes 196640 | tf_op jit(solution)/shard_map/ppermute | solution.py:305
  14.1 0.0 collective-permute-start.3
  14.1 8.9 %collective-permute-done.1.refs_2_ = bf16[4,192,128]{2,1,0:T(8,128)(2,1)S(1)} collective-permute-done((bf16[4,192,128]{2,1,0:T(8,128)(2,1)S(1)}, bf16[4,192,128]{2,1,0:T(8,128)(2,1)S(1)}, u32[]{:S(2)}, u32[]{:S(2)}) %collective-permute-start.1) | collective-permute-done | bytes 196640 | tf_op jit(solution)/shard_map/ppermute | solution.py:305
  22.9 0.0 collective-permute-done.2.refs_3_
  22.9 2.5 %collective-permute-start.5 = (bf16[4,192,128]{2,1,0:T(8,128)(2,1)S(1)}, bf16[4,192,128]{2,1,0:T(8,128)(2,1)S(1)}, u32[]{:S(2)}, u32[]{:S(2)}) collective-permute-start(bf16[4,192,128]{2,1,0:T(8,128)(2,1)S(1)} %get-tuple-element.59), channel_id=1, source_target_pairs={{0,3},{1,2},{2,1},{3,0},{4,7},{5,6},{6,5},{7,4},{8,11},{9,10},{10,... | collective-permute-start | bytes 589832 | tf_op jit(solution)/shard_map/ppermute | solution.py:305
  25.4 0.1 pad_add_fusion.scalars
  25.5 9.9 %shard_map.111 = (bf16[3,192,128]{2,1,0:T(8,128)(2,1)S(1)}, bf16[3,192,128]{2,1,0:T(8,128)(2,1)S(1)}, bf16[3,192,128]{2,1,0:T(8,128)(2,1)S(1)}, bf16[3,192,128]{2,1,0:T(8,128)(2,1)S(1)}, f32[2,32,96]{2,1,0:T(8,128)S(1)}) custom-call(s32[2]{0:T(128)S(1)} %pad_add_fusion.scalars, f32[2,31,96]{2,1,0:T(8,128)S(1)} %get-tuple-element.85.weight_ref, ...), custom_call_target="tpu_custom_call" | custom-call | flops 1207959552 | bytes 1376256 | tf_op jit(solution)/shard_map/pallas_call | solution.py:272
  35.4 12.4 %collective-permute-start.6 = (bf16[3,192,128]{2,1,0:T(8,128)(2,1)S(1)}, bf16[3,192,128]{2,1,0:T(8,128)(2,1)S(1)}, u32[]{:S(2)}, u32[]{:S(2)}) collective-permute-start(bf16[3,192,128]{2,1,0:T(8,128)(2,1)S(1)} %get-tuple-element.63), channel_id=1, source_target_pairs={{0,1},{1,0},{2,3},{3,2},{4,5},{5,4},{6,7},{7,6},{8,9},{9,8},{10,11... | collective-permute-start | bytes 442376 | tf_op jit(solution)/shard_map/ppermute | solution.py:305
  47.8 0.0 collective-permute-start.7
  47.8 2.4 %collective-permute-start.8 = (bf16[3,192,128]{2,1,0:T(8,128)(2,1)S(1)}, bf16[3,192,128]{2,1,0:T(8,128)(2,1)S(1)}, u32[]{:S(2)}, u32[]{:S(2)}) collective-permute-start(bf16[3,192,128]{2,1,0:T(8,128)(2,1)S(1)} %get-tuple-element.69), channel_id=1, source_target_pairs={{0,3},{1,2},{2,1},{3,0},{4,7},{5,6},{6,5},{7,4},{8,11},{9,10},{10,... | collective-permute-start | bytes 442376 | tf_op jit(solution)/shard_map/ppermute | solution.py:305
  50.2 9.9 %shard_map.112 = (bf16[3,192,128]{2,1,0:T(8,128)(2,1)S(1)}, bf16[3,192,128]{2,1,0:T(8,128)(2,1)S(1)}, bf16[3,192,128]{2,1,0:T(8,128)(2,1)S(1)}, bf16[3,192,128]{2,1,0:T(8,128)(2,1)S(1)}, f32[2,32,96]{2,1,0:T(8,128)S(1)}) custom-call(s32[2]{0:T(128)S(1)} %pad_add_fusion.scalars, f32[2,31,96]{2,1,0:T(8,128)S(1)} %get-tuple-element.86.weight_ref, ...), custom_call_target="tpu_custom_call" | custom-call | flops 1207959552 | bytes 1376256 | tf_op jit(solution)/shard_map/pallas_call | solution.py:272
  60.2 1.4 %collective-permute-done.7.refs_2_ = bf16[3,192,128]{2,1,0:T(8,128)(2,1)S(1)} collective-permute-done((bf16[3,192,128]{2,1,0:T(8,128)(2,1)S(1)}, bf16[3,192,128]{2,1,0:T(8,128)(2,1)S(1)}, u32[]{:S(2)}, u32[]{:S(2)}) %collective-permute-start.7) | collective-permute-done | bytes 147488 | tf_op jit(solution)/shard_map/ppermute | solution.py:305
  61.6 0.0 collective-permute-start.11
  61.6 5.2 %collective-permute-start.10 = (bf16[3,192,128]{2,1,0:T(8,128)(2,1)S(1)}, bf16[3,192,128]{2,1,0:T(8,128)(2,1)S(1)}, u32[]{:S(2)}, u32[]{:S(2)}) collective-permute-start(bf16[3,192,128]{2,1,0:T(8,128)(2,1)S(1)} %get-tuple-element.78), channel_id=1, source_target_pairs={{0,2},{1,3},{2,0},{3,1},{4,6},{5,7},{6,4},{7,5},{8,10},{9,11},{10,... | collective-permute-start | bytes 442376 | tf_op jit(solution)/shard_map/ppermute | solution.py:305
  66.8 9.9 %all-gather = f32[32,32,96]{2,1,0:T(8,128)S(1)} all-gather(f32[4,32,96]{2,1,0:T(8,128)S(1)} %pad_maximum_fusion), channel_id=2, replica_groups=mesh['dp'=8,'seq'=4] {'dp'}, dimensions={0}, use_global_device_ids=true | all-gather | bytes 442368 | tf_op jit(solution)/shard_map/all_gather | solution.py:332
  76.7 1.3 %shard_map.113 = (bf16[1,128,1536]{2,1,0:T(8,128)(2,1)}, bf16[1,128,1536]{2,1,0:T(8,128)(2,1)}, bf16[1,128,1536]{2,1,0:T(8,128)(2,1)}, f32[31,384]{1,0:T(8,128)}, f32[1,384]{1,0:T(1,128)S(1)}) custom-call(s32[1]{0:T(128)} %bitcast.rank_ref, f32[8,4,32,96]{3,2,1,0:T(8,128)S(1)} %bitcast.5, bf16[3,192,128]{2,1,0:T(8,128)(2,1)S(1)} %get-tuple-element.72.refs_0_, ...), custom_call_target="tpu_custom_call" | custom-call | bytes 2359296 | tf_op jit(solution)/shard_map/pallas_call | solution.py:95
  78.0 0.6 reduce
  (18 shorter events, 0.1 us)
Async XLA Ops:
  0.6 8.4 %copy-start = (f32[31,1536]{1,0:T(8,128)S(1)}, f32[31,1536]{1,0:T(8,128)}, u32[]{:S(2)}) copy-start(f32[31,1536]{1,0:T(8,128)} %param.11) | copy-start | bytes 571396
  2.6 6.4 %copy-start.1 = (f32[1536]{0:T(1024)S(1)}, f32[1536]{0:T(1024)}, u32[]{:S(2)}) copy-start(f32[1536]{0:T(1024)} %param.12) | copy-start | bytes 18436
  2.6 11.4 %collective-permute-start = (bf16[4,192,128]{2,1,0:T(8,128)(2,1)S(1)}, bf16[4,192,128]{2,1,0:T(8,128)(2,1)S(1)}, u32[]{:S(2)}, u32[]{:S(2)}) collective-permute-start(bf16[4,192,128]{2,1,0:T(8,128)(2,1)S(1)} %get-tuple-element.47), channel_id=1, source_target_pairs={{0,1},{1,0},{2,3},{3,2},{4,5},{5,4},{6,7},{7,6},{8,9},{9,8},{10,11... | collective-permute-start | bytes 589832 | tf_op jit(solution)/shard_map/ppermute | solution.py:305
  5.7 17.2 %collective-permute-start.1 = (bf16[4,192,128]{2,1,0:T(8,128)(2,1)S(1)}, bf16[4,192,128]{2,1,0:T(8,128)(2,1)S(1)}, u32[]{:S(2)}, u32[]{:S(2)}) collective-permute-start(bf16[4,192,128]{2,1,0:T(8,128)(2,1)S(1)} %get-tuple-element.50), channel_id=1, source_target_pairs={{0,2},{1,3},{2,0},{3,1},{4,6},{5,7},{6,4},{7,5},{8,10},{9,11},{10,... | collective-permute-start | bytes 589832 | tf_op jit(solution)/shard_map/ppermute | solution.py:305
  8.3 14.6 %collective-permute-start.2 = (bf16[4,192,128]{2,1,0:T(8,128)(2,1)S(1)}, bf16[4,192,128]{2,1,0:T(8,128)(2,1)S(1)}, u32[]{:S(2)}, u32[]{:S(2)}) collective-permute-start(bf16[4,192,128]{2,1,0:T(8,128)(2,1)S(1)} %get-tuple-element.53), channel_id=1, source_target_pairs={{0,3},{1,2},{2,1},{3,0},{4,7},{5,6},{6,5},{7,4},{8,11},{9,10},{10,... | collective-permute-start | bytes 589832 | tf_op jit(solution)/shard_map/ppermute | solution.py:305
  14.1 33.7 %collective-permute-start.3 = (bf16[4,192,128]{2,1,0:T(8,128)(2,1)S(1)}, bf16[4,192,128]{2,1,0:T(8,128)(2,1)S(1)}, u32[]{:S(2)}, u32[]{:S(2)}) collective-permute-start(bf16[4,192,128]{2,1,0:T(8,128)(2,1)S(1)} %get-tuple-element.57), channel_id=1, source_target_pairs={{0,1},{1,0},{2,3},{3,2},{4,5},{5,4},{6,7},{7,6},{8,9},{9,8},{10,11... | collective-permute-start | bytes 589832 | tf_op jit(solution)/shard_map/ppermute | solution.py:305
  22.9 27.3 %collective-permute-start.4 = (bf16[4,192,128]{2,1,0:T(8,128)(2,1)S(1)}, bf16[4,192,128]{2,1,0:T(8,128)(2,1)S(1)}, u32[]{:S(2)}, u32[]{:S(2)}) collective-permute-start(bf16[4,192,128]{2,1,0:T(8,128)(2,1)S(1)} %get-tuple-element.58), channel_id=1, source_target_pairs={{0,2},{1,3},{2,0},{3,1},{4,6},{5,7},{6,4},{7,5},{8,10},{9,11},{10,... | collective-permute-start | bytes 589832 | tf_op jit(solution)/shard_map/ppermute | solution.py:305
  22.9 27.3 %collective-permute-start.5 = (bf16[4,192,128]{2,1,0:T(8,128)(2,1)S(1)}, bf16[4,192,128]{2,1,0:T(8,128)(2,1)S(1)}, u32[]{:S(2)}, u32[]{:S(2)}) collective-permute-start(bf16[4,192,128]{2,1,0:T(8,128)(2,1)S(1)} %get-tuple-element.59), channel_id=1, source_target_pairs={{0,3},{1,2},{2,1},{3,0},{4,7},{5,6},{6,5},{7,4},{8,11},{9,10},{10,... | collective-permute-start | bytes 589832 | tf_op jit(solution)/shard_map/ppermute | solution.py:305
  35.4 24.8 %collective-permute-start.6 = (bf16[3,192,128]{2,1,0:T(8,128)(2,1)S(1)}, bf16[3,192,128]{2,1,0:T(8,128)(2,1)S(1)}, u32[]{:S(2)}, u32[]{:S(2)}) collective-permute-start(bf16[3,192,128]{2,1,0:T(8,128)(2,1)S(1)} %get-tuple-element.63), channel_id=1, source_target_pairs={{0,1},{1,0},{2,3},{3,2},{4,5},{5,4},{6,7},{7,6},{8,9},{9,8},{10,11... | collective-permute-start | bytes 442376 | tf_op jit(solution)/shard_map/ppermute | solution.py:305
  47.8 13.8 %collective-permute-start.7 = (bf16[3,192,128]{2,1,0:T(8,128)(2,1)S(1)}, bf16[3,192,128]{2,1,0:T(8,128)(2,1)S(1)}, u32[]{:S(2)}, u32[]{:S(2)}) collective-permute-start(bf16[3,192,128]{2,1,0:T(8,128)(2,1)S(1)} %get-tuple-element.66), channel_id=1, source_target_pairs={{0,2},{1,3},{2,0},{3,1},{4,6},{5,7},{6,4},{7,5},{8,10},{9,11},{10,... | collective-permute-start | bytes 442376 | tf_op jit(solution)/shard_map/ppermute | solution.py:305
  47.8 13.8 %collective-permute-start.8 = (bf16[3,192,128]{2,1,0:T(8,128)(2,1)S(1)}, bf16[3,192,128]{2,1,0:T(8,128)(2,1)S(1)}, u32[]{:S(2)}, u32[]{:S(2)}) collective-permute-start(bf16[3,192,128]{2,1,0:T(8,128)(2,1)S(1)} %get-tuple-element.69), channel_id=1, source_target_pairs={{0,3},{1,2},{2,1},{3,0},{4,7},{5,6},{6,5},{7,4},{8,11},{9,10},{10,... | collective-permute-start | bytes 442376 | tf_op jit(solution)/shard_map/ppermute | solution.py:305
  61.6 15.1 %collective-permute-start.11 = (bf16[3,192,128]{2,1,0:T(8,128)(2,1)S(1)}, bf16[3,192,128]{2,1,0:T(8,128)(2,1)S(1)}, u32[]{:S(2)}, u32[]{:S(2)}) collective-permute-start(bf16[3,192,128]{2,1,0:T(8,128)(2,1)S(1)} %get-tuple-element.79), channel_id=1, source_target_pairs={{0,3},{1,2},{2,1},{3,0},{4,7},{5,6},{6,5},{7,4},{8,11},{9,10},{10,... | collective-permute-start | bytes 442376 | tf_op jit(solution)/shard_map/ppermute | solution.py:305
  61.6 15.0 %collective-permute-start.10 = (bf16[3,192,128]{2,1,0:T(8,128)(2,1)S(1)}, bf16[3,192,128]{2,1,0:T(8,128)(2,1)S(1)}, u32[]{:S(2)}, u32[]{:S(2)}) collective-permute-start(bf16[3,192,128]{2,1,0:T(8,128)(2,1)S(1)} %get-tuple-element.78), channel_id=1, source_target_pairs={{0,2},{1,3},{2,0},{3,1},{4,6},{5,7},{6,4},{7,5},{8,10},{9,11},{10,... | collective-permute-start | bytes 442376 | tf_op jit(solution)/shard_map/ppermute | solution.py:305
  66.8 9.9 %collective-permute-start.9 = (bf16[3,192,128]{2,1,0:T(8,128)(2,1)S(1)}, bf16[3,192,128]{2,1,0:T(8,128)(2,1)S(1)}, u32[]{:S(2)}, u32[]{:S(2)}) collective-permute-start(bf16[3,192,128]{2,1,0:T(8,128)(2,1)S(1)} %get-tuple-element.77), channel_id=1, source_target_pairs={{0,1},{1,0},{2,3},{3,2},{4,5},{5,4},{6,7},{7,6},{8,9},{9,8},{10,11... | collective-permute-start | bytes 442376 | tf_op jit(solution)/shard_map/ppermute | solution.py:305
where the time goes:
time: 78.7 us; the launch traced here: 78.6 us
  starting transfers between devices  28.2 us (36%)
  Pallas kernels  23.1 us (29%)
  waiting for transfers between devices  15.1 us (19%)
  blocking collectives  9.86 us (13%)
  between operations  1.41 us (2%)
    ppermute x12, starting transfers between devices, exchanged(): moved.append(lax.ppermute(piece, 'seq', pairs))  28.2 us
    pallas_call x2, Pallas kernels, core(): pl.pallas_call(functools.partial(core_kernel, count, block), out_shape=(p...  19.9 us
    ppermute x12, waiting for transfers between devices, exchanged(): moved.append(lax.ppermute(piece, 'seq', pairs))  15.1 us
    all_gather x1, blocking collectives, on_device(): taps = lax.all_gather(taps, 'dp')  9.86 us
    pallas_call x1, Pallas kernels, pack(): pl.pallas_call(functools.partial(pack_kernel, count, chunks), out_shape=(...  1.96 us
  transfers between devices with their start and end apart: 12, of which 3 were waited for; matrix products, arithmetic and copies ran while one was open for 0% of the time, Pallas kernels for 25%

commit v1 on v0

--- a/solution.py
+++ b/solution.py
@@ -69,14 +69,15 @@
 
 
 def unpack_kernel(count, chunks, rank_ref, taps_ref, *refs):
-    pieces, outs, turned = refs[: count * chunks], refs[-6:-3], refs[-1]
-    weight_ref, bias_ref = refs[-3:-1]
+    pieces, outs = refs[: count * chunks], refs[-7:-4]
+    weight_ref, bias_ref, bias_row, turned = refs[-4:]
     taps = jnp.sum(taps_ref[...], axis=0)
     heads, _, depth = taps.shape
     for head in range(heads):
         at = slice(head * depth, (head + 1) * depth)
         weight_ref[:, at] = taps[head, :KERNEL]
-        bias_ref[:, at] = taps[head, KERNEL:]
+        bias_row[:, at] = taps[head, KERNEL:]
+    bias_ref[...] = bias_row[0]
     rank = rank_ref[0]
     high = pieces[0].shape[1]
     share = high * chunks
@@ -97,11 +98,14 @@
         out_shape=(whole,) * 3
         + (
             jax.ShapeDtypeStruct((KERNEL, width // count), f32),
-            jax.ShapeDtypeStruct((1, width // count), f32),
+            jax.ShapeDtypeStruct((width // count,), f32),
         ),
         in_specs=[SMEM] + [VMEM] * (1 + count * chunks),
         out_specs=(VMEM,) * 5,
-        scratch_shapes=[pltpu.VMEM((3, width, frames), bf16)],
+        scratch_shapes=[
+            pltpu.VMEM((1, width // count), f32),
+            pltpu.VMEM((3, width, frames), bf16),
+        ],
         compiler_params=pltpu.CompilerParams(vmem_limit_bytes=LIMIT),
         cost_estimate=pl.CostEstimate(
             flops=0, bytes_accessed=12 * frames * width, transcendentals=0
@@ -296,13 +300,14 @@
 def exchanged(parts):
     done = []
     for pieces in parts:
+        pieces = list(pieces)
+        if done and len(pieces) > 2:
+            pieces[2:], before = lax.optimization_barrier((pieces[2:], done[-1][1:]))
+            done[-1] = done[-1][:1] + list(before)
         moved = [pieces[0]]
         for distance in range(1, len(pieces)):
-            piece = pieces[distance]
-            if done:
-                piece, done[-1][distance] = lax.optimization_barrier((piece, done[-1][distance]))
             pairs = [(i, i ^ distance) for i in range(len(pieces))]
-            moved.append(lax.ppermute(piece, "seq", pairs))
+            moved.append(lax.ppermute(pieces[distance], "seq", pairs))
         done.append(moved)
     return done
 
@@ -330,10 +335,7 @@
     returned = exchanged(kept)
     taps, returned[0] = lax.optimization_barrier((jnp.concatenate(taps, axis=0), returned[0]))
     taps = lax.all_gather(taps, "dp")
-    query_grad, key_grad, value_grad, weight_grad, bias_grad = unpack(
-        rank[None], taps, returned, count, chunks
-    )
-    return query_grad, key_grad, value_grad, weight_grad, bias_grad[0]
+    return unpack(rank[None], taps, returned, count, chunks)
 
 
 def solution(mesh):

time: 78.7 us -> 75.5 us (0.959)
  starting transfers between devices: 28.2 us -> 26.5 us
  waiting for transfers between devices: 15.1 us -> 14.1 us
    ppermute x12, starting transfers between devices: 28.2 us -> 26.5 us  [exchanged(): moved.append(lax.ppermute(pieces[distance], 'seq', pairs))]
    ppermute x12, waiting for transfers between devices: 15.1 us -> 14.1 us  [exchanged(): moved.append(lax.ppermute(pieces[distance], 'seq', pairs))]
  transfers between devices with their start and end apart: 12 -> 12, of which waited for: 3 -> 3; matrix products, arithmetic and copies ran while one was open for 0% -> 0% of each run, Pallas kernels for 25% -> 26%
where the time goes in v1:
time: 75.5 us; the launch traced here: 75.3 us
  starting transfers between devices  26.5 us (35%)
  Pallas kernels  23.1 us (31%)
  waiting for transfers between devices  14.1 us (19%)
  blocking collectives  9.88 us (13%)
  between operations  1.42 us (2%)
    ppermute x12, starting transfers between devices, exchanged(): moved.append(lax.ppermute(pieces[distance], 'seq', pairs))  26.5 us
    pallas_call x2, Pallas kernels, core(): pl.pallas_call(functools.partial(core_kernel, count, block), out_shape=(p...  19.8 us
    ppermute x12, waiting for transfers between devices, exchanged(): moved.append(lax.ppermute(pieces[distance], 'seq', pairs))  14.1 us
    all_gather x1, blocking collectives, on_device(): taps = lax.all_gather(taps, 'dp')  9.88 us
    pallas_call x1, Pallas kernels, pack(): pl.pallas_call(functools.partial(pack_kernel, count, chunks), out_shape=(...  1.96 us
  transfers between devices with their start and end apart: 12, of which 3 were waited for; matrix products, arithmetic and copies ran while one was open for 0% of the time, Pallas kernels for 26%

profile of v1, /device:TPU:0, one launch (start us, length us, event | category | flops | bytes accessed | tf_op | source)
XLA Modules:
  0.0 75.3 jit_solution(6934283361406831428)
XLA Ops:
  0.6 2.0 %shard_map.110 = (bf16[4,192,128]{2,1,0:T(8,128)(2,1)S(1)}, bf16[4,192,128]{2,1,0:T(8,128)(2,1)S(1)}, bf16[4,192,128]{2,1,0:T(8,128)(2,1)S(1)}, bf16[4,192,128]{...) custom-call(s32[1]{0:T(128)} %bitcast.rank_ref, ...), custom_call_target="tpu_custom_call" | custom-call | bytes 3145728 | tf_op jit(solution)/shard_map/pallas_call | solution.py:53
  2.6 0.0 copy-start.1
  2.6 3.1 %collective-permute-start = (bf16[4,192,128]{2,1,0:T(8,128)(2,1)S(1)}, bf16[4,192,128]{2,1,0:T(8,128)(2,1)S(1)}, u32[]{:S(2)}, u32[]{:S(2)}) collective-permute-start(bf16[4,192,128]{2,1,0:T(8,128)(2,1)S(1)} %get-tuple-element.41), channel_id=1, source_target_pairs={{0,1},{1,0},{2,3},{3,2},{4,5},{5,4},{6,7},{7,6},{8,9},{9,8},{10,11... | collective-permute-start | bytes 589832 | tf_op jit(solution)/shard_map/ppermute | solution.py:310
  5.7 2.6 %collective-permute-start.1 = (bf16[4,192,128]{2,1,0:T(8,128)(2,1)S(1)}, bf16[4,192,128]{2,1,0:T(8,128)(2,1)S(1)}, u32[]{:S(2)}, u32[]{:S(2)}) collective-permute-start(bf16[4,192,128]{2,1,0:T(8,128)(2,1)S(1)} %get-tuple-element.42), channel_id=1, source_target_pairs={{0,2},{1,3},{2,0},{3,1},{4,6},{5,7},{6,4},{7,5},{8,10},{9,11},{10,... | collective-permute-start | bytes 589832 | tf_op jit(solution)/shard_map/ppermute | solution.py:310
  8.3 0.0 collective-permute-start.2
  8.3 0.9 %collective-permute-start.3 = (bf16[4,192,128]{2,1,0:T(8,128)(2,1)S(1)}, bf16[4,192,128]{2,1,0:T(8,128)(2,1)S(1)}, u32[]{:S(2)}, u32[]{:S(2)}) collective-permute-start(bf16[4,192,128]{2,1,0:T(8,128)(2,1)S(1)} %get-tuple-element.49), channel_id=1, source_target_pairs={{0,1},{1,0},{2,3},{3,2},{4,5},{5,4},{6,7},{7,6},{8,9},{9,8},{10,11... | collective-permute-start | bytes 589832 | tf_op jit(solution)/shard_map/ppermute | solution.py:310
  9.9 0.1 reshape.17
  10.0 0.1 reshape.16
  10.2 4.7 %collective-permute-done.refs_1_ = bf16[4,192,128]{2,1,0:T(8,128)(2,1)S(1)} collective-permute-done((bf16[4,192,128]{2,1,0:T(8,128)(2,1)S(1)}, bf16[4,192,128]{2,1,0:T(8,128)(2,1)S(1)}, u32[]{:S(2)}, u32[]{:S(2)}) %collective-permute-start) | collective-permute-done | bytes 196640 | tf_op jit(solution)/shard_map/ppermute | solution.py:310
  14.9 8.0 %collective-permute-done.1.refs_2_ = bf16[4,192,128]{2,1,0:T(8,128)(2,1)S(1)} collective-permute-done((bf16[4,192,128]{2,1,0:T(8,128)(2,1)S(1)}, bf16[4,192,128]{2,1,0:T(8,128)(2,1)S(1)}, u32[]{:S(2)}, u32[]{:S(2)}) %collective-permute-start.1) | collective-permute-done | bytes 196640 | tf_op jit(solution)/shard_map/ppermute | solution.py:310
  22.9 0.0 collective-permute-done.2.refs_3_
  22.9 4.4 %collective-permute-start.4 = (bf16[4,192,128]{2,1,0:T(8,128)(2,1)S(1)}, bf16[4,192,128]{2,1,0:T(8,128)(2,1)S(1)}, u32[]{:S(2)}, u32[]{:S(2)}) collective-permute-start(bf16[4,192,128]{2,1,0:T(8,128)(2,1)S(1)} %get-tuple-element.50), channel_id=1, source_target_pairs={{0,2},{1,3},{2,0},{3,1},{4,6},{5,7},{6,4},{7,5},{8,10},{9,11},{10,... | collective-permute-start | bytes 589832 | tf_op jit(solution)/shard_map/ppermute | solution.py:310
  27.3 1.3 %collective-permute-start.5 = (bf16[4,192,128]{2,1,0:T(8,128)(2,1)S(1)}, bf16[4,192,128]{2,1,0:T(8,128)(2,1)S(1)}, u32[]{:S(2)}, u32[]{:S(2)}) collective-permute-start(bf16[4,192,128]{2,1,0:T(8,128)(2,1)S(1)} %get-tuple-element.51), channel_id=1, source_target_pairs={{0,3},{1,2},{2,1},{3,0},{4,7},{5,6},{6,5},{7,4},{8,11},{9,10},{10,... | collective-permute-start | bytes 589832 | tf_op jit(solution)/shard_map/ppermute | solution.py:310
  28.6 0.1 pad_add_fusion.scalars
  28.7 9.9 %shard_map.111 = (bf16[3,192,128]{2,1,0:T(8,128)(2,1)S(1)}, bf16[3,192,128]{2,1,0:T(8,128)(2,1)S(1)}, bf16[3,192,128]{2,1,0:T(8,128)(2,1)S(1)}, bf16[3,192,128]{2,1,0:T(8,128)(2,1)S(1)}, f32[2,32,96]{2,1,0:T(8,128)S(1)}) custom-call(s32[2]{0:T(128)S(1)} %pad_add_fusion.scalars, f32[2,31,96]{2,1,0:T(8,128)S(1)} %get-tuple-element.71.weight_ref, ...), custom_call_target="tpu_custom_call" | custom-call | flops 1207959552 | bytes 1376256 | tf_op jit(solution)/shard_map/pallas_call | solution.py:276
  38.6 0.1 collective-permute-start.6
  38.7 3.0 %collective-permute-start.7 = (bf16[3,192,128]{2,1,0:T(8,128)(2,1)S(1)}, bf16[3,192,128]{2,1,0:T(8,128)(2,1)S(1)}, u32[]{:S(2)}, u32[]{:S(2)}) collective-permute-start(bf16[3,192,128]{2,1,0:T(8,128)(2,1)S(1)} %get-tuple-element.57), channel_id=1, source_target_pairs={{0,2},{1,3},{2,0},{3,1},{4,6},{5,7},{6,4},{7,5},{8,10},{9,11},{10,... | collective-permute-start | bytes 442376 | tf_op jit(solution)/shard_map/ppermute | solution.py:310
  41.8 1.3 %collective-permute-start.8 = (bf16[3,192,128]{2,1,0:T(8,128)(2,1)S(1)}, bf16[3,192,128]{2,1,0:T(8,128)(2,1)S(1)}, u32[]{:S(2)}, u32[]{:S(2)}) collective-permute-start(bf16[3,192,128]{2,1,0:T(8,128)(2,1)S(1)} %get-tuple-element.58), channel_id=1, source_target_pairs={{0,3},{1,2},{2,1},{3,0},{4,7},{5,6},{6,5},{7,4},{8,11},{9,10},{10,... | collective-permute-start | bytes 442376 | tf_op jit(solution)/shard_map/ppermute | solution.py:310
  43.1 9.9 %shard_map.112 = (bf16[3,192,128]{2,1,0:T(8,128)(2,1)S(1)}, bf16[3,192,128]{2,1,0:T(8,128)(2,1)S(1)}, bf16[3,192,128]{2,1,0:T(8,128)(2,1)S(1)}, bf16[3,192,128]{2,1,0:T(8,128)(2,1)S(1)}, f32[2,32,96]{2,1,0:T(8,128)S(1)}) custom-call(s32[2]{0:T(128)S(1)} %pad_add_fusion.scalars, f32[2,31,96]{2,1,0:T(8,128)S(1)} %get-tuple-element.72.weight_ref, ...), custom_call_target="tpu_custom_call" | custom-call | flops 1207959552 | bytes 1376256 | tf_op jit(solution)/shard_map/pallas_call | solution.py:276
  53.0 1.3 %collective-permute-done.7.refs_2_ = bf16[3,192,128]{2,1,0:T(8,128)(2,1)S(1)} collective-permute-done((bf16[3,192,128]{2,1,0:T(8,128)(2,1)S(1)}, bf16[3,192,128]{2,1,0:T(8,128)(2,1)S(1)}, u32[]{:S(2)}, u32[]{:S(2)}) %collective-permute-start.7) | collective-permute-done | bytes 147488 | tf_op jit(solution)/shard_map/ppermute | solution.py:310
  54.4 8.1 %collective-permute-start.10 = (bf16[3,192,128]{2,1,0:T(8,128)(2,1)S(1)}, bf16[3,192,128]{2,1,0:T(8,128)(2,1)S(1)}, u32[]{:S(2)}, u32[]{:S(2)}) collective-permute-start(bf16[3,192,128]{2,1,0:T(8,128)(2,1)S(1)} %get-tuple-element.69), channel_id=1, source_target_pairs={{0,2},{1,3},{2,0},{3,1},{4,6},{5,7},{6,4},{7,5},{8,10},{9,11},{10,... | collective-permute-start | bytes 442376 | tf_op jit(solution)/shard_map/ppermute | solution.py:310
  62.5 1.6 %collective-permute-start.11 = (bf16[3,192,128]{2,1,0:T(8,128)(2,1)S(1)}, bf16[3,192,128]{2,1,0:T(8,128)(2,1)S(1)}, u32[]{:S(2)}, u32[]{:S(2)}) collective-permute-start(bf16[3,192,128]{2,1,0:T(8,128)(2,1)S(1)} %get-tuple-element.70), channel_id=1, source_target_pairs={{0,3},{1,2},{2,1},{3,0},{4,7},{5,6},{6,5},{7,4},{8,11},{9,10},{10,... | collective-permute-start | bytes 442376 | tf_op jit(solution)/shard_map/ppermute | solution.py:310
  64.2 9.9 %all-gather = f32[32,32,96]{2,1,0:T(8,128)S(1)} all-gather(f32[4,32,96]{2,1,0:T(8,128)S(1)} %pad_maximum_fusion), channel_id=2, replica_groups=mesh['dp'=8,'seq'=4] {'dp'}, dimensions={0}, use_global_device_ids=true | all-gather | bytes 442368 | tf_op jit(solution)/shard_map/all_gather | solution.py:337
  74.1 1.3 %shard_map.113 = (bf16[1,128,1536]{2,1,0:T(8,128)(2,1)}, bf16[1,128,1536]{2,1,0:T(8,128)(2,1)}, bf16[1,128,1536]{2,1,0:T(8,128)(2,1)}, f32[31,384]{1,0:T(8,128)}, f32[384]{0:T(512)}) custom-call(s32[1]{0:T(128)} %bitcast.rank_ref, f32[8,4,32,96]{3,2,1,0:T(8,128)S(1)} %bitcast.5, bf16[3,192,128]{2,1,0:T(8,128)(2,1)S(1)} %get-tuple-element.63.refs_0_, ...), custom_call_target="tpu_custom_call" | custom-call | bytes 2359296 | tf_op jit(solution)/shard_map/pallas_call | solution.py:96
  (17 shorter events, 0.1 us)
Async XLA Ops:
  0.6 9.3 %copy-start = (f32[31,1536]{1,0:T(8,128)S(1)}, f32[31,1536]{1,0:T(8,128)}, u32[]{:S(2)}) copy-start(f32[31,1536]{1,0:T(8,128)} %param.11) | copy-start | bytes 571396
  2.6 7.2 %copy-start.1 = (f32[1536]{0:T(1024)S(1)}, f32[1536]{0:T(1024)}, u32[]{:S(2)}) copy-start(f32[1536]{0:T(1024)} %param.12) | copy-start | bytes 18436
  2.6 12.3 %collective-permute-start = (bf16[4,192,128]{2,1,0:T(8,128)(2,1)S(1)}, bf16[4,192,128]{2,1,0:T(8,128)(2,1)S(1)}, u32[]{:S(2)}, u32[]{:S(2)}) collective-permute-start(bf16[4,192,128]{2,1,0:T(8,128)(2,1)S(1)} %get-tuple-element.41), channel_id=1, source_target_pairs={{0,1},{1,0},{2,3},{3,2},{4,5},{5,4},{6,7},{7,6},{8,9},{9,8},{10,11... | collective-permute-start | bytes 589832 | tf_op jit(solution)/shard_map/ppermute | solution.py:310
  5.7 17.2 %collective-permute-start.1 = (bf16[4,192,128]{2,1,0:T(8,128)(2,1)S(1)}, bf16[4,192,128]{2,1,0:T(8,128)(2,1)S(1)}, u32[]{:S(2)}, u32[]{:S(2)}) collective-permute-start(bf16[4,192,128]{2,1,0:T(8,128)(2,1)S(1)} %get-tuple-element.42), channel_id=1, source_target_pairs={{0,2},{1,3},{2,0},{3,1},{4,6},{5,7},{6,4},{7,5},{8,10},{9,11},{10,... | collective-permute-start | bytes 589832 | tf_op jit(solution)/shard_map/ppermute | solution.py:310
  8.3 14.6 %collective-permute-start.2 = (bf16[4,192,128]{2,1,0:T(8,128)(2,1)S(1)}, bf16[4,192,128]{2,1,0:T(8,128)(2,1)S(1)}, u32[]{:S(2)}, u32[]{:S(2)}) collective-permute-start(bf16[4,192,128]{2,1,0:T(8,128)(2,1)S(1)} %get-tuple-element.43), channel_id=1, source_target_pairs={{0,3},{1,2},{2,1},{3,0},{4,7},{5,6},{6,5},{7,4},{8,11},{9,10},{10,... | collective-permute-start | bytes 589832 | tf_op jit(solution)/shard_map/ppermute | solution.py:310
  8.3 33.4 %collective-permute-start.3 = (bf16[4,192,128]{2,1,0:T(8,128)(2,1)S(1)}, bf16[4,192,128]{2,1,0:T(8,128)(2,1)S(1)}, u32[]{:S(2)}, u32[]{:S(2)}) collective-permute-start(bf16[4,192,128]{2,1,0:T(8,128)(2,1)S(1)} %get-tuple-element.49), channel_id=1, source_target_pairs={{0,1},{1,0},{2,3},{3,2},{4,5},{5,4},{6,7},{7,6},{8,9},{9,8},{10,11... | collective-permute-start | bytes 589832 | tf_op jit(solution)/shard_map/ppermute | solution.py:310
  22.9 20.2 %collective-permute-start.4 = (bf16[4,192,128]{2,1,0:T(8,128)(2,1)S(1)}, bf16[4,192,128]{2,1,0:T(8,128)(2,1)S(1)}, u32[]{:S(2)}, u32[]{:S(2)}) collective-permute-start(bf16[4,192,128]{2,1,0:T(8,128)(2,1)S(1)} %get-tuple-element.50), channel_id=1, source_target_pairs={{0,2},{1,3},{2,0},{3,1},{4,6},{5,7},{6,4},{7,5},{8,10},{9,11},{10,... | collective-permute-start | bytes 589832 | tf_op jit(solution)/shard_map/ppermute | solution.py:310
  27.3 15.8 %collective-permute-start.5 = (bf16[4,192,128]{2,1,0:T(8,128)(2,1)S(1)}, bf16[4,192,128]{2,1,0:T(8,128)(2,1)S(1)}, u32[]{:S(2)}, u32[]{:S(2)}) collective-permute-start(bf16[4,192,128]{2,1,0:T(8,128)(2,1)S(1)} %get-tuple-element.51), channel_id=1, source_target_pairs={{0,3},{1,2},{2,1},{3,0},{4,7},{5,6},{6,5},{7,4},{8,11},{9,10},{10,... | collective-permute-start | bytes 589832 | tf_op jit(solution)/shard_map/ppermute | solution.py:310
  38.6 14.4 %collective-permute-start.6 = (bf16[3,192,128]{2,1,0:T(8,128)(2,1)S(1)}, bf16[3,192,128]{2,1,0:T(8,128)(2,1)S(1)}, u32[]{:S(2)}, u32[]{:S(2)}) collective-permute-start(bf16[3,192,128]{2,1,0:T(8,128)(2,1)S(1)} %get-tuple-element.56), channel_id=1, source_target_pairs={{0,1},{1,0},{2,3},{3,2},{4,5},{5,4},{6,7},{7,6},{8,9},{9,8},{10,11... | collective-permute-start | bytes 442376 | tf_op jit(solution)/shard_map/ppermute | solution.py:310
  38.7 15.7 %collective-permute-start.7 = (bf16[3,192,128]{2,1,0:T(8,128)(2,1)S(1)}, bf16[3,192,128]{2,1,0:T(8,128)(2,1)S(1)}, u32[]{:S(2)}, u32[]{:S(2)}) collective-permute-start(bf16[3,192,128]{2,1,0:T(8,128)(2,1)S(1)} %get-tuple-element.57), channel_id=1, source_target_pairs={{0,2},{1,3},{2,0},{3,1},{4,6},{5,7},{6,4},{7,5},{8,10},{9,11},{10,... | collective-permute-start | bytes 442376 | tf_op jit(solution)/shard_map/ppermute | solution.py:310
  41.8 12.6 %collective-permute-start.8 = (bf16[3,192,128]{2,1,0:T(8,128)(2,1)S(1)}, bf16[3,192,128]{2,1,0:T(8,128)(2,1)S(1)}, u32[]{:S(2)}, u32[]{:S(2)}) collective-permute-start(bf16[3,192,128]{2,1,0:T(8,128)(2,1)S(1)} %get-tuple-element.58), channel_id=1, source_target_pairs={{0,3},{1,2},{2,1},{3,0},{4,7},{5,6},{6,5},{7,4},{8,11},{9,10},{10,... | collective-permute-start | bytes 442376 | tf_op jit(solution)/shard_map/ppermute | solution.py:310
  54.4 19.7 %collective-permute-start.10 = (bf16[3,192,128]{2,1,0:T(8,128)(2,1)S(1)}, bf16[3,192,128]{2,1,0:T(8,128)(2,1)S(1)}, u32[]{:S(2)}, u32[]{:S(2)}) collective-permute-start(bf16[3,192,128]{2,1,0:T(8,128)(2,1)S(1)} %get-tuple-element.69), channel_id=1, source_target_pairs={{0,2},{1,3},{2,0},{3,1},{4,6},{5,7},{6,4},{7,5},{8,10},{9,11},{10,... | collective-permute-start | bytes 442376 | tf_op jit(solution)/shard_map/ppermute | solution.py:310
  62.5 11.5 %collective-permute-start.11 = (bf16[3,192,128]{2,1,0:T(8,128)(2,1)S(1)}, bf16[3,192,128]{2,1,0:T(8,128)(2,1)S(1)}, u32[]{:S(2)}, u32[]{:S(2)}) collective-permute-start(bf16[3,192,128]{2,1,0:T(8,128)(2,1)S(1)} %get-tuple-element.70), channel_id=1, source_target_pairs={{0,3},{1,2},{2,1},{3,0},{4,7},{5,6},{6,5},{7,4},{8,11},{9,10},{10,... | collective-permute-start | bytes 442376 | tf_op jit(solution)/shard_map/ppermute | solution.py:310
  64.2 9.9 %collective-permute-start.9 = (bf16[3,192,128]{2,1,0:T(8,128)(2,1)S(1)}, bf16[3,192,128]{2,1,0:T(8,128)(2,1)S(1)}, u32[]{:S(2)}, u32[]{:S(2)}) collective-permute-start(bf16[3,192,128]{2,1,0:T(8,128)(2,1)S(1)} %get-tuple-element.68), channel_id=1, source_target_pairs={{0,1},{1,0},{2,3},{3,2},{4,5},{5,4},{6,7},{7,6},{8,9},{9,8},{10,11... | collective-permute-start | bytes 442376 | tf_op jit(solution)/shard_map/ppermute | solution.py:310

commit v2 on v1

--- a/solution.py
+++ b/solution.py
@@ -115,7 +115,8 @@
 
 def core_kernel(count, block, scalars, weight_ref, bias_ref, *refs):
     pieces, outs, taps_ref = refs[:count], refs[count : 2 * count], refs[2 * count]
-    q_t, k_t, v_t, a_t, q_n, k_n, v_n, g_n, a_n, probs, shifted, pre_grad = refs[2 * count + 1 :]
+    q_t, k_t, v_t, a_t, q_n, k_n, v_n, g_n, a_n = refs[2 * count + 1 : -7]
+    probs, norm, low, diff, score_grads, shifted, pre_grad = refs[-7:]
     heads, rows, depth = q_n.shape
     frames = pieces[0].shape[2]
     blocks = rows // block
@@ -137,17 +138,39 @@
             v_n[head, at, :] = piece[2, span(head), :].T
             g_n[head, at, :] = piece[3, span(head), :].T
 
+    tile, strip = 128, 256
+    tiles = [slice(first, first + tile) for first in range(0, rows, tile)]
+
+    def strips(index):
+        for first in range(0, block, strip):
+            cols = pl.ds(pl.multiple_of(index * block + first, strip), strip)
+            yield index * block + first, cols, slice(first, first + strip)
+
+    def folded(array):
+        return array.reshape(tile // 8, 8, strip)
+
     def forward(index, head):
-        cols = pl.ds(pl.multiple_of(index * block, block), block)
-        scores = jnp.dot(k_n[head], q_t[span(head), cols], preferred_element_type=f32)
-        key_at = lax.broadcasted_iota(jnp.int32, scores.shape, 0)
-        scores = jnp.where(key_at < length, scores, masked_score)
-        exped = jnp.exp2((scores - jnp.max(scores, axis=0, keepdims=True)) * log_scale)
-        found = exped * (1.0 / jnp.sum(exped, axis=0, keepdims=True))
-        probs[head, :, cols] = found
-        out = jnp.dot(v_t[span(head), :], found.astype(bf16), preferred_element_type=f32)
-        frame_at = index * block + lax.broadcasted_iota(jnp.int32, out.shape, 1)
-        a_t[span(head), cols] = jnp.where(frame_at < length, out, 0.0).astype(bf16)
+        for start, cols, inner in strips(index):
+            queries = q_t[span(head), cols]
+            top = jnp.full((8, strip), masked_score, f32)
+            for at in tiles:
+                scores = jnp.dot(k_n[head, at, :], queries, preferred_element_type=f32)
+                key_at = at.start + lax.broadcasted_iota(jnp.int32, scores.shape, 0)
+                scores = jnp.where(key_at < length, scores, masked_score)
+                probs[head, at, cols] = scores
+                top = jnp.maximum(top, jnp.max(folded(scores), axis=0))
+            top = jnp.max(top, axis=0, keepdims=True)
+            total = jnp.zeros((8, strip), f32)
+            for at in tiles:
+                exped = jnp.exp2((probs[head, at, cols] - top) * log_scale)
+                probs[head, at, cols] = exped
+                low[at, inner] = exped.astype(bf16)
+                total = total + jnp.sum(folded(exped), axis=0)
+            inverse = 1.0 / jnp.sum(total, axis=0, keepdims=True)
+            norm[head, :, cols] = inverse
+            out = jnp.dot(v_t[span(head), :], low[:, inner], preferred_element_type=f32) * inverse
+            frame_at = start + lax.broadcasted_iota(jnp.int32, out.shape, 1)
+            a_t[span(head), cols] = jnp.where(frame_at < length, out, 0.0).astype(bf16)
 
     def each_block(body):
         if blocks == 1:
@@ -227,14 +250,23 @@
             a_t[span(head), first : first + frames] = a_n[head, first : first + frames, :].T
 
     def backward(index, head):
+        for start, cols, inner in strips(index):
+            inverse = norm[head, :, cols]
+            grads = a_t[span(head), cols]
+            total = jnp.zeros((8, strip), f32)
+            for at in tiles:
+                score_grad = jnp.dot(v_n[head, at, :], grads, preferred_element_type=f32)
+                score_grads[at, inner] = score_grad
+                total = total + jnp.sum(folded(probs[head, at, cols] * score_grad), axis=0)
+            delta = jnp.sum(total, axis=0, keepdims=True) * inverse
+            for at in tiles:
+                found = probs[head, at, cols] * inverse
+                low[at, inner] = found.astype(bf16)
+                diff[at, inner] = (found * (score_grads[at, inner] - delta)).astype(bf16)
         cols = pl.ds(pl.multiple_of(index * block, block), block)
-        score_grad = jnp.dot(v_n[head], a_t[span(head), cols], preferred_element_type=f32)
-        found = probs[head, :, cols]
-        delta = jnp.sum(found * score_grad, axis=0, keepdims=True)
-        diff = (found * (score_grad - delta)).astype(bf16)
-        value = jnp.dot(found.astype(bf16), a_n[head, cols, :], preferred_element_type=f32)
-        key = jnp.dot(diff, q_n[head, cols, :], preferred_element_type=f32)
-        query = jnp.dot(k_t[span(head), :], diff, preferred_element_type=f32)
+        value = jnp.dot(low[...], a_n[head, cols, :], preferred_element_type=f32)
+        key = jnp.dot(diff[...], q_n[head, cols, :], preferred_element_type=f32)
+        query = jnp.dot(k_t[span(head), :], diff[...], preferred_element_type=f32)
         q_t[span(head), cols] = (query * scale).astype(bf16)
         return key, value
 
@@ -282,6 +314,10 @@
         + [plain] * 5
         + [
             pltpu.VMEM((heads, rows, rows), f32),
+            pltpu.VMEM((heads, 1, rows), f32),
+            pltpu.VMEM((rows, block), bf16),
+            pltpu.VMEM((rows, block), bf16),
+            pltpu.VMEM((rows, block), f32),
             pltpu.VMEM((8, tall, depth), f32),
             pltpu.VMEM((rows, depth), f32),
         ],
@@ -302,7 +338,7 @@
     for pieces in parts:
         pieces = list(pieces)
         if done and len(pieces) > 2:
-            pieces[2:], before = lax.optimization_barrier((pieces[2:], done[-1][1:]))
+            pieces[1:-1], before = lax.optimization_barrier((pieces[1:-1], done[-1][1:]))
             done[-1] = done[-1][:1] + list(before)
         moved = [pieces[0]]
         for distance in range(1, len(pieces)):

time: 75.5 us -> 73.7 us (0.976)
  starting transfers between devices: 26.5 us -> 24.3 us
    ppermute x12, starting transfers between devices: 26.5 us -> 24.3 us  [exchanged(): moved.append(lax.ppermute(pieces[distance], 'seq', pairs))]
  transfers between devices with their start and end apart: 12 -> 12, of which waited for: 3 -> 2; matrix products, arithmetic and copies ran while one was open for 0% -> 0% of each run, Pallas kernels for 26% -> 28%
where the time goes in v2:
time: 73.7 us; the launch traced here: 73.5 us
  starting transfers between devices  24.3 us (33%)
  Pallas kernels  23.6 us (32%)
  waiting for transfers between devices  14 us (19%)
  blocking collectives  9.87 us (13%)
  between operations  1.42 us (2%)
    ppermute x12, starting transfers between devices, exchanged(): moved.append(lax.ppermute(pieces[distance], 'seq', pairs))  24.3 us
    pallas_call x2, Pallas kernels, core(): pl.pallas_call(functools.partial(core_kernel, count, block), out_shape=(p...  20.4 us
    ppermute x12, waiting for transfers between devices, exchanged(): moved.append(lax.ppermute(pieces[distance], 'seq', pairs))  14 us
    all_gather x1, blocking collectives, on_device(): taps = lax.all_gather(taps, 'dp')  9.87 us
    pallas_call x1, Pallas kernels, pack(): pl.pallas_call(functools.partial(pack_kernel, count, chunks), out_shape=(...  1.96 us
  transfers between devices with their start and end apart: 12, of which 2 were waited for; matrix products, arithmetic and copies ran while one was open for 0% of the time, Pallas kernels for 28%

profile of v2, /device:TPU:0, one launch (start us, length us, event | category | flops | bytes accessed | tf_op | source)
XLA Modules:
  0.0 73.5 jit_solution(16992263973869704140)
XLA Ops:
  0.6 2.0 %shard_map.110 = (bf16[4,192,128]{2,1,0:T(8,128)(2,1)S(1)}, bf16[4,192,128]{2,1,0:T(8,128)(2,1)S(1)}, bf16[4,192,128]{2,1,0:T(8,128)(2,1)S(1)}, bf16[4,192,128]{...) custom-call(s32[1]{0:T(128)} %bitcast.rank_ref, ...), custom_call_target="tpu_custom_call" | custom-call | bytes 3145728 | tf_op jit(solution)/shard_map/pallas_call | solution.py:53
  2.6 0.0 copy-start.1
  2.6 3.1 %collective-permute-start = (bf16[4,192,128]{2,1,0:T(8,128)(2,1)S(1)}, bf16[4,192,128]{2,1,0:T(8,128)(2,1)S(1)}, u32[]{:S(2)}, u32[]{:S(2)}) collective-permute-start(bf16[4,192,128]{2,1,0:T(8,128)(2,1)S(1)} %get-tuple-element.41), channel_id=1, source_target_pairs={{0,1},{1,0},{2,3},{3,2},{4,5},{5,4},{6,7},{7,6},{8,9},{9,8},{10,11... | collective-permute-start | bytes 589832 | tf_op jit(solution)/shard_map/ppermute | solution.py:346
  5.7 2.6 %collective-permute-start.1 = (bf16[4,192,128]{2,1,0:T(8,128)(2,1)S(1)}, bf16[4,192,128]{2,1,0:T(8,128)(2,1)S(1)}, u32[]{:S(2)}, u32[]{:S(2)}) collective-permute-start(bf16[4,192,128]{2,1,0:T(8,128)(2,1)S(1)} %get-tuple-element.42), channel_id=1, source_target_pairs={{0,2},{1,3},{2,0},{3,1},{4,6},{5,7},{6,4},{7,5},{8,10},{9,11},{10,... | collective-permute-start | bytes 589832 | tf_op jit(solution)/shard_map/ppermute | solution.py:346
  8.3 0.0 collective-permute-start.2
  8.3 3.8 %collective-permute-start.5 = (bf16[4,192,128]{2,1,0:T(8,128)(2,1)S(1)}, bf16[4,192,128]{2,1,0:T(8,128)(2,1)S(1)}, u32[]{:S(2)}, u32[]{:S(2)}) collective-permute-start(bf16[4,192,128]{2,1,0:T(8,128)(2,1)S(1)} %get-tuple-element.51), channel_id=1, source_target_pairs={{0,3},{1,2},{2,1},{3,0},{4,7},{5,6},{6,5},{7,4},{8,11},{9,10},{10,... | collective-permute-start | bytes 589832 | tf_op jit(solution)/shard_map/ppermute | solution.py:346
  12.8 0.1 reshape.17
  12.9 0.1 reshape.16
  13.1 1.0 %collective-permute-done.refs_1_ = bf16[4,192,128]{2,1,0:T(8,128)(2,1)S(1)} collective-permute-done((bf16[4,192,128]{2,1,0:T(8,128)(2,1)S(1)}, bf16[4,192,128]{2,1,0:T(8,128)(2,1)S(1)}, u32[]{:S(2)}, u32[]{:S(2)}) %collective-permute-start) | collective-permute-done | bytes 196640 | tf_op jit(solution)/shard_map/ppermute | solution.py:346
  14.1 13.0 %collective-permute-done.1.refs_2_ = bf16[4,192,128]{2,1,0:T(8,128)(2,1)S(1)} collective-permute-done((bf16[4,192,128]{2,1,0:T(8,128)(2,1)S(1)}, bf16[4,192,128]{2,1,0:T(8,128)(2,1)S(1)}, u32[]{:S(2)}, u32[]{:S(2)}) %collective-permute-start.1) | collective-permute-done | bytes 196640 | tf_op jit(solution)/shard_map/ppermute | solution.py:346
  27.1 4.8 %collective-permute-start.3 = (bf16[4,192,128]{2,1,0:T(8,128)(2,1)S(1)}, bf16[4,192,128]{2,1,0:T(8,128)(2,1)S(1)}, u32[]{:S(2)}, u32[]{:S(2)}) collective-permute-start(bf16[4,192,128]{2,1,0:T(8,128)(2,1)S(1)} %get-tuple-element.49), channel_id=1, source_target_pairs={{0,1},{1,0},{2,3},{3,2},{4,5},{5,4},{6,7},{7,6},{8,9},{9,8},{10,11... | collective-permute-start | bytes 589832 | tf_op jit(solution)/shard_map/ppermute | solution.py:346
  31.9 1.0 %collective-permute-start.4 = (bf16[4,192,128]{2,1,0:T(8,128)(2,1)S(1)}, bf16[4,192,128]{2,1,0:T(8,128)(2,1)S(1)}, u32[]{:S(2)}, u32[]{:S(2)}) collective-permute-start(bf16[4,192,128]{2,1,0:T(8,128)(2,1)S(1)} %get-tuple-element.50), channel_id=1, source_target_pairs={{0,2},{1,3},{2,0},{3,1},{4,6},{5,7},{6,4},{7,5},{8,10},{9,11},{10,... | collective-permute-start | bytes 589832 | tf_op jit(solution)/shard_map/ppermute | solution.py:346
  32.9 0.1 pad_add_fusion.scalars
  33.0 10.1 %shard_map.111 = (bf16[3,192,128]{2,1,0:T(8,128)(2,1)S(1)}, bf16[3,192,128]{2,1,0:T(8,128)(2,1)S(1)}, bf16[3,192,128]{2,1,0:T(8,128)(2,1)S(1)}, bf16[3,192,128]{2,1,0:T(8,128)(2,1)S(1)}, f32[2,32,96]{2,1,0:T(8,128)S(1)}) custom-call(s32[2]{0:T(128)S(1)} %pad_add_fusion.scalars, f32[2,31,96]{2,1,0:T(8,128)S(1)} %get-tuple-element.71.weight_ref, ...), custom_call_target="tpu_custom_call" | custom-call | flops 1207959552 | bytes 1376256 | tf_op jit(solution)/shard_map/pallas_call | solution.py:308
  43.1 2.1 %collective-permute-start.6 = (bf16[3,192,128]{2,1,0:T(8,128)(2,1)S(1)}, bf16[3,192,128]{2,1,0:T(8,128)(2,1)S(1)}, u32[]{:S(2)}, u32[]{:S(2)}) collective-permute-start(bf16[3,192,128]{2,1,0:T(8,128)(2,1)S(1)} %get-tuple-element.56), channel_id=1, source_target_pairs={{0,1},{1,0},{2,3},{3,2},{4,5},{5,4},{6,7},{7,6},{8,9},{9,8},{10,11... | collective-permute-start | bytes 442376 | tf_op jit(solution)/shard_map/ppermute | solution.py:346
  45.2 2.4 %collective-permute-start.8 = (bf16[3,192,128]{2,1,0:T(8,128)(2,1)S(1)}, bf16[3,192,128]{2,1,0:T(8,128)(2,1)S(1)}, u32[]{:S(2)}, u32[]{:S(2)}) collective-permute-start(bf16[3,192,128]{2,1,0:T(8,128)(2,1)S(1)} %get-tuple-element.58), channel_id=1, source_target_pairs={{0,3},{1,2},{2,1},{3,0},{4,7},{5,6},{6,5},{7,4},{8,11},{9,10},{10,... | collective-permute-start | bytes 442376 | tf_op jit(solution)/shard_map/ppermute | solution.py:346
  47.6 0.0 collective-permute-done.3.refs_1_
  47.6 0.0 collective-permute-done.4.refs_2_
  47.6 10.2 %shard_map.112 = (bf16[3,192,128]{2,1,0:T(8,128)(2,1)S(1)}, bf16[3,192,128]{2,1,0:T(8,128)(2,1)S(1)}, bf16[3,192,128]{2,1,0:T(8,128)(2,1)S(1)}, bf16[3,192,128]{2,1,0:T(8,128)(2,1)S(1)}, f32[2,32,96]{2,1,0:T(8,128)S(1)}) custom-call(s32[2]{0:T(128)S(1)} %pad_add_fusion.scalars, f32[2,31,96]{2,1,0:T(8,128)S(1)} %get-tuple-element.72.weight_ref, ...), custom_call_target="tpu_custom_call" | custom-call | flops 1207959552 | bytes 1376256 | tf_op jit(solution)/shard_map/pallas_call | solution.py:308
  57.9 1.1 %collective-permute-start.9 = (bf16[3,192,128]{2,1,0:T(8,128)(2,1)S(1)}, bf16[3,192,128]{2,1,0:T(8,128)(2,1)S(1)}, u32[]{:S(2)}, u32[]{:S(2)}) collective-permute-start(bf16[3,192,128]{2,1,0:T(8,128)(2,1)S(1)} %get-tuple-element.68), channel_id=1, source_target_pairs={{0,1},{1,0},{2,3},{3,2},{4,5},{5,4},{6,7},{7,6},{8,9},{9,8},{10,11... | collective-permute-start | bytes 442376 | tf_op jit(solution)/shard_map/ppermute | solution.py:346
  59.0 0.9 %collective-permute-start.10 = (bf16[3,192,128]{2,1,0:T(8,128)(2,1)S(1)}, bf16[3,192,128]{2,1,0:T(8,128)(2,1)S(1)}, u32[]{:S(2)}, u32[]{:S(2)}) collective-permute-start(bf16[3,192,128]{2,1,0:T(8,128)(2,1)S(1)} %get-tuple-element.69), channel_id=1, source_target_pairs={{0,2},{1,3},{2,0},{3,1},{4,6},{5,7},{6,4},{7,5},{8,10},{9,11},{10,... | collective-permute-start | bytes 442376 | tf_op jit(solution)/shard_map/ppermute | solution.py:346
  59.9 2.4 %collective-permute-start.11 = (bf16[3,192,128]{2,1,0:T(8,128)(2,1)S(1)}, bf16[3,192,128]{2,1,0:T(8,128)(2,1)S(1)}, u32[]{:S(2)}, u32[]{:S(2)}) collective-permute-start(bf16[3,192,128]{2,1,0:T(8,128)(2,1)S(1)} %get-tuple-element.70), channel_id=1, source_target_pairs={{0,3},{1,2},{2,1},{3,0},{4,7},{5,6},{6,5},{7,4},{8,11},{9,10},{10,... | collective-permute-start | bytes 442376 | tf_op jit(solution)/shard_map/ppermute | solution.py:346
  62.4 9.9 %all-gather = f32[32,32,96]{2,1,0:T(8,128)S(1)} all-gather(f32[4,32,96]{2,1,0:T(8,128)S(1)} %pad_maximum_fusion), channel_id=2, replica_groups=mesh['dp'=8,'seq'=4] {'dp'}, dimensions={0}, use_global_device_ids=true | all-gather | bytes 442368 | tf_op jit(solution)/shard_map/all_gather | solution.py:373
  72.2 1.3 %shard_map.113 = (bf16[1,128,1536]{2,1,0:T(8,128)(2,1)}, bf16[1,128,1536]{2,1,0:T(8,128)(2,1)}, bf16[1,128,1536]{2,1,0:T(8,128)(2,1)}, f32[31,384]{1,0:T(8,128)}, f32[384]{0:T(512)}) custom-call(s32[1]{0:T(128)} %bitcast.rank_ref, f32[8,4,32,96]{3,2,1,0:T(8,128)S(1)} %bitcast.5, bf16[3,192,128]{2,1,0:T(8,128)(2,1)S(1)} %get-tuple-element.63.refs_0_, ...), custom_call_target="tpu_custom_call" | custom-call | bytes 2359296 | tf_op jit(solution)/shard_map/pallas_call | solution.py:96
  (17 shorter events, 0.1 us)
Async XLA Ops:
  0.6 12.3 %copy-start = (f32[31,1536]{1,0:T(8,128)S(1)}, f32[31,1536]{1,0:T(8,128)}, u32[]{:S(2)}) copy-start(f32[31,1536]{1,0:T(8,128)} %param.11) | copy-start | bytes 571396
  2.6 10.2 %copy-start.1 = (f32[1536]{0:T(1024)S(1)}, f32[1536]{0:T(1024)}, u32[]{:S(2)}) copy-start(f32[1536]{0:T(1024)} %param.12) | copy-start | bytes 18436
  2.6 11.4 %collective-permute-start = (bf16[4,192,128]{2,1,0:T(8,128)(2,1)S(1)}, bf16[4,192,128]{2,1,0:T(8,128)(2,1)S(1)}, u32[]{:S(2)}, u32[]{:S(2)}) collective-permute-start(bf16[4,192,128]{2,1,0:T(8,128)(2,1)S(1)} %get-tuple-element.41), channel_id=1, source_target_pairs={{0,1},{1,0},{2,3},{3,2},{4,5},{5,4},{6,7},{7,6},{8,9},{9,8},{10,11... | collective-permute-start | bytes 589832 | tf_op jit(solution)/shard_map/ppermute | solution.py:346
  5.7 21.4 %collective-permute-start.1 = (bf16[4,192,128]{2,1,0:T(8,128)(2,1)S(1)}, bf16[4,192,128]{2,1,0:T(8,128)(2,1)S(1)}, u32[]{:S(2)}, u32[]{:S(2)}) collective-permute-start(bf16[4,192,128]{2,1,0:T(8,128)(2,1)S(1)} %get-tuple-element.42), channel_id=1, source_target_pairs={{0,2},{1,3},{2,0},{3,1},{4,6},{5,7},{6,4},{7,5},{8,10},{9,11},{10,... | collective-permute-start | bytes 589832 | tf_op jit(solution)/shard_map/ppermute | solution.py:346
  8.3 18.8 %collective-permute-start.2 = (bf16[4,192,128]{2,1,0:T(8,128)(2,1)S(1)}, bf16[4,192,128]{2,1,0:T(8,128)(2,1)S(1)}, u32[]{:S(2)}, u32[]{:S(2)}) collective-permute-start(bf16[4,192,128]{2,1,0:T(8,128)(2,1)S(1)} %get-tuple-element.43), channel_id=1, source_target_pairs={{0,3},{1,2},{2,1},{3,0},{4,7},{5,6},{6,5},{7,4},{8,11},{9,10},{10,... | collective-permute-start | bytes 589832 | tf_op jit(solution)/shard_map/ppermute | solution.py:346
  8.3 36.9 %collective-permute-start.5 = (bf16[4,192,128]{2,1,0:T(8,128)(2,1)S(1)}, bf16[4,192,128]{2,1,0:T(8,128)(2,1)S(1)}, u32[]{:S(2)}, u32[]{:S(2)}) collective-permute-start(bf16[4,192,128]{2,1,0:T(8,128)(2,1)S(1)} %get-tuple-element.51), channel_id=1, source_target_pairs={{0,3},{1,2},{2,1},{3,0},{4,7},{5,6},{6,5},{7,4},{8,11},{9,10},{10,... | collective-permute-start | bytes 589832 | tf_op jit(solution)/shard_map/ppermute | solution.py:346
  27.1 20.5 %collective-permute-start.3 = (bf16[4,192,128]{2,1,0:T(8,128)(2,1)S(1)}, bf16[4,192,128]{2,1,0:T(8,128)(2,1)S(1)}, u32[]{:S(2)}, u32[]{:S(2)}) collective-permute-start(bf16[4,192,128]{2,1,0:T(8,128)(2,1)S(1)} %get-tuple-element.49), channel_id=1, source_target_pairs={{0,1},{1,0},{2,3},{3,2},{4,5},{5,4},{6,7},{7,6},{8,9},{9,8},{10,11... | collective-permute-start | bytes 589832 | tf_op jit(solution)/shard_map/ppermute | solution.py:346
  31.9 15.8 %collective-permute-start.4 = (bf16[4,192,128]{2,1,0:T(8,128)(2,1)S(1)}, bf16[4,192,128]{2,1,0:T(8,128)(2,1)S(1)}, u32[]{:S(2)}, u32[]{:S(2)}) collective-permute-start(bf16[4,192,128]{2,1,0:T(8,128)(2,1)S(1)} %get-tuple-element.50), channel_id=1, source_target_pairs={{0,2},{1,3},{2,0},{3,1},{4,6},{5,7},{6,4},{7,5},{8,10},{9,11},{10,... | collective-permute-start | bytes 589832 | tf_op jit(solution)/shard_map/ppermute | solution.py:346
  43.1 14.8 %collective-permute-start.6 = (bf16[3,192,128]{2,1,0:T(8,128)(2,1)S(1)}, bf16[3,192,128]{2,1,0:T(8,128)(2,1)S(1)}, u32[]{:S(2)}, u32[]{:S(2)}) collective-permute-start(bf16[3,192,128]{2,1,0:T(8,128)(2,1)S(1)} %get-tuple-element.56), channel_id=1, source_target_pairs={{0,1},{1,0},{2,3},{3,2},{4,5},{5,4},{6,7},{7,6},{8,9},{9,8},{10,11... | collective-permute-start | bytes 442376 | tf_op jit(solution)/shard_map/ppermute | solution.py:346
  45.2 12.7 %collective-permute-start.7 = (bf16[3,192,128]{2,1,0:T(8,128)(2,1)S(1)}, bf16[3,192,128]{2,1,0:T(8,128)(2,1)S(1)}, u32[]{:S(2)}, u32[]{:S(2)}) collective-permute-start(bf16[3,192,128]{2,1,0:T(8,128)(2,1)S(1)} %get-tuple-element.57), channel_id=1, source_target_pairs={{0,2},{1,3},{2,0},{3,1},{4,6},{5,7},{6,4},{7,5},{8,10},{9,11},{10,... | collective-permute-start | bytes 442376 | tf_op jit(solution)/shard_map/ppermute | solution.py:346
  45.2 12.7 %collective-permute-start.8 = (bf16[3,192,128]{2,1,0:T(8,128)(2,1)S(1)}, bf16[3,192,128]{2,1,0:T(8,128)(2,1)S(1)}, u32[]{:S(2)}, u32[]{:S(2)}) collective-permute-start(bf16[3,192,128]{2,1,0:T(8,128)(2,1)S(1)} %get-tuple-element.58), channel_id=1, source_target_pairs={{0,3},{1,2},{2,1},{3,0},{4,7},{5,6},{6,5},{7,4},{8,11},{9,10},{10,... | collective-permute-start | bytes 442376 | tf_op jit(solution)/shard_map/ppermute | solution.py:346
  57.9 14.3 %collective-permute-start.9 = (bf16[3,192,128]{2,1,0:T(8,128)(2,1)S(1)}, bf16[3,192,128]{2,1,0:T(8,128)(2,1)S(1)}, u32[]{:S(2)}, u32[]{:S(2)}) collective-permute-start(bf16[3,192,128]{2,1,0:T(8,128)(2,1)S(1)} %get-tuple-element.68), channel_id=1, source_target_pairs={{0,1},{1,0},{2,3},{3,2},{4,5},{5,4},{6,7},{7,6},{8,9},{9,8},{10,11... | collective-permute-start | bytes 442376 | tf_op jit(solution)/shard_map/ppermute | solution.py:346
  59.0 13.2 %collective-permute-start.10 = (bf16[3,192,128]{2,1,0:T(8,128)(2,1)S(1)}, bf16[3,192,128]{2,1,0:T(8,128)(2,1)S(1)}, u32[]{:S(2)}, u32[]{:S(2)}) collective-permute-start(bf16[3,192,128]{2,1,0:T(8,128)(2,1)S(1)} %get-tuple-element.69), channel_id=1, source_target_pairs={{0,2},{1,3},{2,0},{3,1},{4,6},{5,7},{6,4},{7,5},{8,10},{9,11},{10,... | collective-permute-start | bytes 442376 | tf_op jit(solution)/shard_map/ppermute | solution.py:346
  59.9 12.3 %collective-permute-start.11 = (bf16[3,192,128]{2,1,0:T(8,128)(2,1)S(1)}, bf16[3,192,128]{2,1,0:T(8,128)(2,1)S(1)}, u32[]{:S(2)}, u32[]{:S(2)}) collective-permute-start(bf16[3,192,128]{2,1,0:T(8,128)(2,1)S(1)} %get-tuple-element.70), channel_id=1, source_target_pairs={{0,3},{1,2},{2,1},{3,0},{4,7},{5,6},{6,5},{7,4},{8,11},{9,10},{10,... | collective-permute-start | bytes 442376 | tf_op jit(solution)/shard_map/ppermute | solution.py:346

commit v3 on v1

--- a/solution.py
+++ b/solution.py
@@ -115,7 +115,7 @@
 
 def core_kernel(count, block, scalars, weight_ref, bias_ref, *refs):
     pieces, outs, taps_ref = refs[:count], refs[count : 2 * count], refs[2 * count]
-    q_t, k_t, v_t, a_t, q_n, k_n, v_n, g_n, a_n, probs, shifted, pre_grad = refs[2 * count + 1 :]
+    q_t, k_t, v_t, a_t, q_n, k_n, v_n, g_n, a_n, probs, shifted, padded = refs[2 * count + 1 :]
     heads, rows, depth = q_n.shape
     frames = pieces[0].shape[2]
     blocks = rows // block
@@ -164,62 +164,64 @@
 
     each_block(forward)
 
-    tall = shifted.shape[1]
-
-    def shift_all(source_rows):
-        shifted[0, 0:PAD, :] = jnp.zeros((PAD, depth), f32)
-        shifted[0, PAD + rows : tall, :] = jnp.zeros((tall - PAD - rows, depth), f32)
-        for first in range(0, rows, frames):
-            shifted[0, PAD + first : PAD + first + frames, :] = source_rows(first)
-        for s in range(1, 8):
-            shifted[s, 0 : tall - 8, :] = shifted[0, s : tall - 8 + s, :]
-
-    step_rows = 64
-
-    def filtered(head, row, reverse):
+    tall = padded.shape[0]
+    padded[0:PAD, :] = jnp.zeros((PAD, depth), f32)
+    padded[PAD + rows : tall, :] = jnp.zeros((tall - PAD - rows, depth), f32)
+
+    def shift_all():
+        for s in range(8):
+            shifted[s] = padded[s : s + tall - 8, :].reshape(tall // 8 - 1, 8, depth)
+
+    step_tiles = 8
+    step_rows = 8 * step_tiles
+
+    def window(index, offset):
+        return shifted[offset % 8, pl.ds(index * step_tiles + offset // 8, step_tiles)]
+
+    def filtered(head, index, reverse):
         total = None
         for offset in range(1, KERNEL + 1):
-            s, a = offset % 8, offset // 8 * 8
             tap = KERNEL - offset if reverse else offset - 1
-            term = weight_ref[head, tap : tap + 1, :] * shifted[s, pl.ds(row + a, step_rows), :]
+            term = weight_ref[head, tap : tap + 1, :] * window(index, offset)
             total = term if total is None else total + term
         return total
 
-    def eights(array):
-        return jnp.sum(array.reshape(step_rows // 8, 8, depth), axis=0)
+    def loaded(ref, index):
+        at = pl.ds(pl.multiple_of(index * step_rows, step_rows), step_rows)
+        return ref[at, :].astype(f32).reshape(step_tiles, 8, depth)
 
     for head in range(heads):
-        shift_all(lambda first: a_t[span(head), first : first + frames].T.astype(f32))
+        for first in range(0, rows, frames):
+            at = slice(PAD + first, PAD + first + frames)
+            padded[at, :] = a_t[span(head), first : first + frames].T.astype(f32)
+        shift_all()
 
         def conv_step(index, carry, head=head):
-            row = pl.multiple_of(index * step_rows, step_rows)
-            conv_pre = filtered(head, row, False) + bias_ref[head]
+            conv_pre = filtered(head, index, False) + bias_ref[head]
             sig = 1.0 / (1.0 + jnp.exp(-conv_pre))
-            grad = g_n[head, pl.ds(row, step_rows), :].astype(f32)
-            pre = grad * (sig * (1.0 + conv_pre * (1.0 - sig)))
+            pre = loaded(g_n.at[head], index) * (sig * (1.0 + conv_pre * (1.0 - sig)))
             pre = pre.astype(bf16).astype(f32)
-            pre_grad[pl.ds(row, step_rows), :] = pre
+            at = pl.ds(pl.multiple_of(PAD + index * step_rows, PAD), step_rows)
+            padded[at, :] = pre.reshape(step_rows, depth)
             new = []
             for offset in range(1, KERNEL + 1):
-                s, a = offset % 8, offset // 8 * 8
-                term = pre * shifted[s, pl.ds(row + a, step_rows), :]
-                new.append(carry[offset - 1] + eights(term))
-            new.append(carry[KERNEL] + eights(pre))
+                new.append(carry[offset - 1] + jnp.sum(pre * window(index, offset), axis=0))
+            new.append(carry[KERNEL] + jnp.sum(pre, axis=0))
             return tuple(new)
 
         zero = jnp.zeros((8, depth), f32)
         sums = lax.fori_loop(0, rows // step_rows, conv_step, (zero,) * (KERNEL + 1))
         for tap in range(KERNEL + 1):
             taps_ref[head, tap : tap + 1, :] = jnp.sum(sums[tap], axis=0, keepdims=True)
-
-        shift_all(lambda first: pre_grad[first : first + frames, :])
+        shift_all()
 
         def back_step(index, carry, head=head):
-            row = pl.multiple_of(index * step_rows, step_rows)
-            total = g_n[head, pl.ds(row, step_rows), :].astype(f32) + filtered(head, row, True)
-            frame_at = row + lax.broadcasted_iota(jnp.int32, total.shape, 0)
+            total = loaded(g_n.at[head], index) + filtered(head, index, True)
+            total = total.reshape(step_rows, depth)
+            frame_at = index * step_rows + lax.broadcasted_iota(jnp.int32, total.shape, 0)
             total = jnp.where(frame_at < length, total, 0.0)
-            a_n[head, pl.ds(row, step_rows), :] = total.astype(bf16)
+            at = pl.ds(pl.multiple_of(index * step_rows, step_rows), step_rows)
+            a_n[head, at, :] = total.astype(bf16)
             return carry
 
         lax.fori_loop(0, rows // step_rows, back_step, 0)
@@ -282,8 +284,8 @@
         + [plain] * 5
         + [
             pltpu.VMEM((heads, rows, rows), f32),
-            pltpu.VMEM((8, tall, depth), f32),
-            pltpu.VMEM((rows, depth), f32),
+            pltpu.VMEM((8, tall // 8 - 1, 8, depth), f32),
+            pltpu.VMEM((tall, depth), f32),
         ],
         compiler_params=pltpu.CompilerParams(
             vmem_limit_bytes=12 * 2**20 + 8 * heads * rows * rows + 4096 * tall
@@ -297,19 +299,16 @@
     return outs[:count], outs[count]
 
 
-def exchanged(parts):
-    done = []
-    for pieces in parts:
-        pieces = list(pieces)
-        if done and len(pieces) > 2:
-            pieces[2:], before = lax.optimization_barrier((pieces[2:], done[-1][1:]))
-            done[-1] = done[-1][:1] + list(before)
-        moved = [pieces[0]]
-        for distance in range(1, len(pieces)):
-            pairs = [(i, i ^ distance) for i in range(len(pieces))]
-            moved.append(lax.ppermute(pieces[distance], "seq", pairs))
-        done.append(moved)
-    return done
+def exchanged(pieces, before):
+    pieces = list(pieces)
+    if before is not None and len(pieces) > 2:
+        pieces[2:], after = lax.optimization_barrier((pieces[2:], before[1:]))
+        before[1:] = after
+    moved = [pieces[0]]
+    for distance in range(1, len(pieces)):
+        pairs = [(i, i ^ distance) for i in range(len(pieces))]
+        moved.append(lax.ppermute(pieces[distance], "seq", pairs))
+    return moved
 
 
 def on_device(queries, keys, values, grad_out, conv_weight, conv_bias, lengths):
@@ -325,14 +324,16 @@
     bias = lax.dynamic_slice_in_dim(conv_bias.reshape(HEADS, 1, depth), rank * heads, heads, axis=0)
     scalars = jnp.stack([lengths[0], rank])
     sent = pack(rank[None], (queries, keys, values, grad_out), count, chunks)
-    arrived = exchanged(sent)
-    kept, taps = [], []
-    for chunk, pieces in enumerate(arrived):
+    order = []
+    for pieces in sent:
+        order.append(exchanged(pieces, order[-1] if order else None))
+    taps = []
+    for chunk in range(chunks):
         at = slice(chunk * step, (chunk + 1) * step)
-        grads, part = core(scalars, weight[at], bias[at], pieces)
-        kept.append(grads)
+        grads, part = core(scalars, weight[at], bias[at], order[chunk])
+        order.append(exchanged(grads, order[-1]))
         taps.append(part)
-    returned = exchanged(kept)
+    returned = order[chunks:]
     taps, returned[0] = lax.optimization_barrier((jnp.concatenate(taps, axis=0), returned[0]))
     taps = lax.all_gather(taps, "dp")
     return unpack(rank[None], taps, returned, count, chunks)

time: 75.5 us -> 73 us (0.967)
  starting transfers between devices: 26.5 us -> 23.3 us
    ppermute x12, starting transfers between devices: 26.5 us -> 23.3 us  [exchanged(): moved.append(lax.ppermute(pieces[distance], 'seq', pairs))]
  transfers between devices with their start and end apart: 12 -> 12, of which waited for: 3 -> 3; matrix products, arithmetic and copies ran while one was open for 0% -> 0% of each run, Pallas kernels for 26% -> 27%
where the time goes in v3:
time: 73 us; the launch traced here: 72.8 us
  starting transfers between devices  23.3 us (32%)
  Pallas kernels  23.1 us (32%)
  waiting for transfers between devices  14.7 us (20%)
  blocking collectives  9.88 us (14%)
  between operations  1.45 us (2%)
    ppermute x12, starting transfers between devices, exchanged(): moved.append(lax.ppermute(pieces[distance], 'seq', pairs))  23.3 us
    pallas_call x2, Pallas kernels, core(): pl.pallas_call(functools.partial(core_kernel, count, block), out_shape=(p...  19.9 us
    ppermute x12, waiting for transfers between devices, exchanged(): moved.append(lax.ppermute(pieces[distance], 'seq', pairs))  14.7 us
    all_gather x1, blocking collectives, on_device(): taps = lax.all_gather(taps, 'dp')  9.88 us
    pallas_call x1, Pallas kernels, pack(): pl.pallas_call(functools.partial(pack_kernel, count, chunks), out_shape=(...  1.96 us
  transfers between devices with their start and end apart: 12, of which 3 were waited for; matrix products, arithmetic and copies ran while one was open for 0% of the time, Pallas kernels for 27%

profile of v3, /device:TPU:0, one launch (start us, length us, event | category | flops | bytes accessed | tf_op | source)
XLA Modules:
  0.0 72.8 jit_solution(393174015893992917)
XLA Ops:
  0.6 2.0 %shard_map.110 = (bf16[4,192,128]{2,1,0:T(8,128)(2,1)S(1)}, bf16[4,192,128]{2,1,0:T(8,128)(2,1)S(1)}, bf16[4,192,128]{2,1,0:T(8,128)(2,1)S(1)}, bf16[4,192,128]{...) custom-call(s32[1]{0:T(128)} %bitcast.rank_ref, ...), custom_call_target="tpu_custom_call" | custom-call | bytes 3145728 | tf_op jit(solution)/shard_map/pallas_call | solution.py:53
  2.6 0.0 copy-start.1
  2.6 3.1 %collective-permute-start = (bf16[4,192,128]{2,1,0:T(8,128)(2,1)S(1)}, bf16[4,192,128]{2,1,0:T(8,128)(2,1)S(1)}, u32[]{:S(2)}, u32[]{:S(2)}) collective-permute-start(bf16[4,192,128]{2,1,0:T(8,128)(2,1)S(1)} %get-tuple-element.46), channel_id=1, source_target_pairs={{0,1},{1,0},{2,3},{3,2},{4,5},{5,4},{6,7},{7,6},{8,9},{9,8},{10,11... | collective-permute-start | bytes 589832 | tf_op jit(solution)/shard_map/ppermute | solution.py:310
  5.7 2.6 %collective-permute-start.1 = (bf16[4,192,128]{2,1,0:T(8,128)(2,1)S(1)}, bf16[4,192,128]{2,1,0:T(8,128)(2,1)S(1)}, u32[]{:S(2)}, u32[]{:S(2)}) collective-permute-start(bf16[4,192,128]{2,1,0:T(8,128)(2,1)S(1)} %get-tuple-element.47), channel_id=1, source_target_pairs={{0,2},{1,3},{2,0},{3,1},{4,6},{5,7},{6,4},{7,5},{8,10},{9,11},{10,... | collective-permute-start | bytes 589832 | tf_op jit(solution)/shard_map/ppermute | solution.py:310
  8.3 0.9 %collective-permute-start.3 = (bf16[4,192,128]{2,1,0:T(8,128)(2,1)S(1)}, bf16[4,192,128]{2,1,0:T(8,128)(2,1)S(1)}, u32[]{:S(2)}, u32[]{:S(2)}) collective-permute-start(bf16[4,192,128]{2,1,0:T(8,128)(2,1)S(1)} %get-tuple-element.56), channel_id=1, source_target_pairs={{0,1},{1,0},{2,3},{3,2},{4,5},{5,4},{6,7},{7,6},{8,9},{9,8},{10,11... | collective-permute-start | bytes 589832 | tf_op jit(solution)/shard_map/ppermute | solution.py:310
  9.9 0.1 reshape.17
  10.0 0.1 reshape.16
  10.2 4.7 %collective-permute-done.refs_1_ = bf16[4,192,128]{2,1,0:T(8,128)(2,1)S(1)} collective-permute-done((bf16[4,192,128]{2,1,0:T(8,128)(2,1)S(1)}, bf16[4,192,128]{2,1,0:T(8,128)(2,1)S(1)}, u32[]{:S(2)}, u32[]{:S(2)}) %collective-permute-start) | collective-permute-done | bytes 196640 | tf_op jit(solution)/shard_map/ppermute | solution.py:310
  14.9 8.0 %collective-permute-done.1.refs_2_ = bf16[4,192,128]{2,1,0:T(8,128)(2,1)S(1)} collective-permute-done((bf16[4,192,128]{2,1,0:T(8,128)(2,1)S(1)}, bf16[4,192,128]{2,1,0:T(8,128)(2,1)S(1)}, u32[]{:S(2)}, u32[]{:S(2)}) %collective-permute-start.1) | collective-permute-done | bytes 196640 | tf_op jit(solution)/shard_map/ppermute | solution.py:310
  22.9 4.4 %collective-permute-start.4 = (bf16[4,192,128]{2,1,0:T(8,128)(2,1)S(1)}, bf16[4,192,128]{2,1,0:T(8,128)(2,1)S(1)}, u32[]{:S(2)}, u32[]{:S(2)}) collective-permute-start(bf16[4,192,128]{2,1,0:T(8,128)(2,1)S(1)} %get-tuple-element.57), channel_id=1, source_target_pairs={{0,2},{1,3},{2,0},{3,1},{4,6},{5,7},{6,4},{7,5},{8,10},{9,11},{10,... | collective-permute-start | bytes 589832 | tf_op jit(solution)/shard_map/ppermute | solution.py:310
  27.3 1.3 %collective-permute-start.5 = (bf16[4,192,128]{2,1,0:T(8,128)(2,1)S(1)}, bf16[4,192,128]{2,1,0:T(8,128)(2,1)S(1)}, u32[]{:S(2)}, u32[]{:S(2)}) collective-permute-start(bf16[4,192,128]{2,1,0:T(8,128)(2,1)S(1)} %get-tuple-element.58), channel_id=1, source_target_pairs={{0,3},{1,2},{2,1},{3,0},{4,7},{5,6},{6,5},{7,4},{8,11},{9,10},{10,... | collective-permute-start | bytes 589832 | tf_op jit(solution)/shard_map/ppermute | solution.py:310
  28.6 0.1 pad_add_fusion.scalars
  28.7 9.9 %shard_map.111 = (bf16[3,192,128]{2,1,0:T(8,128)(2,1)S(1)}, bf16[3,192,128]{2,1,0:T(8,128)(2,1)S(1)}, bf16[3,192,128]{2,1,0:T(8,128)(2,1)S(1)}, bf16[3,192,128]{2,1,0:T(8,128)(2,1)S(1)}, f32[2,32,96]{2,1,0:T(8,128)S(1)}) custom-call(s32[2]{0:T(128)S(1)} %pad_add_fusion.scalars, f32[2,31,96]{2,1,0:T(8,128)S(1)} %get-tuple-element.81.weight_ref, ...), custom_call_target="tpu_custom_call" | custom-call | flops 1207959552 | bytes 1376256 | tf_op jit(solution)/shard_map/pallas_call | solution.py:278
  38.7 0.1 collective-permute-start.6
  38.7 0.0 collective-permute-done.3.refs_1_
  38.7 1.9 %collective-permute-done.4.refs_2_ = bf16[4,192,128]{2,1,0:T(8,128)(2,1)S(1)} collective-permute-done((bf16[4,192,128]{2,1,0:T(8,128)(2,1)S(1)}, bf16[4,192,128]{2,1,0:T(8,128)(2,1)S(1)}, u32[]{:S(2)}, u32[]{:S(2)}) %collective-permute-start.4) | collective-permute-done | bytes 196640 | tf_op jit(solution)/shard_map/ppermute | solution.py:310
  40.7 3.4 %collective-permute-start.7 = (bf16[3,192,128]{2,1,0:T(8,128)(2,1)S(1)}, bf16[3,192,128]{2,1,0:T(8,128)(2,1)S(1)}, u32[]{:S(2)}, u32[]{:S(2)}) collective-permute-start(bf16[3,192,128]{2,1,0:T(8,128)(2,1)S(1)} %get-tuple-element.67), channel_id=1, source_target_pairs={{0,2},{1,3},{2,0},{3,1},{4,6},{5,7},{6,4},{7,5},{8,10},{9,11},{10,... | collective-permute-start | bytes 442376 | tf_op jit(solution)/shard_map/ppermute | solution.py:310
  44.1 3.0 %collective-permute-start.8 = (bf16[3,192,128]{2,1,0:T(8,128)(2,1)S(1)}, bf16[3,192,128]{2,1,0:T(8,128)(2,1)S(1)}, u32[]{:S(2)}, u32[]{:S(2)}) collective-permute-start(bf16[3,192,128]{2,1,0:T(8,128)(2,1)S(1)} %get-tuple-element.68), channel_id=1, source_target_pairs={{0,3},{1,2},{2,1},{3,0},{4,7},{5,6},{6,5},{7,4},{8,11},{9,10},{10,... | collective-permute-start | bytes 442376 | tf_op jit(solution)/shard_map/ppermute | solution.py:310
  47.2 9.9 %shard_map.112 = (bf16[3,192,128]{2,1,0:T(8,128)(2,1)S(1)}, bf16[3,192,128]{2,1,0:T(8,128)(2,1)S(1)}, bf16[3,192,128]{2,1,0:T(8,128)(2,1)S(1)}, bf16[3,192,128]{2,1,0:T(8,128)(2,1)S(1)}, f32[2,32,96]{2,1,0:T(8,128)S(1)}) custom-call(s32[2]{0:T(128)S(1)} %pad_add_fusion.scalars, f32[2,31,96]{2,1,0:T(8,128)S(1)} %get-tuple-element.82.weight_ref, ...), custom_call_target="tpu_custom_call" | custom-call | flops 1207959552 | bytes 1376256 | tf_op jit(solution)/shard_map/pallas_call | solution.py:278
  57.1 0.1 collective-permute-start.9
  57.2 1.4 %collective-permute-start.10 = (bf16[3,192,128]{2,1,0:T(8,128)(2,1)S(1)}, bf16[3,192,128]{2,1,0:T(8,128)(2,1)S(1)}, u32[]{:S(2)}, u32[]{:S(2)}) collective-permute-start(bf16[3,192,128]{2,1,0:T(8,128)(2,1)S(1)} %get-tuple-element.79), channel_id=1, source_target_pairs={{0,2},{1,3},{2,0},{3,1},{4,6},{5,7},{6,4},{7,5},{8,10},{9,11},{10,... | collective-permute-start | bytes 442376 | tf_op jit(solution)/shard_map/ppermute | solution.py:310
  58.6 3.0 %collective-permute-start.11 = (bf16[3,192,128]{2,1,0:T(8,128)(2,1)S(1)}, bf16[3,192,128]{2,1,0:T(8,128)(2,1)S(1)}, u32[]{:S(2)}, u32[]{:S(2)}) collective-permute-start(bf16[3,192,128]{2,1,0:T(8,128)(2,1)S(1)} %get-tuple-element.80), channel_id=1, source_target_pairs={{0,3},{1,2},{2,1},{3,0},{4,7},{5,6},{6,5},{7,4},{8,11},{9,10},{10,... | collective-permute-start | bytes 442376 | tf_op jit(solution)/shard_map/ppermute | solution.py:310
  61.7 9.9 %all-gather = f32[32,32,96]{2,1,0:T(8,128)S(1)} all-gather(f32[4,32,96]{2,1,0:T(8,128)S(1)} %pad_maximum_fusion), channel_id=2, replica_groups=mesh['dp'=8,'seq'=4] {'dp'}, dimensions={0}, use_global_device_ids=true | all-gather | bytes 442368 | tf_op jit(solution)/shard_map/all_gather | solution.py:338
  71.6 1.3 %shard_map.113 = (bf16[1,128,1536]{2,1,0:T(8,128)(2,1)}, bf16[1,128,1536]{2,1,0:T(8,128)(2,1)}, bf16[1,128,1536]{2,1,0:T(8,128)(2,1)}, f32[31,384]{1,0:T(8,128)}, f32[384]{0:T(512)}) custom-call(s32[1]{0:T(128)} %bitcast.rank_ref, f32[8,4,32,96]{3,2,1,0:T(8,128)S(1)} %bitcast.5, bf16[3,192,128]{2,1,0:T(8,128)(2,1)S(1)} %get-tuple-element.73.refs_0_, ...), custom_call_target="tpu_custom_call" | custom-call | bytes 2359296 | tf_op jit(solution)/shard_map/pallas_call | solution.py:96
  (17 shorter events, 0.1 us)
Async XLA Ops:
  0.6 9.3 %copy-start = (f32[31,1536]{1,0:T(8,128)S(1)}, f32[31,1536]{1,0:T(8,128)}, u32[]{:S(2)}) copy-start(f32[31,1536]{1,0:T(8,128)} %param.11) | copy-start | bytes 571396
  2.6 7.2 %copy-start.1 = (f32[1536]{0:T(1024)S(1)}, f32[1536]{0:T(1024)}, u32[]{:S(2)}) copy-start(f32[1536]{0:T(1024)} %param.12) | copy-start | bytes 18436
  2.6 12.3 %collective-permute-start = (bf16[4,192,128]{2,1,0:T(8,128)(2,1)S(1)}, bf16[4,192,128]{2,1,0:T(8,128)(2,1)S(1)}, u32[]{:S(2)}, u32[]{:S(2)}) collective-permute-start(bf16[4,192,128]{2,1,0:T(8,128)(2,1)S(1)} %get-tuple-element.46), channel_id=1, source_target_pairs={{0,1},{1,0},{2,3},{3,2},{4,5},{5,4},{6,7},{7,6},{8,9},{9,8},{10,11... | collective-permute-start | bytes 589832 | tf_op jit(solution)/shard_map/ppermute | solution.py:310
  5.7 17.2 %collective-permute-start.1 = (bf16[4,192,128]{2,1,0:T(8,128)(2,1)S(1)}, bf16[4,192,128]{2,1,0:T(8,128)(2,1)S(1)}, u32[]{:S(2)}, u32[]{:S(2)}) collective-permute-start(bf16[4,192,128]{2,1,0:T(8,128)(2,1)S(1)} %get-tuple-element.47), channel_id=1, source_target_pairs={{0,2},{1,3},{2,0},{3,1},{4,6},{5,7},{6,4},{7,5},{8,10},{9,11},{10,... | collective-permute-start | bytes 589832 | tf_op jit(solution)/shard_map/ppermute | solution.py:310
  8.3 14.6 %collective-permute-start.2 = (bf16[4,192,128]{2,1,0:T(8,128)(2,1)S(1)}, bf16[4,192,128]{2,1,0:T(8,128)(2,1)S(1)}, u32[]{:S(2)}, u32[]{:S(2)}) collective-permute-start(bf16[4,192,128]{2,1,0:T(8,128)(2,1)S(1)} %get-tuple-element.48), channel_id=1, source_target_pairs={{0,3},{1,2},{2,1},{3,0},{4,7},{5,6},{6,5},{7,4},{8,11},{9,10},{10,... | collective-permute-start | bytes 589832 | tf_op jit(solution)/shard_map/ppermute | solution.py:310
  8.3 30.4 %collective-permute-start.3 = (bf16[4,192,128]{2,1,0:T(8,128)(2,1)S(1)}, bf16[4,192,128]{2,1,0:T(8,128)(2,1)S(1)}, u32[]{:S(2)}, u32[]{:S(2)}) collective-permute-start(bf16[4,192,128]{2,1,0:T(8,128)(2,1)S(1)} %get-tuple-element.56), channel_id=1, source_target_pairs={{0,1},{1,0},{2,3},{3,2},{4,5},{5,4},{6,7},{7,6},{8,9},{9,8},{10,11... | collective-permute-start | bytes 589832 | tf_op jit(solution)/shard_map/ppermute | solution.py:310
  22.9 17.8 %collective-permute-start.4 = (bf16[4,192,128]{2,1,0:T(8,128)(2,1)S(1)}, bf16[4,192,128]{2,1,0:T(8,128)(2,1)S(1)}, u32[]{:S(2)}, u32[]{:S(2)}) collective-permute-start(bf16[4,192,128]{2,1,0:T(8,128)(2,1)S(1)} %get-tuple-element.57), channel_id=1, source_target_pairs={{0,2},{1,3},{2,0},{3,1},{4,6},{5,7},{6,4},{7,5},{8,10},{9,11},{10,... | collective-permute-start | bytes 589832 | tf_op jit(solution)/shard_map/ppermute | solution.py:310
  27.3 13.4 %collective-permute-start.5 = (bf16[4,192,128]{2,1,0:T(8,128)(2,1)S(1)}, bf16[4,192,128]{2,1,0:T(8,128)(2,1)S(1)}, u32[]{:S(2)}, u32[]{:S(2)}) collective-permute-start(bf16[4,192,128]{2,1,0:T(8,128)(2,1)S(1)} %get-tuple-element.58), channel_id=1, source_target_pairs={{0,3},{1,2},{2,1},{3,0},{4,7},{5,6},{6,5},{7,4},{8,11},{9,10},{10,... | collective-permute-start | bytes 589832 | tf_op jit(solution)/shard_map/ppermute | solution.py:310
  38.7 18.5 %collective-permute-start.6 = (bf16[3,192,128]{2,1,0:T(8,128)(2,1)S(1)}, bf16[3,192,128]{2,1,0:T(8,128)(2,1)S(1)}, u32[]{:S(2)}, u32[]{:S(2)}) collective-permute-start(bf16[3,192,128]{2,1,0:T(8,128)(2,1)S(1)} %get-tuple-element.66), channel_id=1, source_target_pairs={{0,1},{1,0},{2,3},{3,2},{4,5},{5,4},{6,7},{7,6},{8,9},{9,8},{10,11... | collective-permute-start | bytes 442376 | tf_op jit(solution)/shard_map/ppermute | solution.py:310
  40.7 16.5 %collective-permute-start.7 = (bf16[3,192,128]{2,1,0:T(8,128)(2,1)S(1)}, bf16[3,192,128]{2,1,0:T(8,128)(2,1)S(1)}, u32[]{:S(2)}, u32[]{:S(2)}) collective-permute-start(bf16[3,192,128]{2,1,0:T(8,128)(2,1)S(1)} %get-tuple-element.67), channel_id=1, source_target_pairs={{0,2},{1,3},{2,0},{3,1},{4,6},{5,7},{6,4},{7,5},{8,10},{9,11},{10,... | collective-permute-start | bytes 442376 | tf_op jit(solution)/shard_map/ppermute | solution.py:310
  44.1 13.1 %collective-permute-start.8 = (bf16[3,192,128]{2,1,0:T(8,128)(2,1)S(1)}, bf16[3,192,128]{2,1,0:T(8,128)(2,1)S(1)}, u32[]{:S(2)}, u32[]{:S(2)}) collective-permute-start(bf16[3,192,128]{2,1,0:T(8,128)(2,1)S(1)} %get-tuple-element.68), channel_id=1, source_target_pairs={{0,3},{1,2},{2,1},{3,0},{4,7},{5,6},{6,5},{7,4},{8,11},{9,10},{10,... | collective-permute-start | bytes 442376 | tf_op jit(solution)/shard_map/ppermute | solution.py:310
  57.1 14.4 %collective-permute-start.9 = (bf16[3,192,128]{2,1,0:T(8,128)(2,1)S(1)}, bf16[3,192,128]{2,1,0:T(8,128)(2,1)S(1)}, u32[]{:S(2)}, u32[]{:S(2)}) collective-permute-start(bf16[3,192,128]{2,1,0:T(8,128)(2,1)S(1)} %get-tuple-element.78), channel_id=1, source_target_pairs={{0,1},{1,0},{2,3},{3,2},{4,5},{5,4},{6,7},{7,6},{8,9},{9,8},{10,11... | collective-permute-start | bytes 442376 | tf_op jit(solution)/shard_map/ppermute | solution.py:310
  57.2 14.3 %collective-permute-start.10 = (bf16[3,192,128]{2,1,0:T(8,128)(2,1)S(1)}, bf16[3,192,128]{2,1,0:T(8,128)(2,1)S(1)}, u32[]{:S(2)}, u32[]{:S(2)}) collective-permute-start(bf16[3,192,128]{2,1,0:T(8,128)(2,1)S(1)} %get-tuple-element.79), channel_id=1, source_target_pairs={{0,2},{1,3},{2,0},{3,1},{4,6},{5,7},{6,4},{7,5},{8,10},{9,11},{10,... | collective-permute-start | bytes 442376 | tf_op jit(solution)/shard_map/ppermute | solution.py:310
  58.6 12.9 %collective-permute-start.11 = (bf16[3,192,128]{2,1,0:T(8,128)(2,1)S(1)}, bf16[3,192,128]{2,1,0:T(8,128)(2,1)S(1)}, u32[]{:S(2)}, u32[]{:S(2)}) collective-permute-start(bf16[3,192,128]{2,1,0:T(8,128)(2,1)S(1)} %get-tuple-element.80), channel_id=1, source_target_pairs={{0,3},{1,2},{2,1},{3,0},{4,7},{5,6},{6,5},{7,4},{8,11},{9,10},{10,... | collective-permute-start | bytes 442376 | tf_op jit(solution)/shard_map/ppermute | solution.py:310

commit v4 on v3

--- a/solution.py
+++ b/solution.py
@@ -68,25 +68,39 @@
     return [outs[chunk * count : (chunk + 1) * count] for chunk in range(chunks)]
 
 
-def unpack_kernel(count, chunks, rank_ref, taps_ref, *refs):
-    pieces, outs = refs[: count * chunks], refs[-7:-4]
-    weight_ref, bias_ref, bias_row, turned = refs[-4:]
-    taps = jnp.sum(taps_ref[...], axis=0)
+def unpack_kernel(count, chunks, rank_ref, *refs):
+    pieces, refs = refs[: count * chunks], refs[count * chunks :]
+    taps_refs, outs = refs[:-9], refs[-9:-6]
+    weight_ref, bias_ref, bias_row, turned, plain, sems = refs[-6:]
+    rank = rank_ref[0]
+    high = pieces[0].shape[1]
+    share = high * chunks
+    frames = plain.shape[1]
+    cut = frames // CUTS
+    copies = []
+    for which, out in enumerate(outs):
+        for distance in range(count):
+            for chunk in range(chunks):
+                first = pl.multiple_of((rank ^ distance) * share + chunk * high, 16)
+                turned[which, pl.ds(first, high), :] = pieces[chunk * count + distance][which]
+        plain[which] = turned[which].T
+        for part in range(CUTS):
+            at = pl.ds(part * cut, cut)
+            copies.append(
+                pltpu.make_async_copy(
+                    plain.at[which, at, :], out.at[0, at, :], sems.at[which, part]
+                )
+            )
+            copies[-1].start()
+    taps = tree_sum([ref[...] for ref in taps_refs])
     heads, _, depth = taps.shape
     for head in range(heads):
         at = slice(head * depth, (head + 1) * depth)
         weight_ref[:, at] = taps[head, :KERNEL]
         bias_row[:, at] = taps[head, KERNEL:]
     bias_ref[...] = bias_row[0]
-    rank = rank_ref[0]
-    high = pieces[0].shape[1]
-    share = high * chunks
-    for which, out in enumerate(outs):
-        for distance in range(count):
-            for chunk in range(chunks):
-                first = pl.multiple_of((rank ^ distance) * share + chunk * high, 16)
-                turned[which, pl.ds(first, high), :] = pieces[chunk * count + distance][which]
-        out[0] = turned[which].T
+    for copy in copies:
+        copy.wait()
 
 
 def unpack(rank, taps, pieces, count, chunks):
@@ -100,17 +114,19 @@
             jax.ShapeDtypeStruct((KERNEL, width // count), f32),
             jax.ShapeDtypeStruct((width // count,), f32),
         ),
-        in_specs=[SMEM] + [VMEM] * (1 + count * chunks),
-        out_specs=(VMEM,) * 5,
+        in_specs=[SMEM] + [VMEM] * (count * chunks + len(taps)),
+        out_specs=(pl.BlockSpec(memory_space=pltpu.HBM),) * 3 + (VMEM,) * 2,
         scratch_shapes=[
             pltpu.VMEM((1, width // count), f32),
             pltpu.VMEM((3, width, frames), bf16),
+            pltpu.VMEM((3, frames, width), bf16),
+            pltpu.SemaphoreType.DMA((3, CUTS)),
         ],
         compiler_params=pltpu.CompilerParams(vmem_limit_bytes=LIMIT),
         cost_estimate=pl.CostEstimate(
             flops=0, bytes_accessed=12 * frames * width, transcendentals=0
         ),
-    )(rank, taps, *[piece for part in pieces for piece in part])
+    )(rank, *[piece for part in pieces for piece in part], *taps)
 
 
 def core_kernel(count, block, scalars, weight_ref, bias_ref, *refs):
@@ -304,11 +320,26 @@
     if before is not None and len(pieces) > 2:
         pieces[2:], after = lax.optimization_barrier((pieces[2:], before[1:]))
         before[1:] = after
-    moved = [pieces[0]]
-    for distance in range(1, len(pieces)):
+    moved = pieces[:1] * len(pieces)
+    for distance in range(len(pieces) - 1, 0, -1):
         pairs = [(i, i ^ distance) for i in range(len(pieces))]
-        moved.append(lax.ppermute(pieces[distance], "seq", pairs))
+        moved[distance] = lax.ppermute(pieces[distance], "seq", pairs)
     return moved
+
+
+def terms(array, axis, stride, reach):
+    count = lax.axis_size(axis)
+    found = [array]
+    for distance in range(stride, reach, stride):
+        pairs = [(i, i ^ distance) for i in range(count)]
+        found.append(lax.ppermute(array, axis, pairs))
+    return found
+
+
+def tree_sum(found):
+    while len(found) > 1:
+        found = [a + b for a, b in zip(found[::2], found[1::2])]
+    return found[0]
 
 
 def on_device(queries, keys, values, grad_out, conv_weight, conv_bias, lengths):
@@ -335,8 +366,8 @@
         taps.append(part)
     returned = order[chunks:]
     taps, returned[0] = lax.optimization_barrier((jnp.concatenate(taps, axis=0), returned[0]))
-    taps = lax.all_gather(taps, "dp")
-    return unpack(rank[None], taps, returned, count, chunks)
+    taps = tree_sum(terms(taps, "dp", 1, 2))
+    return unpack(rank[None], terms(taps, "dp", 2, lax.axis_size("dp")), returned, count, chunks)
 
 
 def solution(mesh):

time: 73 us -> 72.6 us (level)
  blocking collectives: 9.88 us -> 0 us
  waiting for transfers between devices: 14.7 us -> 19.5 us
  starting transfers between devices: 23.3 us -> 27 us
  Pallas kernels: 23.1 us -> 24 us
    all_gather x1 -> x0, blocking collectives: 9.88 us -> none  [on_device(): taps = lax.all_gather(taps, 'dp')]
    ppermute x12 -> x16, waiting for transfers between devices: 14.7 us -> 19.5 us  [the longest x12 14.5 us: exchanged(): moved[distance] = lax.ppermute(pieces[distance], 'seq', pairs)]
    ppermute x12 -> x16, starting transfers between devices: 23.3 us -> 27 us  [the longest x12 23.3 us: exchanged(): moved[distance] = lax.ppermute(pieces[distance], 'seq', pairs)]
  transfers between devices with their start and end apart: 12 -> 16, of which waited for: 3 -> 7; matrix products, arithmetic and copies ran while one was open for 0% -> 0% of each run, Pallas kernels for 27% -> 28%
where the time goes in v4:
time: 72.6 us; the launch traced here: 72.4 us
  starting transfers between devices  27 us (37%)
  Pallas kernels  24 us (33%)
  waiting for transfers between devices  19.5 us (27%)
  between operations  1.62 us (2%)
    ppermute x12, starting transfers between devices, exchanged(): moved[distance] = lax.ppermute(pieces[distance], 'seq', pairs)  23.3 us
    pallas_call x2, Pallas kernels, core(): pl.pallas_call(functools.partial(core_kernel, count, block), out_shape=(p...  20.1 us
    ppermute x12, waiting for transfers between devices, exchanged(): moved[distance] = lax.ppermute(pieces[distance], 'seq', pairs)  14.5 us
    ppermute x4, waiting for transfers between devices, terms(): found.append(lax.ppermute(array, axis, pairs))  4.97 us
    ppermute x4, starting transfers between devices, terms(): found.append(lax.ppermute(array, axis, pairs))  3.63 us
    pallas_call x1, Pallas kernels, pack(): pl.pallas_call(functools.partial(pack_kernel, count, chunks), out_shape=(...  1.96 us
    pallas_call x1, Pallas kernels, unpack(): pl.pallas_call(functools.partial(unpack_kernel, count, chunks), out_shape...  1.95 us
  transfers between devices with their start and end apart: 16, of which 7 were waited for; matrix products, arithmetic and copies ran while one was open for 0% of the time, Pallas kernels for 28%

profile of v4, /device:TPU:0, one launch (start us, length us, event | category | flops | bytes accessed | tf_op | source)
XLA Modules:
  0.0 72.4 jit_solution(15134616227047919535)
XLA Ops:
  0.6 2.0 %shard_map.110 = (bf16[4,192,128]{2,1,0:T(8,128)(2,1)S(1)}, bf16[4,192,128]{2,1,0:T(8,128)(2,1)S(1)}, bf16[4,192,128]{2,1,0:T(8,128)(2,1)S(1)}, bf16[4,192,128]{...) custom-call(s32[1]{0:T(128)} %bitcast.rank_ref, ...), custom_call_target="tpu_custom_call" | custom-call | bytes 3145728 | tf_op jit(solution)/shard_map/pallas_call | solution.py:53
  2.6 3.1 %collective-permute-start = (bf16[4,192,128]{2,1,0:T(8,128)(2,1)S(1)}, bf16[4,192,128]{2,1,0:T(8,128)(2,1)S(1)}, u32[]{:S(2)}, u32[]{:S(2)}) collective-permute-start(bf16[4,192,128]{2,1,0:T(8,128)(2,1)S(1)} %get-tuple-element.46), channel_id=1, source_target_pairs={{0,1},{1,0},{2,3},{3,2},{4,5},{5,4},{6,7},{7,6},{8,9},{9,8},{10,11... | collective-permute-start | bytes 589832 | tf_op jit(solution)/shard_map/ppermute | solution.py:326
  5.7 2.6 %collective-permute-start.1 = (bf16[4,192,128]{2,1,0:T(8,128)(2,1)S(1)}, bf16[4,192,128]{2,1,0:T(8,128)(2,1)S(1)}, u32[]{:S(2)}, u32[]{:S(2)}) collective-permute-start(bf16[4,192,128]{2,1,0:T(8,128)(2,1)S(1)} %get-tuple-element.47), channel_id=1, source_target_pairs={{0,2},{1,3},{2,0},{3,1},{4,6},{5,7},{6,4},{7,5},{8,10},{9,11},{10,... | collective-permute-start | bytes 589832 | tf_op jit(solution)/shard_map/ppermute | solution.py:326
  8.3 0.9 %collective-permute-start.3 = (bf16[4,192,128]{2,1,0:T(8,128)(2,1)S(1)}, bf16[4,192,128]{2,1,0:T(8,128)(2,1)S(1)}, u32[]{:S(2)}, u32[]{:S(2)}) collective-permute-start(bf16[4,192,128]{2,1,0:T(8,128)(2,1)S(1)} %get-tuple-element.56), channel_id=1, source_target_pairs={{0,1},{1,0},{2,3},{3,2},{4,5},{5,4},{6,7},{7,6},{8,9},{9,8},{10,11... | collective-permute-start | bytes 589832 | tf_op jit(solution)/shard_map/ppermute | solution.py:326
  10.0 0.1 reshape.16
  10.2 4.7 %collective-permute-done.refs_1_ = bf16[4,192,128]{2,1,0:T(8,128)(2,1)S(1)} collective-permute-done((bf16[4,192,128]{2,1,0:T(8,128)(2,1)S(1)}, bf16[4,192,128]{2,1,0:T(8,128)(2,1)S(1)}, u32[]{:S(2)}, u32[]{:S(2)}) %collective-permute-start) | collective-permute-done | bytes 196640 | tf_op jit(solution)/shard_map/ppermute | solution.py:326
  14.9 8.0 %collective-permute-done.1.refs_2_ = bf16[4,192,128]{2,1,0:T(8,128)(2,1)S(1)} collective-permute-done((bf16[4,192,128]{2,1,0:T(8,128)(2,1)S(1)}, bf16[4,192,128]{2,1,0:T(8,128)(2,1)S(1)}, u32[]{:S(2)}, u32[]{:S(2)}) %collective-permute-start.1) | collective-permute-done | bytes 196640 | tf_op jit(solution)/shard_map/ppermute | solution.py:326
  22.9 4.4 %collective-permute-start.4 = (bf16[4,192,128]{2,1,0:T(8,128)(2,1)S(1)}, bf16[4,192,128]{2,1,0:T(8,128)(2,1)S(1)}, u32[]{:S(2)}, u32[]{:S(2)}) collective-permute-start(bf16[4,192,128]{2,1,0:T(8,128)(2,1)S(1)} %get-tuple-element.57), channel_id=1, source_target_pairs={{0,2},{1,3},{2,0},{3,1},{4,6},{5,7},{6,4},{7,5},{8,10},{9,11},{10,... | collective-permute-start | bytes 589832 | tf_op jit(solution)/shard_map/ppermute | solution.py:326
  27.3 1.3 %collective-permute-start.5 = (bf16[4,192,128]{2,1,0:T(8,128)(2,1)S(1)}, bf16[4,192,128]{2,1,0:T(8,128)(2,1)S(1)}, u32[]{:S(2)}, u32[]{:S(2)}) collective-permute-start(bf16[4,192,128]{2,1,0:T(8,128)(2,1)S(1)} %get-tuple-element.58), channel_id=1, source_target_pairs={{0,3},{1,2},{2,1},{3,0},{4,7},{5,6},{6,5},{7,4},{8,11},{9,10},{10,... | collective-permute-start | bytes 589832 | tf_op jit(solution)/shard_map/ppermute | solution.py:326
  28.7 10.1 %shard_map.111 = (bf16[3,192,128]{2,1,0:T(8,128)(2,1)S(1)}, bf16[3,192,128]{2,1,0:T(8,128)(2,1)S(1)}, bf16[3,192,128]{2,1,0:T(8,128)(2,1)S(1)}, bf16[3,192,128]{2,1,0:T(8,128)(2,1)S(1)}, f32[2,32,96]{2,1,0:T(8,128)S(1)}) custom-call(s32[2]{0:T(128)S(1)} %pad_add_fusion.scalars, f32[2,31,96]{2,1,0:T(8,128)S(1)} %get-tuple-element.81.weight_ref, ...), custom_call_target="tpu_custom_call" | custom-call | flops 1207959552 | bytes 1376256 | tf_op jit(solution)/shard_map/pallas_call | solution.py:294
  38.9 1.8 %collective-permute-done.4.refs_2_ = bf16[4,192,128]{2,1,0:T(8,128)(2,1)S(1)} collective-permute-done((bf16[4,192,128]{2,1,0:T(8,128)(2,1)S(1)}, bf16[4,192,128]{2,1,0:T(8,128)(2,1)S(1)}, u32[]{:S(2)}, u32[]{:S(2)}) %collective-permute-start.4) | collective-permute-done | bytes 196640 | tf_op jit(solution)/shard_map/ppermute | solution.py:326
  40.7 3.4 %collective-permute-start.7 = (bf16[3,192,128]{2,1,0:T(8,128)(2,1)S(1)}, bf16[3,192,128]{2,1,0:T(8,128)(2,1)S(1)}, u32[]{:S(2)}, u32[]{:S(2)}) collective-permute-start(bf16[3,192,128]{2,1,0:T(8,128)(2,1)S(1)} %get-tuple-element.67), channel_id=1, source_target_pairs={{0,2},{1,3},{2,0},{3,1},{4,6},{5,7},{6,4},{7,5},{8,10},{9,11},{10,... | collective-permute-start | bytes 442376 | tf_op jit(solution)/shard_map/ppermute | solution.py:326
  44.1 3.0 %collective-permute-start.8 = (bf16[3,192,128]{2,1,0:T(8,128)(2,1)S(1)}, bf16[3,192,128]{2,1,0:T(8,128)(2,1)S(1)}, u32[]{:S(2)}, u32[]{:S(2)}) collective-permute-start(bf16[3,192,128]{2,1,0:T(8,128)(2,1)S(1)} %get-tuple-element.68), channel_id=1, source_target_pairs={{0,3},{1,2},{2,1},{3,0},{4,7},{5,6},{6,5},{7,4},{8,11},{9,10},{10,... | collective-permute-start | bytes 442376 | tf_op jit(solution)/shard_map/ppermute | solution.py:326
  47.2 10.0 %shard_map.112 = (bf16[3,192,128]{2,1,0:T(8,128)(2,1)S(1)}, bf16[3,192,128]{2,1,0:T(8,128)(2,1)S(1)}, bf16[3,192,128]{2,1,0:T(8,128)(2,1)S(1)}, bf16[3,192,128]{2,1,0:T(8,128)(2,1)S(1)}, f32[2,32,96]{2,1,0:T(8,128)S(1)}) custom-call(s32[2]{0:T(128)S(1)} %pad_add_fusion.scalars, f32[2,31,96]{2,1,0:T(8,128)S(1)} %get-tuple-element.82.weight_ref, ...), custom_call_target="tpu_custom_call" | custom-call | flops 1207959552 | bytes 1376256 | tf_op jit(solution)/shard_map/pallas_call | solution.py:294
  57.2 1.4 %collective-permute-start.10 = (bf16[3,192,128]{2,1,0:T(8,128)(2,1)S(1)}, bf16[3,192,128]{2,1,0:T(8,128)(2,1)S(1)}, u32[]{:S(2)}, u32[]{:S(2)}) collective-permute-start(bf16[3,192,128]{2,1,0:T(8,128)(2,1)S(1)} %get-tuple-element.78), channel_id=1, source_target_pairs={{0,2},{1,3},{2,0},{3,1},{4,6},{5,7},{6,4},{7,5},{8,10},{9,11},{10,... | collective-permute-start | bytes 442376 | tf_op jit(solution)/shard_map/ppermute | solution.py:326
  58.6 3.0 %collective-permute-start.11 = (bf16[3,192,128]{2,1,0:T(8,128)(2,1)S(1)}, bf16[3,192,128]{2,1,0:T(8,128)(2,1)S(1)}, u32[]{:S(2)}, u32[]{:S(2)}) collective-permute-start(bf16[3,192,128]{2,1,0:T(8,128)(2,1)S(1)} %get-tuple-element.79), channel_id=1, source_target_pairs={{0,3},{1,2},{2,1},{3,0},{4,7},{5,6},{6,5},{7,4},{8,11},{9,10},{10,... | collective-permute-start | bytes 442376 | tf_op jit(solution)/shard_map/ppermute | solution.py:326
  61.8 1.2 %collective-permute-done.12 = f32[4,32,96]{2,1,0:T(8,128)S(1)} collective-permute-done((f32[4,32,96]{2,1,0:T(8,128)S(1)}, f32[4,32,96]{2,1,0:T(8,128)S(1)}, u32[]{:S(2)}, u32[]{:S(2)}) %collective-permute-start.12) | collective-permute-done | bytes 49184 | tf_op jit(solution)/shard_map/ppermute | solution.py:335
  63.0 2.5 %collective-permute-start.15 = (f32[4,32,96]{2,1,0:T(8,128)S(1)}, f32[4,32,96]{2,1,0:T(8,128)S(1)}, u32[]{:S(2)}, u32[]{:S(2)}) collective-permute-start(f32[4,32,96]{2,1,0:T(8,128)S(1)} %add.8.refs_8_), channel_id=1, source_target_pairs={{0,24},{4,28},{8,16},{12,20},{16,8},{20,12},{24,0},{28,4},{1,25},{... | collective-permute-start | bytes 147464 | tf_op jit(solution)/shard_map/ppermute | solution.py:335
  65.5 0.5 collective-permute-start.14
  66.0 0.5 collective-permute-start.13
  66.6 1.7 %collective-permute-done.15.refs_11_ = f32[4,32,96]{2,1,0:T(8,128)S(1)} collective-permute-done((f32[4,32,96]{2,1,0:T(8,128)S(1)}, f32[4,32,96]{2,1,0:T(8,128)S(1)}, u32[]{:S(2)}, u32[]{:S(2)}) %collective-permute-start.15) | collective-permute-done | bytes 49184 | tf_op jit(solution)/shard_map/ppermute | solution.py:335
  68.3 1.5 %collective-permute-done.14.refs_10_ = f32[4,32,96]{2,1,0:T(8,128)S(1)} collective-permute-done((f32[4,32,96]{2,1,0:T(8,128)S(1)}, f32[4,32,96]{2,1,0:T(8,128)S(1)}, u32[]{:S(2)}, u32[]{:S(2)}) %collective-permute-start.14) | collective-permute-done | bytes 49184 | tf_op jit(solution)/shard_map/ppermute | solution.py:335
  69.8 0.5 collective-permute-done.13.refs_9_
  70.3 1.9 %shard_map.113 = (bf16[1,128,1536]{2,1,0:T(8,128)(2,1)}, bf16[1,128,1536]{2,1,0:T(8,128)(2,1)}, bf16[1,128,1536]{2,1,0:T(8,128)(2,1)}, f32[31,384]{1,0:T(8,128)}, f32[384]{0:T(512)}) custom-call(s32[1]{0:T(128)} %bitcast.rank_ref, bf16[3,192,128]{2,1,0:T(8,128)(2,1)S(1)} %get-tuple-element.72.refs_0_, ...), custom_call_target="tpu_custom_call" | custom-call | bytes 2359296 | tf_op jit(solution)/shard_map/pallas_call | solution.py:110
  (25 shorter events, 0.5 us)
Async XLA Ops:
  0.6 9.3 %copy-start = (f32[31,1536]{1,0:T(8,128)S(1)}, f32[31,1536]{1,0:T(8,128)}, u32[]{:S(2)}) copy-start(f32[31,1536]{1,0:T(8,128)} %param.11) | copy-start | bytes 571396
  2.6 7.2 %copy-start.1 = (f32[1536]{0:T(1024)S(1)}, f32[1536]{0:T(1024)}, u32[]{:S(2)}) copy-start(f32[1536]{0:T(1024)} %param.12) | copy-start | bytes 18436
  2.6 12.3 %collective-permute-start = (bf16[4,192,128]{2,1,0:T(8,128)(2,1)S(1)}, bf16[4,192,128]{2,1,0:T(8,128)(2,1)S(1)}, u32[]{:S(2)}, u32[]{:S(2)}) collective-permute-start(bf16[4,192,128]{2,1,0:T(8,128)(2,1)S(1)} %get-tuple-element.46), channel_id=1, source_target_pairs={{0,1},{1,0},{2,3},{3,2},{4,5},{5,4},{6,7},{7,6},{8,9},{9,8},{10,11... | collective-permute-start | bytes 589832 | tf_op jit(solution)/shard_map/ppermute | solution.py:326
  5.7 17.2 %collective-permute-start.1 = (bf16[4,192,128]{2,1,0:T(8,128)(2,1)S(1)}, bf16[4,192,128]{2,1,0:T(8,128)(2,1)S(1)}, u32[]{:S(2)}, u32[]{:S(2)}) collective-permute-start(bf16[4,192,128]{2,1,0:T(8,128)(2,1)S(1)} %get-tuple-element.47), channel_id=1, source_target_pairs={{0,2},{1,3},{2,0},{3,1},{4,6},{5,7},{6,4},{7,5},{8,10},{9,11},{10,... | collective-permute-start | bytes 589832 | tf_op jit(solution)/shard_map/ppermute | solution.py:326
  8.3 14.6 %collective-permute-start.2 = (bf16[4,192,128]{2,1,0:T(8,128)(2,1)S(1)}, bf16[4,192,128]{2,1,0:T(8,128)(2,1)S(1)}, u32[]{:S(2)}, u32[]{:S(2)}) collective-permute-start(bf16[4,192,128]{2,1,0:T(8,128)(2,1)S(1)} %get-tuple-element.48), channel_id=1, source_target_pairs={{0,3},{1,2},{2,1},{3,0},{4,7},{5,6},{6,5},{7,4},{8,11},{9,10},{10,... | collective-permute-start | bytes 589832 | tf_op jit(solution)/shard_map/ppermute | solution.py:326
  8.3 30.6 %collective-permute-start.3 = (bf16[4,192,128]{2,1,0:T(8,128)(2,1)S(1)}, bf16[4,192,128]{2,1,0:T(8,128)(2,1)S(1)}, u32[]{:S(2)}, u32[]{:S(2)}) collective-permute-start(bf16[4,192,128]{2,1,0:T(8,128)(2,1)S(1)} %get-tuple-element.56), channel_id=1, source_target_pairs={{0,1},{1,0},{2,3},{3,2},{4,5},{5,4},{6,7},{7,6},{8,9},{9,8},{10,11... | collective-permute-start | bytes 589832 | tf_op jit(solution)/shard_map/ppermute | solution.py:326
  22.9 17.8 %collective-permute-start.4 = (bf16[4,192,128]{2,1,0:T(8,128)(2,1)S(1)}, bf16[4,192,128]{2,1,0:T(8,128)(2,1)S(1)}, u32[]{:S(2)}, u32[]{:S(2)}) collective-permute-start(bf16[4,192,128]{2,1,0:T(8,128)(2,1)S(1)} %get-tuple-element.57), channel_id=1, source_target_pairs={{0,2},{1,3},{2,0},{3,1},{4,6},{5,7},{6,4},{7,5},{8,10},{9,11},{10,... | collective-permute-start | bytes 589832 | tf_op jit(solution)/shard_map/ppermute | solution.py:326
  27.3 13.4 %collective-permute-start.5 = (bf16[4,192,128]{2,1,0:T(8,128)(2,1)S(1)}, bf16[4,192,128]{2,1,0:T(8,128)(2,1)S(1)}, u32[]{:S(2)}, u32[]{:S(2)}) collective-permute-start(bf16[4,192,128]{2,1,0:T(8,128)(2,1)S(1)} %get-tuple-element.58), channel_id=1, source_target_pairs={{0,3},{1,2},{2,1},{3,0},{4,7},{5,6},{6,5},{7,4},{8,11},{9,10},{10,... | collective-permute-start | bytes 589832 | tf_op jit(solution)/shard_map/ppermute | solution.py:326
  38.8 18.4 %collective-permute-start.6 = (bf16[3,192,128]{2,1,0:T(8,128)(2,1)S(1)}, bf16[3,192,128]{2,1,0:T(8,128)(2,1)S(1)}, u32[]{:S(2)}, u32[]{:S(2)}) collective-permute-start(bf16[3,192,128]{2,1,0:T(8,128)(2,1)S(1)} %get-tuple-element.66), channel_id=1, source_target_pairs={{0,1},{1,0},{2,3},{3,2},{4,5},{5,4},{6,7},{7,6},{8,9},{9,8},{10,11... | collective-permute-start | bytes 442376 | tf_op jit(solution)/shard_map/ppermute | solution.py:326
  40.7 16.5 %collective-permute-start.7 = (bf16[3,192,128]{2,1,0:T(8,128)(2,1)S(1)}, bf16[3,192,128]{2,1,0:T(8,128)(2,1)S(1)}, u32[]{:S(2)}, u32[]{:S(2)}) collective-permute-start(bf16[3,192,128]{2,1,0:T(8,128)(2,1)S(1)} %get-tuple-element.67), channel_id=1, source_target_pairs={{0,2},{1,3},{2,0},{3,1},{4,6},{5,7},{6,4},{7,5},{8,10},{9,11},{10,... | collective-permute-start | bytes 442376 | tf_op jit(solution)/shard_map/ppermute | solution.py:326
  44.1 13.1 %collective-permute-start.8 = (bf16[3,192,128]{2,1,0:T(8,128)(2,1)S(1)}, bf16[3,192,128]{2,1,0:T(8,128)(2,1)S(1)}, u32[]{:S(2)}, u32[]{:S(2)}) collective-permute-start(bf16[3,192,128]{2,1,0:T(8,128)(2,1)S(1)} %get-tuple-element.68), channel_id=1, source_target_pairs={{0,3},{1,2},{2,1},{3,0},{4,7},{5,6},{6,5},{7,4},{8,11},{9,10},{10,... | collective-permute-start | bytes 442376 | tf_op jit(solution)/shard_map/ppermute | solution.py:326
  57.1 8.9 %collective-permute-start.9 = (bf16[3,192,128]{2,1,0:T(8,128)(2,1)S(1)}, bf16[3,192,128]{2,1,0:T(8,128)(2,1)S(1)}, u32[]{:S(2)}, u32[]{:S(2)}) collective-permute-start(bf16[3,192,128]{2,1,0:T(8,128)(2,1)S(1)} %get-tuple-element.77), channel_id=1, source_target_pairs={{0,1},{1,0},{2,3},{3,2},{4,5},{5,4},{6,7},{7,6},{8,9},{9,8},{10,11... | collective-permute-start | bytes 442376 | tf_op jit(solution)/shard_map/ppermute | solution.py:326
  57.2 13.1 %collective-permute-start.10 = (bf16[3,192,128]{2,1,0:T(8,128)(2,1)S(1)}, bf16[3,192,128]{2,1,0:T(8,128)(2,1)S(1)}, u32[]{:S(2)}, u32[]{:S(2)}) collective-permute-start(bf16[3,192,128]{2,1,0:T(8,128)(2,1)S(1)} %get-tuple-element.78), channel_id=1, source_target_pairs={{0,2},{1,3},{2,0},{3,1},{4,6},{5,7},{6,4},{7,5},{8,10},{9,11},{10,... | collective-permute-start | bytes 442376 | tf_op jit(solution)/shard_map/ppermute | solution.py:326
  58.6 11.7 %collective-permute-start.11 = (bf16[3,192,128]{2,1,0:T(8,128)(2,1)S(1)}, bf16[3,192,128]{2,1,0:T(8,128)(2,1)S(1)}, u32[]{:S(2)}, u32[]{:S(2)}) collective-permute-start(bf16[3,192,128]{2,1,0:T(8,128)(2,1)S(1)} %get-tuple-element.79), channel_id=1, source_target_pairs={{0,3},{1,2},{2,1},{3,0},{4,7},{5,6},{6,5},{7,4},{8,11},{9,10},{10,... | collective-permute-start | bytes 442376 | tf_op jit(solution)/shard_map/ppermute | solution.py:326
  61.7 1.3 %collective-permute-start.12 = (f32[4,32,96]{2,1,0:T(8,128)S(1)}, f32[4,32,96]{2,1,0:T(8,128)S(1)}, u32[]{:S(2)}, u32[]{:S(2)}) collective-permute-start(f32[4,32,96]{2,1,0:T(8,128)S(1)} %pad_maximum_fusion), channel_id=1, source_target_pairs={{0,4},{4,0},{8,12},{12,8},{16,20},{20,16},{24,28},{28,24},{1,5},{5... | collective-permute-start | bytes 147464 | tf_op jit(solution)/shard_map/ppermute | solution.py:335
  63.0 5.3 %collective-permute-start.15 = (f32[4,32,96]{2,1,0:T(8,128)S(1)}, f32[4,32,96]{2,1,0:T(8,128)S(1)}, u32[]{:S(2)}, u32[]{:S(2)}) collective-permute-start(f32[4,32,96]{2,1,0:T(8,128)S(1)} %add.8.refs_8_), channel_id=1, source_target_pairs={{0,24},{4,28},{8,16},{12,20},{16,8},{20,12},{24,0},{28,4},{1,25},{... | collective-permute-start | bytes 147464 | tf_op jit(solution)/shard_map/ppermute | solution.py:335
  65.5 4.3 %collective-permute-start.14 = (f32[4,32,96]{2,1,0:T(8,128)S(1)}, f32[4,32,96]{2,1,0:T(8,128)S(1)}, u32[]{:S(2)}, u32[]{:S(2)}) collective-permute-start(f32[4,32,96]{2,1,0:T(8,128)S(1)} %add.8.refs_8_), channel_id=1, source_target_pairs={{0,16},{4,20},{8,24},{12,28},{16,0},{20,4},{24,8},{28,12},{1,17},{... | collective-permute-start | bytes 147464 | tf_op jit(solution)/shard_map/ppermute | solution.py:335
  66.0 4.3 %collective-permute-start.13 = (f32[4,32,96]{2,1,0:T(8,128)S(1)}, f32[4,32,96]{2,1,0:T(8,128)S(1)}, u32[]{:S(2)}, u32[]{:S(2)}) collective-permute-start(f32[4,32,96]{2,1,0:T(8,128)S(1)} %add.8.refs_8_), channel_id=1, source_target_pairs={{0,8},{4,12},{8,0},{12,4},{16,24},{20,28},{24,16},{28,20},{1,9},{5... | collective-permute-start | bytes 147464 | tf_op jit(solution)/shard_map/ppermute | solution.py:335

commit v5 on v4

--- a/solution.py
+++ b/solution.py
@@ -11,7 +11,6 @@
 HEADS = 16
 KERNEL = 31
 PAD = 16
-CUTS = 4
 masked_score = -1e30
 VMEM = pl.BlockSpec(memory_space=pltpu.VMEM)
 SMEM = pl.BlockSpec(memory_space=pltpu.SMEM)
@@ -20,26 +19,12 @@
 
 
 def pack_kernel(count, chunks, rank_ref, *refs):
-    arrays, outs, (plain, turned, sems) = refs[:4], refs[4:-3], refs[-3:]
+    arrays, outs, turned = refs[:4], refs[4:-1], refs[-1]
     rank = rank_ref[0]
     high = outs[0].shape[1]
     share = high * chunks
-    frames = plain.shape[1]
-    cut = frames // CUTS
-
-    def copy(which, part):
-        at = pl.ds(part * cut, cut)
-        return pltpu.make_async_copy(
-            arrays[which].at[0, at, :], plain.at[which, at, :], sems.at[which, part]
-        )
-
-    for which in range(4):
-        for part in range(CUTS):
-            copy(which, part).start()
-    for which in range(4):
-        for part in range(CUTS):
-            copy(which, part).wait()
-        turned[which] = plain[which].T
+    for which, array in enumerate(arrays):
+        turned[which] = array[0].T
         for distance in range(count):
             for chunk in range(chunks):
                 first = pl.multiple_of((rank ^ distance) * share + chunk * high, 16)
@@ -53,13 +38,9 @@
     outs = pl.pallas_call(
         functools.partial(pack_kernel, count, chunks),
         out_shape=(piece,) * (count * chunks),
-        in_specs=[SMEM] + [pl.BlockSpec(memory_space=pltpu.HBM)] * 4,
+        in_specs=[SMEM] + [VMEM] * 4,
         out_specs=(VMEM,) * (count * chunks),
-        scratch_shapes=[
-            pltpu.VMEM((4, frames, width), bf16),
-            pltpu.VMEM((4, width, frames), bf16),
-            pltpu.SemaphoreType.DMA((4, CUTS)),
-        ],
+        scratch_shapes=[pltpu.VMEM((4, width, frames), bf16)],
         compiler_params=pltpu.CompilerParams(vmem_limit_bytes=LIMIT),
         cost_estimate=pl.CostEstimate(
             flops=0, bytes_accessed=16 * frames * width, transcendentals=0
@@ -68,30 +49,23 @@
     return [outs[chunk * count : (chunk + 1) * count] for chunk in range(chunks)]
 
 
+def taken(count):
+    return [0] + list(range(count - 1, 0, -1))
+
+
 def unpack_kernel(count, chunks, rank_ref, *refs):
     pieces, refs = refs[: count * chunks], refs[count * chunks :]
-    taps_refs, outs = refs[:-9], refs[-9:-6]
-    weight_ref, bias_ref, bias_row, turned, plain, sems = refs[-6:]
+    taps_refs, outs = refs[:-7], refs[-7:-4]
+    weight_ref, bias_ref, bias_row, turned = refs[-4:]
     rank = rank_ref[0]
     high = pieces[0].shape[1]
     share = high * chunks
-    frames = plain.shape[1]
-    cut = frames // CUTS
-    copies = []
     for which, out in enumerate(outs):
-        for distance in range(count):
-            for chunk in range(chunks):
+        for chunk in range(chunks):
+            for place, distance in enumerate(taken(count)):
                 first = pl.multiple_of((rank ^ distance) * share + chunk * high, 16)
-                turned[which, pl.ds(first, high), :] = pieces[chunk * count + distance][which]
-        plain[which] = turned[which].T
-        for part in range(CUTS):
-            at = pl.ds(part * cut, cut)
-            copies.append(
-                pltpu.make_async_copy(
-                    plain.at[which, at, :], out.at[0, at, :], sems.at[which, part]
-                )
-            )
-            copies[-1].start()
+                turned[which, pl.ds(first, high), :] = pieces[chunk * count + place][which]
+        out[0] = turned[which].T
     taps = tree_sum([ref[...] for ref in taps_refs])
     heads, _, depth = taps.shape
     for head in range(heads):
@@ -99,8 +73,6 @@
         weight_ref[:, at] = taps[head, :KERNEL]
         bias_row[:, at] = taps[head, KERNEL:]
     bias_ref[...] = bias_row[0]
-    for copy in copies:
-        copy.wait()
 
 
 def unpack(rank, taps, pieces, count, chunks):
@@ -115,18 +87,16 @@
             jax.ShapeDtypeStruct((width // count,), f32),
         ),
         in_specs=[SMEM] + [VMEM] * (count * chunks + len(taps)),
-        out_specs=(pl.BlockSpec(memory_space=pltpu.HBM),) * 3 + (VMEM,) * 2,
+        out_specs=(VMEM,) * 5,
         scratch_shapes=[
             pltpu.VMEM((1, width // count), f32),
             pltpu.VMEM((3, width, frames), bf16),
-            pltpu.VMEM((3, frames, width), bf16),
-            pltpu.SemaphoreType.DMA((3, CUTS)),
         ],
         compiler_params=pltpu.CompilerParams(vmem_limit_bytes=LIMIT),
         cost_estimate=pl.CostEstimate(
             flops=0, bytes_accessed=12 * frames * width, transcendentals=0
         ),
-    )(rank, *[piece for part in pieces for piece in part], *taps)
+    )(rank, *[part[distance] for part in pieces for distance in taken(count)], *taps)
 
 
 def core_kernel(count, block, scalars, weight_ref, bias_ref, *refs):
@@ -142,7 +112,7 @@
     def span(head):
         return slice(head * depth, (head + 1) * depth)
 
-    for distance, piece in enumerate(pieces):
+    for distance, piece in zip(taken(count), pieces):
         at = pl.ds(pl.multiple_of((rank ^ distance) * frames, 128), frames)
         q_t[:, at] = piece[0]
         k_t[:, at] = piece[1]
@@ -311,15 +281,14 @@
             bytes_accessed=14 * rows * high,
             transcendentals=heads * rows * rows,
         ),
-    )(scalars, weight, bias, *pieces)
+    )(scalars, weight, bias, *[pieces[distance] for distance in taken(count)])
     return outs[:count], outs[count]
 
 
 def exchanged(pieces, before):
     pieces = list(pieces)
     if before is not None and len(pieces) > 2:
-        pieces[2:], after = lax.optimization_barrier((pieces[2:], before[1:]))
-        before[1:] = after
+        pieces[:1:-1], before[:0:-1] = lax.optimization_barrier((pieces[:1:-1], before[:0:-1]))
     moved = pieces[:1] * len(pieces)
     for distance in range(len(pieces) - 1, 0, -1):
         pairs = [(i, i ^ distance) for i in range(len(pieces))]

time: 72.6 us -> 72.2 us (level)
  waiting for transfers between devices: 19.5 us -> 25.5 us
  starting transfers between devices: 27 us -> 21.5 us
    ppermute x12, waiting for transfers between devices: 14.5 us -> 20.5 us  [exchanged(): moved[distance] = lax.ppermute(pieces[distance], 'seq', pairs)]
    ppermute x12, starting transfers between devices: 23.3 us -> 17.8 us  [exchanged(): moved[distance] = lax.ppermute(pieces[distance], 'seq', pairs)]
  transfers between devices with their start and end apart: 16 -> 16, of which waited for: 7 -> 8; matrix products, arithmetic and copies ran while one was open for 0% -> 0% of each run, Pallas kernels for 28% -> 28%
where the time goes in v5:
time: 72.2 us; the launch traced here: 72 us
  waiting for transfers between devices  25.5 us (35%)
  Pallas kernels  23.3 us (32%)
  starting transfers between devices  21.5 us (30%)
  between operations  1.42 us (2%)
    ppermute x12, waiting for transfers between devices, exchanged(): moved[distance] = lax.ppermute(pieces[distance], 'seq', pairs)  20.5 us
    pallas_call x2, Pallas kernels, core(): pl.pallas_call(functools.partial(core_kernel, count, block), out_shape=(p...  19.9 us
    ppermute x12, starting transfers between devices, exchanged(): moved[distance] = lax.ppermute(pieces[distance], 'seq', pairs)  17.8 us
    ppermute x4, waiting for transfers between devices, terms(): found.append(lax.ppermute(array, axis, pairs))  4.97 us
    ppermute x4, starting transfers between devices, terms(): found.append(lax.ppermute(array, axis, pairs))  3.63 us
    pallas_call x1, Pallas kernels, pack(): pl.pallas_call(functools.partial(pack_kernel, count, chunks), out_shape=(...  2.03 us
  transfers between devices with their start and end apart: 16, of which 8 were waited for; matrix products, arithmetic and copies ran while one was open for 0% of the time, Pallas kernels for 28%

profile of v5, /device:TPU:0, one launch (start us, length us, event | category | flops | bytes accessed | tf_op | source)
XLA Modules:
  0.0 72.0 jit_solution(8749920649893766887)
XLA Ops:
  0.6 2.0 %shard_map.110 = (bf16[4,192,128]{2,1,0:T(8,128)(2,1)S(1)}, bf16[4,192,128]{2,1,0:T(8,128)(2,1)S(1)}, bf16[4,192,128]{2,1,0:T(8,128)(2,1)S(1)}, bf16[4,192,128]{...) custom-call(s32[1]{0:T(128)} %bitcast.rank_ref, ...), custom_call_target="tpu_custom_call" | custom-call | bytes 3145728 | tf_op jit(solution)/shard_map/pallas_call | solution.py:38
  2.7 5.1 %collective-permute-start = (bf16[4,192,128]{2,1,0:T(8,128)(2,1)S(1)}, bf16[4,192,128]{2,1,0:T(8,128)(2,1)S(1)}, u32[]{:S(2)}, u32[]{:S(2)}) collective-permute-start(bf16[4,192,128]{2,1,0:T(8,128)(2,1)S(1)} %get-tuple-element.46), channel_id=1, source_target_pairs={{0,3},{1,2},{2,1},{3,0},{4,7},{5,6},{6,5},{7,4},{8,11},{9,10},{10,... | collective-permute-start | bytes 589832 | tf_op jit(solution)/shard_map/ppermute | solution.py:295
  7.8 0.6 collective-permute-start.2
  8.5 1.4 %collective-permute-start.5 = (bf16[4,192,128]{2,1,0:T(8,128)(2,1)S(1)}, bf16[4,192,128]{2,1,0:T(8,128)(2,1)S(1)}, u32[]{:S(2)}, u32[]{:S(2)}) collective-permute-start(bf16[4,192,128]{2,1,0:T(8,128)(2,1)S(1)} %get-tuple-element.58), channel_id=1, source_target_pairs={{0,1},{1,0},{2,3},{3,2},{4,5},{5,4},{6,7},{7,6},{8,9},{9,8},{10,11... | collective-permute-start | bytes 589832 | tf_op jit(solution)/shard_map/ppermute | solution.py:295
  10.6 0.1 reshape.16
  10.8 2.9 %collective-permute-done.refs_1_ = bf16[4,192,128]{2,1,0:T(8,128)(2,1)S(1)} collective-permute-done((bf16[4,192,128]{2,1,0:T(8,128)(2,1)S(1)}, bf16[4,192,128]{2,1,0:T(8,128)(2,1)S(1)}, u32[]{:S(2)}, u32[]{:S(2)}) %collective-permute-start) | collective-permute-done | bytes 196640 | tf_op jit(solution)/shard_map/ppermute | solution.py:295
  13.7 10.9 %collective-permute-done.1.refs_2_ = bf16[4,192,128]{2,1,0:T(8,128)(2,1)S(1)} collective-permute-done((bf16[4,192,128]{2,1,0:T(8,128)(2,1)S(1)}, bf16[4,192,128]{2,1,0:T(8,128)(2,1)S(1)}, u32[]{:S(2)}, u32[]{:S(2)}) %collective-permute-start.1) | collective-permute-done | bytes 196640 | tf_op jit(solution)/shard_map/ppermute | solution.py:295
  24.6 2.6 %collective-permute-start.3 = (bf16[4,192,128]{2,1,0:T(8,128)(2,1)S(1)}, bf16[4,192,128]{2,1,0:T(8,128)(2,1)S(1)}, u32[]{:S(2)}, u32[]{:S(2)}) collective-permute-start(bf16[4,192,128]{2,1,0:T(8,128)(2,1)S(1)} %get-tuple-element.56), channel_id=1, source_target_pairs={{0,3},{1,2},{2,1},{3,0},{4,7},{5,6},{6,5},{7,4},{8,11},{9,10},{10,... | collective-permute-start | bytes 589832 | tf_op jit(solution)/shard_map/ppermute | solution.py:295
  27.3 9.9 %shard_map.111 = (bf16[3,192,128]{2,1,0:T(8,128)(2,1)S(1)}, bf16[3,192,128]{2,1,0:T(8,128)(2,1)S(1)}, bf16[3,192,128]{2,1,0:T(8,128)(2,1)S(1)}, bf16[3,192,128]{2,1,0:T(8,128)(2,1)S(1)}, f32[2,32,96]{2,1,0:T(8,128)S(1)}) custom-call(s32[2]{0:T(128)S(1)} %pad_add_fusion.scalars, f32[2,31,96]{2,1,0:T(8,128)S(1)} %get-tuple-element.81.weight_ref, ...), custom_call_target="tpu_custom_call" | custom-call | flops 1207959552 | bytes 1376256 | tf_op jit(solution)/shard_map/pallas_call | solution.py:264
  37.3 1.8 %collective-permute-start.8 = (bf16[3,192,128]{2,1,0:T(8,128)(2,1)S(1)}, bf16[3,192,128]{2,1,0:T(8,128)(2,1)S(1)}, u32[]{:S(2)}, u32[]{:S(2)}) collective-permute-start(bf16[3,192,128]{2,1,0:T(8,128)(2,1)S(1)} %get-tuple-element.68), channel_id=1, source_target_pairs={{0,1},{1,0},{2,3},{3,2},{4,5},{5,4},{6,7},{7,6},{8,9},{9,8},{10,11... | collective-permute-start | bytes 442376 | tf_op jit(solution)/shard_map/ppermute | solution.py:295
  39.1 3.2 %collective-permute-done.4.refs_2_ = bf16[4,192,128]{2,1,0:T(8,128)(2,1)S(1)} collective-permute-done((bf16[4,192,128]{2,1,0:T(8,128)(2,1)S(1)}, bf16[4,192,128]{2,1,0:T(8,128)(2,1)S(1)}, u32[]{:S(2)}, u32[]{:S(2)}) %collective-permute-start.4) | collective-permute-done | bytes 196640 | tf_op jit(solution)/shard_map/ppermute | solution.py:295
  42.3 1.7 %collective-permute-start.6 = (bf16[3,192,128]{2,1,0:T(8,128)(2,1)S(1)}, bf16[3,192,128]{2,1,0:T(8,128)(2,1)S(1)}, u32[]{:S(2)}, u32[]{:S(2)}) collective-permute-start(bf16[3,192,128]{2,1,0:T(8,128)(2,1)S(1)} %get-tuple-element.66), channel_id=1, source_target_pairs={{0,3},{1,2},{2,1},{3,0},{4,7},{5,6},{6,5},{7,4},{8,11},{9,10},{10,... | collective-permute-start | bytes 442376 | tf_op jit(solution)/shard_map/ppermute | solution.py:295
  44.0 10.0 %shard_map.112 = (bf16[3,192,128]{2,1,0:T(8,128)(2,1)S(1)}, bf16[3,192,128]{2,1,0:T(8,128)(2,1)S(1)}, bf16[3,192,128]{2,1,0:T(8,128)(2,1)S(1)}, bf16[3,192,128]{2,1,0:T(8,128)(2,1)S(1)}, f32[2,32,96]{2,1,0:T(8,128)S(1)}) custom-call(s32[2]{0:T(128)S(1)} %pad_add_fusion.scalars, f32[2,31,96]{2,1,0:T(8,128)S(1)} %get-tuple-element.82.weight_ref, ...), custom_call_target="tpu_custom_call" | custom-call | flops 1207959552 | bytes 1376256 | tf_op jit(solution)/shard_map/pallas_call | solution.py:264
  53.9 2.8 %collective-permute-start.11 = (bf16[3,192,128]{2,1,0:T(8,128)(2,1)S(1)}, bf16[3,192,128]{2,1,0:T(8,128)(2,1)S(1)}, u32[]{:S(2)}, u32[]{:S(2)}) collective-permute-start(bf16[3,192,128]{2,1,0:T(8,128)(2,1)S(1)} %get-tuple-element.79), channel_id=1, source_target_pairs={{0,1},{1,0},{2,3},{3,2},{4,5},{5,4},{6,7},{7,6},{8,9},{9,8},{10,11... | collective-permute-start | bytes 442376 | tf_op jit(solution)/shard_map/ppermute | solution.py:295
  56.7 1.8 %collective-permute-start.9 = (bf16[3,192,128]{2,1,0:T(8,128)(2,1)S(1)}, bf16[3,192,128]{2,1,0:T(8,128)(2,1)S(1)}, u32[]{:S(2)}, u32[]{:S(2)}) collective-permute-start(bf16[3,192,128]{2,1,0:T(8,128)(2,1)S(1)} %get-tuple-element.77), channel_id=1, source_target_pairs={{0,3},{1,2},{2,1},{3,0},{4,7},{5,6},{6,5},{7,4},{8,11},{9,10},{10,... | collective-permute-start | bytes 442376 | tf_op jit(solution)/shard_map/ppermute | solution.py:295
  58.6 1.2 %collective-permute-done.12 = f32[4,32,96]{2,1,0:T(8,128)S(1)} collective-permute-done((f32[4,32,96]{2,1,0:T(8,128)S(1)}, f32[4,32,96]{2,1,0:T(8,128)S(1)}, u32[]{:S(2)}, u32[]{:S(2)}) %collective-permute-start.12) | collective-permute-done | bytes 49184 | tf_op jit(solution)/shard_map/ppermute | solution.py:304
  59.8 2.5 %collective-permute-start.15 = (f32[4,32,96]{2,1,0:T(8,128)S(1)}, f32[4,32,96]{2,1,0:T(8,128)S(1)}, u32[]{:S(2)}, u32[]{:S(2)}) collective-permute-start(f32[4,32,96]{2,1,0:T(8,128)S(1)} %add.8.refs_8_), channel_id=1, source_target_pairs={{0,24},{4,28},{8,16},{12,20},{16,8},{20,12},{24,0},{28,4},{1,25},{... | collective-permute-start | bytes 147464 | tf_op jit(solution)/shard_map/ppermute | solution.py:304
  62.3 0.5 collective-permute-start.14
  62.8 0.5 collective-permute-start.13
  63.4 1.7 %collective-permute-done.15.refs_11_ = f32[4,32,96]{2,1,0:T(8,128)S(1)} collective-permute-done((f32[4,32,96]{2,1,0:T(8,128)S(1)}, f32[4,32,96]{2,1,0:T(8,128)S(1)}, u32[]{:S(2)}, u32[]{:S(2)}) %collective-permute-start.15) | collective-permute-done | bytes 49184 | tf_op jit(solution)/shard_map/ppermute | solution.py:304
  65.1 1.5 %collective-permute-done.14.refs_10_ = f32[4,32,96]{2,1,0:T(8,128)S(1)} collective-permute-done((f32[4,32,96]{2,1,0:T(8,128)S(1)}, f32[4,32,96]{2,1,0:T(8,128)S(1)}, u32[]{:S(2)}, u32[]{:S(2)}) %collective-permute-start.14) | collective-permute-done | bytes 49184 | tf_op jit(solution)/shard_map/ppermute | solution.py:304
  66.6 0.5 collective-permute-done.13.refs_9_
  67.1 3.5 %collective-permute-done.10.refs_6_ = bf16[3,192,128]{2,1,0:T(8,128)(2,1)S(1)} collective-permute-done((bf16[3,192,128]{2,1,0:T(8,128)(2,1)S(1)}, bf16[3,192,128]{2,1,0:T(8,128)(2,1)S(1)}, u32[]{:S(2)}, u32[]{:S(2)}) %collective-permute-start.10) | collective-permute-done | bytes 147488 | tf_op jit(solution)/shard_map/ppermute | solution.py:295
  70.7 1.4 %shard_map.113 = (bf16[1,128,1536]{2,1,0:T(8,128)(2,1)}, bf16[1,128,1536]{2,1,0:T(8,128)(2,1)}, bf16[1,128,1536]{2,1,0:T(8,128)(2,1)}, f32[31,384]{1,0:T(8,128)}, f32[384]{0:T(512)}) custom-call(s32[1]{0:T(128)} %bitcast.rank_ref, bf16[3,192,128]{2,1,0:T(8,128)(2,1)S(1)} %get-tuple-element.72.refs_0_, ...), custom_call_target="tpu_custom_call" | custom-call | bytes 2359296 | tf_op jit(solution)/shard_map/pallas_call | solution.py:82
  (25 shorter events, 0.3 us)
Async XLA Ops:
  0.6 10.0 %copy-start = (f32[31,1536]{1,0:T(8,128)S(1)}, f32[31,1536]{1,0:T(8,128)}, u32[]{:S(2)}) copy-start(f32[31,1536]{1,0:T(8,128)} %param.11) | copy-start | bytes 571396
  2.7 7.8 %copy-start.1 = (f32[1536]{0:T(1024)S(1)}, f32[1536]{0:T(1024)}, u32[]{:S(2)}) copy-start(f32[1536]{0:T(1024)} %param.12) | copy-start | bytes 18436
  2.7 11.0 %collective-permute-start = (bf16[4,192,128]{2,1,0:T(8,128)(2,1)S(1)}, bf16[4,192,128]{2,1,0:T(8,128)(2,1)S(1)}, u32[]{:S(2)}, u32[]{:S(2)}) collective-permute-start(bf16[4,192,128]{2,1,0:T(8,128)(2,1)S(1)} %get-tuple-element.46), channel_id=1, source_target_pairs={{0,3},{1,2},{2,1},{3,0},{4,7},{5,6},{6,5},{7,4},{8,11},{9,10},{10,... | collective-permute-start | bytes 589832 | tf_op jit(solution)/shard_map/ppermute | solution.py:295
  7.8 16.8 %collective-permute-start.1 = (bf16[4,192,128]{2,1,0:T(8,128)(2,1)S(1)}, bf16[4,192,128]{2,1,0:T(8,128)(2,1)S(1)}, u32[]{:S(2)}, u32[]{:S(2)}) collective-permute-start(bf16[4,192,128]{2,1,0:T(8,128)(2,1)S(1)} %get-tuple-element.47), channel_id=1, source_target_pairs={{0,2},{1,3},{2,0},{3,1},{4,6},{5,7},{6,4},{7,5},{8,10},{9,11},{10,... | collective-permute-start | bytes 589832 | tf_op jit(solution)/shard_map/ppermute | solution.py:295
  7.8 16.8 %collective-permute-start.2 = (bf16[4,192,128]{2,1,0:T(8,128)(2,1)S(1)}, bf16[4,192,128]{2,1,0:T(8,128)(2,1)S(1)}, u32[]{:S(2)}, u32[]{:S(2)}) collective-permute-start(bf16[4,192,128]{2,1,0:T(8,128)(2,1)S(1)} %get-tuple-element.48), channel_id=1, source_target_pairs={{0,1},{1,0},{2,3},{3,2},{4,5},{5,4},{6,7},{7,6},{8,9},{9,8},{10,11... | collective-permute-start | bytes 589832 | tf_op jit(solution)/shard_map/ppermute | solution.py:295
  8.5 30.6 %collective-permute-start.5 = (bf16[4,192,128]{2,1,0:T(8,128)(2,1)S(1)}, bf16[4,192,128]{2,1,0:T(8,128)(2,1)S(1)}, u32[]{:S(2)}, u32[]{:S(2)}) collective-permute-start(bf16[4,192,128]{2,1,0:T(8,128)(2,1)S(1)} %get-tuple-element.58), channel_id=1, source_target_pairs={{0,1},{1,0},{2,3},{3,2},{4,5},{5,4},{6,7},{7,6},{8,9},{9,8},{10,11... | collective-permute-start | bytes 589832 | tf_op jit(solution)/shard_map/ppermute | solution.py:295
  24.6 14.5 %collective-permute-start.3 = (bf16[4,192,128]{2,1,0:T(8,128)(2,1)S(1)}, bf16[4,192,128]{2,1,0:T(8,128)(2,1)S(1)}, u32[]{:S(2)}, u32[]{:S(2)}) collective-permute-start(bf16[4,192,128]{2,1,0:T(8,128)(2,1)S(1)} %get-tuple-element.56), channel_id=1, source_target_pairs={{0,3},{1,2},{2,1},{3,0},{4,7},{5,6},{6,5},{7,4},{8,11},{9,10},{10,... | collective-permute-start | bytes 589832 | tf_op jit(solution)/shard_map/ppermute | solution.py:295
  27.2 15.0 %collective-permute-start.4 = (bf16[4,192,128]{2,1,0:T(8,128)(2,1)S(1)}, bf16[4,192,128]{2,1,0:T(8,128)(2,1)S(1)}, u32[]{:S(2)}, u32[]{:S(2)}) collective-permute-start(bf16[4,192,128]{2,1,0:T(8,128)(2,1)S(1)} %get-tuple-element.57), channel_id=1, source_target_pairs={{0,2},{1,3},{2,0},{3,1},{4,6},{5,7},{6,4},{7,5},{8,10},{9,11},{10,... | collective-permute-start | bytes 589832 | tf_op jit(solution)/shard_map/ppermute | solution.py:295
  37.3 19.4 %collective-permute-start.8 = (bf16[3,192,128]{2,1,0:T(8,128)(2,1)S(1)}, bf16[3,192,128]{2,1,0:T(8,128)(2,1)S(1)}, u32[]{:S(2)}, u32[]{:S(2)}) collective-permute-start(bf16[3,192,128]{2,1,0:T(8,128)(2,1)S(1)} %get-tuple-element.68), channel_id=1, source_target_pairs={{0,1},{1,0},{2,3},{3,2},{4,5},{5,4},{6,7},{7,6},{8,9},{9,8},{10,11... | collective-permute-start | bytes 442376 | tf_op jit(solution)/shard_map/ppermute | solution.py:295
  42.3 14.4 %collective-permute-start.6 = (bf16[3,192,128]{2,1,0:T(8,128)(2,1)S(1)}, bf16[3,192,128]{2,1,0:T(8,128)(2,1)S(1)}, u32[]{:S(2)}, u32[]{:S(2)}) collective-permute-start(bf16[3,192,128]{2,1,0:T(8,128)(2,1)S(1)} %get-tuple-element.66), channel_id=1, source_target_pairs={{0,3},{1,2},{2,1},{3,0},{4,7},{5,6},{6,5},{7,4},{8,11},{9,10},{10,... | collective-permute-start | bytes 442376 | tf_op jit(solution)/shard_map/ppermute | solution.py:295
  44.0 12.7 %collective-permute-start.7 = (bf16[3,192,128]{2,1,0:T(8,128)(2,1)S(1)}, bf16[3,192,128]{2,1,0:T(8,128)(2,1)S(1)}, u32[]{:S(2)}, u32[]{:S(2)}) collective-permute-start(bf16[3,192,128]{2,1,0:T(8,128)(2,1)S(1)} %get-tuple-element.67), channel_id=1, source_target_pairs={{0,2},{1,3},{2,0},{3,1},{4,6},{5,7},{6,4},{7,5},{8,10},{9,11},{10,... | collective-permute-start | bytes 442376 | tf_op jit(solution)/shard_map/ppermute | solution.py:295
  53.9 8.9 %collective-permute-start.11 = (bf16[3,192,128]{2,1,0:T(8,128)(2,1)S(1)}, bf16[3,192,128]{2,1,0:T(8,128)(2,1)S(1)}, u32[]{:S(2)}, u32[]{:S(2)}) collective-permute-start(bf16[3,192,128]{2,1,0:T(8,128)(2,1)S(1)} %get-tuple-element.79), channel_id=1, source_target_pairs={{0,1},{1,0},{2,3},{3,2},{4,5},{5,4},{6,7},{7,6},{8,9},{9,8},{10,11... | collective-permute-start | bytes 442376 | tf_op jit(solution)/shard_map/ppermute | solution.py:295
  56.7 10.4 %collective-permute-start.9 = (bf16[3,192,128]{2,1,0:T(8,128)(2,1)S(1)}, bf16[3,192,128]{2,1,0:T(8,128)(2,1)S(1)}, u32[]{:S(2)}, u32[]{:S(2)}) collective-permute-start(bf16[3,192,128]{2,1,0:T(8,128)(2,1)S(1)} %get-tuple-element.77), channel_id=1, source_target_pairs={{0,3},{1,2},{2,1},{3,0},{4,7},{5,6},{6,5},{7,4},{8,11},{9,10},{10,... | collective-permute-start | bytes 442376 | tf_op jit(solution)/shard_map/ppermute | solution.py:295
  58.5 12.2 %collective-permute-start.10 = (bf16[3,192,128]{2,1,0:T(8,128)(2,1)S(1)}, bf16[3,192,128]{2,1,0:T(8,128)(2,1)S(1)}, u32[]{:S(2)}, u32[]{:S(2)}) collective-permute-start(bf16[3,192,128]{2,1,0:T(8,128)(2,1)S(1)} %get-tuple-element.78), channel_id=1, source_target_pairs={{0,2},{1,3},{2,0},{3,1},{4,6},{5,7},{6,4},{7,5},{8,10},{9,11},{10,... | collective-permute-start | bytes 442376 | tf_op jit(solution)/shard_map/ppermute | solution.py:295
  58.5 1.3 %collective-permute-start.12 = (f32[4,32,96]{2,1,0:T(8,128)S(1)}, f32[4,32,96]{2,1,0:T(8,128)S(1)}, u32[]{:S(2)}, u32[]{:S(2)}) collective-permute-start(f32[4,32,96]{2,1,0:T(8,128)S(1)} %pad_maximum_fusion), channel_id=1, source_target_pairs={{0,4},{4,0},{8,12},{12,8},{16,20},{20,16},{24,28},{28,24},{1,5},{5... | collective-permute-start | bytes 147464 | tf_op jit(solution)/shard_map/ppermute | solution.py:304
  59.8 5.3 %collective-permute-start.15 = (f32[4,32,96]{2,1,0:T(8,128)S(1)}, f32[4,32,96]{2,1,0:T(8,128)S(1)}, u32[]{:S(2)}, u32[]{:S(2)}) collective-permute-start(f32[4,32,96]{2,1,0:T(8,128)S(1)} %add.8.refs_8_), channel_id=1, source_target_pairs={{0,24},{4,28},{8,16},{12,20},{16,8},{20,12},{24,0},{28,4},{1,25},{... | collective-permute-start | bytes 147464 | tf_op jit(solution)/shard_map/ppermute | solution.py:304
  62.3 4.3 %collective-permute-start.14 = (f32[4,32,96]{2,1,0:T(8,128)S(1)}, f32[4,32,96]{2,1,0:T(8,128)S(1)}, u32[]{:S(2)}, u32[]{:S(2)}) collective-permute-start(f32[4,32,96]{2,1,0:T(8,128)S(1)} %add.8.refs_8_), channel_id=1, source_target_pairs={{0,16},{4,20},{8,24},{12,28},{16,0},{20,4},{24,8},{28,12},{1,17},{... | collective-permute-start | bytes 147464 | tf_op jit(solution)/shard_map/ppermute | solution.py:304
  62.8 4.3 %collective-permute-start.13 = (f32[4,32,96]{2,1,0:T(8,128)S(1)}, f32[4,32,96]{2,1,0:T(8,128)S(1)}, u32[]{:S(2)}, u32[]{:S(2)}) collective-permute-start(f32[4,32,96]{2,1,0:T(8,128)S(1)} %add.8.refs_8_), channel_id=1, source_target_pairs={{0,8},{4,12},{8,0},{12,4},{16,24},{20,28},{24,16},{28,20},{1,9},{5... | collective-permute-start | bytes 147464 | tf_op jit(solution)/shard_map/ppermute | solution.py:304

commit v6 on v5

--- a/solution.py
+++ b/solution.py
@@ -66,7 +66,7 @@
                 first = pl.multiple_of((rank ^ distance) * share + chunk * high, 16)
                 turned[which, pl.ds(first, high), :] = pieces[chunk * count + place][which]
         out[0] = turned[which].T
-    taps = tree_sum([ref[...] for ref in taps_refs])
+    taps = taps_refs[0][...] + taps_refs[1][...]
     heads, _, depth = taps.shape
     for head in range(heads):
         at = slice(head * depth, (head + 1) * depth)
@@ -285,8 +285,10 @@
     return outs[:count], outs[count]
 
 
-def exchanged(pieces, before):
+def exchanged(pieces, before, late=None):
     pieces = list(pieces)
+    if late is not None:
+        pieces[1], late = lax.optimization_barrier((pieces[1], late))
     if before is not None and len(pieces) > 2:
         pieces[:1:-1], before[:0:-1] = lax.optimization_barrier((pieces[:1:-1], before[:0:-1]))
     moved = pieces[:1] * len(pieces)
@@ -296,19 +298,9 @@
     return moved
 
 
-def terms(array, axis, stride, reach):
-    count = lax.axis_size(axis)
-    found = [array]
-    for distance in range(stride, reach, stride):
-        pairs = [(i, i ^ distance) for i in range(count)]
-        found.append(lax.ppermute(array, axis, pairs))
-    return found
-
-
-def tree_sum(found):
-    while len(found) > 1:
-        found = [a + b for a, b in zip(found[::2], found[1::2])]
-    return found[0]
+def with_partner(array, axis, distance):
+    pairs = [(i, i ^ distance) for i in range(lax.axis_size(axis))]
+    return [array, lax.ppermute(array, axis, pairs)]
 
 
 def on_device(queries, keys, values, grad_out, conv_weight, conv_bias, lengths):
@@ -331,12 +323,20 @@
     for chunk in range(chunks):
         at = slice(chunk * step, (chunk + 1) * step)
         grads, part = core(scalars, weight[at], bias[at], order[chunk])
-        order.append(exchanged(grads, order[-1]))
         taps.append(part)
-    returned = order[chunks:]
-    taps, returned[0] = lax.optimization_barrier((jnp.concatenate(taps, axis=0), returned[0]))
-    taps = tree_sum(terms(taps, "dp", 1, 2))
-    return unpack(rank[None], terms(taps, "dp", 2, lax.axis_size("dp")), returned, count, chunks)
+        if chunk < chunks - 1:
+            order.append(exchanged(grads, order[-1]))
+    before = order[-1]
+    taps, before[:0:-1] = lax.optimization_barrier((jnp.concatenate(taps, axis=0), before[:0:-1]))
+    pair = with_partner(taps, "dp", 1)
+    distance = 2
+    while distance < lax.axis_size("dp"):
+        total = pair[0] + pair[1]
+        if distance == 2:
+            order.append(exchanged(grads, order[-1], total))
+        pair = with_partner(total, "dp", distance)
+        distance *= 2
+    return unpack(rank[None], pair, order[chunks:], count, chunks)
 
 
 def solution(mesh):

time: 72.2 us -> 73.5 us (1.018)
  waiting for transfers between devices: 25.5 us -> 27.4 us
    ppermute x12, waiting for transfers between devices: 20.5 us -> 24.6 us  [exchanged(): moved[distance] = lax.ppermute(pieces[distance], 'seq', pairs)]
    ppermute x4 -> x3, waiting for transfers between devices: 4.97 us -> 2.78 us  [with_partner(): return [array, lax.ppermute(array, axis, pairs)]]
    ppermute x4 -> x3, starting transfers between devices: 3.63 us -> 3.08 us  [with_partner(): return [array, lax.ppermute(array, axis, pairs)]]
  transfers between devices with their start and end apart: 16 -> 15, of which waited for: 8 -> 6; matrix products, arithmetic and copies ran while one was open for 0% -> 0% of each run, Pallas kernels for 28% -> 27%
where the time goes in v6:
time: 73.5 us; the launch traced here: 73.3 us
  waiting for transfers between devices  27.4 us (37%)
  Pallas kernels  23.3 us (32%)
  starting transfers between devices  20.8 us (28%)
  between operations  1.43 us (2%)
    ppermute x12, waiting for transfers between devices, exchanged(): moved[distance] = lax.ppermute(pieces[distance], 'seq', pairs)  24.6 us
    pallas_call x2, Pallas kernels, core(): pl.pallas_call(functools.partial(core_kernel, count, block), out_shape=(p...  19.9 us
    ppermute x12, starting transfers between devices, exchanged(): moved[distance] = lax.ppermute(pieces[distance], 'seq', pairs)  17.8 us
    ppermute x3, starting transfers between devices, with_partner(): return [array, lax.ppermute(array, axis, pairs)]  3.08 us
    ppermute x3, waiting for transfers between devices, with_partner(): return [array, lax.ppermute(array, axis, pairs)]  2.78 us
    pallas_call x1, Pallas kernels, pack(): pl.pallas_call(functools.partial(pack_kernel, count, chunks), out_shape=(...  2.03 us
  transfers between devices with their start and end apart: 15, of which 6 were waited for; matrix products, arithmetic and copies ran while one was open for 0% of the time, Pallas kernels for 27%

profile of v6, /device:TPU:0, one launch (start us, length us, event | category | flops | bytes accessed | tf_op | source)
XLA Modules:
  0.0 73.3 jit_solution(14771868306234703340)
XLA Ops:
  0.6 2.0 %shard_map.110 = (bf16[4,192,128]{2,1,0:T(8,128)(2,1)S(1)}, bf16[4,192,128]{2,1,0:T(8,128)(2,1)S(1)}, bf16[4,192,128]{2,1,0:T(8,128)(2,1)S(1)}, bf16[4,192,128]{...) custom-call(s32[1]{0:T(128)} %bitcast.rank_ref, ...), custom_call_target="tpu_custom_call" | custom-call | bytes 3145728 | tf_op jit(solution)/shard_map/pallas_call | solution.py:38
  2.7 5.1 %collective-permute-start = (bf16[4,192,128]{2,1,0:T(8,128)(2,1)S(1)}, bf16[4,192,128]{2,1,0:T(8,128)(2,1)S(1)}, u32[]{:S(2)}, u32[]{:S(2)}) collective-permute-start(bf16[4,192,128]{2,1,0:T(8,128)(2,1)S(1)} %get-tuple-element.46), channel_id=1, source_target_pairs={{0,3},{1,2},{2,1},{3,0},{4,7},{5,6},{6,5},{7,4},{8,11},{9,10},{10,... | collective-permute-start | bytes 589832 | tf_op jit(solution)/shard_map/ppermute | solution.py:297
  7.8 0.6 collective-permute-start.2
  8.5 1.4 %collective-permute-start.5 = (bf16[4,192,128]{2,1,0:T(8,128)(2,1)S(1)}, bf16[4,192,128]{2,1,0:T(8,128)(2,1)S(1)}, u32[]{:S(2)}, u32[]{:S(2)}) collective-permute-start(bf16[4,192,128]{2,1,0:T(8,128)(2,1)S(1)} %get-tuple-element.58), channel_id=1, source_target_pairs={{0,1},{1,0},{2,3},{3,2},{4,5},{5,4},{6,7},{7,6},{8,9},{9,8},{10,11... | collective-permute-start | bytes 589832 | tf_op jit(solution)/shard_map/ppermute | solution.py:297
  10.5 0.1 reshape.17
  10.6 0.1 reshape.16
  10.8 2.9 %collective-permute-done.refs_1_ = bf16[4,192,128]{2,1,0:T(8,128)(2,1)S(1)} collective-permute-done((bf16[4,192,128]{2,1,0:T(8,128)(2,1)S(1)}, bf16[4,192,128]{2,1,0:T(8,128)(2,1)S(1)}, u32[]{:S(2)}, u32[]{:S(2)}) %collective-permute-start) | collective-permute-done | bytes 196640 | tf_op jit(solution)/shard_map/ppermute | solution.py:297
  13.7 10.9 %collective-permute-done.1.refs_2_ = bf16[4,192,128]{2,1,0:T(8,128)(2,1)S(1)} collective-permute-done((bf16[4,192,128]{2,1,0:T(8,128)(2,1)S(1)}, bf16[4,192,128]{2,1,0:T(8,128)(2,1)S(1)}, u32[]{:S(2)}, u32[]{:S(2)}) %collective-permute-start.1) | collective-permute-done | bytes 196640 | tf_op jit(solution)/shard_map/ppermute | solution.py:297
  24.6 2.6 %collective-permute-start.3 = (bf16[4,192,128]{2,1,0:T(8,128)(2,1)S(1)}, bf16[4,192,128]{2,1,0:T(8,128)(2,1)S(1)}, u32[]{:S(2)}, u32[]{:S(2)}) collective-permute-start(bf16[4,192,128]{2,1,0:T(8,128)(2,1)S(1)} %get-tuple-element.56), channel_id=1, source_target_pairs={{0,3},{1,2},{2,1},{3,0},{4,7},{5,6},{6,5},{7,4},{8,11},{9,10},{10,... | collective-permute-start | bytes 589832 | tf_op jit(solution)/shard_map/ppermute | solution.py:297
  27.3 0.1 pad_add_fusion.scalars
  27.3 9.9 %shard_map.111 = (bf16[3,192,128]{2,1,0:T(8,128)(2,1)S(1)}, bf16[3,192,128]{2,1,0:T(8,128)(2,1)S(1)}, bf16[3,192,128]{2,1,0:T(8,128)(2,1)S(1)}, bf16[3,192,128]{2,1,0:T(8,128)(2,1)S(1)}, f32[2,32,96]{2,1,0:T(8,128)S(1)}) custom-call(s32[2]{0:T(128)S(1)} %pad_add_fusion.scalars, f32[2,31,96]{2,1,0:T(8,128)S(1)} %get-tuple-element.82.weight_ref, ...), custom_call_target="tpu_custom_call" | custom-call | flops 1207959552 | bytes 1376256 | tf_op jit(solution)/shard_map/pallas_call | solution.py:264
  37.3 1.8 %collective-permute-start.8 = (bf16[3,192,128]{2,1,0:T(8,128)(2,1)S(1)}, bf16[3,192,128]{2,1,0:T(8,128)(2,1)S(1)}, u32[]{:S(2)}, u32[]{:S(2)}) collective-permute-start(bf16[3,192,128]{2,1,0:T(8,128)(2,1)S(1)} %get-tuple-element.68), channel_id=1, source_target_pairs={{0,1},{1,0},{2,3},{3,2},{4,5},{5,4},{6,7},{7,6},{8,9},{9,8},{10,11... | collective-permute-start | bytes 442376 | tf_op jit(solution)/shard_map/ppermute | solution.py:297
  39.1 3.2 %collective-permute-done.4.refs_2_ = bf16[4,192,128]{2,1,0:T(8,128)(2,1)S(1)} collective-permute-done((bf16[4,192,128]{2,1,0:T(8,128)(2,1)S(1)}, bf16[4,192,128]{2,1,0:T(8,128)(2,1)S(1)}, u32[]{:S(2)}, u32[]{:S(2)}) %collective-permute-start.4) | collective-permute-done | bytes 196640 | tf_op jit(solution)/shard_map/ppermute | solution.py:297
  42.3 1.7 %collective-permute-start.6 = (bf16[3,192,128]{2,1,0:T(8,128)(2,1)S(1)}, bf16[3,192,128]{2,1,0:T(8,128)(2,1)S(1)}, u32[]{:S(2)}, u32[]{:S(2)}) collective-permute-start(bf16[3,192,128]{2,1,0:T(8,128)(2,1)S(1)} %get-tuple-element.66), channel_id=1, source_target_pairs={{0,3},{1,2},{2,1},{3,0},{4,7},{5,6},{6,5},{7,4},{8,11},{9,10},{10,... | collective-permute-start | bytes 442376 | tf_op jit(solution)/shard_map/ppermute | solution.py:297
  44.0 10.0 %shard_map.112 = (bf16[3,192,128]{2,1,0:T(8,128)(2,1)S(1)}, bf16[3,192,128]{2,1,0:T(8,128)(2,1)S(1)}, bf16[3,192,128]{2,1,0:T(8,128)(2,1)S(1)}, bf16[3,192,128]{2,1,0:T(8,128)(2,1)S(1)}, f32[2,32,96]{2,1,0:T(8,128)S(1)}) custom-call(s32[2]{0:T(128)S(1)} %pad_add_fusion.scalars, f32[2,31,96]{2,1,0:T(8,128)S(1)} %get-tuple-element.81.weight_ref, ...), custom_call_target="tpu_custom_call" | custom-call | flops 1207959552 | bytes 1376256 | tf_op jit(solution)/shard_map/pallas_call | solution.py:264
  54.0 1.2 %collective-permute-done.7.refs_2_ = bf16[3,192,128]{2,1,0:T(8,128)(2,1)S(1)} collective-permute-done((bf16[3,192,128]{2,1,0:T(8,128)(2,1)S(1)}, bf16[3,192,128]{2,1,0:T(8,128)(2,1)S(1)}, u32[]{:S(2)}, u32[]{:S(2)}) %collective-permute-start.7) | collective-permute-done | bytes 147488 | tf_op jit(solution)/shard_map/ppermute | solution.py:297
  55.2 2.2 %collective-permute-start.9 = (bf16[3,192,128]{2,1,0:T(8,128)(2,1)S(1)}, bf16[3,192,128]{2,1,0:T(8,128)(2,1)S(1)}, u32[]{:S(2)}, u32[]{:S(2)}) collective-permute-start(bf16[3,192,128]{2,1,0:T(8,128)(2,1)S(1)} %get-tuple-element.76), channel_id=1, source_target_pairs={{0,3},{1,2},{2,1},{3,0},{4,7},{5,6},{6,5},{7,4},{8,11},{9,10},{10,... | collective-permute-start | bytes 442376 | tf_op jit(solution)/shard_map/ppermute | solution.py:297
  57.4 0.9 %collective-permute-start.10 = (bf16[3,192,128]{2,1,0:T(8,128)(2,1)S(1)}, bf16[3,192,128]{2,1,0:T(8,128)(2,1)S(1)}, u32[]{:S(2)}, u32[]{:S(2)}) collective-permute-start(bf16[3,192,128]{2,1,0:T(8,128)(2,1)S(1)} %get-tuple-element.77), channel_id=1, source_target_pairs={{0,2},{1,3},{2,0},{3,1},{4,6},{5,7},{6,4},{7,5},{8,10},{9,11},{10,... | collective-permute-start | bytes 442376 | tf_op jit(solution)/shard_map/ppermute | solution.py:297
  58.3 1.4 %collective-permute-start.12 = (bf16[3,192,128]{2,1,0:T(8,128)(2,1)S(1)}, bf16[3,192,128]{2,1,0:T(8,128)(2,1)S(1)}, u32[]{:S(2)}, u32[]{:S(2)}) collective-permute-start(bf16[3,192,128]{2,1,0:T(8,128)(2,1)S(1)} %get-tuple-element.80), channel_id=1, source_target_pairs={{0,1},{1,0},{2,3},{3,2},{4,5},{5,4},{6,7},{7,6},{8,9},{9,8},{10,11... | collective-permute-start | bytes 442376 | tf_op jit(solution)/shard_map/ppermute | solution.py:297
  59.7 1.5 %collective-permute-start.13 = (f32[4,32,96]{2,1,0:T(8,128)S(1)}, f32[4,32,96]{2,1,0:T(8,128)S(1)}, u32[]{:S(2)}, u32[]{:S(2)}) collective-permute-start(f32[4,32,96]{2,1,0:T(8,128)S(1)} %add.11), channel_id=1, source_target_pairs={{0,8},{4,12},{8,0},{12,4},{16,24},{20,28},{24,16},{28,20},{1,9},{5... | collective-permute-start | bytes 147464 | tf_op jit(solution)/shard_map/ppermute | solution.py:303
  61.2 2.8 %collective-permute-done.13 = f32[4,32,96]{2,1,0:T(8,128)S(1)} collective-permute-done((f32[4,32,96]{2,1,0:T(8,128)S(1)}, f32[4,32,96]{2,1,0:T(8,128)S(1)}, u32[]{:S(2)}, u32[]{:S(2)}) %collective-permute-start.13) | collective-permute-done | bytes 49184 | tf_op jit(solution)/shard_map/ppermute | solution.py:303
  64.0 1.6 %collective-permute-start.14 = (f32[4,32,96]{2,1,0:T(8,128)S(1)}, f32[4,32,96]{2,1,0:T(8,128)S(1)}, u32[]{:S(2)}, u32[]{:S(2)}) collective-permute-start(f32[4,32,96]{2,1,0:T(8,128)S(1)} %add.12.refs_8_), channel_id=1, source_target_pairs={{0,16},{4,20},{8,24},{12,28},{16,0},{20,4},{24,8},{28,12},{1,17},{... | collective-permute-start | bytes 147464 | tf_op jit(solution)/shard_map/ppermute | solution.py:303
  65.5 6.4 %collective-permute-done.10.refs_6_ = bf16[3,192,128]{2,1,0:T(8,128)(2,1)S(1)} collective-permute-done((bf16[3,192,128]{2,1,0:T(8,128)(2,1)S(1)}, bf16[3,192,128]{2,1,0:T(8,128)(2,1)S(1)}, u32[]{:S(2)}, u32[]{:S(2)}) %collective-permute-start.10) | collective-permute-done | bytes 147488 | tf_op jit(solution)/shard_map/ppermute | solution.py:297
  72.0 1.4 %shard_map.113 = (bf16[1,128,1536]{2,1,0:T(8,128)(2,1)}, bf16[1,128,1536]{2,1,0:T(8,128)(2,1)}, bf16[1,128,1536]{2,1,0:T(8,128)(2,1)}, f32[31,384]{1,0:T(8,128)}, f32[384]{0:T(512)}) custom-call(s32[1]{0:T(128)} %bitcast.rank_ref, bf16[3,192,128]{2,1,0:T(8,128)(2,1)S(1)} %get-tuple-element.52.refs_0_, ...), custom_call_target="tpu_custom_call" | custom-call | bytes 2359296 | tf_op jit(solution)/shard_map/pallas_call | solution.py:82
  (24 shorter events, 0.1 us)
Async XLA Ops:
  0.6 10.0 %copy-start = (f32[31,1536]{1,0:T(8,128)S(1)}, f32[31,1536]{1,0:T(8,128)}, u32[]{:S(2)}) copy-start(f32[31,1536]{1,0:T(8,128)} %param.11) | copy-start | bytes 571396
  2.7 7.8 %copy-start.1 = (f32[1536]{0:T(1024)S(1)}, f32[1536]{0:T(1024)}, u32[]{:S(2)}) copy-start(f32[1536]{0:T(1024)} %param.12) | copy-start | bytes 18436
  2.7 11.0 %collective-permute-start = (bf16[4,192,128]{2,1,0:T(8,128)(2,1)S(1)}, bf16[4,192,128]{2,1,0:T(8,128)(2,1)S(1)}, u32[]{:S(2)}, u32[]{:S(2)}) collective-permute-start(bf16[4,192,128]{2,1,0:T(8,128)(2,1)S(1)} %get-tuple-element.46), channel_id=1, source_target_pairs={{0,3},{1,2},{2,1},{3,0},{4,7},{5,6},{6,5},{7,4},{8,11},{9,10},{10,... | collective-permute-start | bytes 589832 | tf_op jit(solution)/shard_map/ppermute | solution.py:297
  7.8 16.8 %collective-permute-start.1 = (bf16[4,192,128]{2,1,0:T(8,128)(2,1)S(1)}, bf16[4,192,128]{2,1,0:T(8,128)(2,1)S(1)}, u32[]{:S(2)}, u32[]{:S(2)}) collective-permute-start(bf16[4,192,128]{2,1,0:T(8,128)(2,1)S(1)} %get-tuple-element.47), channel_id=1, source_target_pairs={{0,2},{1,3},{2,0},{3,1},{4,6},{5,7},{6,4},{7,5},{8,10},{9,11},{10,... | collective-permute-start | bytes 589832 | tf_op jit(solution)/shard_map/ppermute | solution.py:297
  7.8 16.8 %collective-permute-start.2 = (bf16[4,192,128]{2,1,0:T(8,128)(2,1)S(1)}, bf16[4,192,128]{2,1,0:T(8,128)(2,1)S(1)}, u32[]{:S(2)}, u32[]{:S(2)}) collective-permute-start(bf16[4,192,128]{2,1,0:T(8,128)(2,1)S(1)} %get-tuple-element.48), channel_id=1, source_target_pairs={{0,1},{1,0},{2,3},{3,2},{4,5},{5,4},{6,7},{7,6},{8,9},{9,8},{10,11... | collective-permute-start | bytes 589832 | tf_op jit(solution)/shard_map/ppermute | solution.py:297
  8.5 30.6 %collective-permute-start.5 = (bf16[4,192,128]{2,1,0:T(8,128)(2,1)S(1)}, bf16[4,192,128]{2,1,0:T(8,128)(2,1)S(1)}, u32[]{:S(2)}, u32[]{:S(2)}) collective-permute-start(bf16[4,192,128]{2,1,0:T(8,128)(2,1)S(1)} %get-tuple-element.58), channel_id=1, source_target_pairs={{0,1},{1,0},{2,3},{3,2},{4,5},{5,4},{6,7},{7,6},{8,9},{9,8},{10,11... | collective-permute-start | bytes 589832 | tf_op jit(solution)/shard_map/ppermute | solution.py:297
  24.6 14.5 %collective-permute-start.3 = (bf16[4,192,128]{2,1,0:T(8,128)(2,1)S(1)}, bf16[4,192,128]{2,1,0:T(8,128)(2,1)S(1)}, u32[]{:S(2)}, u32[]{:S(2)}) collective-permute-start(bf16[4,192,128]{2,1,0:T(8,128)(2,1)S(1)} %get-tuple-element.56), channel_id=1, source_target_pairs={{0,3},{1,2},{2,1},{3,0},{4,7},{5,6},{6,5},{7,4},{8,11},{9,10},{10,... | collective-permute-start | bytes 589832 | tf_op jit(solution)/shard_map/ppermute | solution.py:297
  27.2 15.0 %collective-permute-start.4 = (bf16[4,192,128]{2,1,0:T(8,128)(2,1)S(1)}, bf16[4,192,128]{2,1,0:T(8,128)(2,1)S(1)}, u32[]{:S(2)}, u32[]{:S(2)}) collective-permute-start(bf16[4,192,128]{2,1,0:T(8,128)(2,1)S(1)} %get-tuple-element.57), channel_id=1, source_target_pairs={{0,2},{1,3},{2,0},{3,1},{4,6},{5,7},{6,4},{7,5},{8,10},{9,11},{10,... | collective-permute-start | bytes 589832 | tf_op jit(solution)/shard_map/ppermute | solution.py:297
  37.3 16.7 %collective-permute-start.8 = (bf16[3,192,128]{2,1,0:T(8,128)(2,1)S(1)}, bf16[3,192,128]{2,1,0:T(8,128)(2,1)S(1)}, u32[]{:S(2)}, u32[]{:S(2)}) collective-permute-start(bf16[3,192,128]{2,1,0:T(8,128)(2,1)S(1)} %get-tuple-element.68), channel_id=1, source_target_pairs={{0,1},{1,0},{2,3},{3,2},{4,5},{5,4},{6,7},{7,6},{8,9},{9,8},{10,11... | collective-permute-start | bytes 442376 | tf_op jit(solution)/shard_map/ppermute | solution.py:297
  42.3 11.7 %collective-permute-start.6 = (bf16[3,192,128]{2,1,0:T(8,128)(2,1)S(1)}, bf16[3,192,128]{2,1,0:T(8,128)(2,1)S(1)}, u32[]{:S(2)}, u32[]{:S(2)}) collective-permute-start(bf16[3,192,128]{2,1,0:T(8,128)(2,1)S(1)} %get-tuple-element.66), channel_id=1, source_target_pairs={{0,3},{1,2},{2,1},{3,0},{4,7},{5,6},{6,5},{7,4},{8,11},{9,10},{10,... | collective-permute-start | bytes 442376 | tf_op jit(solution)/shard_map/ppermute | solution.py:297
  44.0 11.2 %collective-permute-start.7 = (bf16[3,192,128]{2,1,0:T(8,128)(2,1)S(1)}, bf16[3,192,128]{2,1,0:T(8,128)(2,1)S(1)}, u32[]{:S(2)}, u32[]{:S(2)}) collective-permute-start(bf16[3,192,128]{2,1,0:T(8,128)(2,1)S(1)} %get-tuple-element.67), channel_id=1, source_target_pairs={{0,2},{1,3},{2,0},{3,1},{4,6},{5,7},{6,4},{7,5},{8,10},{9,11},{10,... | collective-permute-start | bytes 442376 | tf_op jit(solution)/shard_map/ppermute | solution.py:297
  55.2 3.1 %collective-permute-start.11 = (f32[4,32,96]{2,1,0:T(8,128)S(1)}, f32[4,32,96]{2,1,0:T(8,128)S(1)}, u32[]{:S(2)}, u32[]{:S(2)}) collective-permute-start(f32[4,32,96]{2,1,0:T(8,128)S(1)} %pad_maximum_fusion), channel_id=1, source_target_pairs={{0,4},{4,0},{8,12},{12,8},{16,20},{20,16},{24,28},{28,24},{1,5},{5... | collective-permute-start | bytes 147464 | tf_op jit(solution)/shard_map/ppermute | solution.py:303
  55.2 10.3 %collective-permute-start.9 = (bf16[3,192,128]{2,1,0:T(8,128)(2,1)S(1)}, bf16[3,192,128]{2,1,0:T(8,128)(2,1)S(1)}, u32[]{:S(2)}, u32[]{:S(2)}) collective-permute-start(bf16[3,192,128]{2,1,0:T(8,128)(2,1)S(1)} %get-tuple-element.76), channel_id=1, source_target_pairs={{0,3},{1,2},{2,1},{3,0},{4,7},{5,6},{6,5},{7,4},{8,11},{9,10},{10,... | collective-permute-start | bytes 442376 | tf_op jit(solution)/shard_map/ppermute | solution.py:297
  57.4 14.6 %collective-permute-start.10 = (bf16[3,192,128]{2,1,0:T(8,128)(2,1)S(1)}, bf16[3,192,128]{2,1,0:T(8,128)(2,1)S(1)}, u32[]{:S(2)}, u32[]{:S(2)}) collective-permute-start(bf16[3,192,128]{2,1,0:T(8,128)(2,1)S(1)} %get-tuple-element.77), channel_id=1, source_target_pairs={{0,2},{1,3},{2,0},{3,1},{4,6},{5,7},{6,4},{7,5},{8,10},{9,11},{10,... | collective-permute-start | bytes 442376 | tf_op jit(solution)/shard_map/ppermute | solution.py:297
  58.3 13.6 %collective-permute-start.12 = (bf16[3,192,128]{2,1,0:T(8,128)(2,1)S(1)}, bf16[3,192,128]{2,1,0:T(8,128)(2,1)S(1)}, u32[]{:S(2)}, u32[]{:S(2)}) collective-permute-start(bf16[3,192,128]{2,1,0:T(8,128)(2,1)S(1)} %get-tuple-element.80), channel_id=1, source_target_pairs={{0,1},{1,0},{2,3},{3,2},{4,5},{5,4},{6,7},{7,6},{8,9},{9,8},{10,11... | collective-permute-start | bytes 442376 | tf_op jit(solution)/shard_map/ppermute | solution.py:297
  59.7 4.3 %collective-permute-start.13 = (f32[4,32,96]{2,1,0:T(8,128)S(1)}, f32[4,32,96]{2,1,0:T(8,128)S(1)}, u32[]{:S(2)}, u32[]{:S(2)}) collective-permute-start(f32[4,32,96]{2,1,0:T(8,128)S(1)} %add.11), channel_id=1, source_target_pairs={{0,8},{4,12},{8,0},{12,4},{16,24},{20,28},{24,16},{28,20},{1,9},{5... | collective-permute-start | bytes 147464 | tf_op jit(solution)/shard_map/ppermute | solution.py:303
  64.0 8.0 %collective-permute-start.14 = (f32[4,32,96]{2,1,0:T(8,128)S(1)}, f32[4,32,96]{2,1,0:T(8,128)S(1)}, u32[]{:S(2)}, u32[]{:S(2)}) collective-permute-start(f32[4,32,96]{2,1,0:T(8,128)S(1)} %add.12.refs_8_), channel_id=1, source_target_pairs={{0,16},{4,20},{8,24},{12,28},{16,0},{20,4},{24,8},{28,12},{1,17},{... | collective-permute-start | bytes 147464 | tf_op jit(solution)/shard_map/ppermute | solution.py:303

commit v7 on v5

--- a/solution.py
+++ b/solution.py
@@ -331,12 +331,20 @@
     for chunk in range(chunks):
         at = slice(chunk * step, (chunk + 1) * step)
         grads, part = core(scalars, weight[at], bias[at], order[chunk])
-        order.append(exchanged(grads, order[-1]))
         taps.append(part)
-    returned = order[chunks:]
-    taps, returned[0] = lax.optimization_barrier((jnp.concatenate(taps, axis=0), returned[0]))
+        if chunk < chunks - 1:
+            order.append(exchanged(grads, order[-1]))
+    before, grads = order[-1], list(grads)
+    if chunks > 1:
+        for distance in range(count - 1, 0, -1):
+            early = count - 1 if distance < count - 1 else 1
+            grads[distance], before[early] = lax.optimization_barrier(
+                (grads[distance], before[early])
+            )
+    order.append(exchanged(grads, None))
+    taps, before[:0:-1] = lax.optimization_barrier((jnp.concatenate(taps, axis=0), before[:0:-1]))
     taps = tree_sum(terms(taps, "dp", 1, 2))
-    return unpack(rank[None], terms(taps, "dp", 2, lax.axis_size("dp")), returned, count, chunks)
+    return unpack(rank[None], terms(taps, "dp", 2, lax.axis_size("dp")), order[chunks:], count, chunks)
 
 
 def solution(mesh):

time: 72.2 us -> 71.1 us (0.985)
  waiting for transfers between devices: 25.5 us -> 23.7 us
    ppermute x12, waiting for transfers between devices: 20.5 us -> 19.5 us  [exchanged(): moved[distance] = lax.ppermute(pieces[distance], 'seq', pairs)]
    ppermute x4, starting transfers between devices: 3.63 us -> 4.41 us  [terms(): found.append(lax.ppermute(array, axis, pairs))]
    ppermute x4, waiting for transfers between devices: 4.97 us -> 4.19 us  [terms(): found.append(lax.ppermute(array, axis, pairs))]
where the time goes in v7:
time: 71.1 us; the launch traced here: 71 us
  waiting for transfers between devices  23.7 us (33%)
  Pallas kernels  23.3 us (33%)
  starting transfers between devices  22.2 us (31%)
  between operations  1.43 us (2%)
    pallas_call x2, Pallas kernels, core(): pl.pallas_call(functools.partial(core_kernel, count, block), out_shape=(p...  19.9 us
    ppermute x12, waiting for transfers between devices, exchanged(): moved[distance] = lax.ppermute(pieces[distance], 'seq', pairs)  19.5 us
    ppermute x12, starting transfers between devices, exchanged(): moved[distance] = lax.ppermute(pieces[distance], 'seq', pairs)  17.8 us
    ppermute x4, starting transfers between devices, terms(): found.append(lax.ppermute(array, axis, pairs))  4.41 us
    ppermute x4, waiting for transfers between devices, terms(): found.append(lax.ppermute(array, axis, pairs))  4.19 us
    pallas_call x1, Pallas kernels, pack(): pl.pallas_call(functools.partial(pack_kernel, count, chunks), out_shape=(...  2.03 us
  transfers between devices with their start and end apart: 16, of which 8 were waited for; matrix products, arithmetic and copies ran while one was open for 0% of the time, Pallas kernels for 28%

profile of v7, /device:TPU:0, one launch (start us, length us, event | category | flops | bytes accessed | tf_op | source)
XLA Modules:
  0.0 71.0 jit_solution(18226661518423141884)
XLA Ops:
  0.6 2.0 %shard_map.110 = (bf16[4,192,128]{2,1,0:T(8,128)(2,1)S(1)}, bf16[4,192,128]{2,1,0:T(8,128)(2,1)S(1)}, bf16[4,192,128]{2,1,0:T(8,128)(2,1)S(1)}, bf16[4,192,128]{...) custom-call(s32[1]{0:T(128)} %bitcast.rank_ref, ...), custom_call_target="tpu_custom_call" | custom-call | bytes 3145728 | tf_op jit(solution)/shard_map/pallas_call | solution.py:38
  2.7 5.1 %collective-permute-start = (bf16[4,192,128]{2,1,0:T(8,128)(2,1)S(1)}, bf16[4,192,128]{2,1,0:T(8,128)(2,1)S(1)}, u32[]{:S(2)}, u32[]{:S(2)}) collective-permute-start(bf16[4,192,128]{2,1,0:T(8,128)(2,1)S(1)} %get-tuple-element.46), channel_id=1, source_target_pairs={{0,3},{1,2},{2,1},{3,0},{4,7},{5,6},{6,5},{7,4},{8,11},{9,10},{10,... | collective-permute-start | bytes 589832 | tf_op jit(solution)/shard_map/ppermute | solution.py:295
  7.8 0.6 collective-permute-start.2
  8.5 1.4 %collective-permute-start.5 = (bf16[4,192,128]{2,1,0:T(8,128)(2,1)S(1)}, bf16[4,192,128]{2,1,0:T(8,128)(2,1)S(1)}, u32[]{:S(2)}, u32[]{:S(2)}) collective-permute-start(bf16[4,192,128]{2,1,0:T(8,128)(2,1)S(1)} %get-tuple-element.59), channel_id=1, source_target_pairs={{0,1},{1,0},{2,3},{3,2},{4,5},{5,4},{6,7},{7,6},{8,9},{9,8},{10,11... | collective-permute-start | bytes 589832 | tf_op jit(solution)/shard_map/ppermute | solution.py:295
  10.8 2.9 %collective-permute-done.refs_1_ = bf16[4,192,128]{2,1,0:T(8,128)(2,1)S(1)} collective-permute-done((bf16[4,192,128]{2,1,0:T(8,128)(2,1)S(1)}, bf16[4,192,128]{2,1,0:T(8,128)(2,1)S(1)}, u32[]{:S(2)}, u32[]{:S(2)}) %collective-permute-start) | collective-permute-done | bytes 196640 | tf_op jit(solution)/shard_map/ppermute | solution.py:295
  13.7 10.9 %collective-permute-done.1.refs_2_ = bf16[4,192,128]{2,1,0:T(8,128)(2,1)S(1)} collective-permute-done((bf16[4,192,128]{2,1,0:T(8,128)(2,1)S(1)}, bf16[4,192,128]{2,1,0:T(8,128)(2,1)S(1)}, u32[]{:S(2)}, u32[]{:S(2)}) %collective-permute-start.1) | collective-permute-done | bytes 196640 | tf_op jit(solution)/shard_map/ppermute | solution.py:295
  24.6 2.6 %collective-permute-start.3 = (bf16[4,192,128]{2,1,0:T(8,128)(2,1)S(1)}, bf16[4,192,128]{2,1,0:T(8,128)(2,1)S(1)}, u32[]{:S(2)}, u32[]{:S(2)}) collective-permute-start(bf16[4,192,128]{2,1,0:T(8,128)(2,1)S(1)} %get-tuple-element.57), channel_id=1, source_target_pairs={{0,3},{1,2},{2,1},{3,0},{4,7},{5,6},{6,5},{7,4},{8,11},{9,10},{10,... | collective-permute-start | bytes 589832 | tf_op jit(solution)/shard_map/ppermute | solution.py:295
  27.3 9.9 %shard_map.111 = (bf16[3,192,128]{2,1,0:T(8,128)(2,1)S(1)}, bf16[3,192,128]{2,1,0:T(8,128)(2,1)S(1)}, bf16[3,192,128]{2,1,0:T(8,128)(2,1)S(1)}, bf16[3,192,128]{2,1,0:T(8,128)(2,1)S(1)}, f32[2,32,96]{2,1,0:T(8,128)S(1)}) custom-call(s32[2]{0:T(128)S(1)} %pad_add_fusion.scalars, f32[2,31,96]{2,1,0:T(8,128)S(1)} %get-tuple-element.82.weight_ref, ...), custom_call_target="tpu_custom_call" | custom-call | flops 1207959552 | bytes 1376256 | tf_op jit(solution)/shard_map/pallas_call | solution.py:264
  37.3 1.8 %collective-permute-start.8 = (bf16[3,192,128]{2,1,0:T(8,128)(2,1)S(1)}, bf16[3,192,128]{2,1,0:T(8,128)(2,1)S(1)}, u32[]{:S(2)}, u32[]{:S(2)}) collective-permute-start(bf16[3,192,128]{2,1,0:T(8,128)(2,1)S(1)} %get-tuple-element.71), channel_id=1, source_target_pairs={{0,1},{1,0},{2,3},{3,2},{4,5},{5,4},{6,7},{7,6},{8,9},{9,8},{10,11... | collective-permute-start | bytes 442376 | tf_op jit(solution)/shard_map/ppermute | solution.py:295
  39.1 3.2 %collective-permute-done.4.refs_2_ = bf16[4,192,128]{2,1,0:T(8,128)(2,1)S(1)} collective-permute-done((bf16[4,192,128]{2,1,0:T(8,128)(2,1)S(1)}, bf16[4,192,128]{2,1,0:T(8,128)(2,1)S(1)}, u32[]{:S(2)}, u32[]{:S(2)}) %collective-permute-start.4) | collective-permute-done | bytes 196640 | tf_op jit(solution)/shard_map/ppermute | solution.py:295
  42.3 1.7 %collective-permute-start.6 = (bf16[3,192,128]{2,1,0:T(8,128)(2,1)S(1)}, bf16[3,192,128]{2,1,0:T(8,128)(2,1)S(1)}, u32[]{:S(2)}, u32[]{:S(2)}) collective-permute-start(bf16[3,192,128]{2,1,0:T(8,128)(2,1)S(1)} %get-tuple-element.66), channel_id=1, source_target_pairs={{0,3},{1,2},{2,1},{3,0},{4,7},{5,6},{6,5},{7,4},{8,11},{9,10},{10,... | collective-permute-start | bytes 442376 | tf_op jit(solution)/shard_map/ppermute | solution.py:295
  44.0 10.0 %shard_map.112 = (bf16[3,192,128]{2,1,0:T(8,128)(2,1)S(1)}, bf16[3,192,128]{2,1,0:T(8,128)(2,1)S(1)}, bf16[3,192,128]{2,1,0:T(8,128)(2,1)S(1)}, bf16[3,192,128]{2,1,0:T(8,128)(2,1)S(1)}, f32[2,32,96]{2,1,0:T(8,128)S(1)}) custom-call(s32[2]{0:T(128)S(1)} %pad_add_fusion.scalars, f32[2,31,96]{2,1,0:T(8,128)S(1)} %get-tuple-element.81.weight_ref, ...), custom_call_target="tpu_custom_call" | custom-call | flops 1207959552 | bytes 1376256 | tf_op jit(solution)/shard_map/pallas_call | solution.py:264
  54.0 2.2 %collective-permute-start.9 = (bf16[3,192,128]{2,1,0:T(8,128)(2,1)S(1)}, bf16[3,192,128]{2,1,0:T(8,128)(2,1)S(1)}, u32[]{:S(2)}, u32[]{:S(2)}) collective-permute-start(bf16[3,192,128]{2,1,0:T(8,128)(2,1)S(1)} %get-tuple-element.77), channel_id=1, source_target_pairs={{0,3},{1,2},{2,1},{3,0},{4,7},{5,6},{6,5},{7,4},{8,11},{9,10},{10,... | collective-permute-start | bytes 442376 | tf_op jit(solution)/shard_map/ppermute | solution.py:295
  56.1 1.4 %collective-permute-start.11 = (bf16[3,192,128]{2,1,0:T(8,128)(2,1)S(1)}, bf16[3,192,128]{2,1,0:T(8,128)(2,1)S(1)}, u32[]{:S(2)}, u32[]{:S(2)}) collective-permute-start(bf16[3,192,128]{2,1,0:T(8,128)(2,1)S(1)} %get-tuple-element.79), channel_id=1, source_target_pairs={{0,1},{1,0},{2,3},{3,2},{4,5},{5,4},{6,7},{7,6},{8,9},{9,8},{10,11... | collective-permute-start | bytes 442376 | tf_op jit(solution)/shard_map/ppermute | solution.py:295
  57.5 0.9 %collective-permute-start.10 = (bf16[3,192,128]{2,1,0:T(8,128)(2,1)S(1)}, bf16[3,192,128]{2,1,0:T(8,128)(2,1)S(1)}, u32[]{:S(2)}, u32[]{:S(2)}) collective-permute-start(bf16[3,192,128]{2,1,0:T(8,128)(2,1)S(1)} %get-tuple-element.78), channel_id=1, source_target_pairs={{0,2},{1,3},{2,0},{3,1},{4,6},{5,7},{6,4},{7,5},{8,10},{9,11},{10,... | collective-permute-start | bytes 442376 | tf_op jit(solution)/shard_map/ppermute | solution.py:295
  58.5 1.2 %collective-permute-done.12 = f32[4,32,96]{2,1,0:T(8,128)S(1)} collective-permute-done((f32[4,32,96]{2,1,0:T(8,128)S(1)}, f32[4,32,96]{2,1,0:T(8,128)S(1)}, u32[]{:S(2)}, u32[]{:S(2)}) %collective-permute-start.12) | collective-permute-done | bytes 49184 | tf_op jit(solution)/shard_map/ppermute | solution.py:304
  59.8 2.5 %collective-permute-start.15 = (f32[4,32,96]{2,1,0:T(8,128)S(1)}, f32[4,32,96]{2,1,0:T(8,128)S(1)}, u32[]{:S(2)}, u32[]{:S(2)}) collective-permute-start(f32[4,32,96]{2,1,0:T(8,128)S(1)} %add.8.refs_8_), channel_id=1, source_target_pairs={{0,24},{4,28},{8,16},{12,20},{16,8},{20,12},{24,0},{28,4},{1,25},{... | collective-permute-start | bytes 147464 | tf_op jit(solution)/shard_map/ppermute | solution.py:304
  62.3 0.5 collective-permute-start.14
  62.8 1.3 %collective-permute-start.13 = (f32[4,32,96]{2,1,0:T(8,128)S(1)}, f32[4,32,96]{2,1,0:T(8,128)S(1)}, u32[]{:S(2)}, u32[]{:S(2)}) collective-permute-start(f32[4,32,96]{2,1,0:T(8,128)S(1)} %add.8.refs_8_), channel_id=1, source_target_pairs={{0,8},{4,12},{8,0},{12,4},{16,24},{20,28},{24,16},{28,20},{1,9},{5... | collective-permute-start | bytes 147464 | tf_op jit(solution)/shard_map/ppermute | solution.py:304
  64.1 0.9 %collective-permute-done.15.refs_11_ = f32[4,32,96]{2,1,0:T(8,128)S(1)} collective-permute-done((f32[4,32,96]{2,1,0:T(8,128)S(1)}, f32[4,32,96]{2,1,0:T(8,128)S(1)}, u32[]{:S(2)}, u32[]{:S(2)}) %collective-permute-start.15) | collective-permute-done | bytes 49184 | tf_op jit(solution)/shard_map/ppermute | solution.py:304
  65.0 1.5 %collective-permute-done.14.refs_10_ = f32[4,32,96]{2,1,0:T(8,128)S(1)} collective-permute-done((f32[4,32,96]{2,1,0:T(8,128)S(1)}, f32[4,32,96]{2,1,0:T(8,128)S(1)}, u32[]{:S(2)}, u32[]{:S(2)}) %collective-permute-start.14) | collective-permute-done | bytes 49184 | tf_op jit(solution)/shard_map/ppermute | solution.py:304
  66.5 0.5 collective-permute-done.13.refs_9_
  67.1 2.5 %collective-permute-done.10.refs_6_ = bf16[3,192,128]{2,1,0:T(8,128)(2,1)S(1)} collective-permute-done((bf16[3,192,128]{2,1,0:T(8,128)(2,1)S(1)}, bf16[3,192,128]{2,1,0:T(8,128)(2,1)S(1)}, u32[]{:S(2)}, u32[]{:S(2)}) %collective-permute-start.10) | collective-permute-done | bytes 147488 | tf_op jit(solution)/shard_map/ppermute | solution.py:295
  69.6 1.4 %shard_map.113 = (bf16[1,128,1536]{2,1,0:T(8,128)(2,1)}, bf16[1,128,1536]{2,1,0:T(8,128)(2,1)}, bf16[1,128,1536]{2,1,0:T(8,128)(2,1)}, f32[31,384]{1,0:T(8,128)}, f32[384]{0:T(512)}) custom-call(s32[1]{0:T(128)} %bitcast.rank_ref, bf16[3,192,128]{2,1,0:T(8,128)(2,1)S(1)} %get-tuple-element.52.refs_0_, ...), custom_call_target="tpu_custom_call" | custom-call | bytes 2359296 | tf_op jit(solution)/shard_map/pallas_call | solution.py:82
  (25 shorter events, 0.4 us)
Async XLA Ops:
  0.6 10.0 %copy-start = (f32[31,1536]{1,0:T(8,128)S(1)}, f32[31,1536]{1,0:T(8,128)}, u32[]{:S(2)}) copy-start(f32[31,1536]{1,0:T(8,128)} %param.11) | copy-start | bytes 571396
  2.7 7.8 %copy-start.1 = (f32[1536]{0:T(1024)S(1)}, f32[1536]{0:T(1024)}, u32[]{:S(2)}) copy-start(f32[1536]{0:T(1024)} %param.12) | copy-start | bytes 18436
  2.7 11.0 %collective-permute-start = (bf16[4,192,128]{2,1,0:T(8,128)(2,1)S(1)}, bf16[4,192,128]{2,1,0:T(8,128)(2,1)S(1)}, u32[]{:S(2)}, u32[]{:S(2)}) collective-permute-start(bf16[4,192,128]{2,1,0:T(8,128)(2,1)S(1)} %get-tuple-element.46), channel_id=1, source_target_pairs={{0,3},{1,2},{2,1},{3,0},{4,7},{5,6},{6,5},{7,4},{8,11},{9,10},{10,... | collective-permute-start | bytes 589832 | tf_op jit(solution)/shard_map/ppermute | solution.py:295
  7.8 16.8 %collective-permute-start.1 = (bf16[4,192,128]{2,1,0:T(8,128)(2,1)S(1)}, bf16[4,192,128]{2,1,0:T(8,128)(2,1)S(1)}, u32[]{:S(2)}, u32[]{:S(2)}) collective-permute-start(bf16[4,192,128]{2,1,0:T(8,128)(2,1)S(1)} %get-tuple-element.47), channel_id=1, source_target_pairs={{0,2},{1,3},{2,0},{3,1},{4,6},{5,7},{6,4},{7,5},{8,10},{9,11},{10,... | collective-permute-start | bytes 589832 | tf_op jit(solution)/shard_map/ppermute | solution.py:295
  7.8 16.8 %collective-permute-start.2 = (bf16[4,192,128]{2,1,0:T(8,128)(2,1)S(1)}, bf16[4,192,128]{2,1,0:T(8,128)(2,1)S(1)}, u32[]{:S(2)}, u32[]{:S(2)}) collective-permute-start(bf16[4,192,128]{2,1,0:T(8,128)(2,1)S(1)} %get-tuple-element.48), channel_id=1, source_target_pairs={{0,1},{1,0},{2,3},{3,2},{4,5},{5,4},{6,7},{7,6},{8,9},{9,8},{10,11... | collective-permute-start | bytes 589832 | tf_op jit(solution)/shard_map/ppermute | solution.py:295
  8.5 30.6 %collective-permute-start.5 = (bf16[4,192,128]{2,1,0:T(8,128)(2,1)S(1)}, bf16[4,192,128]{2,1,0:T(8,128)(2,1)S(1)}, u32[]{:S(2)}, u32[]{:S(2)}) collective-permute-start(bf16[4,192,128]{2,1,0:T(8,128)(2,1)S(1)} %get-tuple-element.59), channel_id=1, source_target_pairs={{0,1},{1,0},{2,3},{3,2},{4,5},{5,4},{6,7},{7,6},{8,9},{9,8},{10,11... | collective-permute-start | bytes 589832 | tf_op jit(solution)/shard_map/ppermute | solution.py:295
  24.6 14.5 %collective-permute-start.3 = (bf16[4,192,128]{2,1,0:T(8,128)(2,1)S(1)}, bf16[4,192,128]{2,1,0:T(8,128)(2,1)S(1)}, u32[]{:S(2)}, u32[]{:S(2)}) collective-permute-start(bf16[4,192,128]{2,1,0:T(8,128)(2,1)S(1)} %get-tuple-element.57), channel_id=1, source_target_pairs={{0,3},{1,2},{2,1},{3,0},{4,7},{5,6},{6,5},{7,4},{8,11},{9,10},{10,... | collective-permute-start | bytes 589832 | tf_op jit(solution)/shard_map/ppermute | solution.py:295
  27.2 15.0 %collective-permute-start.4 = (bf16[4,192,128]{2,1,0:T(8,128)(2,1)S(1)}, bf16[4,192,128]{2,1,0:T(8,128)(2,1)S(1)}, u32[]{:S(2)}, u32[]{:S(2)}) collective-permute-start(bf16[4,192,128]{2,1,0:T(8,128)(2,1)S(1)} %get-tuple-element.58), channel_id=1, source_target_pairs={{0,2},{1,3},{2,0},{3,1},{4,6},{5,7},{6,4},{7,5},{8,10},{9,11},{10,... | collective-permute-start | bytes 589832 | tf_op jit(solution)/shard_map/ppermute | solution.py:295
  37.3 16.7 %collective-permute-start.8 = (bf16[3,192,128]{2,1,0:T(8,128)(2,1)S(1)}, bf16[3,192,128]{2,1,0:T(8,128)(2,1)S(1)}, u32[]{:S(2)}, u32[]{:S(2)}) collective-permute-start(bf16[3,192,128]{2,1,0:T(8,128)(2,1)S(1)} %get-tuple-element.71), channel_id=1, source_target_pairs={{0,1},{1,0},{2,3},{3,2},{4,5},{5,4},{6,7},{7,6},{8,9},{9,8},{10,11... | collective-permute-start | bytes 442376 | tf_op jit(solution)/shard_map/ppermute | solution.py:295
  42.3 13.9 %collective-permute-start.6 = (bf16[3,192,128]{2,1,0:T(8,128)(2,1)S(1)}, bf16[3,192,128]{2,1,0:T(8,128)(2,1)S(1)}, u32[]{:S(2)}, u32[]{:S(2)}) collective-permute-start(bf16[3,192,128]{2,1,0:T(8,128)(2,1)S(1)} %get-tuple-element.66), channel_id=1, source_target_pairs={{0,3},{1,2},{2,1},{3,0},{4,7},{5,6},{6,5},{7,4},{8,11},{9,10},{10,... | collective-permute-start | bytes 442376 | tf_op jit(solution)/shard_map/ppermute | solution.py:295
  44.0 14.4 %collective-permute-start.7 = (bf16[3,192,128]{2,1,0:T(8,128)(2,1)S(1)}, bf16[3,192,128]{2,1,0:T(8,128)(2,1)S(1)}, u32[]{:S(2)}, u32[]{:S(2)}) collective-permute-start(bf16[3,192,128]{2,1,0:T(8,128)(2,1)S(1)} %get-tuple-element.69), channel_id=1, source_target_pairs={{0,2},{1,3},{2,0},{3,1},{4,6},{5,7},{6,4},{7,5},{8,10},{9,11},{10,... | collective-permute-start | bytes 442376 | tf_op jit(solution)/shard_map/ppermute | solution.py:295
  54.0 8.8 %collective-permute-start.9 = (bf16[3,192,128]{2,1,0:T(8,128)(2,1)S(1)}, bf16[3,192,128]{2,1,0:T(8,128)(2,1)S(1)}, u32[]{:S(2)}, u32[]{:S(2)}) collective-permute-start(bf16[3,192,128]{2,1,0:T(8,128)(2,1)S(1)} %get-tuple-element.77), channel_id=1, source_target_pairs={{0,3},{1,2},{2,1},{3,0},{4,7},{5,6},{6,5},{7,4},{8,11},{9,10},{10,... | collective-permute-start | bytes 442376 | tf_op jit(solution)/shard_map/ppermute | solution.py:295
  56.1 10.9 %collective-permute-start.11 = (bf16[3,192,128]{2,1,0:T(8,128)(2,1)S(1)}, bf16[3,192,128]{2,1,0:T(8,128)(2,1)S(1)}, u32[]{:S(2)}, u32[]{:S(2)}) collective-permute-start(bf16[3,192,128]{2,1,0:T(8,128)(2,1)S(1)} %get-tuple-element.79), channel_id=1, source_target_pairs={{0,1},{1,0},{2,3},{3,2},{4,5},{5,4},{6,7},{7,6},{8,9},{9,8},{10,11... | collective-permute-start | bytes 442376 | tf_op jit(solution)/shard_map/ppermute | solution.py:295
  57.5 12.1 %collective-permute-start.10 = (bf16[3,192,128]{2,1,0:T(8,128)(2,1)S(1)}, bf16[3,192,128]{2,1,0:T(8,128)(2,1)S(1)}, u32[]{:S(2)}, u32[]{:S(2)}) collective-permute-start(bf16[3,192,128]{2,1,0:T(8,128)(2,1)S(1)} %get-tuple-element.78), channel_id=1, source_target_pairs={{0,2},{1,3},{2,0},{3,1},{4,6},{5,7},{6,4},{7,5},{8,10},{9,11},{10,... | collective-permute-start | bytes 442376 | tf_op jit(solution)/shard_map/ppermute | solution.py:295
  58.4 1.3 %collective-permute-start.12 = (f32[4,32,96]{2,1,0:T(8,128)S(1)}, f32[4,32,96]{2,1,0:T(8,128)S(1)}, u32[]{:S(2)}, u32[]{:S(2)}) collective-permute-start(f32[4,32,96]{2,1,0:T(8,128)S(1)} %pad_maximum_fusion), channel_id=1, source_target_pairs={{0,4},{4,0},{8,12},{12,8},{16,20},{20,16},{24,28},{28,24},{1,5},{5... | collective-permute-start | bytes 147464 | tf_op jit(solution)/shard_map/ppermute | solution.py:304
  59.8 5.3 %collective-permute-start.15 = (f32[4,32,96]{2,1,0:T(8,128)S(1)}, f32[4,32,96]{2,1,0:T(8,128)S(1)}, u32[]{:S(2)}, u32[]{:S(2)}) collective-permute-start(f32[4,32,96]{2,1,0:T(8,128)S(1)} %add.8.refs_8_), channel_id=1, source_target_pairs={{0,24},{4,28},{8,16},{12,20},{16,8},{20,12},{24,0},{28,4},{1,25},{... | collective-permute-start | bytes 147464 | tf_op jit(solution)/shard_map/ppermute | solution.py:304
  62.3 4.3 %collective-permute-start.14 = (f32[4,32,96]{2,1,0:T(8,128)S(1)}, f32[4,32,96]{2,1,0:T(8,128)S(1)}, u32[]{:S(2)}, u32[]{:S(2)}) collective-permute-start(f32[4,32,96]{2,1,0:T(8,128)S(1)} %add.8.refs_8_), channel_id=1, source_target_pairs={{0,16},{4,20},{8,24},{12,28},{16,0},{20,4},{24,8},{28,12},{1,17},{... | collective-permute-start | bytes 147464 | tf_op jit(solution)/shard_map/ppermute | solution.py:304
  62.8 4.3 %collective-permute-start.13 = (f32[4,32,96]{2,1,0:T(8,128)S(1)}, f32[4,32,96]{2,1,0:T(8,128)S(1)}, u32[]{:S(2)}, u32[]{:S(2)}) collective-permute-start(f32[4,32,96]{2,1,0:T(8,128)S(1)} %add.8.refs_8_), channel_id=1, source_target_pairs={{0,8},{4,12},{8,0},{12,4},{16,24},{20,28},{24,16},{28,20},{1,9},{5... | collective-permute-start | bytes 147464 | tf_op jit(solution)/shard_map/ppermute | solution.py:304

commit v8 on v7

--- a/solution.py
+++ b/solution.py
@@ -285,10 +285,14 @@
     return outs[:count], outs[count]
 
 
-def exchanged(pieces, before):
+def exchanged(pieces, before, eager=False):
     pieces = list(pieces)
-    if before is not None and len(pieces) > 2:
-        pieces[:1:-1], before[:0:-1] = lax.optimization_barrier((pieces[:1:-1], before[:0:-1]))
+    last = len(pieces) - 1
+    if before is not None and eager:
+        pieces[last], before[last] = lax.optimization_barrier((pieces[last], before[last]))
+    if before is not None and last > 1:
+        wait = slice(last - 1 if eager else last, 1, -1)
+        pieces[wait], before[:0:-1] = lax.optimization_barrier((pieces[wait], before[:0:-1]))
     moved = pieces[:1] * len(pieces)
     for distance in range(len(pieces) - 1, 0, -1):
         pairs = [(i, i ^ distance) for i in range(len(pieces))]
@@ -296,10 +300,12 @@
     return moved
 
 
-def terms(array, axis, stride, reach):
+def terms(array, axis, stride, reach, moved=None):
     count = lax.axis_size(axis)
     found = [array]
     for distance in range(stride, reach, stride):
+        if moved is not None and distance + stride == reach:
+            array, moved[1] = lax.optimization_barrier((array, moved[1]))
         pairs = [(i, i ^ distance) for i in range(count)]
         found.append(lax.ppermute(array, axis, pairs))
     return found
@@ -333,7 +339,7 @@
         grads, part = core(scalars, weight[at], bias[at], order[chunk])
         taps.append(part)
         if chunk < chunks - 1:
-            order.append(exchanged(grads, order[-1]))
+            order.append(exchanged(grads, order[-1], True))
     before, grads = order[-1], list(grads)
     if chunks > 1:
         for distance in range(count - 1, 0, -1):
@@ -344,7 +350,8 @@
     order.append(exchanged(grads, None))
     taps, before[:0:-1] = lax.optimization_barrier((jnp.concatenate(taps, axis=0), before[:0:-1]))
     taps = tree_sum(terms(taps, "dp", 1, 2))
-    return unpack(rank[None], terms(taps, "dp", 2, lax.axis_size("dp")), order[chunks:], count, chunks)
+    taps = terms(taps, "dp", 2, lax.axis_size("dp"), order[-1])
+    return unpack(rank[None], taps, order[chunks:], count, chunks)
 
 
 def solution(mesh):

time: 71.1 us -> 71.9 us (1.011)
  starting transfers between devices: 22.2 us -> 24.3 us
  waiting for transfers between devices: 23.7 us -> 22.4 us
    ppermute x4, starting transfers between devices: 4.41 us -> 5.59 us  [terms(): found.append(lax.ppermute(array, axis, pairs))]
    ppermute x12, waiting for transfers between devices: 19.5 us -> 18.4 us  [exchanged(): moved[distance] = lax.ppermute(pieces[distance], 'seq', pairs)]
    ppermute x12, starting transfers between devices: 17.8 us -> 18.7 us  [exchanged(): moved[distance] = lax.ppermute(pieces[distance], 'seq', pairs)]
  transfers between devices with their start and end apart: 16 -> 16, of which waited for: 8 -> 7; matrix products, arithmetic and copies ran while one was open for 0% -> 0% of each run, Pallas kernels for 28% -> 28%
where the time goes in v8:
time: 71.9 us; the launch traced here: 71.7 us
  starting transfers between devices  24.3 us (34%)
  Pallas kernels  23.3 us (32%)
  waiting for transfers between devices  22.4 us (31%)
  between operations  1.44 us (2%)
    pallas_call x2, Pallas kernels, core(): pl.pallas_call(functools.partial(core_kernel, count, block), out_shape=(p...  19.9 us
    ppermute x12, starting transfers between devices, exchanged(): moved[distance] = lax.ppermute(pieces[distance], 'seq', pairs)  18.7 us
    ppermute x12, waiting for transfers between devices, exchanged(): moved[distance] = lax.ppermute(pieces[distance], 'seq', pairs)  18.4 us
    ppermute x4, starting transfers between devices, terms(): found.append(lax.ppermute(array, axis, pairs))  5.59 us
    ppermute x4, waiting for transfers between devices, terms(): found.append(lax.ppermute(array, axis, pairs))  3.94 us
    pallas_call x1, Pallas kernels, pack(): pl.pallas_call(functools.partial(pack_kernel, count, chunks), out_shape=(...  2.03 us
  transfers between devices with their start and end apart: 16, of which 7 were waited for; matrix products, arithmetic and copies ran while one was open for 0% of the time, Pallas kernels for 28%

profile of v8, /device:TPU:0, one launch (start us, length us, event | category | flops | bytes accessed | tf_op | source)
XLA Modules:
  0.0 71.7 jit_solution(8346480683482835041)
XLA Ops:
  0.6 2.0 %shard_map.110 = (bf16[4,192,128]{2,1,0:T(8,128)(2,1)S(1)}, bf16[4,192,128]{2,1,0:T(8,128)(2,1)S(1)}, bf16[4,192,128]{2,1,0:T(8,128)(2,1)S(1)}, bf16[4,192,128]{...) custom-call(s32[1]{0:T(128)} %bitcast.rank_ref, ...), custom_call_target="tpu_custom_call" | custom-call | bytes 3145728 | tf_op jit(solution)/shard_map/pallas_call | solution.py:38
  2.7 5.1 %collective-permute-start = (bf16[4,192,128]{2,1,0:T(8,128)(2,1)S(1)}, bf16[4,192,128]{2,1,0:T(8,128)(2,1)S(1)}, u32[]{:S(2)}, u32[]{:S(2)}) collective-permute-start(bf16[4,192,128]{2,1,0:T(8,128)(2,1)S(1)} %get-tuple-element.49), channel_id=1, source_target_pairs={{0,3},{1,2},{2,1},{3,0},{4,7},{5,6},{6,5},{7,4},{8,11},{9,10},{10,... | collective-permute-start | bytes 589832 | tf_op jit(solution)/shard_map/ppermute | solution.py:299
  7.8 0.6 collective-permute-start.2
  8.5 1.4 %collective-permute-start.5 = (bf16[4,192,128]{2,1,0:T(8,128)(2,1)S(1)}, bf16[4,192,128]{2,1,0:T(8,128)(2,1)S(1)}, u32[]{:S(2)}, u32[]{:S(2)}) collective-permute-start(bf16[4,192,128]{2,1,0:T(8,128)(2,1)S(1)} %get-tuple-element.63), channel_id=1, source_target_pairs={{0,1},{1,0},{2,3},{3,2},{4,5},{5,4},{6,7},{7,6},{8,9},{9,8},{10,11... | collective-permute-start | bytes 589832 | tf_op jit(solution)/shard_map/ppermute | solution.py:299
  10.5 0.1 reshape.17
  10.6 0.1 reshape.16
  10.8 2.9 %collective-permute-done.refs_1_ = bf16[4,192,128]{2,1,0:T(8,128)(2,1)S(1)} collective-permute-done((bf16[4,192,128]{2,1,0:T(8,128)(2,1)S(1)}, bf16[4,192,128]{2,1,0:T(8,128)(2,1)S(1)}, u32[]{:S(2)}, u32[]{:S(2)}) %collective-permute-start) | collective-permute-done | bytes 196640 | tf_op jit(solution)/shard_map/ppermute | solution.py:299
  13.7 10.9 %collective-permute-done.1.refs_2_ = bf16[4,192,128]{2,1,0:T(8,128)(2,1)S(1)} collective-permute-done((bf16[4,192,128]{2,1,0:T(8,128)(2,1)S(1)}, bf16[4,192,128]{2,1,0:T(8,128)(2,1)S(1)}, u32[]{:S(2)}, u32[]{:S(2)}) %collective-permute-start.1) | collective-permute-done | bytes 196640 | tf_op jit(solution)/shard_map/ppermute | solution.py:299
  24.6 2.6 %collective-permute-start.3 = (bf16[4,192,128]{2,1,0:T(8,128)(2,1)S(1)}, bf16[4,192,128]{2,1,0:T(8,128)(2,1)S(1)}, u32[]{:S(2)}, u32[]{:S(2)}) collective-permute-start(bf16[4,192,128]{2,1,0:T(8,128)(2,1)S(1)} %get-tuple-element.60), channel_id=1, source_target_pairs={{0,3},{1,2},{2,1},{3,0},{4,7},{5,6},{6,5},{7,4},{8,11},{9,10},{10,... | collective-permute-start | bytes 589832 | tf_op jit(solution)/shard_map/ppermute | solution.py:299
  27.3 9.9 %shard_map.111 = (bf16[3,192,128]{2,1,0:T(8,128)(2,1)S(1)}, bf16[3,192,128]{2,1,0:T(8,128)(2,1)S(1)}, bf16[3,192,128]{2,1,0:T(8,128)(2,1)S(1)}, bf16[3,192,128]{2,1,0:T(8,128)(2,1)S(1)}, f32[2,32,96]{2,1,0:T(8,128)S(1)}) custom-call(s32[2]{0:T(128)S(1)} %pad_add_fusion.scalars, f32[2,31,96]{2,1,0:T(8,128)S(1)} %get-tuple-element.88.weight_ref, ...), custom_call_target="tpu_custom_call" | custom-call | flops 1207959552 | bytes 1376256 | tf_op jit(solution)/shard_map/pallas_call | solution.py:264
  37.3 1.8 %collective-permute-start.8 = (bf16[3,192,128]{2,1,0:T(8,128)(2,1)S(1)}, bf16[3,192,128]{2,1,0:T(8,128)(2,1)S(1)}, u32[]{:S(2)}, u32[]{:S(2)}) collective-permute-start(bf16[3,192,128]{2,1,0:T(8,128)(2,1)S(1)} %get-tuple-element.75), channel_id=1, source_target_pairs={{0,1},{1,0},{2,3},{3,2},{4,5},{5,4},{6,7},{7,6},{8,9},{9,8},{10,11... | collective-permute-start | bytes 442376 | tf_op jit(solution)/shard_map/ppermute | solution.py:299
  39.1 2.6 %collective-permute-start.6 = (bf16[3,192,128]{2,1,0:T(8,128)(2,1)S(1)}, bf16[3,192,128]{2,1,0:T(8,128)(2,1)S(1)}, u32[]{:S(2)}, u32[]{:S(2)}) collective-permute-start(bf16[3,192,128]{2,1,0:T(8,128)(2,1)S(1)} %get-tuple-element.70), channel_id=1, source_target_pairs={{0,3},{1,2},{2,1},{3,0},{4,7},{5,6},{6,5},{7,4},{8,11},{9,10},{10,... | collective-permute-start | bytes 442376 | tf_op jit(solution)/shard_map/ppermute | solution.py:299
  41.7 4.3 %collective-permute-done.4.refs_2_ = bf16[4,192,128]{2,1,0:T(8,128)(2,1)S(1)} collective-permute-done((bf16[4,192,128]{2,1,0:T(8,128)(2,1)S(1)}, bf16[4,192,128]{2,1,0:T(8,128)(2,1)S(1)}, u32[]{:S(2)}, u32[]{:S(2)}) %collective-permute-start.4) | collective-permute-done | bytes 196640 | tf_op jit(solution)/shard_map/ppermute | solution.py:299
  46.0 9.9 %shard_map.112 = (bf16[3,192,128]{2,1,0:T(8,128)(2,1)S(1)}, bf16[3,192,128]{2,1,0:T(8,128)(2,1)S(1)}, bf16[3,192,128]{2,1,0:T(8,128)(2,1)S(1)}, bf16[3,192,128]{2,1,0:T(8,128)(2,1)S(1)}, f32[2,32,96]{2,1,0:T(8,128)S(1)}) custom-call(s32[2]{0:T(128)S(1)} %pad_add_fusion.scalars, f32[2,31,96]{2,1,0:T(8,128)S(1)} %get-tuple-element.87.weight_ref, ...), custom_call_target="tpu_custom_call" | custom-call | flops 1207959552 | bytes 1376256 | tf_op jit(solution)/shard_map/pallas_call | solution.py:264
  56.1 3.5 %collective-permute-start.12 = (bf16[3,192,128]{2,1,0:T(8,128)(2,1)S(1)}, bf16[3,192,128]{2,1,0:T(8,128)(2,1)S(1)}, u32[]{:S(2)}, u32[]{:S(2)}) collective-permute-start(bf16[3,192,128]{2,1,0:T(8,128)(2,1)S(1)} %get-tuple-element.84), channel_id=1, source_target_pairs={{0,1},{1,0},{2,3},{3,2},{4,5},{5,4},{6,7},{7,6},{8,9},{9,8},{10,11... | collective-permute-start | bytes 442376 | tf_op jit(solution)/shard_map/ppermute | solution.py:299
  59.5 0.9 %collective-permute-start.10 = (bf16[3,192,128]{2,1,0:T(8,128)(2,1)S(1)}, bf16[3,192,128]{2,1,0:T(8,128)(2,1)S(1)}, u32[]{:S(2)}, u32[]{:S(2)}) collective-permute-start(bf16[3,192,128]{2,1,0:T(8,128)(2,1)S(1)} %get-tuple-element.82), channel_id=1, source_target_pairs={{0,2},{1,3},{2,0},{3,1},{4,6},{5,7},{6,4},{7,5},{8,10},{9,11},{10,... | collective-permute-start | bytes 442376 | tf_op jit(solution)/shard_map/ppermute | solution.py:299
  60.5 1.2 %collective-permute-done.11 = f32[4,32,96]{2,1,0:T(8,128)S(1)} collective-permute-done((f32[4,32,96]{2,1,0:T(8,128)S(1)}, f32[4,32,96]{2,1,0:T(8,128)S(1)}, u32[]{:S(2)}, u32[]{:S(2)}) %collective-permute-start.11) | collective-permute-done | bytes 49184 | tf_op jit(solution)/shard_map/ppermute | solution.py:310
  61.8 1.6 %collective-permute-start.14 = (f32[4,32,96]{2,1,0:T(8,128)S(1)}, f32[4,32,96]{2,1,0:T(8,128)S(1)}, u32[]{:S(2)}, u32[]{:S(2)}) collective-permute-start(f32[4,32,96]{2,1,0:T(8,128)S(1)} %add.8.refs_8_), channel_id=1, source_target_pairs={{0,16},{4,20},{8,24},{12,28},{16,0},{20,4},{24,8},{28,12},{1,17},{... | collective-permute-start | bytes 147464 | tf_op jit(solution)/shard_map/ppermute | solution.py:310
  63.4 1.5 %collective-permute-start.13 = (f32[4,32,96]{2,1,0:T(8,128)S(1)}, f32[4,32,96]{2,1,0:T(8,128)S(1)}, u32[]{:S(2)}, u32[]{:S(2)}) collective-permute-start(f32[4,32,96]{2,1,0:T(8,128)S(1)} %add.8.refs_8_), channel_id=1, source_target_pairs={{0,8},{4,12},{8,0},{12,4},{16,24},{20,28},{24,16},{28,20},{1,9},{5... | collective-permute-start | bytes 147464 | tf_op jit(solution)/shard_map/ppermute | solution.py:310
  64.8 0.4 collective-permute-done.12.refs_7_
  65.2 2.5 %collective-permute-start.15 = (f32[4,32,96]{2,1,0:T(8,128)S(1)}, f32[4,32,96]{2,1,0:T(8,128)S(1)}, u32[]{:S(2)}, u32[]{:S(2)}) collective-permute-start(f32[4,32,96]{2,1,0:T(8,128)S(1)} %add.8.refs_8_), channel_id=1, source_target_pairs={{0,24},{4,28},{8,16},{12,20},{16,8},{20,12},{24,0},{28,4},{1,25},{... | collective-permute-start | bytes 147464 | tf_op jit(solution)/shard_map/ppermute | solution.py:310
  67.7 0.6 collective-permute-done.13.refs_9_
  68.3 2.1 %collective-permute-done.15.refs_11_ = f32[4,32,96]{2,1,0:T(8,128)S(1)} collective-permute-done((f32[4,32,96]{2,1,0:T(8,128)S(1)}, f32[4,32,96]{2,1,0:T(8,128)S(1)}, u32[]{:S(2)}, u32[]{:S(2)}) %collective-permute-start.15) | collective-permute-done | bytes 49184 | tf_op jit(solution)/shard_map/ppermute | solution.py:310
  70.4 1.4 %shard_map.113 = (bf16[1,128,1536]{2,1,0:T(8,128)(2,1)}, bf16[1,128,1536]{2,1,0:T(8,128)(2,1)}, bf16[1,128,1536]{2,1,0:T(8,128)(2,1)}, f32[31,384]{1,0:T(8,128)}, f32[384]{0:T(512)}) custom-call(s32[1]{0:T(128)} %bitcast.rank_ref, bf16[3,192,128]{2,1,0:T(8,128)(2,1)S(1)} %get-tuple-element.55.refs_0_, ...), custom_call_target="tpu_custom_call" | custom-call | bytes 2359296 | tf_op jit(solution)/shard_map/pallas_call | solution.py:82
  (25 shorter events, 0.3 us)
Async XLA Ops:
  0.6 10.0 %copy-start = (f32[31,1536]{1,0:T(8,128)S(1)}, f32[31,1536]{1,0:T(8,128)}, u32[]{:S(2)}) copy-start(f32[31,1536]{1,0:T(8,128)} %param.11) | copy-start | bytes 571396
  2.7 7.8 %copy-start.1 = (f32[1536]{0:T(1024)S(1)}, f32[1536]{0:T(1024)}, u32[]{:S(2)}) copy-start(f32[1536]{0:T(1024)} %param.12) | copy-start | bytes 18436
  2.7 11.0 %collective-permute-start = (bf16[4,192,128]{2,1,0:T(8,128)(2,1)S(1)}, bf16[4,192,128]{2,1,0:T(8,128)(2,1)S(1)}, u32[]{:S(2)}, u32[]{:S(2)}) collective-permute-start(bf16[4,192,128]{2,1,0:T(8,128)(2,1)S(1)} %get-tuple-element.49), channel_id=1, source_target_pairs={{0,3},{1,2},{2,1},{3,0},{4,7},{5,6},{6,5},{7,4},{8,11},{9,10},{10,... | collective-permute-start | bytes 589832 | tf_op jit(solution)/shard_map/ppermute | solution.py:299
  7.8 16.8 %collective-permute-start.1 = (bf16[4,192,128]{2,1,0:T(8,128)(2,1)S(1)}, bf16[4,192,128]{2,1,0:T(8,128)(2,1)S(1)}, u32[]{:S(2)}, u32[]{:S(2)}) collective-permute-start(bf16[4,192,128]{2,1,0:T(8,128)(2,1)S(1)} %get-tuple-element.50), channel_id=1, source_target_pairs={{0,2},{1,3},{2,0},{3,1},{4,6},{5,7},{6,4},{7,5},{8,10},{9,11},{10,... | collective-permute-start | bytes 589832 | tf_op jit(solution)/shard_map/ppermute | solution.py:299
  7.8 16.8 %collective-permute-start.2 = (bf16[4,192,128]{2,1,0:T(8,128)(2,1)S(1)}, bf16[4,192,128]{2,1,0:T(8,128)(2,1)S(1)}, u32[]{:S(2)}, u32[]{:S(2)}) collective-permute-start(bf16[4,192,128]{2,1,0:T(8,128)(2,1)S(1)} %get-tuple-element.51), channel_id=1, source_target_pairs={{0,1},{1,0},{2,3},{3,2},{4,5},{5,4},{6,7},{7,6},{8,9},{9,8},{10,11... | collective-permute-start | bytes 589832 | tf_op jit(solution)/shard_map/ppermute | solution.py:299
  8.5 33.3 %collective-permute-start.5 = (bf16[4,192,128]{2,1,0:T(8,128)(2,1)S(1)}, bf16[4,192,128]{2,1,0:T(8,128)(2,1)S(1)}, u32[]{:S(2)}, u32[]{:S(2)}) collective-permute-start(bf16[4,192,128]{2,1,0:T(8,128)(2,1)S(1)} %get-tuple-element.63), channel_id=1, source_target_pairs={{0,1},{1,0},{2,3},{3,2},{4,5},{5,4},{6,7},{7,6},{8,9},{9,8},{10,11... | collective-permute-start | bytes 589832 | tf_op jit(solution)/shard_map/ppermute | solution.py:299
  24.6 14.5 %collective-permute-start.3 = (bf16[4,192,128]{2,1,0:T(8,128)(2,1)S(1)}, bf16[4,192,128]{2,1,0:T(8,128)(2,1)S(1)}, u32[]{:S(2)}, u32[]{:S(2)}) collective-permute-start(bf16[4,192,128]{2,1,0:T(8,128)(2,1)S(1)} %get-tuple-element.60), channel_id=1, source_target_pairs={{0,3},{1,2},{2,1},{3,0},{4,7},{5,6},{6,5},{7,4},{8,11},{9,10},{10,... | collective-permute-start | bytes 589832 | tf_op jit(solution)/shard_map/ppermute | solution.py:299
  27.2 18.7 %collective-permute-start.4 = (bf16[4,192,128]{2,1,0:T(8,128)(2,1)S(1)}, bf16[4,192,128]{2,1,0:T(8,128)(2,1)S(1)}, u32[]{:S(2)}, u32[]{:S(2)}) collective-permute-start(bf16[4,192,128]{2,1,0:T(8,128)(2,1)S(1)} %get-tuple-element.62), channel_id=1, source_target_pairs={{0,2},{1,3},{2,0},{3,1},{4,6},{5,7},{6,4},{7,5},{8,10},{9,11},{10,... | collective-permute-start | bytes 589832 | tf_op jit(solution)/shard_map/ppermute | solution.py:299
  37.3 18.7 %collective-permute-start.8 = (bf16[3,192,128]{2,1,0:T(8,128)(2,1)S(1)}, bf16[3,192,128]{2,1,0:T(8,128)(2,1)S(1)}, u32[]{:S(2)}, u32[]{:S(2)}) collective-permute-start(bf16[3,192,128]{2,1,0:T(8,128)(2,1)S(1)} %get-tuple-element.75), channel_id=1, source_target_pairs={{0,1},{1,0},{2,3},{3,2},{4,5},{5,4},{6,7},{7,6},{8,9},{9,8},{10,11... | collective-permute-start | bytes 442376 | tf_op jit(solution)/shard_map/ppermute | solution.py:299
  39.1 16.9 %collective-permute-start.6 = (bf16[3,192,128]{2,1,0:T(8,128)(2,1)S(1)}, bf16[3,192,128]{2,1,0:T(8,128)(2,1)S(1)}, u32[]{:S(2)}, u32[]{:S(2)}) collective-permute-start(bf16[3,192,128]{2,1,0:T(8,128)(2,1)S(1)} %get-tuple-element.70), channel_id=1, source_target_pairs={{0,3},{1,2},{2,1},{3,0},{4,7},{5,6},{6,5},{7,4},{8,11},{9,10},{10,... | collective-permute-start | bytes 442376 | tf_op jit(solution)/shard_map/ppermute | solution.py:299
  46.0 14.4 %collective-permute-start.7 = (bf16[3,192,128]{2,1,0:T(8,128)(2,1)S(1)}, bf16[3,192,128]{2,1,0:T(8,128)(2,1)S(1)}, u32[]{:S(2)}, u32[]{:S(2)}) collective-permute-start(bf16[3,192,128]{2,1,0:T(8,128)(2,1)S(1)} %get-tuple-element.73), channel_id=1, source_target_pairs={{0,2},{1,3},{2,0},{3,1},{4,6},{5,7},{6,4},{7,5},{8,10},{9,11},{10,... | collective-permute-start | bytes 442376 | tf_op jit(solution)/shard_map/ppermute | solution.py:299
  56.0 11.7 %collective-permute-start.9 = (bf16[3,192,128]{2,1,0:T(8,128)(2,1)S(1)}, bf16[3,192,128]{2,1,0:T(8,128)(2,1)S(1)}, u32[]{:S(2)}, u32[]{:S(2)}) collective-permute-start(bf16[3,192,128]{2,1,0:T(8,128)(2,1)S(1)} %get-tuple-element.81), channel_id=1, source_target_pairs={{0,3},{1,2},{2,1},{3,0},{4,7},{5,6},{6,5},{7,4},{8,11},{9,10},{10,... | collective-permute-start | bytes 442376 | tf_op jit(solution)/shard_map/ppermute | solution.py:299
  56.1 9.2 %collective-permute-start.12 = (bf16[3,192,128]{2,1,0:T(8,128)(2,1)S(1)}, bf16[3,192,128]{2,1,0:T(8,128)(2,1)S(1)}, u32[]{:S(2)}, u32[]{:S(2)}) collective-permute-start(bf16[3,192,128]{2,1,0:T(8,128)(2,1)S(1)} %get-tuple-element.84), channel_id=1, source_target_pairs={{0,1},{1,0},{2,3},{3,2},{4,5},{5,4},{6,7},{7,6},{8,9},{9,8},{10,11... | collective-permute-start | bytes 442376 | tf_op jit(solution)/shard_map/ppermute | solution.py:299
  59.5 8.8 %collective-permute-start.10 = (bf16[3,192,128]{2,1,0:T(8,128)(2,1)S(1)}, bf16[3,192,128]{2,1,0:T(8,128)(2,1)S(1)}, u32[]{:S(2)}, u32[]{:S(2)}) collective-permute-start(bf16[3,192,128]{2,1,0:T(8,128)(2,1)S(1)} %get-tuple-element.82), channel_id=1, source_target_pairs={{0,2},{1,3},{2,0},{3,1},{4,6},{5,7},{6,4},{7,5},{8,10},{9,11},{10,... | collective-permute-start | bytes 442376 | tf_op jit(solution)/shard_map/ppermute | solution.py:299
  60.4 1.3 %collective-permute-start.11 = (f32[4,32,96]{2,1,0:T(8,128)S(1)}, f32[4,32,96]{2,1,0:T(8,128)S(1)}, u32[]{:S(2)}, u32[]{:S(2)}) collective-permute-start(f32[4,32,96]{2,1,0:T(8,128)S(1)} %pad_maximum_fusion), channel_id=1, source_target_pairs={{0,4},{4,0},{8,12},{12,8},{16,20},{20,16},{24,28},{28,24},{1,5},{5... | collective-permute-start | bytes 147464 | tf_op jit(solution)/shard_map/ppermute | solution.py:310
  61.8 5.9 %collective-permute-start.14 = (f32[4,32,96]{2,1,0:T(8,128)S(1)}, f32[4,32,96]{2,1,0:T(8,128)S(1)}, u32[]{:S(2)}, u32[]{:S(2)}) collective-permute-start(f32[4,32,96]{2,1,0:T(8,128)S(1)} %add.8.refs_8_), channel_id=1, source_target_pairs={{0,16},{4,20},{8,24},{12,28},{16,0},{20,4},{24,8},{28,12},{1,17},{... | collective-permute-start | bytes 147464 | tf_op jit(solution)/shard_map/ppermute | solution.py:310
  63.4 4.9 %collective-permute-start.13 = (f32[4,32,96]{2,1,0:T(8,128)S(1)}, f32[4,32,96]{2,1,0:T(8,128)S(1)}, u32[]{:S(2)}, u32[]{:S(2)}) collective-permute-start(f32[4,32,96]{2,1,0:T(8,128)S(1)} %add.8.refs_8_), channel_id=1, source_target_pairs={{0,8},{4,12},{8,0},{12,4},{16,24},{20,28},{24,16},{28,20},{1,9},{5... | collective-permute-start | bytes 147464 | tf_op jit(solution)/shard_map/ppermute | solution.py:310
  65.2 5.2 %collective-permute-start.15 = (f32[4,32,96]{2,1,0:T(8,128)S(1)}, f32[4,32,96]{2,1,0:T(8,128)S(1)}, u32[]{:S(2)}, u32[]{:S(2)}) collective-permute-start(f32[4,32,96]{2,1,0:T(8,128)S(1)} %add.8.refs_8_), channel_id=1, source_target_pairs={{0,24},{4,28},{8,16},{12,20},{16,8},{20,12},{24,0},{28,4},{1,25},{... | collective-permute-start | bytes 147464 | tf_op jit(solution)/shard_map/ppermute | solution.py:310

commit v9 on v8

--- a/solution.py
+++ b/solution.py
@@ -66,7 +66,7 @@
                 first = pl.multiple_of((rank ^ distance) * share + chunk * high, 16)
                 turned[which, pl.ds(first, high), :] = pieces[chunk * count + place][which]
         out[0] = turned[which].T
-    taps = tree_sum([ref[...] for ref in taps_refs])
+    taps = taps_refs[0][...] + taps_refs[1][...]
     heads, _, depth = taps.shape
     for head in range(heads):
         at = slice(head * depth, (head + 1) * depth)
@@ -300,21 +300,15 @@
     return moved
 
 
-def terms(array, axis, stride, reach, moved=None):
+def doubled(array, axis):
     count = lax.axis_size(axis)
-    found = [array]
-    for distance in range(stride, reach, stride):
-        if moved is not None and distance + stride == reach:
-            array, moved[1] = lax.optimization_barrier((array, moved[1]))
+    pair, distance = (array, jnp.zeros_like(array)), 1
+    while distance < count:
+        total = array if distance == 1 else pair[0] + pair[1]
         pairs = [(i, i ^ distance) for i in range(count)]
-        found.append(lax.ppermute(array, axis, pairs))
-    return found
-
-
-def tree_sum(found):
-    while len(found) > 1:
-        found = [a + b for a, b in zip(found[::2], found[1::2])]
-    return found[0]
+        pair = (total, lax.ppermute(total, axis, pairs))
+        distance *= 2
+    return pair
 
 
 def on_device(queries, keys, values, grad_out, conv_weight, conv_bias, lengths):
@@ -340,18 +334,16 @@
         taps.append(part)
         if chunk < chunks - 1:
             order.append(exchanged(grads, order[-1], True))
-    before, grads = order[-1], list(grads)
-    if chunks > 1:
-        for distance in range(count - 1, 0, -1):
-            early = count - 1 if distance < count - 1 else 1
-            grads[distance], before[early] = lax.optimization_barrier(
-                (grads[distance], before[early])
-            )
+    before, grads, taps = order[-1], list(grads), jnp.concatenate(taps, axis=0)
+    last = count - 1
+    grads[last], before[1] = lax.optimization_barrier((grads[last], before[1]))
+    if last > 2:
+        (grads[last - 1], taps), before[last] = lax.optimization_barrier(
+            ((grads[last - 1], taps), before[last])
+        )
+        grads[1], before[last - 1] = lax.optimization_barrier((grads[1], before[last - 1]))
     order.append(exchanged(grads, None))
-    taps, before[:0:-1] = lax.optimization_barrier((jnp.concatenate(taps, axis=0), before[:0:-1]))
-    taps = tree_sum(terms(taps, "dp", 1, 2))
-    taps = terms(taps, "dp", 2, lax.axis_size("dp"), order[-1])
-    return unpack(rank[None], taps, order[chunks:], count, chunks)
+    return unpack(rank[None], doubled(taps, "dp"), order[chunks:], count, chunks)
 
 
 def solution(mesh):

time: 71.9 us -> 71.4 us (level)
  starting transfers between devices: 24.3 us -> 22 us
  waiting for transfers between devices: 22.4 us -> 24.2 us
    ppermute x12, waiting for transfers between devices: 18.4 us -> 21.4 us  [exchanged(): moved[distance] = lax.ppermute(pieces[distance], 'seq', pairs)]
    ppermute x4 -> x3, starting transfers between devices: 5.59 us -> 3.21 us  [doubled(): pair = (total, lax.ppermute(total, axis, pairs))]
    ppermute x4 -> x3, waiting for transfers between devices: 3.94 us -> 2.78 us  [doubled(): pair = (total, lax.ppermute(total, axis, pairs))]
  transfers between devices with their start and end apart: 16 -> 15, of which waited for: 7 -> 5; matrix products, arithmetic and copies ran while one was open for 0% -> 0% of each run, Pallas kernels for 28% -> 28%
where the time goes in v9:
time: 71.4 us; the launch traced here: 71.3 us
  waiting for transfers between devices  24.2 us (34%)
  Pallas kernels  23.3 us (33%)
  starting transfers between devices  22 us (31%)
  between operations  1.44 us (2%)
    ppermute x12, waiting for transfers between devices, exchanged(): moved[distance] = lax.ppermute(pieces[distance], 'seq', pairs)  21.4 us
    pallas_call x2, Pallas kernels, core(): pl.pallas_call(functools.partial(core_kernel, count, block), out_shape=(p...  19.9 us
    ppermute x12, starting transfers between devices, exchanged(): moved[distance] = lax.ppermute(pieces[distance], 'seq', pairs)  18.7 us
    ppermute x3, starting transfers between devices, doubled(): pair = (total, lax.ppermute(total, axis, pairs))  3.21 us
    ppermute x3, waiting for transfers between devices, doubled(): pair = (total, lax.ppermute(total, axis, pairs))  2.78 us
    pallas_call x1, Pallas kernels, pack(): pl.pallas_call(functools.partial(pack_kernel, count, chunks), out_shape=(...  2.03 us
  transfers between devices with their start and end apart: 15, of which 5 were waited for; matrix products, arithmetic and copies ran while one was open for 0% of the time, Pallas kernels for 28%

profile of v9, /device:TPU:0, one launch (start us, length us, event | category | flops | bytes accessed | tf_op | source)
XLA Modules:
  0.0 71.3 jit_solution(8505106757743849330)
XLA Ops:
  0.6 2.0 %shard_map.110 = (bf16[4,192,128]{2,1,0:T(8,128)(2,1)S(1)}, bf16[4,192,128]{2,1,0:T(8,128)(2,1)S(1)}, bf16[4,192,128]{2,1,0:T(8,128)(2,1)S(1)}, bf16[4,192,128]{...) custom-call(s32[1]{0:T(128)} %bitcast.rank_ref, ...), custom_call_target="tpu_custom_call" | custom-call | bytes 3145728 | tf_op jit(solution)/shard_map/pallas_call | solution.py:38
  2.7 5.1 %collective-permute-start = (bf16[4,192,128]{2,1,0:T(8,128)(2,1)S(1)}, bf16[4,192,128]{2,1,0:T(8,128)(2,1)S(1)}, u32[]{:S(2)}, u32[]{:S(2)}) collective-permute-start(bf16[4,192,128]{2,1,0:T(8,128)(2,1)S(1)} %get-tuple-element.44), channel_id=1, source_target_pairs={{0,3},{1,2},{2,1},{3,0},{4,7},{5,6},{6,5},{7,4},{8,11},{9,10},{10,... | collective-permute-start | bytes 589832 | tf_op jit(solution)/shard_map/ppermute | solution.py:299
  7.8 0.6 collective-permute-start.2
  8.5 1.4 %collective-permute-start.5 = (bf16[4,192,128]{2,1,0:T(8,128)(2,1)S(1)}, bf16[4,192,128]{2,1,0:T(8,128)(2,1)S(1)}, u32[]{:S(2)}, u32[]{:S(2)}) collective-permute-start(bf16[4,192,128]{2,1,0:T(8,128)(2,1)S(1)} %get-tuple-element.57), channel_id=1, source_target_pairs={{0,1},{1,0},{2,3},{3,2},{4,5},{5,4},{6,7},{7,6},{8,9},{9,8},{10,11... | collective-permute-start | bytes 589832 | tf_op jit(solution)/shard_map/ppermute | solution.py:299
  10.5 0.1 reshape.17
  10.6 0.1 reshape.16
  10.8 2.9 %collective-permute-done.refs_1_ = bf16[4,192,128]{2,1,0:T(8,128)(2,1)S(1)} collective-permute-done((bf16[4,192,128]{2,1,0:T(8,128)(2,1)S(1)}, bf16[4,192,128]{2,1,0:T(8,128)(2,1)S(1)}, u32[]{:S(2)}, u32[]{:S(2)}) %collective-permute-start) | collective-permute-done | bytes 196640 | tf_op jit(solution)/shard_map/ppermute | solution.py:299
  13.7 10.9 %collective-permute-done.1.refs_2_ = bf16[4,192,128]{2,1,0:T(8,128)(2,1)S(1)} collective-permute-done((bf16[4,192,128]{2,1,0:T(8,128)(2,1)S(1)}, bf16[4,192,128]{2,1,0:T(8,128)(2,1)S(1)}, u32[]{:S(2)}, u32[]{:S(2)}) %collective-permute-start.1) | collective-permute-done | bytes 196640 | tf_op jit(solution)/shard_map/ppermute | solution.py:299
  24.6 2.6 %collective-permute-start.3 = (bf16[4,192,128]{2,1,0:T(8,128)(2,1)S(1)}, bf16[4,192,128]{2,1,0:T(8,128)(2,1)S(1)}, u32[]{:S(2)}, u32[]{:S(2)}) collective-permute-start(bf16[4,192,128]{2,1,0:T(8,128)(2,1)S(1)} %get-tuple-element.54), channel_id=1, source_target_pairs={{0,3},{1,2},{2,1},{3,0},{4,7},{5,6},{6,5},{7,4},{8,11},{9,10},{10,... | collective-permute-start | bytes 589832 | tf_op jit(solution)/shard_map/ppermute | solution.py:299
  27.3 0.1 pad_add_fusion.scalars
  27.3 9.9 %shard_map.111 = (bf16[3,192,128]{2,1,0:T(8,128)(2,1)S(1)}, bf16[3,192,128]{2,1,0:T(8,128)(2,1)S(1)}, bf16[3,192,128]{2,1,0:T(8,128)(2,1)S(1)}, bf16[3,192,128]{2,1,0:T(8,128)(2,1)S(1)}, f32[2,32,96]{2,1,0:T(8,128)S(1)}) custom-call(s32[2]{0:T(128)S(1)} %pad_add_fusion.scalars, f32[2,31,96]{2,1,0:T(8,128)S(1)} %get-tuple-element.78.weight_ref, ...), custom_call_target="tpu_custom_call" | custom-call | flops 1207959552 | bytes 1376256 | tf_op jit(solution)/shard_map/pallas_call | solution.py:264
  37.3 1.8 %collective-permute-start.8 = (bf16[3,192,128]{2,1,0:T(8,128)(2,1)S(1)}, bf16[3,192,128]{2,1,0:T(8,128)(2,1)S(1)}, u32[]{:S(2)}, u32[]{:S(2)}) collective-permute-start(bf16[3,192,128]{2,1,0:T(8,128)(2,1)S(1)} %get-tuple-element.70), channel_id=1, source_target_pairs={{0,1},{1,0},{2,3},{3,2},{4,5},{5,4},{6,7},{7,6},{8,9},{9,8},{10,11... | collective-permute-start | bytes 442376 | tf_op jit(solution)/shard_map/ppermute | solution.py:299
  39.1 2.6 %collective-permute-start.6 = (bf16[3,192,128]{2,1,0:T(8,128)(2,1)S(1)}, bf16[3,192,128]{2,1,0:T(8,128)(2,1)S(1)}, u32[]{:S(2)}, u32[]{:S(2)}) collective-permute-start(bf16[3,192,128]{2,1,0:T(8,128)(2,1)S(1)} %get-tuple-element.64), channel_id=1, source_target_pairs={{0,3},{1,2},{2,1},{3,0},{4,7},{5,6},{6,5},{7,4},{8,11},{9,10},{10,... | collective-permute-start | bytes 442376 | tf_op jit(solution)/shard_map/ppermute | solution.py:299
  41.7 4.3 %collective-permute-done.4.refs_2_ = bf16[4,192,128]{2,1,0:T(8,128)(2,1)S(1)} collective-permute-done((bf16[4,192,128]{2,1,0:T(8,128)(2,1)S(1)}, bf16[4,192,128]{2,1,0:T(8,128)(2,1)S(1)}, u32[]{:S(2)}, u32[]{:S(2)}) %collective-permute-start.4) | collective-permute-done | bytes 196640 | tf_op jit(solution)/shard_map/ppermute | solution.py:299
  46.0 9.9 %shard_map.112 = (bf16[3,192,128]{2,1,0:T(8,128)(2,1)S(1)}, bf16[3,192,128]{2,1,0:T(8,128)(2,1)S(1)}, bf16[3,192,128]{2,1,0:T(8,128)(2,1)S(1)}, bf16[3,192,128]{2,1,0:T(8,128)(2,1)S(1)}, f32[2,32,96]{2,1,0:T(8,128)S(1)}) custom-call(s32[2]{0:T(128)S(1)} %pad_add_fusion.scalars, f32[2,31,96]{2,1,0:T(8,128)S(1)} %get-tuple-element.77.weight_ref, ...), custom_call_target="tpu_custom_call" | custom-call | flops 1207959552 | bytes 1376256 | tf_op jit(solution)/shard_map/pallas_call | solution.py:264
  56.0 0.1 collective-permute-start.9
  56.1 0.1 collective-permute-start.12
  56.1 3.0 %collective-permute-start.10 = (bf16[3,192,128]{2,1,0:T(8,128)(2,1)S(1)}, bf16[3,192,128]{2,1,0:T(8,128)(2,1)S(1)}, u32[]{:S(2)}, u32[]{:S(2)}) collective-permute-start(bf16[3,192,128]{2,1,0:T(8,128)(2,1)S(1)} %get-tuple-element.74), channel_id=1, source_target_pairs={{0,2},{1,3},{2,0},{3,1},{4,6},{5,7},{6,4},{7,5},{8,10},{9,11},{10,... | collective-permute-start | bytes 442376 | tf_op jit(solution)/shard_map/ppermute | solution.py:299
  59.1 1.4 %collective-permute-start.11 = (bf16[3,192,128]{2,1,0:T(8,128)(2,1)S(1)}, bf16[3,192,128]{2,1,0:T(8,128)(2,1)S(1)}, u32[]{:S(2)}, u32[]{:S(2)}) collective-permute-start(bf16[3,192,128]{2,1,0:T(8,128)(2,1)S(1)} %get-tuple-element.75), channel_id=1, source_target_pairs={{0,1},{1,0},{2,3},{3,2},{4,5},{5,4},{6,7},{7,6},{8,9},{9,8},{10,11... | collective-permute-start | bytes 442376 | tf_op jit(solution)/shard_map/ppermute | solution.py:299
  60.6 1.6 %collective-permute-start.13 = (f32[4,32,96]{2,1,0:T(8,128)S(1)}, f32[4,32,96]{2,1,0:T(8,128)S(1)}, u32[]{:S(2)}, u32[]{:S(2)}) collective-permute-start(f32[4,32,96]{2,1,0:T(8,128)S(1)} %add.11), channel_id=1, source_target_pairs={{0,8},{4,12},{8,0},{12,4},{16,24},{20,28},{24,16},{28,20},{1,9},{5... | collective-permute-start | bytes 147464 | tf_op jit(solution)/shard_map/ppermute | solution.py:309
  62.2 2.8 %collective-permute-done.13 = f32[4,32,96]{2,1,0:T(8,128)S(1)} collective-permute-done((f32[4,32,96]{2,1,0:T(8,128)S(1)}, f32[4,32,96]{2,1,0:T(8,128)S(1)}, u32[]{:S(2)}, u32[]{:S(2)}) %collective-permute-start.13) | collective-permute-done | bytes 49184 | tf_op jit(solution)/shard_map/ppermute | solution.py:309
  64.9 1.6 %collective-permute-start.14 = (f32[4,32,96]{2,1,0:T(8,128)S(1)}, f32[4,32,96]{2,1,0:T(8,128)S(1)}, u32[]{:S(2)}, u32[]{:S(2)}) collective-permute-start(f32[4,32,96]{2,1,0:T(8,128)S(1)} %add.12.refs_8_), channel_id=1, source_target_pairs={{0,16},{4,20},{8,24},{12,28},{16,0},{20,4},{24,8},{28,12},{1,17},{... | collective-permute-start | bytes 147464 | tf_op jit(solution)/shard_map/ppermute | solution.py:309
  66.5 3.4 %collective-permute-done.10.refs_6_ = bf16[3,192,128]{2,1,0:T(8,128)(2,1)S(1)} collective-permute-done((bf16[3,192,128]{2,1,0:T(8,128)(2,1)S(1)}, bf16[3,192,128]{2,1,0:T(8,128)(2,1)S(1)}, u32[]{:S(2)}, u32[]{:S(2)}) %collective-permute-start.10) | collective-permute-done | bytes 147488 | tf_op jit(solution)/shard_map/ppermute | solution.py:299
  69.9 1.4 %shard_map.113 = (bf16[1,128,1536]{2,1,0:T(8,128)(2,1)}, bf16[1,128,1536]{2,1,0:T(8,128)(2,1)}, bf16[1,128,1536]{2,1,0:T(8,128)(2,1)}, f32[31,384]{1,0:T(8,128)}, f32[384]{0:T(512)}) custom-call(s32[1]{0:T(128)} %bitcast.rank_ref, bf16[3,192,128]{2,1,0:T(8,128)(2,1)S(1)} %get-tuple-element.50.refs_0_, ...), custom_call_target="tpu_custom_call" | custom-call | bytes 2359296 | tf_op jit(solution)/shard_map/pallas_call | solution.py:82
  (24 shorter events, 0.1 us)
Async XLA Ops:
  0.6 10.0 %copy-start = (f32[31,1536]{1,0:T(8,128)S(1)}, f32[31,1536]{1,0:T(8,128)}, u32[]{:S(2)}) copy-start(f32[31,1536]{1,0:T(8,128)} %param.11) | copy-start | bytes 571396
  2.7 7.8 %copy-start.1 = (f32[1536]{0:T(1024)S(1)}, f32[1536]{0:T(1024)}, u32[]{:S(2)}) copy-start(f32[1536]{0:T(1024)} %param.12) | copy-start | bytes 18436
  2.7 11.0 %collective-permute-start = (bf16[4,192,128]{2,1,0:T(8,128)(2,1)S(1)}, bf16[4,192,128]{2,1,0:T(8,128)(2,1)S(1)}, u32[]{:S(2)}, u32[]{:S(2)}) collective-permute-start(bf16[4,192,128]{2,1,0:T(8,128)(2,1)S(1)} %get-tuple-element.44), channel_id=1, source_target_pairs={{0,3},{1,2},{2,1},{3,0},{4,7},{5,6},{6,5},{7,4},{8,11},{9,10},{10,... | collective-permute-start | bytes 589832 | tf_op jit(solution)/shard_map/ppermute | solution.py:299
  7.8 16.8 %collective-permute-start.1 = (bf16[4,192,128]{2,1,0:T(8,128)(2,1)S(1)}, bf16[4,192,128]{2,1,0:T(8,128)(2,1)S(1)}, u32[]{:S(2)}, u32[]{:S(2)}) collective-permute-start(bf16[4,192,128]{2,1,0:T(8,128)(2,1)S(1)} %get-tuple-element.45), channel_id=1, source_target_pairs={{0,2},{1,3},{2,0},{3,1},{4,6},{5,7},{6,4},{7,5},{8,10},{9,11},{10,... | collective-permute-start | bytes 589832 | tf_op jit(solution)/shard_map/ppermute | solution.py:299
  7.8 16.8 %collective-permute-start.2 = (bf16[4,192,128]{2,1,0:T(8,128)(2,1)S(1)}, bf16[4,192,128]{2,1,0:T(8,128)(2,1)S(1)}, u32[]{:S(2)}, u32[]{:S(2)}) collective-permute-start(bf16[4,192,128]{2,1,0:T(8,128)(2,1)S(1)} %get-tuple-element.46), channel_id=1, source_target_pairs={{0,1},{1,0},{2,3},{3,2},{4,5},{5,4},{6,7},{7,6},{8,9},{9,8},{10,11... | collective-permute-start | bytes 589832 | tf_op jit(solution)/shard_map/ppermute | solution.py:299
  8.5 33.3 %collective-permute-start.5 = (bf16[4,192,128]{2,1,0:T(8,128)(2,1)S(1)}, bf16[4,192,128]{2,1,0:T(8,128)(2,1)S(1)}, u32[]{:S(2)}, u32[]{:S(2)}) collective-permute-start(bf16[4,192,128]{2,1,0:T(8,128)(2,1)S(1)} %get-tuple-element.57), channel_id=1, source_target_pairs={{0,1},{1,0},{2,3},{3,2},{4,5},{5,4},{6,7},{7,6},{8,9},{9,8},{10,11... | collective-permute-start | bytes 589832 | tf_op jit(solution)/shard_map/ppermute | solution.py:299
  24.6 14.5 %collective-permute-start.3 = (bf16[4,192,128]{2,1,0:T(8,128)(2,1)S(1)}, bf16[4,192,128]{2,1,0:T(8,128)(2,1)S(1)}, u32[]{:S(2)}, u32[]{:S(2)}) collective-permute-start(bf16[4,192,128]{2,1,0:T(8,128)(2,1)S(1)} %get-tuple-element.54), channel_id=1, source_target_pairs={{0,3},{1,2},{2,1},{3,0},{4,7},{5,6},{6,5},{7,4},{8,11},{9,10},{10,... | collective-permute-start | bytes 589832 | tf_op jit(solution)/shard_map/ppermute | solution.py:299
  27.2 18.7 %collective-permute-start.4 = (bf16[4,192,128]{2,1,0:T(8,128)(2,1)S(1)}, bf16[4,192,128]{2,1,0:T(8,128)(2,1)S(1)}, u32[]{:S(2)}, u32[]{:S(2)}) collective-permute-start(bf16[4,192,128]{2,1,0:T(8,128)(2,1)S(1)} %get-tuple-element.56), channel_id=1, source_target_pairs={{0,2},{1,3},{2,0},{3,1},{4,6},{5,7},{6,4},{7,5},{8,10},{9,11},{10,... | collective-permute-start | bytes 589832 | tf_op jit(solution)/shard_map/ppermute | solution.py:299
  37.3 18.7 %collective-permute-start.8 = (bf16[3,192,128]{2,1,0:T(8,128)(2,1)S(1)}, bf16[3,192,128]{2,1,0:T(8,128)(2,1)S(1)}, u32[]{:S(2)}, u32[]{:S(2)}) collective-permute-start(bf16[3,192,128]{2,1,0:T(8,128)(2,1)S(1)} %get-tuple-element.70), channel_id=1, source_target_pairs={{0,1},{1,0},{2,3},{3,2},{4,5},{5,4},{6,7},{7,6},{8,9},{9,8},{10,11... | collective-permute-start | bytes 442376 | tf_op jit(solution)/shard_map/ppermute | solution.py:299
  39.1 17.0 %collective-permute-start.6 = (bf16[3,192,128]{2,1,0:T(8,128)(2,1)S(1)}, bf16[3,192,128]{2,1,0:T(8,128)(2,1)S(1)}, u32[]{:S(2)}, u32[]{:S(2)}) collective-permute-start(bf16[3,192,128]{2,1,0:T(8,128)(2,1)S(1)} %get-tuple-element.64), channel_id=1, source_target_pairs={{0,3},{1,2},{2,1},{3,0},{4,7},{5,6},{6,5},{7,4},{8,11},{9,10},{10,... | collective-permute-start | bytes 442376 | tf_op jit(solution)/shard_map/ppermute | solution.py:299
  46.0 13.1 %collective-permute-start.7 = (bf16[3,192,128]{2,1,0:T(8,128)(2,1)S(1)}, bf16[3,192,128]{2,1,0:T(8,128)(2,1)S(1)}, u32[]{:S(2)}, u32[]{:S(2)}) collective-permute-start(bf16[3,192,128]{2,1,0:T(8,128)(2,1)S(1)} %get-tuple-element.67), channel_id=1, source_target_pairs={{0,2},{1,3},{2,0},{3,1},{4,6},{5,7},{6,4},{7,5},{8,10},{9,11},{10,... | collective-permute-start | bytes 442376 | tf_op jit(solution)/shard_map/ppermute | solution.py:299
  56.0 10.6 %collective-permute-start.9 = (bf16[3,192,128]{2,1,0:T(8,128)(2,1)S(1)}, bf16[3,192,128]{2,1,0:T(8,128)(2,1)S(1)}, u32[]{:S(2)}, u32[]{:S(2)}) collective-permute-start(bf16[3,192,128]{2,1,0:T(8,128)(2,1)S(1)} %get-tuple-element.73), channel_id=1, source_target_pairs={{0,3},{1,2},{2,1},{3,0},{4,7},{5,6},{6,5},{7,4},{8,11},{9,10},{10,... | collective-permute-start | bytes 442376 | tf_op jit(solution)/shard_map/ppermute | solution.py:299
  56.1 4.5 %collective-permute-start.12 = (f32[4,32,96]{2,1,0:T(8,128)S(1)}, f32[4,32,96]{2,1,0:T(8,128)S(1)}, u32[]{:S(2)}, u32[]{:S(2)}) collective-permute-start(f32[4,32,96]{2,1,0:T(8,128)S(1)} %pad_maximum_fusion), channel_id=1, source_target_pairs={{0,4},{4,0},{8,12},{12,8},{16,20},{20,16},{24,28},{28,24},{1,5},{5... | collective-permute-start | bytes 147464 | tf_op jit(solution)/shard_map/ppermute | solution.py:309
  56.1 13.7 %collective-permute-start.10 = (bf16[3,192,128]{2,1,0:T(8,128)(2,1)S(1)}, bf16[3,192,128]{2,1,0:T(8,128)(2,1)S(1)}, u32[]{:S(2)}, u32[]{:S(2)}) collective-permute-start(bf16[3,192,128]{2,1,0:T(8,128)(2,1)S(1)} %get-tuple-element.74), channel_id=1, source_target_pairs={{0,2},{1,3},{2,0},{3,1},{4,6},{5,7},{6,4},{7,5},{8,10},{9,11},{10,... | collective-permute-start | bytes 442376 | tf_op jit(solution)/shard_map/ppermute | solution.py:299
  59.1 10.8 %collective-permute-start.11 = (bf16[3,192,128]{2,1,0:T(8,128)(2,1)S(1)}, bf16[3,192,128]{2,1,0:T(8,128)(2,1)S(1)}, u32[]{:S(2)}, u32[]{:S(2)}) collective-permute-start(bf16[3,192,128]{2,1,0:T(8,128)(2,1)S(1)} %get-tuple-element.75), channel_id=1, source_target_pairs={{0,1},{1,0},{2,3},{3,2},{4,5},{5,4},{6,7},{7,6},{8,9},{9,8},{10,11... | collective-permute-start | bytes 442376 | tf_op jit(solution)/shard_map/ppermute | solution.py:299
  60.6 4.3 %collective-permute-start.13 = (f32[4,32,96]{2,1,0:T(8,128)S(1)}, f32[4,32,96]{2,1,0:T(8,128)S(1)}, u32[]{:S(2)}, u32[]{:S(2)}) collective-permute-start(f32[4,32,96]{2,1,0:T(8,128)S(1)} %add.11), channel_id=1, source_target_pairs={{0,8},{4,12},{8,0},{12,4},{16,24},{20,28},{24,16},{28,20},{1,9},{5... | collective-permute-start | bytes 147464 | tf_op jit(solution)/shard_map/ppermute | solution.py:309
  64.9 5.0 %collective-permute-start.14 = (f32[4,32,96]{2,1,0:T(8,128)S(1)}, f32[4,32,96]{2,1,0:T(8,128)S(1)}, u32[]{:S(2)}, u32[]{:S(2)}) collective-permute-start(f32[4,32,96]{2,1,0:T(8,128)S(1)} %add.12.refs_8_), channel_id=1, source_target_pairs={{0,16},{4,20},{8,24},{12,28},{16,0},{20,4},{24,8},{28,12},{1,17},{... | collective-permute-start | bytes 147464 | tf_op jit(solution)/shard_map/ppermute | solution.py:309

commit v10 on v9

--- a/solution.py
+++ b/solution.py
@@ -285,14 +285,10 @@
     return outs[:count], outs[count]
 
 
-def exchanged(pieces, before, eager=False):
+def exchanged(pieces, before):
     pieces = list(pieces)
-    last = len(pieces) - 1
-    if before is not None and eager:
-        pieces[last], before[last] = lax.optimization_barrier((pieces[last], before[last]))
-    if before is not None and last > 1:
-        wait = slice(last - 1 if eager else last, 1, -1)
-        pieces[wait], before[:0:-1] = lax.optimization_barrier((pieces[wait], before[:0:-1]))
+    if before is not None and len(pieces) > 2:
+        pieces[:1:-1], before[:0:-1] = lax.optimization_barrier((pieces[:1:-1], before[:0:-1]))
     moved = pieces[:1] * len(pieces)
     for distance in range(len(pieces) - 1, 0, -1):
         pairs = [(i, i ^ distance) for i in range(len(pieces))]
@@ -333,7 +329,7 @@
         grads, part = core(scalars, weight[at], bias[at], order[chunk])
         taps.append(part)
         if chunk < chunks - 1:
-            order.append(exchanged(grads, order[-1], True))
+            order.append(exchanged(grads, order[-1]))
     before, grads, taps = order[-1], list(grads), jnp.concatenate(taps, axis=0)
     last = count - 1
     grads[last], before[1] = lax.optimization_barrier((grads[last], before[1]))

time: 71.4 us -> 71.1 us (level)
  starting transfers between devices: 22 us -> 21 us
    ppermute x12, starting transfers between devices: 18.7 us -> 17.8 us  [exchanged(): moved[distance] = lax.ppermute(pieces[distance], 'seq', pairs)]
where the time goes in v10:
time: 71.1 us; the launch traced here: 71 us
  waiting for transfers between devices  24.8 us (35%)
  Pallas kernels  23.3 us (33%)
  starting transfers between devices  21 us (30%)
  between operations  1.43 us (2%)
    ppermute x12, waiting for transfers between devices, exchanged(): moved[distance] = lax.ppermute(pieces[distance], 'seq', pairs)  22.1 us
    pallas_call x2, Pallas kernels, core(): pl.pallas_call(functools.partial(core_kernel, count, block), out_shape=(p...  19.9 us
    ppermute x12, starting transfers between devices, exchanged(): moved[distance] = lax.ppermute(pieces[distance], 'seq', pairs)  17.8 us
    ppermute x3, starting transfers between devices, doubled(): pair = (total, lax.ppermute(total, axis, pairs))  3.23 us
    ppermute x3, waiting for transfers between devices, doubled(): pair = (total, lax.ppermute(total, axis, pairs))  2.77 us
    pallas_call x1, Pallas kernels, pack(): pl.pallas_call(functools.partial(pack_kernel, count, chunks), out_shape=(...  2.03 us
  transfers between devices with their start and end apart: 15, of which 5 were waited for; matrix products, arithmetic and copies ran while one was open for 0% of the time, Pallas kernels for 28%

profile of v10, /device:TPU:0, one launch (start us, length us, event | category | flops | bytes accessed | tf_op | source)
XLA Modules:
  0.0 71.0 jit_solution(5233032538160760169)
XLA Ops:
  0.6 2.0 %shard_map.110 = (bf16[4,192,128]{2,1,0:T(8,128)(2,1)S(1)}, bf16[4,192,128]{2,1,0:T(8,128)(2,1)S(1)}, bf16[4,192,128]{2,1,0:T(8,128)(2,1)S(1)}, bf16[4,192,128]{...) custom-call(s32[1]{0:T(128)} %bitcast.rank_ref, ...), custom_call_target="tpu_custom_call" | custom-call | bytes 3145728 | tf_op jit(solution)/shard_map/pallas_call | solution.py:38
  2.7 5.1 %collective-permute-start = (bf16[4,192,128]{2,1,0:T(8,128)(2,1)S(1)}, bf16[4,192,128]{2,1,0:T(8,128)(2,1)S(1)}, u32[]{:S(2)}, u32[]{:S(2)}) collective-permute-start(bf16[4,192,128]{2,1,0:T(8,128)(2,1)S(1)} %get-tuple-element.43), channel_id=1, source_target_pairs={{0,3},{1,2},{2,1},{3,0},{4,7},{5,6},{6,5},{7,4},{8,11},{9,10},{10,... | collective-permute-start | bytes 589832 | tf_op jit(solution)/shard_map/ppermute | solution.py:295
  7.8 0.6 collective-permute-start.2
  8.5 1.4 %collective-permute-start.5 = (bf16[4,192,128]{2,1,0:T(8,128)(2,1)S(1)}, bf16[4,192,128]{2,1,0:T(8,128)(2,1)S(1)}, u32[]{:S(2)}, u32[]{:S(2)}) collective-permute-start(bf16[4,192,128]{2,1,0:T(8,128)(2,1)S(1)} %get-tuple-element.55), channel_id=1, source_target_pairs={{0,1},{1,0},{2,3},{3,2},{4,5},{5,4},{6,7},{7,6},{8,9},{9,8},{10,11... | collective-permute-start | bytes 589832 | tf_op jit(solution)/shard_map/ppermute | solution.py:295
  10.5 0.1 reshape.17
  10.6 0.1 reshape.16
  10.8 2.9 %collective-permute-done.refs_1_ = bf16[4,192,128]{2,1,0:T(8,128)(2,1)S(1)} collective-permute-done((bf16[4,192,128]{2,1,0:T(8,128)(2,1)S(1)}, bf16[4,192,128]{2,1,0:T(8,128)(2,1)S(1)}, u32[]{:S(2)}, u32[]{:S(2)}) %collective-permute-start) | collective-permute-done | bytes 196640 | tf_op jit(solution)/shard_map/ppermute | solution.py:295
  13.7 10.9 %collective-permute-done.1.refs_2_ = bf16[4,192,128]{2,1,0:T(8,128)(2,1)S(1)} collective-permute-done((bf16[4,192,128]{2,1,0:T(8,128)(2,1)S(1)}, bf16[4,192,128]{2,1,0:T(8,128)(2,1)S(1)}, u32[]{:S(2)}, u32[]{:S(2)}) %collective-permute-start.1) | collective-permute-done | bytes 196640 | tf_op jit(solution)/shard_map/ppermute | solution.py:295
  24.6 2.6 %collective-permute-start.3 = (bf16[4,192,128]{2,1,0:T(8,128)(2,1)S(1)}, bf16[4,192,128]{2,1,0:T(8,128)(2,1)S(1)}, u32[]{:S(2)}, u32[]{:S(2)}) collective-permute-start(bf16[4,192,128]{2,1,0:T(8,128)(2,1)S(1)} %get-tuple-element.53), channel_id=1, source_target_pairs={{0,3},{1,2},{2,1},{3,0},{4,7},{5,6},{6,5},{7,4},{8,11},{9,10},{10,... | collective-permute-start | bytes 589832 | tf_op jit(solution)/shard_map/ppermute | solution.py:295
  27.3 0.1 pad_add_fusion.scalars
  27.3 9.9 %shard_map.111 = (bf16[3,192,128]{2,1,0:T(8,128)(2,1)S(1)}, bf16[3,192,128]{2,1,0:T(8,128)(2,1)S(1)}, bf16[3,192,128]{2,1,0:T(8,128)(2,1)S(1)}, bf16[3,192,128]{2,1,0:T(8,128)(2,1)S(1)}, f32[2,32,96]{2,1,0:T(8,128)S(1)}) custom-call(s32[2]{0:T(128)S(1)} %pad_add_fusion.scalars, f32[2,31,96]{2,1,0:T(8,128)S(1)} %get-tuple-element.76.weight_ref, ...), custom_call_target="tpu_custom_call" | custom-call | flops 1207959552 | bytes 1376256 | tf_op jit(solution)/shard_map/pallas_call | solution.py:264
  37.3 1.8 %collective-permute-start.8 = (bf16[3,192,128]{2,1,0:T(8,128)(2,1)S(1)}, bf16[3,192,128]{2,1,0:T(8,128)(2,1)S(1)}, u32[]{:S(2)}, u32[]{:S(2)}) collective-permute-start(bf16[3,192,128]{2,1,0:T(8,128)(2,1)S(1)} %get-tuple-element.68), channel_id=1, source_target_pairs={{0,1},{1,0},{2,3},{3,2},{4,5},{5,4},{6,7},{7,6},{8,9},{9,8},{10,11... | collective-permute-start | bytes 442376 | tf_op jit(solution)/shard_map/ppermute | solution.py:295
  39.1 3.2 %collective-permute-done.4.refs_2_ = bf16[4,192,128]{2,1,0:T(8,128)(2,1)S(1)} collective-permute-done((bf16[4,192,128]{2,1,0:T(8,128)(2,1)S(1)}, bf16[4,192,128]{2,1,0:T(8,128)(2,1)S(1)}, u32[]{:S(2)}, u32[]{:S(2)}) %collective-permute-start.4) | collective-permute-done | bytes 196640 | tf_op jit(solution)/shard_map/ppermute | solution.py:295
  42.3 1.7 %collective-permute-start.6 = (bf16[3,192,128]{2,1,0:T(8,128)(2,1)S(1)}, bf16[3,192,128]{2,1,0:T(8,128)(2,1)S(1)}, u32[]{:S(2)}, u32[]{:S(2)}) collective-permute-start(bf16[3,192,128]{2,1,0:T(8,128)(2,1)S(1)} %get-tuple-element.62), channel_id=1, source_target_pairs={{0,3},{1,2},{2,1},{3,0},{4,7},{5,6},{6,5},{7,4},{8,11},{9,10},{10,... | collective-permute-start | bytes 442376 | tf_op jit(solution)/shard_map/ppermute | solution.py:295
  44.0 10.0 %shard_map.112 = (bf16[3,192,128]{2,1,0:T(8,128)(2,1)S(1)}, bf16[3,192,128]{2,1,0:T(8,128)(2,1)S(1)}, bf16[3,192,128]{2,1,0:T(8,128)(2,1)S(1)}, bf16[3,192,128]{2,1,0:T(8,128)(2,1)S(1)}, f32[2,32,96]{2,1,0:T(8,128)S(1)}) custom-call(s32[2]{0:T(128)S(1)} %pad_add_fusion.scalars, f32[2,31,96]{2,1,0:T(8,128)S(1)} %get-tuple-element.75.weight_ref, ...), custom_call_target="tpu_custom_call" | custom-call | flops 1207959552 | bytes 1376256 | tf_op jit(solution)/shard_map/pallas_call | solution.py:264
  54.0 2.2 %collective-permute-start.9 = (bf16[3,192,128]{2,1,0:T(8,128)(2,1)S(1)}, bf16[3,192,128]{2,1,0:T(8,128)(2,1)S(1)}, u32[]{:S(2)}, u32[]{:S(2)}) collective-permute-start(bf16[3,192,128]{2,1,0:T(8,128)(2,1)S(1)} %get-tuple-element.71), channel_id=1, source_target_pairs={{0,3},{1,2},{2,1},{3,0},{4,7},{5,6},{6,5},{7,4},{8,11},{9,10},{10,... | collective-permute-start | bytes 442376 | tf_op jit(solution)/shard_map/ppermute | solution.py:295
  56.2 0.1 collective-permute-start.12
  56.2 2.1 %collective-permute-start.10 = (bf16[3,192,128]{2,1,0:T(8,128)(2,1)S(1)}, bf16[3,192,128]{2,1,0:T(8,128)(2,1)S(1)}, u32[]{:S(2)}, u32[]{:S(2)}) collective-permute-start(bf16[3,192,128]{2,1,0:T(8,128)(2,1)S(1)} %get-tuple-element.72), channel_id=1, source_target_pairs={{0,2},{1,3},{2,0},{3,1},{4,6},{5,7},{6,4},{7,5},{8,10},{9,11},{10,... | collective-permute-start | bytes 442376 | tf_op jit(solution)/shard_map/ppermute | solution.py:295
  58.4 0.2 collective-permute-start.11
  58.6 1.6 %collective-permute-start.13 = (f32[4,32,96]{2,1,0:T(8,128)S(1)}, f32[4,32,96]{2,1,0:T(8,128)S(1)}, u32[]{:S(2)}, u32[]{:S(2)}) collective-permute-start(f32[4,32,96]{2,1,0:T(8,128)S(1)} %add.11), channel_id=1, source_target_pairs={{0,8},{4,12},{8,0},{12,4},{16,24},{20,28},{24,16},{28,20},{1,9},{5... | collective-permute-start | bytes 147464 | tf_op jit(solution)/shard_map/ppermute | solution.py:305
  60.2 2.8 %collective-permute-done.13 = f32[4,32,96]{2,1,0:T(8,128)S(1)} collective-permute-done((f32[4,32,96]{2,1,0:T(8,128)S(1)}, f32[4,32,96]{2,1,0:T(8,128)S(1)}, u32[]{:S(2)}, u32[]{:S(2)}) %collective-permute-start.13) | collective-permute-done | bytes 49184 | tf_op jit(solution)/shard_map/ppermute | solution.py:305
  62.9 1.6 %collective-permute-start.14 = (f32[4,32,96]{2,1,0:T(8,128)S(1)}, f32[4,32,96]{2,1,0:T(8,128)S(1)}, u32[]{:S(2)}, u32[]{:S(2)}) collective-permute-start(f32[4,32,96]{2,1,0:T(8,128)S(1)} %add.12.refs_8_), channel_id=1, source_target_pairs={{0,16},{4,20},{8,24},{12,28},{16,0},{20,4},{24,8},{28,12},{1,17},{... | collective-permute-start | bytes 147464 | tf_op jit(solution)/shard_map/ppermute | solution.py:305
  64.5 5.0 %collective-permute-done.10.refs_6_ = bf16[3,192,128]{2,1,0:T(8,128)(2,1)S(1)} collective-permute-done((bf16[3,192,128]{2,1,0:T(8,128)(2,1)S(1)}, bf16[3,192,128]{2,1,0:T(8,128)(2,1)S(1)}, u32[]{:S(2)}, u32[]{:S(2)}) %collective-permute-start.10) | collective-permute-done | bytes 147488 | tf_op jit(solution)/shard_map/ppermute | solution.py:295
  69.6 1.4 %shard_map.113 = (bf16[1,128,1536]{2,1,0:T(8,128)(2,1)}, bf16[1,128,1536]{2,1,0:T(8,128)(2,1)}, bf16[1,128,1536]{2,1,0:T(8,128)(2,1)}, f32[31,384]{1,0:T(8,128)}, f32[384]{0:T(512)}) custom-call(s32[1]{0:T(128)} %bitcast.rank_ref, bf16[3,192,128]{2,1,0:T(8,128)(2,1)S(1)} %get-tuple-element.49.refs_0_, ...), custom_call_target="tpu_custom_call" | custom-call | bytes 2359296 | tf_op jit(solution)/shard_map/pallas_call | solution.py:82
  (24 shorter events, 0.1 us)
Async XLA Ops:
  0.6 10.0 %copy-start = (f32[31,1536]{1,0:T(8,128)S(1)}, f32[31,1536]{1,0:T(8,128)}, u32[]{:S(2)}) copy-start(f32[31,1536]{1,0:T(8,128)} %param.11) | copy-start | bytes 571396
  2.7 7.8 %copy-start.1 = (f32[1536]{0:T(1024)S(1)}, f32[1536]{0:T(1024)}, u32[]{:S(2)}) copy-start(f32[1536]{0:T(1024)} %param.12) | copy-start | bytes 18436
  2.7 11.0 %collective-permute-start = (bf16[4,192,128]{2,1,0:T(8,128)(2,1)S(1)}, bf16[4,192,128]{2,1,0:T(8,128)(2,1)S(1)}, u32[]{:S(2)}, u32[]{:S(2)}) collective-permute-start(bf16[4,192,128]{2,1,0:T(8,128)(2,1)S(1)} %get-tuple-element.43), channel_id=1, source_target_pairs={{0,3},{1,2},{2,1},{3,0},{4,7},{5,6},{6,5},{7,4},{8,11},{9,10},{10,... | collective-permute-start | bytes 589832 | tf_op jit(solution)/shard_map/ppermute | solution.py:295
  7.8 16.8 %collective-permute-start.1 = (bf16[4,192,128]{2,1,0:T(8,128)(2,1)S(1)}, bf16[4,192,128]{2,1,0:T(8,128)(2,1)S(1)}, u32[]{:S(2)}, u32[]{:S(2)}) collective-permute-start(bf16[4,192,128]{2,1,0:T(8,128)(2,1)S(1)} %get-tuple-element.44), channel_id=1, source_target_pairs={{0,2},{1,3},{2,0},{3,1},{4,6},{5,7},{6,4},{7,5},{8,10},{9,11},{10,... | collective-permute-start | bytes 589832 | tf_op jit(solution)/shard_map/ppermute | solution.py:295
  7.8 16.8 %collective-permute-start.2 = (bf16[4,192,128]{2,1,0:T(8,128)(2,1)S(1)}, bf16[4,192,128]{2,1,0:T(8,128)(2,1)S(1)}, u32[]{:S(2)}, u32[]{:S(2)}) collective-permute-start(bf16[4,192,128]{2,1,0:T(8,128)(2,1)S(1)} %get-tuple-element.45), channel_id=1, source_target_pairs={{0,1},{1,0},{2,3},{3,2},{4,5},{5,4},{6,7},{7,6},{8,9},{9,8},{10,11... | collective-permute-start | bytes 589832 | tf_op jit(solution)/shard_map/ppermute | solution.py:295
  8.5 30.6 %collective-permute-start.5 = (bf16[4,192,128]{2,1,0:T(8,128)(2,1)S(1)}, bf16[4,192,128]{2,1,0:T(8,128)(2,1)S(1)}, u32[]{:S(2)}, u32[]{:S(2)}) collective-permute-start(bf16[4,192,128]{2,1,0:T(8,128)(2,1)S(1)} %get-tuple-element.55), channel_id=1, source_target_pairs={{0,1},{1,0},{2,3},{3,2},{4,5},{5,4},{6,7},{7,6},{8,9},{9,8},{10,11... | collective-permute-start | bytes 589832 | tf_op jit(solution)/shard_map/ppermute | solution.py:295
  24.6 14.5 %collective-permute-start.3 = (bf16[4,192,128]{2,1,0:T(8,128)(2,1)S(1)}, bf16[4,192,128]{2,1,0:T(8,128)(2,1)S(1)}, u32[]{:S(2)}, u32[]{:S(2)}) collective-permute-start(bf16[4,192,128]{2,1,0:T(8,128)(2,1)S(1)} %get-tuple-element.53), channel_id=1, source_target_pairs={{0,3},{1,2},{2,1},{3,0},{4,7},{5,6},{6,5},{7,4},{8,11},{9,10},{10,... | collective-permute-start | bytes 589832 | tf_op jit(solution)/shard_map/ppermute | solution.py:295
  27.2 15.0 %collective-permute-start.4 = (bf16[4,192,128]{2,1,0:T(8,128)(2,1)S(1)}, bf16[4,192,128]{2,1,0:T(8,128)(2,1)S(1)}, u32[]{:S(2)}, u32[]{:S(2)}) collective-permute-start(bf16[4,192,128]{2,1,0:T(8,128)(2,1)S(1)} %get-tuple-element.54), channel_id=1, source_target_pairs={{0,2},{1,3},{2,0},{3,1},{4,6},{5,7},{6,4},{7,5},{8,10},{9,11},{10,... | collective-permute-start | bytes 589832 | tf_op jit(solution)/shard_map/ppermute | solution.py:295
  37.3 16.7 %collective-permute-start.8 = (bf16[3,192,128]{2,1,0:T(8,128)(2,1)S(1)}, bf16[3,192,128]{2,1,0:T(8,128)(2,1)S(1)}, u32[]{:S(2)}, u32[]{:S(2)}) collective-permute-start(bf16[3,192,128]{2,1,0:T(8,128)(2,1)S(1)} %get-tuple-element.68), channel_id=1, source_target_pairs={{0,1},{1,0},{2,3},{3,2},{4,5},{5,4},{6,7},{7,6},{8,9},{9,8},{10,11... | collective-permute-start | bytes 442376 | tf_op jit(solution)/shard_map/ppermute | solution.py:295
  42.3 13.9 %collective-permute-start.6 = (bf16[3,192,128]{2,1,0:T(8,128)(2,1)S(1)}, bf16[3,192,128]{2,1,0:T(8,128)(2,1)S(1)}, u32[]{:S(2)}, u32[]{:S(2)}) collective-permute-start(bf16[3,192,128]{2,1,0:T(8,128)(2,1)S(1)} %get-tuple-element.62), channel_id=1, source_target_pairs={{0,3},{1,2},{2,1},{3,0},{4,7},{5,6},{6,5},{7,4},{8,11},{9,10},{10,... | collective-permute-start | bytes 442376 | tf_op jit(solution)/shard_map/ppermute | solution.py:295
  44.0 14.4 %collective-permute-start.7 = (bf16[3,192,128]{2,1,0:T(8,128)(2,1)S(1)}, bf16[3,192,128]{2,1,0:T(8,128)(2,1)S(1)}, u32[]{:S(2)}, u32[]{:S(2)}) collective-permute-start(bf16[3,192,128]{2,1,0:T(8,128)(2,1)S(1)} %get-tuple-element.65), channel_id=1, source_target_pairs={{0,2},{1,3},{2,0},{3,1},{4,6},{5,7},{6,4},{7,5},{8,10},{9,11},{10,... | collective-permute-start | bytes 442376 | tf_op jit(solution)/shard_map/ppermute | solution.py:295
  54.0 10.6 %collective-permute-start.9 = (bf16[3,192,128]{2,1,0:T(8,128)(2,1)S(1)}, bf16[3,192,128]{2,1,0:T(8,128)(2,1)S(1)}, u32[]{:S(2)}, u32[]{:S(2)}) collective-permute-start(bf16[3,192,128]{2,1,0:T(8,128)(2,1)S(1)} %get-tuple-element.71), channel_id=1, source_target_pairs={{0,3},{1,2},{2,1},{3,0},{4,7},{5,6},{6,5},{7,4},{8,11},{9,10},{10,... | collective-permute-start | bytes 442376 | tf_op jit(solution)/shard_map/ppermute | solution.py:295
  56.2 2.4 %collective-permute-start.12 = (f32[4,32,96]{2,1,0:T(8,128)S(1)}, f32[4,32,96]{2,1,0:T(8,128)S(1)}, u32[]{:S(2)}, u32[]{:S(2)}) collective-permute-start(f32[4,32,96]{2,1,0:T(8,128)S(1)} %pad_maximum_fusion), channel_id=1, source_target_pairs={{0,4},{4,0},{8,12},{12,8},{16,20},{20,16},{24,28},{28,24},{1,5},{5... | collective-permute-start | bytes 147464 | tf_op jit(solution)/shard_map/ppermute | solution.py:305
  56.2 13.3 %collective-permute-start.10 = (bf16[3,192,128]{2,1,0:T(8,128)(2,1)S(1)}, bf16[3,192,128]{2,1,0:T(8,128)(2,1)S(1)}, u32[]{:S(2)}, u32[]{:S(2)}) collective-permute-start(bf16[3,192,128]{2,1,0:T(8,128)(2,1)S(1)} %get-tuple-element.72), channel_id=1, source_target_pairs={{0,2},{1,3},{2,0},{3,1},{4,6},{5,7},{6,4},{7,5},{8,10},{9,11},{10,... | collective-permute-start | bytes 442376 | tf_op jit(solution)/shard_map/ppermute | solution.py:295
  58.4 11.2 %collective-permute-start.11 = (bf16[3,192,128]{2,1,0:T(8,128)(2,1)S(1)}, bf16[3,192,128]{2,1,0:T(8,128)(2,1)S(1)}, u32[]{:S(2)}, u32[]{:S(2)}) collective-permute-start(bf16[3,192,128]{2,1,0:T(8,128)(2,1)S(1)} %get-tuple-element.73), channel_id=1, source_target_pairs={{0,1},{1,0},{2,3},{3,2},{4,5},{5,4},{6,7},{7,6},{8,9},{9,8},{10,11... | collective-permute-start | bytes 442376 | tf_op jit(solution)/shard_map/ppermute | solution.py:295
  58.6 4.3 %collective-permute-start.13 = (f32[4,32,96]{2,1,0:T(8,128)S(1)}, f32[4,32,96]{2,1,0:T(8,128)S(1)}, u32[]{:S(2)}, u32[]{:S(2)}) collective-permute-start(f32[4,32,96]{2,1,0:T(8,128)S(1)} %add.11), channel_id=1, source_target_pairs={{0,8},{4,12},{8,0},{12,4},{16,24},{20,28},{24,16},{28,20},{1,9},{5... | collective-permute-start | bytes 147464 | tf_op jit(solution)/shard_map/ppermute | solution.py:305
  62.9 6.6 %collective-permute-start.14 = (f32[4,32,96]{2,1,0:T(8,128)S(1)}, f32[4,32,96]{2,1,0:T(8,128)S(1)}, u32[]{:S(2)}, u32[]{:S(2)}) collective-permute-start(f32[4,32,96]{2,1,0:T(8,128)S(1)} %add.12.refs_8_), channel_id=1, source_target_pairs={{0,16},{4,20},{8,24},{12,28},{16,0},{20,4},{24,8},{28,12},{1,17},{... | collective-permute-start | bytes 147464 | tf_op jit(solution)/shard_map/ppermute | solution.py:305

commit v11 on v9

--- a/solution.py
+++ b/solution.py
@@ -326,20 +326,20 @@
     sent = pack(rank[None], (queries, keys, values, grad_out), count, chunks)
     order = []
     for pieces in sent:
-        order.append(exchanged(pieces, order[-1] if order else None))
+        order.append(exchanged(pieces, order[-1] if order else None, True))
     taps = []
     for chunk in range(chunks):
         at = slice(chunk * step, (chunk + 1) * step)
         grads, part = core(scalars, weight[at], bias[at], order[chunk])
         taps.append(part)
         if chunk < chunks - 1:
-            order.append(exchanged(grads, order[-1], True))
+            order.append(exchanged(grads, order[-1]))
     before, grads, taps = order[-1], list(grads), jnp.concatenate(taps, axis=0)
     last = count - 1
-    grads[last], before[1] = lax.optimization_barrier((grads[last], before[1]))
+    grads[last - 1], before[1] = lax.optimization_barrier((grads[last - 1], before[1]))
     if last > 2:
-        (grads[last - 1], taps), before[last] = lax.optimization_barrier(
-            ((grads[last - 1], taps), before[last])
+        (grads[last], taps), before[last] = lax.optimization_barrier(
+            ((grads[last], taps), before[last])
         )
         grads[1], before[last - 1] = lax.optimization_barrier((grads[1], before[last - 1]))
     order.append(exchanged(grads, None))

time: 71.4 us -> 70.2 us (0.983)
  waiting for transfers between devices: 24.2 us -> 21.2 us
  starting transfers between devices: 22 us -> 23.8 us
    ppermute x12, waiting for transfers between devices: 21.4 us -> 18.4 us  [exchanged(): moved[distance] = lax.ppermute(pieces[distance], 'seq', pairs)]
    ppermute x12, starting transfers between devices: 18.7 us -> 20.6 us  [exchanged(): moved[distance] = lax.ppermute(pieces[distance], 'seq', pairs)]
  transfers between devices with their start and end apart: 15 -> 15, of which waited for: 5 -> 6; matrix products, arithmetic and copies ran while one was open for 0% -> 0% of each run, Pallas kernels for 28% -> 28%
where the time goes in v11:
time: 70.2 us; the launch traced here: 70.1 us
  starting transfers between devices  23.8 us (34%)
  Pallas kernels  23.3 us (33%)
  waiting for transfers between devices  21.2 us (30%)
  between operations  1.44 us (2%)
    ppermute x12, starting transfers between devices, exchanged(): moved[distance] = lax.ppermute(pieces[distance], 'seq', pairs)  20.6 us
    pallas_call x2, Pallas kernels, core(): pl.pallas_call(functools.partial(core_kernel, count, block), out_shape=(p...  19.9 us
    ppermute x12, waiting for transfers between devices, exchanged(): moved[distance] = lax.ppermute(pieces[distance], 'seq', pairs)  18.4 us
    ppermute x3, starting transfers between devices, doubled(): pair = (total, lax.ppermute(total, axis, pairs))  3.21 us
    ppermute x3, waiting for transfers between devices, doubled(): pair = (total, lax.ppermute(total, axis, pairs))  2.78 us
    pallas_call x1, Pallas kernels, pack(): pl.pallas_call(functools.partial(pack_kernel, count, chunks), out_shape=(...  2.03 us
  transfers between devices with their start and end apart: 15, of which 6 were waited for; matrix products, arithmetic and copies ran while one was open for 0% of the time, Pallas kernels for 28%

profile of v11, /device:TPU:0, one launch (start us, length us, event | category | flops | bytes accessed | tf_op | source)
XLA Modules:
  0.0 70.1 jit_solution(4497665018496610343)
XLA Ops:
  0.6 2.0 %shard_map.110 = (bf16[4,192,128]{2,1,0:T(8,128)(2,1)S(1)}, bf16[4,192,128]{2,1,0:T(8,128)(2,1)S(1)}, bf16[4,192,128]{2,1,0:T(8,128)(2,1)S(1)}, bf16[4,192,128]{...) custom-call(s32[1]{0:T(128)} %bitcast.rank_ref, ...), custom_call_target="tpu_custom_call" | custom-call | bytes 3145728 | tf_op jit(solution)/shard_map/pallas_call | solution.py:38
  2.7 5.1 %collective-permute-start = (bf16[4,192,128]{2,1,0:T(8,128)(2,1)S(1)}, bf16[4,192,128]{2,1,0:T(8,128)(2,1)S(1)}, u32[]{:S(2)}, u32[]{:S(2)}) collective-permute-start(bf16[4,192,128]{2,1,0:T(8,128)(2,1)S(1)} %get-tuple-element.44), channel_id=1, source_target_pairs={{0,3},{1,2},{2,1},{3,0},{4,7},{5,6},{6,5},{7,4},{8,11},{9,10},{10,... | collective-permute-start | bytes 589832 | tf_op jit(solution)/shard_map/ppermute | solution.py:299
  7.8 0.6 collective-permute-start.2
  8.5 1.4 %collective-permute-start.5 = (bf16[4,192,128]{2,1,0:T(8,128)(2,1)S(1)}, bf16[4,192,128]{2,1,0:T(8,128)(2,1)S(1)}, u32[]{:S(2)}, u32[]{:S(2)}) collective-permute-start(bf16[4,192,128]{2,1,0:T(8,128)(2,1)S(1)} %get-tuple-element.57), channel_id=1, source_target_pairs={{0,1},{1,0},{2,3},{3,2},{4,5},{5,4},{6,7},{7,6},{8,9},{9,8},{10,11... | collective-permute-start | bytes 589832 | tf_op jit(solution)/shard_map/ppermute | solution.py:299
  10.5 0.1 reshape.17
  10.6 0.1 reshape.16
  10.8 2.9 %collective-permute-done.refs_1_ = bf16[4,192,128]{2,1,0:T(8,128)(2,1)S(1)} collective-permute-done((bf16[4,192,128]{2,1,0:T(8,128)(2,1)S(1)}, bf16[4,192,128]{2,1,0:T(8,128)(2,1)S(1)}, u32[]{:S(2)}, u32[]{:S(2)}) %collective-permute-start) | collective-permute-done | bytes 196640 | tf_op jit(solution)/shard_map/ppermute | solution.py:299
  13.7 3.8 %collective-permute-start.3 = (bf16[4,192,128]{2,1,0:T(8,128)(2,1)S(1)}, bf16[4,192,128]{2,1,0:T(8,128)(2,1)S(1)}, u32[]{:S(2)}, u32[]{:S(2)}) collective-permute-start(bf16[4,192,128]{2,1,0:T(8,128)(2,1)S(1)} %get-tuple-element.55), channel_id=1, source_target_pairs={{0,3},{1,2},{2,1},{3,0},{4,7},{5,6},{6,5},{7,4},{8,11},{9,10},{10,... | collective-permute-start | bytes 589832 | tf_op jit(solution)/shard_map/ppermute | solution.py:299
  17.5 8.9 %collective-permute-done.1.refs_2_ = bf16[4,192,128]{2,1,0:T(8,128)(2,1)S(1)} collective-permute-done((bf16[4,192,128]{2,1,0:T(8,128)(2,1)S(1)}, bf16[4,192,128]{2,1,0:T(8,128)(2,1)S(1)}, u32[]{:S(2)}, u32[]{:S(2)}) %collective-permute-start.1) | collective-permute-done | bytes 196640 | tf_op jit(solution)/shard_map/ppermute | solution.py:299
  26.4 0.1 pad_add_fusion.scalars
  26.4 10.0 %shard_map.111 = (bf16[3,192,128]{2,1,0:T(8,128)(2,1)S(1)}, bf16[3,192,128]{2,1,0:T(8,128)(2,1)S(1)}, bf16[3,192,128]{2,1,0:T(8,128)(2,1)S(1)}, bf16[3,192,128]{2,1,0:T(8,128)(2,1)S(1)}, f32[2,32,96]{2,1,0:T(8,128)S(1)}) custom-call(s32[2]{0:T(128)S(1)} %pad_add_fusion.scalars, f32[2,31,96]{2,1,0:T(8,128)S(1)} %get-tuple-element.78.weight_ref, ...), custom_call_target="tpu_custom_call" | custom-call | flops 1207959552 | bytes 1376256 | tf_op jit(solution)/shard_map/pallas_call | solution.py:264
  36.4 2.7 %collective-permute-start.8 = (bf16[3,192,128]{2,1,0:T(8,128)(2,1)S(1)}, bf16[3,192,128]{2,1,0:T(8,128)(2,1)S(1)}, u32[]{:S(2)}, u32[]{:S(2)}) collective-permute-start(bf16[3,192,128]{2,1,0:T(8,128)(2,1)S(1)} %get-tuple-element.70), channel_id=1, source_target_pairs={{0,1},{1,0},{2,3},{3,2},{4,5},{5,4},{6,7},{7,6},{8,9},{9,8},{10,11... | collective-permute-start | bytes 442376 | tf_op jit(solution)/shard_map/ppermute | solution.py:299
  39.1 2.4 %collective-permute-done.4.refs_2_ = bf16[4,192,128]{2,1,0:T(8,128)(2,1)S(1)} collective-permute-done((bf16[4,192,128]{2,1,0:T(8,128)(2,1)S(1)}, bf16[4,192,128]{2,1,0:T(8,128)(2,1)S(1)}, u32[]{:S(2)}, u32[]{:S(2)}) %collective-permute-start.4) | collective-permute-done | bytes 196640 | tf_op jit(solution)/shard_map/ppermute | solution.py:299
  41.5 2.6 %collective-permute-start.6 = (bf16[3,192,128]{2,1,0:T(8,128)(2,1)S(1)}, bf16[3,192,128]{2,1,0:T(8,128)(2,1)S(1)}, u32[]{:S(2)}, u32[]{:S(2)}) collective-permute-start(bf16[3,192,128]{2,1,0:T(8,128)(2,1)S(1)} %get-tuple-element.64), channel_id=1, source_target_pairs={{0,3},{1,2},{2,1},{3,0},{4,7},{5,6},{6,5},{7,4},{8,11},{9,10},{10,... | collective-permute-start | bytes 442376 | tf_op jit(solution)/shard_map/ppermute | solution.py:299
  44.1 10.0 %shard_map.112 = (bf16[3,192,128]{2,1,0:T(8,128)(2,1)S(1)}, bf16[3,192,128]{2,1,0:T(8,128)(2,1)S(1)}, bf16[3,192,128]{2,1,0:T(8,128)(2,1)S(1)}, bf16[3,192,128]{2,1,0:T(8,128)(2,1)S(1)}, f32[2,32,96]{2,1,0:T(8,128)S(1)}) custom-call(s32[2]{0:T(128)S(1)} %pad_add_fusion.scalars, f32[2,31,96]{2,1,0:T(8,128)S(1)} %get-tuple-element.77.weight_ref, ...), custom_call_target="tpu_custom_call" | custom-call | flops 1207959552 | bytes 1376256 | tf_op jit(solution)/shard_map/pallas_call | solution.py:264
  54.1 3.0 %collective-permute-start.10 = (bf16[3,192,128]{2,1,0:T(8,128)(2,1)S(1)}, bf16[3,192,128]{2,1,0:T(8,128)(2,1)S(1)}, u32[]{:S(2)}, u32[]{:S(2)}) collective-permute-start(bf16[3,192,128]{2,1,0:T(8,128)(2,1)S(1)} %get-tuple-element.74), channel_id=1, source_target_pairs={{0,2},{1,3},{2,0},{3,1},{4,6},{5,7},{6,4},{7,5},{8,10},{9,11},{10,... | collective-permute-start | bytes 442376 | tf_op jit(solution)/shard_map/ppermute | solution.py:299
  57.1 0.1 collective-permute-start.12
  57.2 1.3 %collective-permute-start.9 = (bf16[3,192,128]{2,1,0:T(8,128)(2,1)S(1)}, bf16[3,192,128]{2,1,0:T(8,128)(2,1)S(1)}, u32[]{:S(2)}, u32[]{:S(2)}) collective-permute-start(bf16[3,192,128]{2,1,0:T(8,128)(2,1)S(1)} %get-tuple-element.73), channel_id=1, source_target_pairs={{0,3},{1,2},{2,1},{3,0},{4,7},{5,6},{6,5},{7,4},{8,11},{9,10},{10,... | collective-permute-start | bytes 442376 | tf_op jit(solution)/shard_map/ppermute | solution.py:299
  58.5 1.6 %collective-permute-start.13 = (f32[4,32,96]{2,1,0:T(8,128)S(1)}, f32[4,32,96]{2,1,0:T(8,128)S(1)}, u32[]{:S(2)}, u32[]{:S(2)}) collective-permute-start(f32[4,32,96]{2,1,0:T(8,128)S(1)} %add.11), channel_id=1, source_target_pairs={{0,8},{4,12},{8,0},{12,4},{16,24},{20,28},{24,16},{28,20},{1,9},{5... | collective-permute-start | bytes 147464 | tf_op jit(solution)/shard_map/ppermute | solution.py:309
  60.0 2.8 %collective-permute-done.13 = f32[4,32,96]{2,1,0:T(8,128)S(1)} collective-permute-done((f32[4,32,96]{2,1,0:T(8,128)S(1)}, f32[4,32,96]{2,1,0:T(8,128)S(1)}, u32[]{:S(2)}, u32[]{:S(2)}) %collective-permute-start.13) | collective-permute-done | bytes 49184 | tf_op jit(solution)/shard_map/ppermute | solution.py:309
  62.8 1.6 %collective-permute-start.14 = (f32[4,32,96]{2,1,0:T(8,128)S(1)}, f32[4,32,96]{2,1,0:T(8,128)S(1)}, u32[]{:S(2)}, u32[]{:S(2)}) collective-permute-start(f32[4,32,96]{2,1,0:T(8,128)S(1)} %add.12.refs_8_), channel_id=1, source_target_pairs={{0,16},{4,20},{8,24},{12,28},{16,0},{20,4},{24,8},{28,12},{1,17},{... | collective-permute-start | bytes 147464 | tf_op jit(solution)/shard_map/ppermute | solution.py:309
  64.4 2.6 %collective-permute-done.10.refs_6_ = bf16[3,192,128]{2,1,0:T(8,128)(2,1)S(1)} collective-permute-done((bf16[3,192,128]{2,1,0:T(8,128)(2,1)S(1)}, bf16[3,192,128]{2,1,0:T(8,128)(2,1)S(1)}, u32[]{:S(2)}, u32[]{:S(2)}) %collective-permute-start.10) | collective-permute-done | bytes 147488 | tf_op jit(solution)/shard_map/ppermute | solution.py:299
  67.0 1.7 %collective-permute-done.11.refs_7_ = bf16[3,192,128]{2,1,0:T(8,128)(2,1)S(1)} collective-permute-done((bf16[3,192,128]{2,1,0:T(8,128)(2,1)S(1)}, bf16[3,192,128]{2,1,0:T(8,128)(2,1)S(1)}, u32[]{:S(2)}, u32[]{:S(2)}) %collective-permute-start.11) | collective-permute-done | bytes 147488 | tf_op jit(solution)/shard_map/ppermute | solution.py:299
  68.7 1.4 %shard_map.113 = (bf16[1,128,1536]{2,1,0:T(8,128)(2,1)}, bf16[1,128,1536]{2,1,0:T(8,128)(2,1)}, bf16[1,128,1536]{2,1,0:T(8,128)(2,1)}, f32[31,384]{1,0:T(8,128)}, f32[384]{0:T(512)}) custom-call(s32[1]{0:T(128)} %bitcast.rank_ref, bf16[3,192,128]{2,1,0:T(8,128)(2,1)S(1)} %get-tuple-element.51.refs_0_, ...), custom_call_target="tpu_custom_call" | custom-call | bytes 2359296 | tf_op jit(solution)/shard_map/pallas_call | solution.py:82
  (24 shorter events, 0.1 us)
Async XLA Ops:
  0.6 10.0 %copy-start = (f32[31,1536]{1,0:T(8,128)S(1)}, f32[31,1536]{1,0:T(8,128)}, u32[]{:S(2)}) copy-start(f32[31,1536]{1,0:T(8,128)} %param.11) | copy-start | bytes 571396
  2.7 7.8 %copy-start.1 = (f32[1536]{0:T(1024)S(1)}, f32[1536]{0:T(1024)}, u32[]{:S(2)}) copy-start(f32[1536]{0:T(1024)} %param.12) | copy-start | bytes 18436
  2.7 11.0 %collective-permute-start = (bf16[4,192,128]{2,1,0:T(8,128)(2,1)S(1)}, bf16[4,192,128]{2,1,0:T(8,128)(2,1)S(1)}, u32[]{:S(2)}, u32[]{:S(2)}) collective-permute-start(bf16[4,192,128]{2,1,0:T(8,128)(2,1)S(1)} %get-tuple-element.44), channel_id=1, source_target_pairs={{0,3},{1,2},{2,1},{3,0},{4,7},{5,6},{6,5},{7,4},{8,11},{9,10},{10,... | collective-permute-start | bytes 589832 | tf_op jit(solution)/shard_map/ppermute | solution.py:299
  7.8 18.5 %collective-permute-start.1 = (bf16[4,192,128]{2,1,0:T(8,128)(2,1)S(1)}, bf16[4,192,128]{2,1,0:T(8,128)(2,1)S(1)}, u32[]{:S(2)}, u32[]{:S(2)}) collective-permute-start(bf16[4,192,128]{2,1,0:T(8,128)(2,1)S(1)} %get-tuple-element.46), channel_id=1, source_target_pairs={{0,2},{1,3},{2,0},{3,1},{4,6},{5,7},{6,4},{7,5},{8,10},{9,11},{10,... | collective-permute-start | bytes 589832 | tf_op jit(solution)/shard_map/ppermute | solution.py:299
  7.8 18.5 %collective-permute-start.2 = (bf16[4,192,128]{2,1,0:T(8,128)(2,1)S(1)}, bf16[4,192,128]{2,1,0:T(8,128)(2,1)S(1)}, u32[]{:S(2)}, u32[]{:S(2)}) collective-permute-start(bf16[4,192,128]{2,1,0:T(8,128)(2,1)S(1)} %get-tuple-element.47), channel_id=1, source_target_pairs={{0,1},{1,0},{2,3},{3,2},{4,5},{5,4},{6,7},{7,6},{8,9},{9,8},{10,11... | collective-permute-start | bytes 589832 | tf_op jit(solution)/shard_map/ppermute | solution.py:299
  8.5 30.7 %collective-permute-start.5 = (bf16[4,192,128]{2,1,0:T(8,128)(2,1)S(1)}, bf16[4,192,128]{2,1,0:T(8,128)(2,1)S(1)}, u32[]{:S(2)}, u32[]{:S(2)}) collective-permute-start(bf16[4,192,128]{2,1,0:T(8,128)(2,1)S(1)} %get-tuple-element.57), channel_id=1, source_target_pairs={{0,1},{1,0},{2,3},{3,2},{4,5},{5,4},{6,7},{7,6},{8,9},{9,8},{10,11... | collective-permute-start | bytes 589832 | tf_op jit(solution)/shard_map/ppermute | solution.py:299
  13.7 25.4 %collective-permute-start.3 = (bf16[4,192,128]{2,1,0:T(8,128)(2,1)S(1)}, bf16[4,192,128]{2,1,0:T(8,128)(2,1)S(1)}, u32[]{:S(2)}, u32[]{:S(2)}) collective-permute-start(bf16[4,192,128]{2,1,0:T(8,128)(2,1)S(1)} %get-tuple-element.55), channel_id=1, source_target_pairs={{0,3},{1,2},{2,1},{3,0},{4,7},{5,6},{6,5},{7,4},{8,11},{9,10},{10,... | collective-permute-start | bytes 589832 | tf_op jit(solution)/shard_map/ppermute | solution.py:299
  26.4 15.2 %collective-permute-start.4 = (bf16[4,192,128]{2,1,0:T(8,128)(2,1)S(1)}, bf16[4,192,128]{2,1,0:T(8,128)(2,1)S(1)}, u32[]{:S(2)}, u32[]{:S(2)}) collective-permute-start(bf16[4,192,128]{2,1,0:T(8,128)(2,1)S(1)} %get-tuple-element.56), channel_id=1, source_target_pairs={{0,2},{1,3},{2,0},{3,1},{4,6},{5,7},{6,4},{7,5},{8,10},{9,11},{10,... | collective-permute-start | bytes 589832 | tf_op jit(solution)/shard_map/ppermute | solution.py:299
  36.4 17.7 %collective-permute-start.8 = (bf16[3,192,128]{2,1,0:T(8,128)(2,1)S(1)}, bf16[3,192,128]{2,1,0:T(8,128)(2,1)S(1)}, u32[]{:S(2)}, u32[]{:S(2)}) collective-permute-start(bf16[3,192,128]{2,1,0:T(8,128)(2,1)S(1)} %get-tuple-element.70), channel_id=1, source_target_pairs={{0,1},{1,0},{2,3},{3,2},{4,5},{5,4},{6,7},{7,6},{8,9},{9,8},{10,11... | collective-permute-start | bytes 442376 | tf_op jit(solution)/shard_map/ppermute | solution.py:299
  41.5 15.6 %collective-permute-start.6 = (bf16[3,192,128]{2,1,0:T(8,128)(2,1)S(1)}, bf16[3,192,128]{2,1,0:T(8,128)(2,1)S(1)}, u32[]{:S(2)}, u32[]{:S(2)}) collective-permute-start(bf16[3,192,128]{2,1,0:T(8,128)(2,1)S(1)} %get-tuple-element.64), channel_id=1, source_target_pairs={{0,3},{1,2},{2,1},{3,0},{4,7},{5,6},{6,5},{7,4},{8,11},{9,10},{10,... | collective-permute-start | bytes 442376 | tf_op jit(solution)/shard_map/ppermute | solution.py:299
  44.1 14.3 %collective-permute-start.7 = (bf16[3,192,128]{2,1,0:T(8,128)(2,1)S(1)}, bf16[3,192,128]{2,1,0:T(8,128)(2,1)S(1)}, u32[]{:S(2)}, u32[]{:S(2)}) collective-permute-start(bf16[3,192,128]{2,1,0:T(8,128)(2,1)S(1)} %get-tuple-element.67), channel_id=1, source_target_pairs={{0,2},{1,3},{2,0},{3,1},{4,6},{5,7},{6,4},{7,5},{8,10},{9,11},{10,... | collective-permute-start | bytes 442376 | tf_op jit(solution)/shard_map/ppermute | solution.py:299
  54.1 12.9 %collective-permute-start.10 = (bf16[3,192,128]{2,1,0:T(8,128)(2,1)S(1)}, bf16[3,192,128]{2,1,0:T(8,128)(2,1)S(1)}, u32[]{:S(2)}, u32[]{:S(2)}) collective-permute-start(bf16[3,192,128]{2,1,0:T(8,128)(2,1)S(1)} %get-tuple-element.74), channel_id=1, source_target_pairs={{0,2},{1,3},{2,0},{3,1},{4,6},{5,7},{6,4},{7,5},{8,10},{9,11},{10,... | collective-permute-start | bytes 442376 | tf_op jit(solution)/shard_map/ppermute | solution.py:299
  57.1 1.3 %collective-permute-start.12 = (f32[4,32,96]{2,1,0:T(8,128)S(1)}, f32[4,32,96]{2,1,0:T(8,128)S(1)}, u32[]{:S(2)}, u32[]{:S(2)}) collective-permute-start(f32[4,32,96]{2,1,0:T(8,128)S(1)} %pad_maximum_fusion), channel_id=1, source_target_pairs={{0,4},{4,0},{8,12},{12,8},{16,20},{20,16},{24,28},{28,24},{1,5},{5... | collective-permute-start | bytes 147464 | tf_op jit(solution)/shard_map/ppermute | solution.py:309
  57.2 9.8 %collective-permute-start.9 = (bf16[3,192,128]{2,1,0:T(8,128)(2,1)S(1)}, bf16[3,192,128]{2,1,0:T(8,128)(2,1)S(1)}, u32[]{:S(2)}, u32[]{:S(2)}) collective-permute-start(bf16[3,192,128]{2,1,0:T(8,128)(2,1)S(1)} %get-tuple-element.73), channel_id=1, source_target_pairs={{0,3},{1,2},{2,1},{3,0},{4,7},{5,6},{6,5},{7,4},{8,11},{9,10},{10,... | collective-permute-start | bytes 442376 | tf_op jit(solution)/shard_map/ppermute | solution.py:299
  58.5 10.3 %collective-permute-start.11 = (bf16[3,192,128]{2,1,0:T(8,128)(2,1)S(1)}, bf16[3,192,128]{2,1,0:T(8,128)(2,1)S(1)}, u32[]{:S(2)}, u32[]{:S(2)}) collective-permute-start(bf16[3,192,128]{2,1,0:T(8,128)(2,1)S(1)} %get-tuple-element.75), channel_id=1, source_target_pairs={{0,1},{1,0},{2,3},{3,2},{4,5},{5,4},{6,7},{7,6},{8,9},{9,8},{10,11... | collective-permute-start | bytes 442376 | tf_op jit(solution)/shard_map/ppermute | solution.py:299
  58.5 4.3 %collective-permute-start.13 = (f32[4,32,96]{2,1,0:T(8,128)S(1)}, f32[4,32,96]{2,1,0:T(8,128)S(1)}, u32[]{:S(2)}, u32[]{:S(2)}) collective-permute-start(f32[4,32,96]{2,1,0:T(8,128)S(1)} %add.11), channel_id=1, source_target_pairs={{0,8},{4,12},{8,0},{12,4},{16,24},{20,28},{24,16},{28,20},{1,9},{5... | collective-permute-start | bytes 147464 | tf_op jit(solution)/shard_map/ppermute | solution.py:309
  62.8 5.9 %collective-permute-start.14 = (f32[4,32,96]{2,1,0:T(8,128)S(1)}, f32[4,32,96]{2,1,0:T(8,128)S(1)}, u32[]{:S(2)}, u32[]{:S(2)}) collective-permute-start(f32[4,32,96]{2,1,0:T(8,128)S(1)} %add.12.refs_8_), channel_id=1, source_target_pairs={{0,16},{4,20},{8,24},{12,28},{16,0},{20,4},{24,8},{28,12},{1,17},{... | collective-permute-start | bytes 147464 | tf_op jit(solution)/shard_map/ppermute | solution.py:309

commit v12 on v11

--- a/solution.py
+++ b/solution.py
@@ -18,35 +18,77 @@
 bf16, f32 = jnp.bfloat16, jnp.float32
 
 
-def pack_kernel(count, chunks, rank_ref, *refs):
+def pack_first_kernel(far, share, rank_ref, *refs):
+    arrays, outs, (plain, sems) = refs[:4], refs[4:-2], refs[-2:]
+    high = outs[0].shape[1]
+    wide = plain.shape[3]
+    copies = []
+    for place, distance in enumerate(far):
+        at = pl.ds(pl.multiple_of((rank_ref[0] ^ distance) * share, 128), wide)
+        for which, array in enumerate(arrays):
+            copies.append(
+                pltpu.make_async_copy(
+                    array.at[0, :, at], plain.at[place, which], sems.at[place, which]
+                )
+            )
+            copies[-1].start()
+    for index, copy in enumerate(copies):
+        copy.wait()
+        place, which = divmod(index, 4)
+        outs[place][which] = plain[place, which].T[:high]
+
+
+def pack_kernel(wanted, share, rank_ref, *refs):
     arrays, outs, turned = refs[:4], refs[4:-1], refs[-1]
-    rank = rank_ref[0]
     high = outs[0].shape[1]
-    share = high * chunks
     for which, array in enumerate(arrays):
         turned[which] = array[0].T
-        for distance in range(count):
-            for chunk in range(chunks):
-                first = pl.multiple_of((rank ^ distance) * share + chunk * high, 16)
-                outs[chunk * count + distance][which] = turned[which, pl.ds(first, high), :]
+        for (chunk, distance), out in zip(wanted, outs):
+            first = pl.multiple_of((rank_ref[0] ^ distance) * share + chunk * high, 16)
+            out[which] = turned[which, pl.ds(first, high), :]
 
 
 def pack(rank, arrays, count, chunks):
     _, frames, width = arrays[0].shape
-    high = width // count // chunks
+    share = width // count
+    high = share // chunks
     piece = jax.ShapeDtypeStruct((4, high, frames), bf16)
+    wide = -(-high // 128) * 128
+    far = tuple(range(count - 1, 1, -1)) if share % 128 == 0 and wide <= share else ()
+    params = pltpu.CompilerParams(vmem_limit_bytes=LIMIT)
+    arrays = [pltpu.with_memory_space_constraint(array, pltpu.HBM) for array in arrays]
+    found = {}
+    if far:
+        outs = pl.pallas_call(
+            functools.partial(pack_first_kernel, far, share),
+            out_shape=(piece,) * len(far),
+            in_specs=[SMEM] + [pl.BlockSpec(memory_space=pltpu.HBM)] * 4,
+            out_specs=(VMEM,) * len(far),
+            scratch_shapes=[
+                pltpu.VMEM((len(far), 4, frames, wide), bf16),
+                pltpu.SemaphoreType.DMA((len(far), 4)),
+            ],
+            compiler_params=params,
+            cost_estimate=pl.CostEstimate(
+                flops=0, bytes_accessed=16 * frames * wide * len(far), transcendentals=0
+            ),
+        )(rank, *arrays)
+        found.update(zip([(0, distance) for distance in far], outs))
+    every = [(chunk, distance) for chunk in range(chunks) for distance in range(count)]
+    wanted = tuple(key for key in every if key not in found)
     outs = pl.pallas_call(
-        functools.partial(pack_kernel, count, chunks),
-        out_shape=(piece,) * (count * chunks),
+        functools.partial(pack_kernel, wanted, share),
+        out_shape=(piece,) * len(wanted),
         in_specs=[SMEM] + [VMEM] * 4,
-        out_specs=(VMEM,) * (count * chunks),
+        out_specs=(VMEM,) * len(wanted),
         scratch_shapes=[pltpu.VMEM((4, width, frames), bf16)],
-        compiler_params=pltpu.CompilerParams(vmem_limit_bytes=LIMIT),
+        compiler_params=params,
         cost_estimate=pl.CostEstimate(
             flops=0, bytes_accessed=16 * frames * width, transcendentals=0
         ),
-    )(rank, *[pltpu.with_memory_space_constraint(array, pltpu.HBM) for array in arrays])
-    return [outs[chunk * count : (chunk + 1) * count] for chunk in range(chunks)]
+    )(rank, *arrays)
+    found.update(zip(wanted, outs))
+    return [[found[chunk, distance] for distance in range(count)] for chunk in range(chunks)]
 
 
 def taken(count):
@@ -338,10 +380,8 @@
     last = count - 1
     grads[last - 1], before[1] = lax.optimization_barrier((grads[last - 1], before[1]))
     if last > 2:
-        (grads[last], taps), before[last] = lax.optimization_barrier(
-            ((grads[last], taps), before[last])
-        )
-        grads[1], before[last - 1] = lax.optimization_barrier((grads[1], before[last - 1]))
+        (grads[1], taps), before[last] = lax.optimization_barrier(((grads[1], taps), before[last]))
+        grads[last], before[last - 1] = lax.optimization_barrier((grads[last], before[last - 1]))
     order.append(exchanged(grads, None))
     return unpack(rank[None], doubled(taps, "dp"), order[chunks:], count, chunks)
 

time: 70.2 us -> 73.4 us (1.046)
  waiting for transfers between devices: 21.2 us -> 23.2 us
  Pallas kernels: 23.3 us -> 24.9 us
    ppermute x12, waiting for transfers between devices: 18.4 us -> 20.4 us  [exchanged(): moved[distance] = lax.ppermute(pieces[distance], 'seq', pairs)]
    pallas_call x1 -> x2, Pallas kernels: 2.03 us -> 3.45 us  [the longest x1 1.96 us: pack(): pl.pallas_call(functools.partial(pack_kernel, wanted, share), out_shape=(...]
  transfers between devices with their start and end apart: 15 -> 15, of which waited for: 6 -> 4; matrix products, arithmetic and copies ran while one was open for 0% -> 0% of each run, Pallas kernels for 28% -> 30%
where the time goes in v12:
time: 73.4 us; the launch traced here: 73.2 us
  Pallas kernels  24.9 us (34%)
  starting transfers between devices  23.2 us (32%)
  waiting for transfers between devices  23.2 us (32%)
  between operations  1.47 us (2%)
    ppermute x12, waiting for transfers between devices, exchanged(): moved[distance] = lax.ppermute(pieces[distance], 'seq', pairs)  20.4 us
    pallas_call x2, Pallas kernels, core(): pl.pallas_call(functools.partial(core_kernel, count, block), out_shape=(p...  20.1 us
    ppermute x12, starting transfers between devices, exchanged(): moved[distance] = lax.ppermute(pieces[distance], 'seq', pairs)  20 us
    ppermute x3, starting transfers between devices, doubled(): pair = (total, lax.ppermute(total, axis, pairs))  3.21 us
    ppermute x3, waiting for transfers between devices, doubled(): pair = (total, lax.ppermute(total, axis, pairs))  2.77 us
    pallas_call x1, Pallas kernels, pack(): pl.pallas_call(functools.partial(pack_kernel, wanted, share), out_shape=(...  1.96 us
    pallas_call x1, Pallas kernels, pack(): pl.pallas_call(functools.partial(pack_first_kernel, far, share), out_shap...  1.49 us
  transfers between devices with their start and end apart: 15, of which 4 were waited for; matrix products, arithmetic and copies ran while one was open for 0% of the time, Pallas kernels for 30%

profile of v12, /device:TPU:0, one launch (start us, length us, event | category | flops | bytes accessed | tf_op | source)
XLA Modules:
  0.0 73.2 jit_solution(2540060417345653357)
XLA Ops:
  0.6 1.5 %shard_map.111 = (bf16[4,192,128]{2,1,0:T(8,128)(2,1)S(1)}, bf16[4,192,128]{2,1,0:T(8,128)(2,1)S(1)}) custom-call(s32[1]{0:T(128)} %bitcast.rank_ref, bf16[1,128,1536]{2,1,0:T(8,128)(2,1)} %refs_0_.3, bf16[1,128,1536]{2,1,0:T(8,128)(2,1)} %refs_1_.3, bf16[1,128,1536]{2,1,0:T(8,128)(2,1)} %refs_2_.3, bf16[1,128,1536]{2,1,0:T(8,128)(2,1)} %refs_3_.3), custom_call_target="tpu_custom_call" | custom-call | bytes 1048576 | tf_op jit(solution)/shard_map/pallas_call | solution.py:62
  2.1 5.1 %collective-permute-start = (bf16[4,192,128]{2,1,0:T(8,128)(2,1)S(1)}, bf16[4,192,128]{2,1,0:T(8,128)(2,1)S(1)}, u32[]{:S(2)}, u32[]{:S(2)}) collective-permute-start(bf16[4,192,128]{2,1,0:T(8,128)(2,1)S(1)} %get-tuple-element.44), channel_id=1, source_target_pairs={{0,3},{1,2},{2,1},{3,0},{4,7},{5,6},{6,5},{7,4},{8,11},{9,10},{10,... | collective-permute-start | bytes 589832 | tf_op jit(solution)/shard_map/ppermute | solution.py:341
  7.2 2.0 %shard_map.110 = (bf16[4,192,128]{2,1,0:T(8,128)(2,1)S(1)}, bf16[4,192,128]{2,1,0:T(8,128)(2,1)S(1)}, bf16[4,192,128]{2,1,0:T(8,128)(2,1)S(1)}, bf16[4,192,128]{...) custom-call(s32[1]{0:T(128)} %bitcast.rank_ref, ...), custom_call_target="tpu_custom_call" | custom-call | bytes 3145728 | tf_op jit(solution)/shard_map/pallas_call | solution.py:79
  9.2 0.7 collective-permute-start.2
  9.9 1.4 %collective-permute-start.5 = (bf16[4,192,128]{2,1,0:T(8,128)(2,1)S(1)}, bf16[4,192,128]{2,1,0:T(8,128)(2,1)S(1)}, u32[]{:S(2)}, u32[]{:S(2)}) collective-permute-start(bf16[4,192,128]{2,1,0:T(8,128)(2,1)S(1)} %get-tuple-element.57), channel_id=1, source_target_pairs={{0,1},{1,0},{2,3},{3,2},{4,5},{5,4},{6,7},{7,6},{8,9},{9,8},{10,11... | collective-permute-start | bytes 589832 | tf_op jit(solution)/shard_map/ppermute | solution.py:341
  12.0 0.1 reshape.17
  12.1 0.1 reshape.16
  12.3 0.8 %collective-permute-done.refs_1_ = bf16[4,192,128]{2,1,0:T(8,128)(2,1)S(1)} collective-permute-done((bf16[4,192,128]{2,1,0:T(8,128)(2,1)S(1)}, bf16[4,192,128]{2,1,0:T(8,128)(2,1)S(1)}, u32[]{:S(2)}, u32[]{:S(2)}) %collective-permute-start) | collective-permute-done | bytes 196640 | tf_op jit(solution)/shard_map/ppermute | solution.py:341
  13.1 3.8 %collective-permute-start.3 = (bf16[4,192,128]{2,1,0:T(8,128)(2,1)S(1)}, bf16[4,192,128]{2,1,0:T(8,128)(2,1)S(1)}, u32[]{:S(2)}, u32[]{:S(2)}) collective-permute-start(bf16[4,192,128]{2,1,0:T(8,128)(2,1)S(1)} %get-tuple-element.55), channel_id=1, source_target_pairs={{0,3},{1,2},{2,1},{3,0},{4,7},{5,6},{6,5},{7,4},{8,11},{9,10},{10,... | collective-permute-start | bytes 589832 | tf_op jit(solution)/shard_map/ppermute | solution.py:341
  16.9 16.5 %collective-permute-done.1.refs_2_ = bf16[4,192,128]{2,1,0:T(8,128)(2,1)S(1)} collective-permute-done((bf16[4,192,128]{2,1,0:T(8,128)(2,1)S(1)}, bf16[4,192,128]{2,1,0:T(8,128)(2,1)S(1)}, u32[]{:S(2)}, u32[]{:S(2)}) %collective-permute-start.1) | collective-permute-done | bytes 196640 | tf_op jit(solution)/shard_map/ppermute | solution.py:341
  33.4 0.1 pad_add_fusion.scalars
  33.4 10.1 %shard_map.112 = (bf16[3,192,128]{2,1,0:T(8,128)(2,1)S(1)}, bf16[3,192,128]{2,1,0:T(8,128)(2,1)S(1)}, bf16[3,192,128]{2,1,0:T(8,128)(2,1)S(1)}, bf16[3,192,128]{2,1,0:T(8,128)(2,1)S(1)}, f32[2,32,96]{2,1,0:T(8,128)S(1)}) custom-call(s32[2]{0:T(128)S(1)} %pad_add_fusion.scalars, f32[2,31,96]{2,1,0:T(8,128)S(1)} %get-tuple-element.78.weight_ref, ...), custom_call_target="tpu_custom_call" | custom-call | flops 1207959552 | bytes 1376256 | tf_op jit(solution)/shard_map/pallas_call | solution.py:306
  43.6 0.1 collective-permute-start.8
  43.7 4.4 %collective-permute-start.6 = (bf16[3,192,128]{2,1,0:T(8,128)(2,1)S(1)}, bf16[3,192,128]{2,1,0:T(8,128)(2,1)S(1)}, u32[]{:S(2)}, u32[]{:S(2)}) collective-permute-start(bf16[3,192,128]{2,1,0:T(8,128)(2,1)S(1)} %get-tuple-element.64), channel_id=1, source_target_pairs={{0,3},{1,2},{2,1},{3,0},{4,7},{5,6},{6,5},{7,4},{8,11},{9,10},{10,... | collective-permute-start | bytes 442376 | tf_op jit(solution)/shard_map/ppermute | solution.py:341
  48.1 9.9 %shard_map.113 = (bf16[3,192,128]{2,1,0:T(8,128)(2,1)S(1)}, bf16[3,192,128]{2,1,0:T(8,128)(2,1)S(1)}, bf16[3,192,128]{2,1,0:T(8,128)(2,1)S(1)}, bf16[3,192,128]{2,1,0:T(8,128)(2,1)S(1)}, f32[2,32,96]{2,1,0:T(8,128)S(1)}) custom-call(s32[2]{0:T(128)S(1)} %pad_add_fusion.scalars, f32[2,31,96]{2,1,0:T(8,128)S(1)} %get-tuple-element.77.weight_ref, ...), custom_call_target="tpu_custom_call" | custom-call | flops 1207959552 | bytes 1376256 | tf_op jit(solution)/shard_map/pallas_call | solution.py:306
  58.1 3.0 %collective-permute-start.10 = (bf16[3,192,128]{2,1,0:T(8,128)(2,1)S(1)}, bf16[3,192,128]{2,1,0:T(8,128)(2,1)S(1)}, u32[]{:S(2)}, u32[]{:S(2)}) collective-permute-start(bf16[3,192,128]{2,1,0:T(8,128)(2,1)S(1)} %get-tuple-element.74), channel_id=1, source_target_pairs={{0,2},{1,3},{2,0},{3,1},{4,6},{5,7},{6,4},{7,5},{8,10},{9,11},{10,... | collective-permute-start | bytes 442376 | tf_op jit(solution)/shard_map/ppermute | solution.py:341
  61.1 0.1 collective-permute-start.12
  61.2 0.1 collective-permute-start.11
  61.3 1.5 %collective-permute-start.9 = (bf16[3,192,128]{2,1,0:T(8,128)(2,1)S(1)}, bf16[3,192,128]{2,1,0:T(8,128)(2,1)S(1)}, u32[]{:S(2)}, u32[]{:S(2)}) collective-permute-start(bf16[3,192,128]{2,1,0:T(8,128)(2,1)S(1)} %get-tuple-element.73), channel_id=1, source_target_pairs={{0,3},{1,2},{2,1},{3,0},{4,7},{5,6},{6,5},{7,4},{8,11},{9,10},{10,... | collective-permute-start | bytes 442376 | tf_op jit(solution)/shard_map/ppermute | solution.py:341
  62.7 1.6 %collective-permute-start.13 = (f32[4,32,96]{2,1,0:T(8,128)S(1)}, f32[4,32,96]{2,1,0:T(8,128)S(1)}, u32[]{:S(2)}, u32[]{:S(2)}) collective-permute-start(f32[4,32,96]{2,1,0:T(8,128)S(1)} %add.11), channel_id=1, source_target_pairs={{0,8},{4,12},{8,0},{12,4},{16,24},{20,28},{24,16},{28,20},{1,9},{5... | collective-permute-start | bytes 147464 | tf_op jit(solution)/shard_map/ppermute | solution.py:351
  64.3 2.8 %collective-permute-done.13 = f32[4,32,96]{2,1,0:T(8,128)S(1)} collective-permute-done((f32[4,32,96]{2,1,0:T(8,128)S(1)}, f32[4,32,96]{2,1,0:T(8,128)S(1)}, u32[]{:S(2)}, u32[]{:S(2)}) %collective-permute-start.13) | collective-permute-done | bytes 49184 | tf_op jit(solution)/shard_map/ppermute | solution.py:351
  67.1 1.6 %collective-permute-start.14 = (f32[4,32,96]{2,1,0:T(8,128)S(1)}, f32[4,32,96]{2,1,0:T(8,128)S(1)}, u32[]{:S(2)}, u32[]{:S(2)}) collective-permute-start(f32[4,32,96]{2,1,0:T(8,128)S(1)} %add.12.refs_8_), channel_id=1, source_target_pairs={{0,16},{4,20},{8,24},{12,28},{16,0},{20,4},{24,8},{28,12},{1,17},{... | collective-permute-start | bytes 147464 | tf_op jit(solution)/shard_map/ppermute | solution.py:351
  68.7 3.1 %collective-permute-done.11.refs_7_ = bf16[3,192,128]{2,1,0:T(8,128)(2,1)S(1)} collective-permute-done((bf16[3,192,128]{2,1,0:T(8,128)(2,1)S(1)}, bf16[3,192,128]{2,1,0:T(8,128)(2,1)S(1)}, u32[]{:S(2)}, u32[]{:S(2)}) %collective-permute-start.11) | collective-permute-done | bytes 147488 | tf_op jit(solution)/shard_map/ppermute | solution.py:341
  71.8 1.4 %shard_map.114 = (bf16[1,128,1536]{2,1,0:T(8,128)(2,1)}, bf16[1,128,1536]{2,1,0:T(8,128)(2,1)}, bf16[1,128,1536]{2,1,0:T(8,128)(2,1)}, f32[31,384]{1,0:T(8,128)}, f32[384]{0:T(512)}) custom-call(s32[1]{0:T(128)} %bitcast.rank_ref, bf16[3,192,128]{2,1,0:T(8,128)(2,1)S(1)} %get-tuple-element.51.refs_0_, ...), custom_call_target="tpu_custom_call" | custom-call | bytes 2359296 | tf_op jit(solution)/shard_map/pallas_call | solution.py:124
  (25 shorter events, 0.1 us)
Async XLA Ops:
  2.1 10.9 %collective-permute-start = (bf16[4,192,128]{2,1,0:T(8,128)(2,1)S(1)}, bf16[4,192,128]{2,1,0:T(8,128)(2,1)S(1)}, u32[]{:S(2)}, u32[]{:S(2)}) collective-permute-start(bf16[4,192,128]{2,1,0:T(8,128)(2,1)S(1)} %get-tuple-element.44), channel_id=1, source_target_pairs={{0,3},{1,2},{2,1},{3,0},{4,7},{5,6},{6,5},{7,4},{8,11},{9,10},{10,... | collective-permute-start | bytes 589832 | tf_op jit(solution)/shard_map/ppermute | solution.py:341
  7.2 4.8 %copy-start = (f32[31,1536]{1,0:T(8,128)S(1)}, f32[31,1536]{1,0:T(8,128)}, u32[]{:S(2)}) copy-start(f32[31,1536]{1,0:T(8,128)} %param.11) | copy-start | bytes 571396
  7.2 26.1 %collective-permute-start.1 = (bf16[4,192,128]{2,1,0:T(8,128)(2,1)S(1)}, bf16[4,192,128]{2,1,0:T(8,128)(2,1)S(1)}, u32[]{:S(2)}, u32[]{:S(2)}) collective-permute-start(bf16[4,192,128]{2,1,0:T(8,128)(2,1)S(1)} %get-tuple-element.46), channel_id=1, source_target_pairs={{0,2},{1,3},{2,0},{3,1},{4,6},{5,7},{6,4},{7,5},{8,10},{9,11},{10,... | collective-permute-start | bytes 589832 | tf_op jit(solution)/shard_map/ppermute | solution.py:341
  9.2 2.8 %copy-start.1 = (f32[1536]{0:T(1024)S(1)}, f32[1536]{0:T(1024)}, u32[]{:S(2)}) copy-start(f32[1536]{0:T(1024)} %param.12) | copy-start | bytes 18436
  9.2 24.1 %collective-permute-start.2 = (bf16[4,192,128]{2,1,0:T(8,128)(2,1)S(1)}, bf16[4,192,128]{2,1,0:T(8,128)(2,1)S(1)}, u32[]{:S(2)}, u32[]{:S(2)}) collective-permute-start(bf16[4,192,128]{2,1,0:T(8,128)(2,1)S(1)} %get-tuple-element.47), channel_id=1, source_target_pairs={{0,1},{1,0},{2,3},{3,2},{4,5},{5,4},{6,7},{7,6},{8,9},{9,8},{10,11... | collective-permute-start | bytes 589832 | tf_op jit(solution)/shard_map/ppermute | solution.py:341
  9.9 33.8 %collective-permute-start.5 = (bf16[4,192,128]{2,1,0:T(8,128)(2,1)S(1)}, bf16[4,192,128]{2,1,0:T(8,128)(2,1)S(1)}, u32[]{:S(2)}, u32[]{:S(2)}) collective-permute-start(bf16[4,192,128]{2,1,0:T(8,128)(2,1)S(1)} %get-tuple-element.57), channel_id=1, source_target_pairs={{0,1},{1,0},{2,3},{3,2},{4,5},{5,4},{6,7},{7,6},{8,9},{9,8},{10,11... | collective-permute-start | bytes 589832 | tf_op jit(solution)/shard_map/ppermute | solution.py:341
  13.1 30.6 %collective-permute-start.3 = (bf16[4,192,128]{2,1,0:T(8,128)(2,1)S(1)}, bf16[4,192,128]{2,1,0:T(8,128)(2,1)S(1)}, u32[]{:S(2)}, u32[]{:S(2)}) collective-permute-start(bf16[4,192,128]{2,1,0:T(8,128)(2,1)S(1)} %get-tuple-element.55), channel_id=1, source_target_pairs={{0,3},{1,2},{2,1},{3,0},{4,7},{5,6},{6,5},{7,4},{8,11},{9,10},{10,... | collective-permute-start | bytes 589832 | tf_op jit(solution)/shard_map/ppermute | solution.py:341
  33.4 10.3 %collective-permute-start.4 = (bf16[4,192,128]{2,1,0:T(8,128)(2,1)S(1)}, bf16[4,192,128]{2,1,0:T(8,128)(2,1)S(1)}, u32[]{:S(2)}, u32[]{:S(2)}) collective-permute-start(bf16[4,192,128]{2,1,0:T(8,128)(2,1)S(1)} %get-tuple-element.56), channel_id=1, source_target_pairs={{0,2},{1,3},{2,0},{3,1},{4,6},{5,7},{6,4},{7,5},{8,10},{9,11},{10,... | collective-permute-start | bytes 589832 | tf_op jit(solution)/shard_map/ppermute | solution.py:341
  43.6 14.5 %collective-permute-start.8 = (bf16[3,192,128]{2,1,0:T(8,128)(2,1)S(1)}, bf16[3,192,128]{2,1,0:T(8,128)(2,1)S(1)}, u32[]{:S(2)}, u32[]{:S(2)}) collective-permute-start(bf16[3,192,128]{2,1,0:T(8,128)(2,1)S(1)} %get-tuple-element.70), channel_id=1, source_target_pairs={{0,1},{1,0},{2,3},{3,2},{4,5},{5,4},{6,7},{7,6},{8,9},{9,8},{10,11... | collective-permute-start | bytes 442376 | tf_op jit(solution)/shard_map/ppermute | solution.py:341
  43.7 17.4 %collective-permute-start.6 = (bf16[3,192,128]{2,1,0:T(8,128)(2,1)S(1)}, bf16[3,192,128]{2,1,0:T(8,128)(2,1)S(1)}, u32[]{:S(2)}, u32[]{:S(2)}) collective-permute-start(bf16[3,192,128]{2,1,0:T(8,128)(2,1)S(1)} %get-tuple-element.64), channel_id=1, source_target_pairs={{0,3},{1,2},{2,1},{3,0},{4,7},{5,6},{6,5},{7,4},{8,11},{9,10},{10,... | collective-permute-start | bytes 442376 | tf_op jit(solution)/shard_map/ppermute | solution.py:341
  48.1 13.1 %collective-permute-start.7 = (bf16[3,192,128]{2,1,0:T(8,128)(2,1)S(1)}, bf16[3,192,128]{2,1,0:T(8,128)(2,1)S(1)}, u32[]{:S(2)}, u32[]{:S(2)}) collective-permute-start(bf16[3,192,128]{2,1,0:T(8,128)(2,1)S(1)} %get-tuple-element.67), channel_id=1, source_target_pairs={{0,2},{1,3},{2,0},{3,1},{4,6},{5,7},{6,4},{7,5},{8,10},{9,11},{10,... | collective-permute-start | bytes 442376 | tf_op jit(solution)/shard_map/ppermute | solution.py:341
  58.1 10.6 %collective-permute-start.10 = (bf16[3,192,128]{2,1,0:T(8,128)(2,1)S(1)}, bf16[3,192,128]{2,1,0:T(8,128)(2,1)S(1)}, u32[]{:S(2)}, u32[]{:S(2)}) collective-permute-start(bf16[3,192,128]{2,1,0:T(8,128)(2,1)S(1)} %get-tuple-element.74), channel_id=1, source_target_pairs={{0,2},{1,3},{2,0},{3,1},{4,6},{5,7},{6,4},{7,5},{8,10},{9,11},{10,... | collective-permute-start | bytes 442376 | tf_op jit(solution)/shard_map/ppermute | solution.py:341
  61.1 1.6 %collective-permute-start.12 = (f32[4,32,96]{2,1,0:T(8,128)S(1)}, f32[4,32,96]{2,1,0:T(8,128)S(1)}, u32[]{:S(2)}, u32[]{:S(2)}) collective-permute-start(f32[4,32,96]{2,1,0:T(8,128)S(1)} %pad_maximum_fusion), channel_id=1, source_target_pairs={{0,4},{4,0},{8,12},{12,8},{16,20},{20,16},{24,28},{28,24},{1,5},{5... | collective-permute-start | bytes 147464 | tf_op jit(solution)/shard_map/ppermute | solution.py:351
  61.2 10.6 %collective-permute-start.11 = (bf16[3,192,128]{2,1,0:T(8,128)(2,1)S(1)}, bf16[3,192,128]{2,1,0:T(8,128)(2,1)S(1)}, u32[]{:S(2)}, u32[]{:S(2)}) collective-permute-start(bf16[3,192,128]{2,1,0:T(8,128)(2,1)S(1)} %get-tuple-element.75), channel_id=1, source_target_pairs={{0,1},{1,0},{2,3},{3,2},{4,5},{5,4},{6,7},{7,6},{8,9},{9,8},{10,11... | collective-permute-start | bytes 442376 | tf_op jit(solution)/shard_map/ppermute | solution.py:341
  61.3 10.5 %collective-permute-start.9 = (bf16[3,192,128]{2,1,0:T(8,128)(2,1)S(1)}, bf16[3,192,128]{2,1,0:T(8,128)(2,1)S(1)}, u32[]{:S(2)}, u32[]{:S(2)}) collective-permute-start(bf16[3,192,128]{2,1,0:T(8,128)(2,1)S(1)} %get-tuple-element.73), channel_id=1, source_target_pairs={{0,3},{1,2},{2,1},{3,0},{4,7},{5,6},{6,5},{7,4},{8,11},{9,10},{10,... | collective-permute-start | bytes 442376 | tf_op jit(solution)/shard_map/ppermute | solution.py:341
  62.7 4.3 %collective-permute-start.13 = (f32[4,32,96]{2,1,0:T(8,128)S(1)}, f32[4,32,96]{2,1,0:T(8,128)S(1)}, u32[]{:S(2)}, u32[]{:S(2)}) collective-permute-start(f32[4,32,96]{2,1,0:T(8,128)S(1)} %add.11), channel_id=1, source_target_pairs={{0,8},{4,12},{8,0},{12,4},{16,24},{20,28},{24,16},{28,20},{1,9},{5... | collective-permute-start | bytes 147464 | tf_op jit(solution)/shard_map/ppermute | solution.py:351
  67.1 4.7 %collective-permute-start.14 = (f32[4,32,96]{2,1,0:T(8,128)S(1)}, f32[4,32,96]{2,1,0:T(8,128)S(1)}, u32[]{:S(2)}, u32[]{:S(2)}) collective-permute-start(f32[4,32,96]{2,1,0:T(8,128)S(1)} %add.12.refs_8_), channel_id=1, source_target_pairs={{0,16},{4,20},{8,24},{12,28},{16,0},{20,4},{24,8},{28,12},{1,17},{... | collective-permute-start | bytes 147464 | tf_op jit(solution)/shard_map/ppermute | solution.py:351

commit v13 on v12

--- a/solution.py
+++ b/solution.py
@@ -327,14 +327,10 @@
     return outs[:count], outs[count]
 
 
-def exchanged(pieces, before, eager=False):
+def exchanged(pieces, before):
     pieces = list(pieces)
-    last = len(pieces) - 1
-    if before is not None and eager:
-        pieces[last], before[last] = lax.optimization_barrier((pieces[last], before[last]))
-    if before is not None and last > 1:
-        wait = slice(last - 1 if eager else last, 1, -1)
-        pieces[wait], before[:0:-1] = lax.optimization_barrier((pieces[wait], before[:0:-1]))
+    if before is not None and len(pieces) > 2:
+        pieces[:1:-1], before[:0:-1] = lax.optimization_barrier((pieces[:1:-1], before[:0:-1]))
     moved = pieces[:1] * len(pieces)
     for distance in range(len(pieces) - 1, 0, -1):
         pairs = [(i, i ^ distance) for i in range(len(pieces))]
@@ -368,7 +364,7 @@
     sent = pack(rank[None], (queries, keys, values, grad_out), count, chunks)
     order = []
     for pieces in sent:
-        order.append(exchanged(pieces, order[-1] if order else None, True))
+        order.append(exchanged(pieces, order[-1] if order else None))
     taps = []
     for chunk in range(chunks):
         at = slice(chunk * step, (chunk + 1) * step)

time: 73.4 us -> 69.5 us (0.947)
  waiting for transfers between devices: 23.2 us -> 20.7 us
  starting transfers between devices: 23.2 us -> 21.8 us
    ppermute x12, waiting for transfers between devices: 20.4 us -> 18 us  [exchanged(): moved[distance] = lax.ppermute(pieces[distance], 'seq', pairs)]
    ppermute x12, starting transfers between devices: 20 us -> 18.6 us  [exchanged(): moved[distance] = lax.ppermute(pieces[distance], 'seq', pairs)]
  transfers between devices with their start and end apart: 15 -> 15, of which waited for: 4 -> 6; matrix products, arithmetic and copies ran while one was open for 0% -> 1% of each run, Pallas kernels for 30% -> 32%
where the time goes in v13:
time: 69.5 us; the launch traced here: 69.3 us
  Pallas kernels  24.9 us (36%)
  starting transfers between devices  21.8 us (31%)
  waiting for transfers between devices  20.7 us (30%)
  between operations  1.45 us (2%)
    pallas_call x2, Pallas kernels, core(): pl.pallas_call(functools.partial(core_kernel, count, block), out_shape=(p...  20.1 us
    ppermute x12, starting transfers between devices, exchanged(): moved[distance] = lax.ppermute(pieces[distance], 'seq', pairs)  18.6 us
    ppermute x12, waiting for transfers between devices, exchanged(): moved[distance] = lax.ppermute(pieces[distance], 'seq', pairs)  18 us
    ppermute x3, starting transfers between devices, doubled(): pair = (total, lax.ppermute(total, axis, pairs))  3.21 us
    ppermute x3, waiting for transfers between devices, doubled(): pair = (total, lax.ppermute(total, axis, pairs))  2.78 us
    pallas_call x1, Pallas kernels, pack(): pl.pallas_call(functools.partial(pack_kernel, wanted, share), out_shape=(...  1.96 us
    pallas_call x1, Pallas kernels, pack(): pl.pallas_call(functools.partial(pack_first_kernel, far, share), out_shap...  1.49 us
  transfers between devices with their start and end apart: 15, of which 6 were waited for; matrix products, arithmetic and copies ran while one was open for 1% of the time, Pallas kernels for 32%

profile of v13, /device:TPU:0, one launch (start us, length us, event | category | flops | bytes accessed | tf_op | source)
XLA Modules:
  0.0 69.3 jit_solution(5254965567060034574)
XLA Ops:
  0.6 1.5 %shard_map.111 = (bf16[4,192,128]{2,1,0:T(8,128)(2,1)S(1)}, bf16[4,192,128]{2,1,0:T(8,128)(2,1)S(1)}) custom-call(s32[1]{0:T(128)} %bitcast.rank_ref, bf16[1,128,1536]{2,1,0:T(8,128)(2,1)} %refs_0_.3, bf16[1,128,1536]{2,1,0:T(8,128)(2,1)} %refs_1_.3, bf16[1,128,1536]{2,1,0:T(8,128)(2,1)} %refs_2_.3, bf16[1,128,1536]{2,1,0:T(8,128)(2,1)} %refs_3_.3), custom_call_target="tpu_custom_call" | custom-call | bytes 1048576 | tf_op jit(solution)/shard_map/pallas_call | solution.py:62
  2.1 5.1 %collective-permute-start = (bf16[4,192,128]{2,1,0:T(8,128)(2,1)S(1)}, bf16[4,192,128]{2,1,0:T(8,128)(2,1)S(1)}, u32[]{:S(2)}, u32[]{:S(2)}) collective-permute-start(bf16[4,192,128]{2,1,0:T(8,128)(2,1)S(1)} %get-tuple-element.43), channel_id=1, source_target_pairs={{0,3},{1,2},{2,1},{3,0},{4,7},{5,6},{6,5},{7,4},{8,11},{9,10},{10,... | collective-permute-start | bytes 589832 | tf_op jit(solution)/shard_map/ppermute | solution.py:337
  7.2 2.0 %shard_map.110 = (bf16[4,192,128]{2,1,0:T(8,128)(2,1)S(1)}, bf16[4,192,128]{2,1,0:T(8,128)(2,1)S(1)}, bf16[4,192,128]{2,1,0:T(8,128)(2,1)S(1)}, bf16[4,192,128]{...) custom-call(s32[1]{0:T(128)} %bitcast.rank_ref, ...), custom_call_target="tpu_custom_call" | custom-call | bytes 3145728 | tf_op jit(solution)/shard_map/pallas_call | solution.py:79
  9.2 0.7 collective-permute-start.2
  9.9 1.4 %collective-permute-start.5 = (bf16[4,192,128]{2,1,0:T(8,128)(2,1)S(1)}, bf16[4,192,128]{2,1,0:T(8,128)(2,1)S(1)}, u32[]{:S(2)}, u32[]{:S(2)}) collective-permute-start(bf16[4,192,128]{2,1,0:T(8,128)(2,1)S(1)} %get-tuple-element.55), channel_id=1, source_target_pairs={{0,1},{1,0},{2,3},{3,2},{4,5},{5,4},{6,7},{7,6},{8,9},{9,8},{10,11... | collective-permute-start | bytes 589832 | tf_op jit(solution)/shard_map/ppermute | solution.py:337
  12.0 0.1 reshape.17
  12.1 0.1 reshape.16
  12.3 0.8 %collective-permute-done.refs_1_ = bf16[4,192,128]{2,1,0:T(8,128)(2,1)S(1)} collective-permute-done((bf16[4,192,128]{2,1,0:T(8,128)(2,1)S(1)}, bf16[4,192,128]{2,1,0:T(8,128)(2,1)S(1)}, u32[]{:S(2)}, u32[]{:S(2)}) %collective-permute-start) | collective-permute-done | bytes 196640 | tf_op jit(solution)/shard_map/ppermute | solution.py:337
  13.1 11.0 %collective-permute-done.1.refs_2_ = bf16[4,192,128]{2,1,0:T(8,128)(2,1)S(1)} collective-permute-done((bf16[4,192,128]{2,1,0:T(8,128)(2,1)S(1)}, bf16[4,192,128]{2,1,0:T(8,128)(2,1)S(1)}, u32[]{:S(2)}, u32[]{:S(2)}) %collective-permute-start.1) | collective-permute-done | bytes 196640 | tf_op jit(solution)/shard_map/ppermute | solution.py:337
  24.0 2.6 %collective-permute-start.3 = (bf16[4,192,128]{2,1,0:T(8,128)(2,1)S(1)}, bf16[4,192,128]{2,1,0:T(8,128)(2,1)S(1)}, u32[]{:S(2)}, u32[]{:S(2)}) collective-permute-start(bf16[4,192,128]{2,1,0:T(8,128)(2,1)S(1)} %get-tuple-element.53), channel_id=1, source_target_pairs={{0,3},{1,2},{2,1},{3,0},{4,7},{5,6},{6,5},{7,4},{8,11},{9,10},{10,... | collective-permute-start | bytes 589832 | tf_op jit(solution)/shard_map/ppermute | solution.py:337
  26.7 0.1 pad_add_fusion.scalars
  26.8 10.1 %shard_map.112 = (bf16[3,192,128]{2,1,0:T(8,128)(2,1)S(1)}, bf16[3,192,128]{2,1,0:T(8,128)(2,1)S(1)}, bf16[3,192,128]{2,1,0:T(8,128)(2,1)S(1)}, bf16[3,192,128]{2,1,0:T(8,128)(2,1)S(1)}, f32[2,32,96]{2,1,0:T(8,128)S(1)}) custom-call(s32[2]{0:T(128)S(1)} %pad_add_fusion.scalars, f32[2,31,96]{2,1,0:T(8,128)S(1)} %get-tuple-element.76.weight_ref, ...), custom_call_target="tpu_custom_call" | custom-call | flops 1207959552 | bytes 1376256 | tf_op jit(solution)/shard_map/pallas_call | solution.py:306
  36.9 1.8 %collective-permute-start.8 = (bf16[3,192,128]{2,1,0:T(8,128)(2,1)S(1)}, bf16[3,192,128]{2,1,0:T(8,128)(2,1)S(1)}, u32[]{:S(2)}, u32[]{:S(2)}) collective-permute-start(bf16[3,192,128]{2,1,0:T(8,128)(2,1)S(1)} %get-tuple-element.68), channel_id=1, source_target_pairs={{0,1},{1,0},{2,3},{3,2},{4,5},{5,4},{6,7},{7,6},{8,9},{9,8},{10,11... | collective-permute-start | bytes 442376 | tf_op jit(solution)/shard_map/ppermute | solution.py:337
  38.7 3.0 %collective-permute-done.4.refs_2_ = bf16[4,192,128]{2,1,0:T(8,128)(2,1)S(1)} collective-permute-done((bf16[4,192,128]{2,1,0:T(8,128)(2,1)S(1)}, bf16[4,192,128]{2,1,0:T(8,128)(2,1)S(1)}, u32[]{:S(2)}, u32[]{:S(2)}) %collective-permute-start.4) | collective-permute-done | bytes 196640 | tf_op jit(solution)/shard_map/ppermute | solution.py:337
  41.7 1.7 %collective-permute-start.6 = (bf16[3,192,128]{2,1,0:T(8,128)(2,1)S(1)}, bf16[3,192,128]{2,1,0:T(8,128)(2,1)S(1)}, u32[]{:S(2)}, u32[]{:S(2)}) collective-permute-start(bf16[3,192,128]{2,1,0:T(8,128)(2,1)S(1)} %get-tuple-element.62), channel_id=1, source_target_pairs={{0,3},{1,2},{2,1},{3,0},{4,7},{5,6},{6,5},{7,4},{8,11},{9,10},{10,... | collective-permute-start | bytes 442376 | tf_op jit(solution)/shard_map/ppermute | solution.py:337
  43.4 9.9 %shard_map.113 = (bf16[3,192,128]{2,1,0:T(8,128)(2,1)S(1)}, bf16[3,192,128]{2,1,0:T(8,128)(2,1)S(1)}, bf16[3,192,128]{2,1,0:T(8,128)(2,1)S(1)}, bf16[3,192,128]{2,1,0:T(8,128)(2,1)S(1)}, f32[2,32,96]{2,1,0:T(8,128)S(1)}) custom-call(s32[2]{0:T(128)S(1)} %pad_add_fusion.scalars, f32[2,31,96]{2,1,0:T(8,128)S(1)} %get-tuple-element.75.weight_ref, ...), custom_call_target="tpu_custom_call" | custom-call | flops 1207959552 | bytes 1376256 | tf_op jit(solution)/shard_map/pallas_call | solution.py:306
  53.4 3.0 %collective-permute-start.10 = (bf16[3,192,128]{2,1,0:T(8,128)(2,1)S(1)}, bf16[3,192,128]{2,1,0:T(8,128)(2,1)S(1)}, u32[]{:S(2)}, u32[]{:S(2)}) collective-permute-start(bf16[3,192,128]{2,1,0:T(8,128)(2,1)S(1)} %get-tuple-element.72), channel_id=1, source_target_pairs={{0,2},{1,3},{2,0},{3,1},{4,6},{5,7},{6,4},{7,5},{8,10},{9,11},{10,... | collective-permute-start | bytes 442376 | tf_op jit(solution)/shard_map/ppermute | solution.py:337
  56.6 2.2 %collective-permute-start.9 = (bf16[3,192,128]{2,1,0:T(8,128)(2,1)S(1)}, bf16[3,192,128]{2,1,0:T(8,128)(2,1)S(1)}, u32[]{:S(2)}, u32[]{:S(2)}) collective-permute-start(bf16[3,192,128]{2,1,0:T(8,128)(2,1)S(1)} %get-tuple-element.71), channel_id=1, source_target_pairs={{0,3},{1,2},{2,1},{3,0},{4,7},{5,6},{6,5},{7,4},{8,11},{9,10},{10,... | collective-permute-start | bytes 442376 | tf_op jit(solution)/shard_map/ppermute | solution.py:337
  58.8 1.6 %collective-permute-start.13 = (f32[4,32,96]{2,1,0:T(8,128)S(1)}, f32[4,32,96]{2,1,0:T(8,128)S(1)}, u32[]{:S(2)}, u32[]{:S(2)}) collective-permute-start(f32[4,32,96]{2,1,0:T(8,128)S(1)} %add.11), channel_id=1, source_target_pairs={{0,8},{4,12},{8,0},{12,4},{16,24},{20,28},{24,16},{28,20},{1,9},{5... | collective-permute-start | bytes 147464 | tf_op jit(solution)/shard_map/ppermute | solution.py:347
  60.3 2.8 %collective-permute-done.13 = f32[4,32,96]{2,1,0:T(8,128)S(1)} collective-permute-done((f32[4,32,96]{2,1,0:T(8,128)S(1)}, f32[4,32,96]{2,1,0:T(8,128)S(1)}, u32[]{:S(2)}, u32[]{:S(2)}) %collective-permute-start.13) | collective-permute-done | bytes 49184 | tf_op jit(solution)/shard_map/ppermute | solution.py:347
  63.1 1.6 %collective-permute-start.14 = (f32[4,32,96]{2,1,0:T(8,128)S(1)}, f32[4,32,96]{2,1,0:T(8,128)S(1)}, u32[]{:S(2)}, u32[]{:S(2)}) collective-permute-start(f32[4,32,96]{2,1,0:T(8,128)S(1)} %add.12.refs_8_), channel_id=1, source_target_pairs={{0,16},{4,20},{8,24},{12,28},{16,0},{20,4},{24,8},{28,12},{1,17},{... | collective-permute-start | bytes 147464 | tf_op jit(solution)/shard_map/ppermute | solution.py:347
  64.7 0.1 collective-permute-done.11.refs_7_
  64.9 3.0 %collective-permute-done.9.refs_5_ = bf16[3,192,128]{2,1,0:T(8,128)(2,1)S(1)} collective-permute-done((bf16[3,192,128]{2,1,0:T(8,128)(2,1)S(1)}, bf16[3,192,128]{2,1,0:T(8,128)(2,1)S(1)}, u32[]{:S(2)}, u32[]{:S(2)}) %collective-permute-start.9) | collective-permute-done | bytes 147488 | tf_op jit(solution)/shard_map/ppermute | solution.py:337
  67.9 1.4 %shard_map.114 = (bf16[1,128,1536]{2,1,0:T(8,128)(2,1)}, bf16[1,128,1536]{2,1,0:T(8,128)(2,1)}, bf16[1,128,1536]{2,1,0:T(8,128)(2,1)}, f32[31,384]{1,0:T(8,128)}, f32[384]{0:T(512)}) custom-call(s32[1]{0:T(128)} %bitcast.rank_ref, bf16[3,192,128]{2,1,0:T(8,128)(2,1)S(1)} %get-tuple-element.49.refs_0_, ...), custom_call_target="tpu_custom_call" | custom-call | bytes 2359296 | tf_op jit(solution)/shard_map/pallas_call | solution.py:124
  (25 shorter events, 0.3 us)
Async XLA Ops:
  2.1 10.9 %collective-permute-start = (bf16[4,192,128]{2,1,0:T(8,128)(2,1)S(1)}, bf16[4,192,128]{2,1,0:T(8,128)(2,1)S(1)}, u32[]{:S(2)}, u32[]{:S(2)}) collective-permute-start(bf16[4,192,128]{2,1,0:T(8,128)(2,1)S(1)} %get-tuple-element.43), channel_id=1, source_target_pairs={{0,3},{1,2},{2,1},{3,0},{4,7},{5,6},{6,5},{7,4},{8,11},{9,10},{10,... | collective-permute-start | bytes 589832 | tf_op jit(solution)/shard_map/ppermute | solution.py:337
  7.2 4.8 %copy-start = (f32[31,1536]{1,0:T(8,128)S(1)}, f32[31,1536]{1,0:T(8,128)}, u32[]{:S(2)}) copy-start(f32[31,1536]{1,0:T(8,128)} %param.11) | copy-start | bytes 571396
  7.2 16.8 %collective-permute-start.1 = (bf16[4,192,128]{2,1,0:T(8,128)(2,1)S(1)}, bf16[4,192,128]{2,1,0:T(8,128)(2,1)S(1)}, u32[]{:S(2)}, u32[]{:S(2)}) collective-permute-start(bf16[4,192,128]{2,1,0:T(8,128)(2,1)S(1)} %get-tuple-element.44), channel_id=1, source_target_pairs={{0,2},{1,3},{2,0},{3,1},{4,6},{5,7},{6,4},{7,5},{8,10},{9,11},{10,... | collective-permute-start | bytes 589832 | tf_op jit(solution)/shard_map/ppermute | solution.py:337
  9.2 2.8 %copy-start.1 = (f32[1536]{0:T(1024)S(1)}, f32[1536]{0:T(1024)}, u32[]{:S(2)}) copy-start(f32[1536]{0:T(1024)} %param.12) | copy-start | bytes 18436
  9.2 14.8 %collective-permute-start.2 = (bf16[4,192,128]{2,1,0:T(8,128)(2,1)S(1)}, bf16[4,192,128]{2,1,0:T(8,128)(2,1)S(1)}, u32[]{:S(2)}, u32[]{:S(2)}) collective-permute-start(bf16[4,192,128]{2,1,0:T(8,128)(2,1)S(1)} %get-tuple-element.45), channel_id=1, source_target_pairs={{0,1},{1,0},{2,3},{3,2},{4,5},{5,4},{6,7},{7,6},{8,9},{9,8},{10,11... | collective-permute-start | bytes 589832 | tf_op jit(solution)/shard_map/ppermute | solution.py:337
  9.9 28.8 %collective-permute-start.5 = (bf16[4,192,128]{2,1,0:T(8,128)(2,1)S(1)}, bf16[4,192,128]{2,1,0:T(8,128)(2,1)S(1)}, u32[]{:S(2)}, u32[]{:S(2)}) collective-permute-start(bf16[4,192,128]{2,1,0:T(8,128)(2,1)S(1)} %get-tuple-element.55), channel_id=1, source_target_pairs={{0,1},{1,0},{2,3},{3,2},{4,5},{5,4},{6,7},{7,6},{8,9},{9,8},{10,11... | collective-permute-start | bytes 589832 | tf_op jit(solution)/shard_map/ppermute | solution.py:337
  24.0 14.7 %collective-permute-start.3 = (bf16[4,192,128]{2,1,0:T(8,128)(2,1)S(1)}, bf16[4,192,128]{2,1,0:T(8,128)(2,1)S(1)}, u32[]{:S(2)}, u32[]{:S(2)}) collective-permute-start(bf16[4,192,128]{2,1,0:T(8,128)(2,1)S(1)} %get-tuple-element.53), channel_id=1, source_target_pairs={{0,3},{1,2},{2,1},{3,0},{4,7},{5,6},{6,5},{7,4},{8,11},{9,10},{10,... | collective-permute-start | bytes 589832 | tf_op jit(solution)/shard_map/ppermute | solution.py:337
  26.7 15.0 %collective-permute-start.4 = (bf16[4,192,128]{2,1,0:T(8,128)(2,1)S(1)}, bf16[4,192,128]{2,1,0:T(8,128)(2,1)S(1)}, u32[]{:S(2)}, u32[]{:S(2)}) collective-permute-start(bf16[4,192,128]{2,1,0:T(8,128)(2,1)S(1)} %get-tuple-element.54), channel_id=1, source_target_pairs={{0,2},{1,3},{2,0},{3,1},{4,6},{5,7},{6,4},{7,5},{8,10},{9,11},{10,... | collective-permute-start | bytes 589832 | tf_op jit(solution)/shard_map/ppermute | solution.py:337
  36.9 16.5 %collective-permute-start.8 = (bf16[3,192,128]{2,1,0:T(8,128)(2,1)S(1)}, bf16[3,192,128]{2,1,0:T(8,128)(2,1)S(1)}, u32[]{:S(2)}, u32[]{:S(2)}) collective-permute-start(bf16[3,192,128]{2,1,0:T(8,128)(2,1)S(1)} %get-tuple-element.68), channel_id=1, source_target_pairs={{0,1},{1,0},{2,3},{3,2},{4,5},{5,4},{6,7},{7,6},{8,9},{9,8},{10,11... | collective-permute-start | bytes 442376 | tf_op jit(solution)/shard_map/ppermute | solution.py:337
  41.7 14.7 %collective-permute-start.6 = (bf16[3,192,128]{2,1,0:T(8,128)(2,1)S(1)}, bf16[3,192,128]{2,1,0:T(8,128)(2,1)S(1)}, u32[]{:S(2)}, u32[]{:S(2)}) collective-permute-start(bf16[3,192,128]{2,1,0:T(8,128)(2,1)S(1)} %get-tuple-element.62), channel_id=1, source_target_pairs={{0,3},{1,2},{2,1},{3,0},{4,7},{5,6},{6,5},{7,4},{8,11},{9,10},{10,... | collective-permute-start | bytes 442376 | tf_op jit(solution)/shard_map/ppermute | solution.py:337
  43.4 13.1 %collective-permute-start.7 = (bf16[3,192,128]{2,1,0:T(8,128)(2,1)S(1)}, bf16[3,192,128]{2,1,0:T(8,128)(2,1)S(1)}, u32[]{:S(2)}, u32[]{:S(2)}) collective-permute-start(bf16[3,192,128]{2,1,0:T(8,128)(2,1)S(1)} %get-tuple-element.65), channel_id=1, source_target_pairs={{0,2},{1,3},{2,0},{3,1},{4,6},{5,7},{6,4},{7,5},{8,10},{9,11},{10,... | collective-permute-start | bytes 442376 | tf_op jit(solution)/shard_map/ppermute | solution.py:337
  53.4 11.3 %collective-permute-start.10 = (bf16[3,192,128]{2,1,0:T(8,128)(2,1)S(1)}, bf16[3,192,128]{2,1,0:T(8,128)(2,1)S(1)}, u32[]{:S(2)}, u32[]{:S(2)}) collective-permute-start(bf16[3,192,128]{2,1,0:T(8,128)(2,1)S(1)} %get-tuple-element.72), channel_id=1, source_target_pairs={{0,2},{1,3},{2,0},{3,1},{4,6},{5,7},{6,4},{7,5},{8,10},{9,11},{10,... | collective-permute-start | bytes 442376 | tf_op jit(solution)/shard_map/ppermute | solution.py:337
  56.4 2.4 %collective-permute-start.12 = (f32[4,32,96]{2,1,0:T(8,128)S(1)}, f32[4,32,96]{2,1,0:T(8,128)S(1)}, u32[]{:S(2)}, u32[]{:S(2)}) collective-permute-start(f32[4,32,96]{2,1,0:T(8,128)S(1)} %pad_maximum_fusion), channel_id=1, source_target_pairs={{0,4},{4,0},{8,12},{12,8},{16,20},{20,16},{24,28},{28,24},{1,5},{5... | collective-permute-start | bytes 147464 | tf_op jit(solution)/shard_map/ppermute | solution.py:347
  56.5 8.4 %collective-permute-start.11 = (bf16[3,192,128]{2,1,0:T(8,128)(2,1)S(1)}, bf16[3,192,128]{2,1,0:T(8,128)(2,1)S(1)}, u32[]{:S(2)}, u32[]{:S(2)}) collective-permute-start(bf16[3,192,128]{2,1,0:T(8,128)(2,1)S(1)} %get-tuple-element.73), channel_id=1, source_target_pairs={{0,1},{1,0},{2,3},{3,2},{4,5},{5,4},{6,7},{7,6},{8,9},{9,8},{10,11... | collective-permute-start | bytes 442376 | tf_op jit(solution)/shard_map/ppermute | solution.py:337
  56.6 11.3 %collective-permute-start.9 = (bf16[3,192,128]{2,1,0:T(8,128)(2,1)S(1)}, bf16[3,192,128]{2,1,0:T(8,128)(2,1)S(1)}, u32[]{:S(2)}, u32[]{:S(2)}) collective-permute-start(bf16[3,192,128]{2,1,0:T(8,128)(2,1)S(1)} %get-tuple-element.71), channel_id=1, source_target_pairs={{0,3},{1,2},{2,1},{3,0},{4,7},{5,6},{6,5},{7,4},{8,11},{9,10},{10,... | collective-permute-start | bytes 442376 | tf_op jit(solution)/shard_map/ppermute | solution.py:337
  58.8 4.3 %collective-permute-start.13 = (f32[4,32,96]{2,1,0:T(8,128)S(1)}, f32[4,32,96]{2,1,0:T(8,128)S(1)}, u32[]{:S(2)}, u32[]{:S(2)}) collective-permute-start(f32[4,32,96]{2,1,0:T(8,128)S(1)} %add.11), channel_id=1, source_target_pairs={{0,8},{4,12},{8,0},{12,4},{16,24},{20,28},{24,16},{28,20},{1,9},{5... | collective-permute-start | bytes 147464 | tf_op jit(solution)/shard_map/ppermute | solution.py:347
  63.1 4.8 %collective-permute-start.14 = (f32[4,32,96]{2,1,0:T(8,128)S(1)}, f32[4,32,96]{2,1,0:T(8,128)S(1)}, u32[]{:S(2)}, u32[]{:S(2)}) collective-permute-start(f32[4,32,96]{2,1,0:T(8,128)S(1)} %add.12.refs_8_), channel_id=1, source_target_pairs={{0,16},{4,20},{8,24},{12,28},{16,0},{20,4},{24,8},{28,12},{1,17},{... | collective-permute-start | bytes 147464 | tf_op jit(solution)/shard_map/ppermute | solution.py:347

commit v14 on v13

--- a/solution.py
+++ b/solution.py
@@ -54,7 +54,7 @@
     high = share // chunks
     piece = jax.ShapeDtypeStruct((4, high, frames), bf16)
     wide = -(-high // 128) * 128
-    far = tuple(range(count - 1, 1, -1)) if share % 128 == 0 and wide <= share else ()
+    far = tuple(range(2, count)) if share % 128 == 0 and wide <= share else ()
     params = pltpu.CompilerParams(vmem_limit_bytes=LIMIT)
     arrays = [pltpu.with_memory_space_constraint(array, pltpu.HBM) for array in arrays]
     found = {}
@@ -92,7 +92,7 @@
 
 
 def taken(count):
-    return [0] + list(range(count - 1, 0, -1))
+    return [0] + list(range(2, count)) + [1]
 
 
 def unpack_kernel(count, chunks, rank_ref, *refs):
@@ -328,11 +328,15 @@
 
 
 def exchanged(pieces, before):
-    pieces = list(pieces)
+    pieces, order = list(pieces), taken(len(pieces))[1:]
     if before is not None and len(pieces) > 2:
-        pieces[:1:-1], before[:0:-1] = lax.optimization_barrier((pieces[:1:-1], before[:0:-1]))
-    moved = pieces[:1] * len(pieces)
-    for distance in range(len(pieces) - 1, 0, -1):
+        sent, here = lax.optimization_barrier(
+            ([pieces[distance] for distance in order[:-1]], [before[distance] for distance in order])
+        )
+        for distance, piece, arrived in zip(order, sent + [pieces[1]], here):
+            pieces[distance], before[distance] = piece, arrived
+    moved = list(pieces)
+    for distance in order:
         pairs = [(i, i ^ distance) for i in range(len(pieces))]
         moved[distance] = lax.ppermute(pieces[distance], "seq", pairs)
     return moved
@@ -376,8 +380,8 @@
     last = count - 1
     grads[last - 1], before[1] = lax.optimization_barrier((grads[last - 1], before[1]))
     if last > 2:
-        (grads[1], taps), before[last] = lax.optimization_barrier(((grads[1], taps), before[last]))
-        grads[last], before[last - 1] = lax.optimization_barrier((grads[last], before[last - 1]))
+        (grads[1], taps), before[2] = lax.optimization_barrier(((grads[1], taps), before[2]))
+        grads[last], before[last] = lax.optimization_barrier((grads[last], before[last]))
     order.append(exchanged(grads, None))
     return unpack(rank[None], doubled(taps, "dp"), order[chunks:], count, chunks)
 

time: 69.5 us -> 72 us (1.036)
  starting transfers between devices: 21.8 us -> 26.3 us
  waiting for transfers between devices: 20.7 us -> 18.8 us
    ppermute x12, starting transfers between devices: 18.6 us -> 23.1 us  [exchanged(): moved[distance] = lax.ppermute(pieces[distance], 'seq', pairs)]
    ppermute x12, waiting for transfers between devices: 18 us -> 15.4 us  [exchanged(): moved[distance] = lax.ppermute(pieces[distance], 'seq', pairs)]
  transfers between devices with their start and end apart: 15 -> 15, of which waited for: 6 -> 6; matrix products, arithmetic and copies ran while one was open for 1% -> 0% of each run, Pallas kernels for 32% -> 31%
where the time goes in v14:
time: 72 us; the launch traced here: 71.8 us
  starting transfers between devices  26.3 us (37%)
  Pallas kernels  24.8 us (34%)
  waiting for transfers between devices  18.8 us (26%)
  between operations  1.44 us (2%)
    ppermute x12, starting transfers between devices, exchanged(): moved[distance] = lax.ppermute(pieces[distance], 'seq', pairs)  23.1 us
    pallas_call x2, Pallas kernels, core(): pl.pallas_call(functools.partial(core_kernel, count, block), out_shape=(p...  20.1 us
    ppermute x12, waiting for transfers between devices, exchanged(): moved[distance] = lax.ppermute(pieces[distance], 'seq', pairs)  15.4 us
    ppermute x3, waiting for transfers between devices, doubled(): pair = (total, lax.ppermute(total, axis, pairs))  3.38 us
    ppermute x3, starting transfers between devices, doubled(): pair = (total, lax.ppermute(total, axis, pairs))  3.23 us
    pallas_call x1, Pallas kernels, pack(): pl.pallas_call(functools.partial(pack_kernel, wanted, share), out_shape=(...  1.92 us
    pallas_call x1, Pallas kernels, pack(): pl.pallas_call(functools.partial(pack_first_kernel, far, share), out_shap...  1.49 us
  transfers between devices with their start and end apart: 15, of which 6 were waited for; matrix products, arithmetic and copies ran while one was open for 0% of the time, Pallas kernels for 31%

profile of v14, /device:TPU:0, one launch (start us, length us, event | category | flops | bytes accessed | tf_op | source)
XLA Modules:
  0.0 71.8 jit_solution(14907039125150095450)
XLA Ops:
  0.6 1.5 %shard_map.111 = (bf16[4,192,128]{2,1,0:T(8,128)(2,1)S(1)}, bf16[4,192,128]{2,1,0:T(8,128)(2,1)S(1)}) custom-call(s32[1]{0:T(128)} %bitcast.rank_ref, bf16[1,128,1536]{2,1,0:T(8,128)(2,1)} %refs_0_.3, bf16[1,128,1536]{2,1,0:T(8,128)(2,1)} %refs_1_.3, bf16[1,128,1536]{2,1,0:T(8,128)(2,1)} %refs_2_.3, bf16[1,128,1536]{2,1,0:T(8,128)(2,1)} %refs_3_.3), custom_call_target="tpu_custom_call" | custom-call | bytes 1048576 | tf_op jit(solution)/shard_map/pallas_call | solution.py:62
  2.1 4.1 %collective-permute-start = (bf16[4,192,128]{2,1,0:T(8,128)(2,1)S(1)}, bf16[4,192,128]{2,1,0:T(8,128)(2,1)S(1)}, u32[]{:S(2)}, u32[]{:S(2)}) collective-permute-start(bf16[4,192,128]{2,1,0:T(8,128)(2,1)S(1)} %get-tuple-element.43), channel_id=1, source_target_pairs={{0,2},{1,3},{2,0},{3,1},{4,6},{5,7},{6,4},{7,5},{8,10},{9,11},{10,... | collective-permute-start | bytes 589832 | tf_op jit(solution)/shard_map/ppermute | solution.py:341
  6.2 1.3 %collective-permute-start.1 = (bf16[4,192,128]{2,1,0:T(8,128)(2,1)S(1)}, bf16[4,192,128]{2,1,0:T(8,128)(2,1)S(1)}, u32[]{:S(2)}, u32[]{:S(2)}) collective-permute-start(bf16[4,192,128]{2,1,0:T(8,128)(2,1)S(1)} %get-tuple-element.44), channel_id=1, source_target_pairs={{0,3},{1,2},{2,1},{3,0},{4,7},{5,6},{6,5},{7,4},{8,11},{9,10},{10,... | collective-permute-start | bytes 589832 | tf_op jit(solution)/shard_map/ppermute | solution.py:341
  7.6 1.9 %shard_map.110 = (bf16[4,192,128]{2,1,0:T(8,128)(2,1)S(1)}, bf16[4,192,128]{2,1,0:T(8,128)(2,1)S(1)}, bf16[4,192,128]{2,1,0:T(8,128)(2,1)S(1)}, bf16[4,192,128]{...) custom-call(s32[1]{0:T(128)} %bitcast.rank_ref, ...), custom_call_target="tpu_custom_call" | custom-call | bytes 3145728 | tf_op jit(solution)/shard_map/pallas_call | solution.py:79
  9.5 0.3 collective-permute-start.2
  9.9 1.8 %collective-permute-start.5 = (bf16[4,192,128]{2,1,0:T(8,128)(2,1)S(1)}, bf16[4,192,128]{2,1,0:T(8,128)(2,1)S(1)}, u32[]{:S(2)}, u32[]{:S(2)}) collective-permute-start(bf16[4,192,128]{2,1,0:T(8,128)(2,1)S(1)} %get-tuple-element.55), channel_id=1, source_target_pairs={{0,1},{1,0},{2,3},{3,2},{4,5},{5,4},{6,7},{7,6},{8,9},{9,8},{10,11... | collective-permute-start | bytes 589832 | tf_op jit(solution)/shard_map/ppermute | solution.py:341
  12.6 7.9 %collective-permute-done.refs_1_ = bf16[4,192,128]{2,1,0:T(8,128)(2,1)S(1)} collective-permute-done((bf16[4,192,128]{2,1,0:T(8,128)(2,1)S(1)}, bf16[4,192,128]{2,1,0:T(8,128)(2,1)S(1)}, u32[]{:S(2)}, u32[]{:S(2)}) %collective-permute-start) | collective-permute-done | bytes 196640 | tf_op jit(solution)/shard_map/ppermute | solution.py:341
  20.4 3.3 %collective-permute-done.2.refs_3_ = bf16[4,192,128]{2,1,0:T(8,128)(2,1)S(1)} collective-permute-done((bf16[4,192,128]{2,1,0:T(8,128)(2,1)S(1)}, bf16[4,192,128]{2,1,0:T(8,128)(2,1)S(1)}, u32[]{:S(2)}, u32[]{:S(2)}) %collective-permute-start.2) | collective-permute-done | bytes 196640 | tf_op jit(solution)/shard_map/ppermute | solution.py:341
  23.7 2.7 %collective-permute-start.3 = (bf16[4,192,128]{2,1,0:T(8,128)(2,1)S(1)}, bf16[4,192,128]{2,1,0:T(8,128)(2,1)S(1)}, u32[]{:S(2)}, u32[]{:S(2)}) collective-permute-start(bf16[4,192,128]{2,1,0:T(8,128)(2,1)S(1)} %get-tuple-element.53), channel_id=1, source_target_pairs={{0,2},{1,3},{2,0},{3,1},{4,6},{5,7},{6,4},{7,5},{8,10},{9,11},{10,... | collective-permute-start | bytes 589832 | tf_op jit(solution)/shard_map/ppermute | solution.py:341
  26.5 0.8 %collective-permute-start.4 = (bf16[4,192,128]{2,1,0:T(8,128)(2,1)S(1)}, bf16[4,192,128]{2,1,0:T(8,128)(2,1)S(1)}, u32[]{:S(2)}, u32[]{:S(2)}) collective-permute-start(bf16[4,192,128]{2,1,0:T(8,128)(2,1)S(1)} %get-tuple-element.54), channel_id=1, source_target_pairs={{0,3},{1,2},{2,1},{3,0},{4,7},{5,6},{6,5},{7,4},{8,11},{9,10},{10,... | collective-permute-start | bytes 589832 | tf_op jit(solution)/shard_map/ppermute | solution.py:341
  27.3 10.1 %shard_map.112 = (bf16[3,192,128]{2,1,0:T(8,128)(2,1)S(1)}, bf16[3,192,128]{2,1,0:T(8,128)(2,1)S(1)}, bf16[3,192,128]{2,1,0:T(8,128)(2,1)S(1)}, bf16[3,192,128]{2,1,0:T(8,128)(2,1)S(1)}, f32[2,32,96]{2,1,0:T(8,128)S(1)}) custom-call(s32[2]{0:T(128)S(1)} %pad_add_fusion.scalars, f32[2,31,96]{2,1,0:T(8,128)S(1)} %get-tuple-element.76.weight_ref, ...), custom_call_target="tpu_custom_call" | custom-call | flops 1207959552 | bytes 1376256 | tf_op jit(solution)/shard_map/pallas_call | solution.py:306
  37.4 0.6 collective-permute-start.8
  38.1 2.2 %collective-permute-done.3.refs_1_ = bf16[4,192,128]{2,1,0:T(8,128)(2,1)S(1)} collective-permute-done((bf16[4,192,128]{2,1,0:T(8,128)(2,1)S(1)}, bf16[4,192,128]{2,1,0:T(8,128)(2,1)S(1)}, u32[]{:S(2)}, u32[]{:S(2)}) %collective-permute-start.3) | collective-permute-done | bytes 196640 | tf_op jit(solution)/shard_map/ppermute | solution.py:341
  40.2 4.8 %collective-permute-start.6 = (bf16[3,192,128]{2,1,0:T(8,128)(2,1)S(1)}, bf16[3,192,128]{2,1,0:T(8,128)(2,1)S(1)}, u32[]{:S(2)}, u32[]{:S(2)}) collective-permute-start(bf16[3,192,128]{2,1,0:T(8,128)(2,1)S(1)} %get-tuple-element.62), channel_id=1, source_target_pairs={{0,2},{1,3},{2,0},{3,1},{4,6},{5,7},{6,4},{7,5},{8,10},{9,11},{10,... | collective-permute-start | bytes 442376 | tf_op jit(solution)/shard_map/ppermute | solution.py:341
  45.0 2.1 %collective-permute-start.7 = (bf16[3,192,128]{2,1,0:T(8,128)(2,1)S(1)}, bf16[3,192,128]{2,1,0:T(8,128)(2,1)S(1)}, u32[]{:S(2)}, u32[]{:S(2)}) collective-permute-start(bf16[3,192,128]{2,1,0:T(8,128)(2,1)S(1)} %get-tuple-element.65), channel_id=1, source_target_pairs={{0,3},{1,2},{2,1},{3,0},{4,7},{5,6},{6,5},{7,4},{8,11},{9,10},{10,... | collective-permute-start | bytes 442376 | tf_op jit(solution)/shard_map/ppermute | solution.py:341
  47.1 9.9 %shard_map.113 = (bf16[3,192,128]{2,1,0:T(8,128)(2,1)S(1)}, bf16[3,192,128]{2,1,0:T(8,128)(2,1)S(1)}, bf16[3,192,128]{2,1,0:T(8,128)(2,1)S(1)}, bf16[3,192,128]{2,1,0:T(8,128)(2,1)S(1)}, f32[2,32,96]{2,1,0:T(8,128)S(1)}) custom-call(s32[2]{0:T(128)S(1)} %pad_add_fusion.scalars, f32[2,31,96]{2,1,0:T(8,128)S(1)} %get-tuple-element.75.weight_ref, ...), custom_call_target="tpu_custom_call" | custom-call | flops 1207959552 | bytes 1376256 | tf_op jit(solution)/shard_map/pallas_call | solution.py:306
  57.3 2.3 %collective-permute-start.11 = (bf16[3,192,128]{2,1,0:T(8,128)(2,1)S(1)}, bf16[3,192,128]{2,1,0:T(8,128)(2,1)S(1)}, u32[]{:S(2)}, u32[]{:S(2)}) collective-permute-start(bf16[3,192,128]{2,1,0:T(8,128)(2,1)S(1)} %get-tuple-element.73), channel_id=1, source_target_pairs={{0,1},{1,0},{2,3},{3,2},{4,5},{5,4},{6,7},{7,6},{8,9},{9,8},{10,11... | collective-permute-start | bytes 442376 | tf_op jit(solution)/shard_map/ppermute | solution.py:341
  59.6 2.1 %collective-permute-start.10 = (bf16[3,192,128]{2,1,0:T(8,128)(2,1)S(1)}, bf16[3,192,128]{2,1,0:T(8,128)(2,1)S(1)}, u32[]{:S(2)}, u32[]{:S(2)}) collective-permute-start(bf16[3,192,128]{2,1,0:T(8,128)(2,1)S(1)} %get-tuple-element.72), channel_id=1, source_target_pairs={{0,3},{1,2},{2,1},{3,0},{4,7},{5,6},{6,5},{7,4},{8,11},{9,10},{10,... | collective-permute-start | bytes 442376 | tf_op jit(solution)/shard_map/ppermute | solution.py:341
  61.7 1.6 %collective-permute-start.13 = (f32[4,32,96]{2,1,0:T(8,128)S(1)}, f32[4,32,96]{2,1,0:T(8,128)S(1)}, u32[]{:S(2)}, u32[]{:S(2)}) collective-permute-start(f32[4,32,96]{2,1,0:T(8,128)S(1)} %add.11), channel_id=1, source_target_pairs={{0,8},{4,12},{8,0},{12,4},{16,24},{20,28},{24,16},{28,20},{1,9},{5... | collective-permute-start | bytes 147464 | tf_op jit(solution)/shard_map/ppermute | solution.py:351
  63.3 2.8 %collective-permute-done.13 = f32[4,32,96]{2,1,0:T(8,128)S(1)} collective-permute-done((f32[4,32,96]{2,1,0:T(8,128)S(1)}, f32[4,32,96]{2,1,0:T(8,128)S(1)}, u32[]{:S(2)}, u32[]{:S(2)}) %collective-permute-start.13) | collective-permute-done | bytes 49184 | tf_op jit(solution)/shard_map/ppermute | solution.py:351
  66.1 1.6 %collective-permute-start.14 = (f32[4,32,96]{2,1,0:T(8,128)S(1)}, f32[4,32,96]{2,1,0:T(8,128)S(1)}, u32[]{:S(2)}, u32[]{:S(2)}) collective-permute-start(f32[4,32,96]{2,1,0:T(8,128)S(1)} %add.12.refs_8_), channel_id=1, source_target_pairs={{0,16},{4,20},{8,24},{12,28},{16,0},{20,4},{24,8},{28,12},{1,17},{... | collective-permute-start | bytes 147464 | tf_op jit(solution)/shard_map/ppermute | solution.py:351
  67.7 2.1 %collective-permute-done.11.refs_7_ = bf16[3,192,128]{2,1,0:T(8,128)(2,1)S(1)} collective-permute-done((bf16[3,192,128]{2,1,0:T(8,128)(2,1)S(1)}, bf16[3,192,128]{2,1,0:T(8,128)(2,1)S(1)}, u32[]{:S(2)}, u32[]{:S(2)}) %collective-permute-start.11) | collective-permute-done | bytes 147488 | tf_op jit(solution)/shard_map/ppermute | solution.py:341
  69.8 0.6 collective-permute-done.14.refs_9_
  70.4 1.4 %shard_map.114 = (bf16[1,128,1536]{2,1,0:T(8,128)(2,1)}, bf16[1,128,1536]{2,1,0:T(8,128)(2,1)}, bf16[1,128,1536]{2,1,0:T(8,128)(2,1)}, f32[31,384]{1,0:T(8,128)}, f32[384]{0:T(512)}) custom-call(s32[1]{0:T(128)} %bitcast.rank_ref, bf16[3,192,128]{2,1,0:T(8,128)(2,1)S(1)} %get-tuple-element.49.refs_0_, ...), custom_call_target="tpu_custom_call" | custom-call | bytes 2359296 | tf_op jit(solution)/shard_map/pallas_call | solution.py:124
  (25 shorter events, 0.5 us)
Async XLA Ops:
  2.1 18.3 %collective-permute-start = (bf16[4,192,128]{2,1,0:T(8,128)(2,1)S(1)}, bf16[4,192,128]{2,1,0:T(8,128)(2,1)S(1)}, u32[]{:S(2)}, u32[]{:S(2)}) collective-permute-start(bf16[4,192,128]{2,1,0:T(8,128)(2,1)S(1)} %get-tuple-element.43), channel_id=1, source_target_pairs={{0,2},{1,3},{2,0},{3,1},{4,6},{5,7},{6,4},{7,5},{8,10},{9,11},{10,... | collective-permute-start | bytes 589832 | tf_op jit(solution)/shard_map/ppermute | solution.py:341
  6.2 6.1 %copy-start = (f32[31,1536]{1,0:T(8,128)S(1)}, f32[31,1536]{1,0:T(8,128)}, u32[]{:S(2)}) copy-start(f32[31,1536]{1,0:T(8,128)} %param.11) | copy-start | bytes 571396
  6.2 14.2 %collective-permute-start.1 = (bf16[4,192,128]{2,1,0:T(8,128)(2,1)S(1)}, bf16[4,192,128]{2,1,0:T(8,128)(2,1)S(1)}, u32[]{:S(2)}, u32[]{:S(2)}) collective-permute-start(bf16[4,192,128]{2,1,0:T(8,128)(2,1)S(1)} %get-tuple-element.44), channel_id=1, source_target_pairs={{0,3},{1,2},{2,1},{3,0},{4,7},{5,6},{6,5},{7,4},{8,11},{9,10},{10,... | collective-permute-start | bytes 589832 | tf_op jit(solution)/shard_map/ppermute | solution.py:341
  9.5 2.8 %copy-start.1 = (f32[1536]{0:T(1024)S(1)}, f32[1536]{0:T(1024)}, u32[]{:S(2)}) copy-start(f32[1536]{0:T(1024)} %param.12) | copy-start | bytes 18436
  9.5 14.2 %collective-permute-start.2 = (bf16[4,192,128]{2,1,0:T(8,128)(2,1)S(1)}, bf16[4,192,128]{2,1,0:T(8,128)(2,1)S(1)}, u32[]{:S(2)}, u32[]{:S(2)}) collective-permute-start(bf16[4,192,128]{2,1,0:T(8,128)(2,1)S(1)} %get-tuple-element.45), channel_id=1, source_target_pairs={{0,1},{1,0},{2,3},{3,2},{4,5},{5,4},{6,7},{7,6},{8,9},{9,8},{10,11... | collective-permute-start | bytes 589832 | tf_op jit(solution)/shard_map/ppermute | solution.py:341
  9.9 28.2 %collective-permute-start.5 = (bf16[4,192,128]{2,1,0:T(8,128)(2,1)S(1)}, bf16[4,192,128]{2,1,0:T(8,128)(2,1)S(1)}, u32[]{:S(2)}, u32[]{:S(2)}) collective-permute-start(bf16[4,192,128]{2,1,0:T(8,128)(2,1)S(1)} %get-tuple-element.55), channel_id=1, source_target_pairs={{0,1},{1,0},{2,3},{3,2},{4,5},{5,4},{6,7},{7,6},{8,9},{9,8},{10,11... | collective-permute-start | bytes 589832 | tf_op jit(solution)/shard_map/ppermute | solution.py:341
  23.7 16.5 %collective-permute-start.3 = (bf16[4,192,128]{2,1,0:T(8,128)(2,1)S(1)}, bf16[4,192,128]{2,1,0:T(8,128)(2,1)S(1)}, u32[]{:S(2)}, u32[]{:S(2)}) collective-permute-start(bf16[4,192,128]{2,1,0:T(8,128)(2,1)S(1)} %get-tuple-element.53), channel_id=1, source_target_pairs={{0,2},{1,3},{2,0},{3,1},{4,6},{5,7},{6,4},{7,5},{8,10},{9,11},{10,... | collective-permute-start | bytes 589832 | tf_op jit(solution)/shard_map/ppermute | solution.py:341
  26.5 13.8 %collective-permute-start.4 = (bf16[4,192,128]{2,1,0:T(8,128)(2,1)S(1)}, bf16[4,192,128]{2,1,0:T(8,128)(2,1)S(1)}, u32[]{:S(2)}, u32[]{:S(2)}) collective-permute-start(bf16[4,192,128]{2,1,0:T(8,128)(2,1)S(1)} %get-tuple-element.54), channel_id=1, source_target_pairs={{0,3},{1,2},{2,1},{3,0},{4,7},{5,6},{6,5},{7,4},{8,11},{9,10},{10,... | collective-permute-start | bytes 589832 | tf_op jit(solution)/shard_map/ppermute | solution.py:341
  37.4 19.6 %collective-permute-start.8 = (bf16[3,192,128]{2,1,0:T(8,128)(2,1)S(1)}, bf16[3,192,128]{2,1,0:T(8,128)(2,1)S(1)}, u32[]{:S(2)}, u32[]{:S(2)}) collective-permute-start(bf16[3,192,128]{2,1,0:T(8,128)(2,1)S(1)} %get-tuple-element.68), channel_id=1, source_target_pairs={{0,1},{1,0},{2,3},{3,2},{4,5},{5,4},{6,7},{7,6},{8,9},{9,8},{10,11... | collective-permute-start | bytes 442376 | tf_op jit(solution)/shard_map/ppermute | solution.py:341
  40.2 16.9 %collective-permute-start.6 = (bf16[3,192,128]{2,1,0:T(8,128)(2,1)S(1)}, bf16[3,192,128]{2,1,0:T(8,128)(2,1)S(1)}, u32[]{:S(2)}, u32[]{:S(2)}) collective-permute-start(bf16[3,192,128]{2,1,0:T(8,128)(2,1)S(1)} %get-tuple-element.62), channel_id=1, source_target_pairs={{0,2},{1,3},{2,0},{3,1},{4,6},{5,7},{6,4},{7,5},{8,10},{9,11},{10,... | collective-permute-start | bytes 442376 | tf_op jit(solution)/shard_map/ppermute | solution.py:341
  45.0 14.6 %collective-permute-start.7 = (bf16[3,192,128]{2,1,0:T(8,128)(2,1)S(1)}, bf16[3,192,128]{2,1,0:T(8,128)(2,1)S(1)}, u32[]{:S(2)}, u32[]{:S(2)}) collective-permute-start(bf16[3,192,128]{2,1,0:T(8,128)(2,1)S(1)} %get-tuple-element.65), channel_id=1, source_target_pairs={{0,3},{1,2},{2,1},{3,0},{4,7},{5,6},{6,5},{7,4},{8,11},{9,10},{10,... | collective-permute-start | bytes 442376 | tf_op jit(solution)/shard_map/ppermute | solution.py:341
  57.1 10.6 %collective-permute-start.9 = (bf16[3,192,128]{2,1,0:T(8,128)(2,1)S(1)}, bf16[3,192,128]{2,1,0:T(8,128)(2,1)S(1)}, u32[]{:S(2)}, u32[]{:S(2)}) collective-permute-start(bf16[3,192,128]{2,1,0:T(8,128)(2,1)S(1)} %get-tuple-element.71), channel_id=1, source_target_pairs={{0,2},{1,3},{2,0},{3,1},{4,6},{5,7},{6,4},{7,5},{8,10},{9,11},{10,... | collective-permute-start | bytes 442376 | tf_op jit(solution)/shard_map/ppermute | solution.py:341
  57.2 4.5 %collective-permute-start.12 = (f32[4,32,96]{2,1,0:T(8,128)S(1)}, f32[4,32,96]{2,1,0:T(8,128)S(1)}, u32[]{:S(2)}, u32[]{:S(2)}) collective-permute-start(f32[4,32,96]{2,1,0:T(8,128)S(1)} %pad_maximum_fusion), channel_id=1, source_target_pairs={{0,4},{4,0},{8,12},{12,8},{16,20},{20,16},{24,28},{28,24},{1,5},{5... | collective-permute-start | bytes 147464 | tf_op jit(solution)/shard_map/ppermute | solution.py:351
  57.3 12.5 %collective-permute-start.11 = (bf16[3,192,128]{2,1,0:T(8,128)(2,1)S(1)}, bf16[3,192,128]{2,1,0:T(8,128)(2,1)S(1)}, u32[]{:S(2)}, u32[]{:S(2)}) collective-permute-start(bf16[3,192,128]{2,1,0:T(8,128)(2,1)S(1)} %get-tuple-element.73), channel_id=1, source_target_pairs={{0,1},{1,0},{2,3},{3,2},{4,5},{5,4},{6,7},{7,6},{8,9},{9,8},{10,11... | collective-permute-start | bytes 442376 | tf_op jit(solution)/shard_map/ppermute | solution.py:341
  59.6 10.2 %collective-permute-start.10 = (bf16[3,192,128]{2,1,0:T(8,128)(2,1)S(1)}, bf16[3,192,128]{2,1,0:T(8,128)(2,1)S(1)}, u32[]{:S(2)}, u32[]{:S(2)}) collective-permute-start(bf16[3,192,128]{2,1,0:T(8,128)(2,1)S(1)} %get-tuple-element.72), channel_id=1, source_target_pairs={{0,3},{1,2},{2,1},{3,0},{4,7},{5,6},{6,5},{7,4},{8,11},{9,10},{10,... | collective-permute-start | bytes 442376 | tf_op jit(solution)/shard_map/ppermute | solution.py:341
  61.7 4.3 %collective-permute-start.13 = (f32[4,32,96]{2,1,0:T(8,128)S(1)}, f32[4,32,96]{2,1,0:T(8,128)S(1)}, u32[]{:S(2)}, u32[]{:S(2)}) collective-permute-start(f32[4,32,96]{2,1,0:T(8,128)S(1)} %add.11), channel_id=1, source_target_pairs={{0,8},{4,12},{8,0},{12,4},{16,24},{20,28},{24,16},{28,20},{1,9},{5... | collective-permute-start | bytes 147464 | tf_op jit(solution)/shard_map/ppermute | solution.py:351
  66.1 4.3 %collective-permute-start.14 = (f32[4,32,96]{2,1,0:T(8,128)S(1)}, f32[4,32,96]{2,1,0:T(8,128)S(1)}, u32[]{:S(2)}, u32[]{:S(2)}) collective-permute-start(f32[4,32,96]{2,1,0:T(8,128)S(1)} %add.12.refs_8_), channel_id=1, source_target_pairs={{0,16},{4,20},{8,24},{12,28},{16,0},{20,4},{24,8},{28,12},{1,17},{... | collective-permute-start | bytes 147464 | tf_op jit(solution)/shard_map/ppermute | solution.py:351

commit v15 on v13

--- a/solution.py
+++ b/solution.py
@@ -95,6 +95,10 @@
     return [0] + list(range(count - 1, 0, -1))
 
 
+def returned(count):
+    return [0] + list(range(2, count)) + [1]
+
+
 def unpack_kernel(count, chunks, rank_ref, *refs):
     pieces, refs = refs[: count * chunks], refs[count * chunks :]
     taps_refs, outs = refs[:-7], refs[-7:-4]
@@ -104,7 +108,7 @@
     share = high * chunks
     for which, out in enumerate(outs):
         for chunk in range(chunks):
-            for place, distance in enumerate(taken(count)):
+            for place, distance in enumerate(returned(count)):
                 first = pl.multiple_of((rank ^ distance) * share + chunk * high, 16)
                 turned[which, pl.ds(first, high), :] = pieces[chunk * count + place][which]
         out[0] = turned[which].T
@@ -138,7 +142,7 @@
         cost_estimate=pl.CostEstimate(
             flops=0, bytes_accessed=12 * frames * width, transcendentals=0
         ),
-    )(rank, *[part[distance] for part in pieces for distance in taken(count)], *taps)
+    )(rank, *[part[distance] for part in pieces for distance in returned(count)], *taps)
 
 
 def core_kernel(count, block, scalars, weight_ref, bias_ref, *refs):
@@ -327,12 +331,13 @@
     return outs[:count], outs[count]
 
 
-def exchanged(pieces, before):
+def exchanged(pieces, before, farthest_first=True):
     pieces = list(pieces)
     if before is not None and len(pieces) > 2:
         pieces[:1:-1], before[:0:-1] = lax.optimization_barrier((pieces[:1:-1], before[:0:-1]))
     moved = pieces[:1] * len(pieces)
-    for distance in range(len(pieces) - 1, 0, -1):
+    order = range(1, len(pieces))
+    for distance in reversed(order) if farthest_first else [*order[1:], 1]:
         pairs = [(i, i ^ distance) for i in range(len(pieces))]
         moved[distance] = lax.ppermute(pieces[distance], "seq", pairs)
     return moved
@@ -371,14 +376,14 @@
         grads, part = core(scalars, weight[at], bias[at], order[chunk])
         taps.append(part)
         if chunk < chunks - 1:
-            order.append(exchanged(grads, order[-1]))
+            order.append(exchanged(grads, order[-1], False))
     before, grads, taps = order[-1], list(grads), jnp.concatenate(taps, axis=0)
     last = count - 1
     grads[last - 1], before[1] = lax.optimization_barrier((grads[last - 1], before[1]))
     if last > 2:
-        (grads[1], taps), before[last] = lax.optimization_barrier(((grads[1], taps), before[last]))
-        grads[last], before[last - 1] = lax.optimization_barrier((grads[last], before[last - 1]))
-    order.append(exchanged(grads, None))
+        (grads[1], taps), before[2] = lax.optimization_barrier(((grads[1], taps), before[2]))
+        grads[last], before[last] = lax.optimization_barrier((grads[last], before[last]))
+    order.append(exchanged(grads, None, False))
     return unpack(rank[None], doubled(taps, "dp"), order[chunks:], count, chunks)
 
 

time: 69.5 us -> 69.1 us (level)
  starting transfers between devices: 21.8 us -> 21.1 us
    ppermute x12, starting transfers between devices: 18.6 us -> 17.9 us  [exchanged(): moved[distance] = lax.ppermute(pieces[distance], 'seq', pairs)]
where the time goes in v15:
time: 69.1 us; the launch traced here: 68.9 us
  Pallas kernels  24.9 us (36%)
  starting transfers between devices  21.1 us (31%)
  waiting for transfers between devices  21.1 us (31%)
  between operations  1.43 us (2%)
    pallas_call x2, Pallas kernels, core(): pl.pallas_call(functools.partial(core_kernel, count, block), out_shape=(p...  20.1 us
    ppermute x12, waiting for transfers between devices, exchanged(): moved[distance] = lax.ppermute(pieces[distance], 'seq', pairs)  18.3 us
    ppermute x12, starting transfers between devices, exchanged(): moved[distance] = lax.ppermute(pieces[distance], 'seq', pairs)  17.9 us
    ppermute x3, starting transfers between devices, doubled(): pair = (total, lax.ppermute(total, axis, pairs))  3.22 us
    ppermute x3, waiting for transfers between devices, doubled(): pair = (total, lax.ppermute(total, axis, pairs))  2.77 us
    pallas_call x1, Pallas kernels, pack(): pl.pallas_call(functools.partial(pack_kernel, wanted, share), out_shape=(...  1.96 us
    pallas_call x1, Pallas kernels, pack(): pl.pallas_call(functools.partial(pack_first_kernel, far, share), out_shap...  1.49 us
  transfers between devices with their start and end apart: 15, of which 6 were waited for; matrix products, arithmetic and copies ran while one was open for 1% of the time, Pallas kernels for 32%

profile of v15, /device:TPU:0, one launch (start us, length us, event | category | flops | bytes accessed | tf_op | source)
XLA Modules:
  0.0 68.9 jit_solution(8770611037066120859)
XLA Ops:
  0.6 1.5 %shard_map.111 = (bf16[4,192,128]{2,1,0:T(8,128)(2,1)S(1)}, bf16[4,192,128]{2,1,0:T(8,128)(2,1)S(1)}) custom-call(s32[1]{0:T(128)} %bitcast.rank_ref, bf16[1,128,1536]{2,1,0:T(8,128)(2,1)} %refs_0_.3, bf16[1,128,1536]{2,1,0:T(8,128)(2,1)} %refs_1_.3, bf16[1,128,1536]{2,1,0:T(8,128)(2,1)} %refs_2_.3, bf16[1,128,1536]{2,1,0:T(8,128)(2,1)} %refs_3_.3), custom_call_target="tpu_custom_call" | custom-call | bytes 1048576 | tf_op jit(solution)/shard_map/pallas_call | solution.py:62
  2.1 5.1 %collective-permute-start = (bf16[4,192,128]{2,1,0:T(8,128)(2,1)S(1)}, bf16[4,192,128]{2,1,0:T(8,128)(2,1)S(1)}, u32[]{:S(2)}, u32[]{:S(2)}) collective-permute-start(bf16[4,192,128]{2,1,0:T(8,128)(2,1)S(1)} %get-tuple-element.43), channel_id=1, source_target_pairs={{0,3},{1,2},{2,1},{3,0},{4,7},{5,6},{6,5},{7,4},{8,11},{9,10},{10,... | collective-permute-start | bytes 589832 | tf_op jit(solution)/shard_map/ppermute | solution.py:342
  7.2 2.0 %shard_map.110 = (bf16[4,192,128]{2,1,0:T(8,128)(2,1)S(1)}, bf16[4,192,128]{2,1,0:T(8,128)(2,1)S(1)}, bf16[4,192,128]{2,1,0:T(8,128)(2,1)S(1)}, bf16[4,192,128]{...) custom-call(s32[1]{0:T(128)} %bitcast.rank_ref, ...), custom_call_target="tpu_custom_call" | custom-call | bytes 3145728 | tf_op jit(solution)/shard_map/pallas_call | solution.py:79
  9.2 0.7 collective-permute-start.2
  9.9 1.4 %collective-permute-start.5 = (bf16[4,192,128]{2,1,0:T(8,128)(2,1)S(1)}, bf16[4,192,128]{2,1,0:T(8,128)(2,1)S(1)}, u32[]{:S(2)}, u32[]{:S(2)}) collective-permute-start(bf16[4,192,128]{2,1,0:T(8,128)(2,1)S(1)} %get-tuple-element.55), channel_id=1, source_target_pairs={{0,1},{1,0},{2,3},{3,2},{4,5},{5,4},{6,7},{7,6},{8,9},{9,8},{10,11... | collective-permute-start | bytes 589832 | tf_op jit(solution)/shard_map/ppermute | solution.py:342
  12.0 0.1 reshape.17
  12.1 0.1 reshape.16
  12.3 0.8 %collective-permute-done.refs_1_ = bf16[4,192,128]{2,1,0:T(8,128)(2,1)S(1)} collective-permute-done((bf16[4,192,128]{2,1,0:T(8,128)(2,1)S(1)}, bf16[4,192,128]{2,1,0:T(8,128)(2,1)S(1)}, u32[]{:S(2)}, u32[]{:S(2)}) %collective-permute-start) | collective-permute-done | bytes 196640 | tf_op jit(solution)/shard_map/ppermute | solution.py:342
  13.1 11.0 %collective-permute-done.1.refs_2_ = bf16[4,192,128]{2,1,0:T(8,128)(2,1)S(1)} collective-permute-done((bf16[4,192,128]{2,1,0:T(8,128)(2,1)S(1)}, bf16[4,192,128]{2,1,0:T(8,128)(2,1)S(1)}, u32[]{:S(2)}, u32[]{:S(2)}) %collective-permute-start.1) | collective-permute-done | bytes 196640 | tf_op jit(solution)/shard_map/ppermute | solution.py:342
  24.0 2.6 %collective-permute-start.3 = (bf16[4,192,128]{2,1,0:T(8,128)(2,1)S(1)}, bf16[4,192,128]{2,1,0:T(8,128)(2,1)S(1)}, u32[]{:S(2)}, u32[]{:S(2)}) collective-permute-start(bf16[4,192,128]{2,1,0:T(8,128)(2,1)S(1)} %get-tuple-element.53), channel_id=1, source_target_pairs={{0,3},{1,2},{2,1},{3,0},{4,7},{5,6},{6,5},{7,4},{8,11},{9,10},{10,... | collective-permute-start | bytes 589832 | tf_op jit(solution)/shard_map/ppermute | solution.py:342
  26.7 0.1 pad_add_fusion.scalars
  26.8 10.1 %shard_map.112 = (bf16[3,192,128]{2,1,0:T(8,128)(2,1)S(1)}, bf16[3,192,128]{2,1,0:T(8,128)(2,1)S(1)}, bf16[3,192,128]{2,1,0:T(8,128)(2,1)S(1)}, bf16[3,192,128]{2,1,0:T(8,128)(2,1)S(1)}, f32[2,32,96]{2,1,0:T(8,128)S(1)}) custom-call(s32[2]{0:T(128)S(1)} %pad_add_fusion.scalars, f32[2,31,96]{2,1,0:T(8,128)S(1)} %get-tuple-element.76.weight_ref, ...), custom_call_target="tpu_custom_call" | custom-call | flops 1207959552 | bytes 1376256 | tf_op jit(solution)/shard_map/pallas_call | solution.py:310
  36.9 1.8 %collective-permute-start.8 = (bf16[3,192,128]{2,1,0:T(8,128)(2,1)S(1)}, bf16[3,192,128]{2,1,0:T(8,128)(2,1)S(1)}, u32[]{:S(2)}, u32[]{:S(2)}) collective-permute-start(bf16[3,192,128]{2,1,0:T(8,128)(2,1)S(1)} %get-tuple-element.68), channel_id=1, source_target_pairs={{0,1},{1,0},{2,3},{3,2},{4,5},{5,4},{6,7},{7,6},{8,9},{9,8},{10,11... | collective-permute-start | bytes 442376 | tf_op jit(solution)/shard_map/ppermute | solution.py:342
  38.7 3.0 %collective-permute-done.4.refs_2_ = bf16[4,192,128]{2,1,0:T(8,128)(2,1)S(1)} collective-permute-done((bf16[4,192,128]{2,1,0:T(8,128)(2,1)S(1)}, bf16[4,192,128]{2,1,0:T(8,128)(2,1)S(1)}, u32[]{:S(2)}, u32[]{:S(2)}) %collective-permute-start.4) | collective-permute-done | bytes 196640 | tf_op jit(solution)/shard_map/ppermute | solution.py:342
  41.7 1.7 %collective-permute-start.7 = (bf16[3,192,128]{2,1,0:T(8,128)(2,1)S(1)}, bf16[3,192,128]{2,1,0:T(8,128)(2,1)S(1)}, u32[]{:S(2)}, u32[]{:S(2)}) collective-permute-start(bf16[3,192,128]{2,1,0:T(8,128)(2,1)S(1)} %get-tuple-element.65), channel_id=1, source_target_pairs={{0,3},{1,2},{2,1},{3,0},{4,7},{5,6},{6,5},{7,4},{8,11},{9,10},{10,... | collective-permute-start | bytes 442376 | tf_op jit(solution)/shard_map/ppermute | solution.py:342
  43.4 9.9 %shard_map.113 = (bf16[3,192,128]{2,1,0:T(8,128)(2,1)S(1)}, bf16[3,192,128]{2,1,0:T(8,128)(2,1)S(1)}, bf16[3,192,128]{2,1,0:T(8,128)(2,1)S(1)}, bf16[3,192,128]{2,1,0:T(8,128)(2,1)S(1)}, f32[2,32,96]{2,1,0:T(8,128)S(1)}) custom-call(s32[2]{0:T(128)S(1)} %pad_add_fusion.scalars, f32[2,31,96]{2,1,0:T(8,128)S(1)} %get-tuple-element.75.weight_ref, ...), custom_call_target="tpu_custom_call" | custom-call | flops 1207959552 | bytes 1376256 | tf_op jit(solution)/shard_map/pallas_call | solution.py:310
  53.4 2.1 %collective-permute-start.9 = (bf16[3,192,128]{2,1,0:T(8,128)(2,1)S(1)}, bf16[3,192,128]{2,1,0:T(8,128)(2,1)S(1)}, u32[]{:S(2)}, u32[]{:S(2)}) collective-permute-start(bf16[3,192,128]{2,1,0:T(8,128)(2,1)S(1)} %get-tuple-element.71), channel_id=1, source_target_pairs={{0,2},{1,3},{2,0},{3,1},{4,6},{5,7},{6,4},{7,5},{8,10},{9,11},{10,... | collective-permute-start | bytes 442376 | tf_op jit(solution)/shard_map/ppermute | solution.py:342
  55.6 0.7 %collective-permute-start.11 = (bf16[3,192,128]{2,1,0:T(8,128)(2,1)S(1)}, bf16[3,192,128]{2,1,0:T(8,128)(2,1)S(1)}, u32[]{:S(2)}, u32[]{:S(2)}) collective-permute-start(bf16[3,192,128]{2,1,0:T(8,128)(2,1)S(1)} %get-tuple-element.73), channel_id=1, source_target_pairs={{0,1},{1,0},{2,3},{3,2},{4,5},{5,4},{6,7},{7,6},{8,9},{9,8},{10,11... | collective-permute-start | bytes 442376 | tf_op jit(solution)/shard_map/ppermute | solution.py:342
  56.3 1.7 %collective-permute-start.10 = (bf16[3,192,128]{2,1,0:T(8,128)(2,1)S(1)}, bf16[3,192,128]{2,1,0:T(8,128)(2,1)S(1)}, u32[]{:S(2)}, u32[]{:S(2)}) collective-permute-start(bf16[3,192,128]{2,1,0:T(8,128)(2,1)S(1)} %get-tuple-element.72), channel_id=1, source_target_pairs={{0,3},{1,2},{2,1},{3,0},{4,7},{5,6},{6,5},{7,4},{8,11},{9,10},{10,... | collective-permute-start | bytes 442376 | tf_op jit(solution)/shard_map/ppermute | solution.py:342
  58.0 1.6 %collective-permute-start.13 = (f32[4,32,96]{2,1,0:T(8,128)S(1)}, f32[4,32,96]{2,1,0:T(8,128)S(1)}, u32[]{:S(2)}, u32[]{:S(2)}) collective-permute-start(f32[4,32,96]{2,1,0:T(8,128)S(1)} %add.11), channel_id=1, source_target_pairs={{0,8},{4,12},{8,0},{12,4},{16,24},{20,28},{24,16},{28,20},{1,9},{5... | collective-permute-start | bytes 147464 | tf_op jit(solution)/shard_map/ppermute | solution.py:352
  59.6 2.8 %collective-permute-done.13 = f32[4,32,96]{2,1,0:T(8,128)S(1)} collective-permute-done((f32[4,32,96]{2,1,0:T(8,128)S(1)}, f32[4,32,96]{2,1,0:T(8,128)S(1)}, u32[]{:S(2)}, u32[]{:S(2)}) %collective-permute-start.13) | collective-permute-done | bytes 49184 | tf_op jit(solution)/shard_map/ppermute | solution.py:352
  62.4 1.6 %collective-permute-start.14 = (f32[4,32,96]{2,1,0:T(8,128)S(1)}, f32[4,32,96]{2,1,0:T(8,128)S(1)}, u32[]{:S(2)}, u32[]{:S(2)}) collective-permute-start(f32[4,32,96]{2,1,0:T(8,128)S(1)} %add.12.refs_8_), channel_id=1, source_target_pairs={{0,16},{4,20},{8,24},{12,28},{16,0},{20,4},{24,8},{28,12},{1,17},{... | collective-permute-start | bytes 147464 | tf_op jit(solution)/shard_map/ppermute | solution.py:352
  64.0 3.5 %collective-permute-done.11.refs_7_ = bf16[3,192,128]{2,1,0:T(8,128)(2,1)S(1)} collective-permute-done((bf16[3,192,128]{2,1,0:T(8,128)(2,1)S(1)}, bf16[3,192,128]{2,1,0:T(8,128)(2,1)S(1)}, u32[]{:S(2)}, u32[]{:S(2)}) %collective-permute-start.11) | collective-permute-done | bytes 147488 | tf_op jit(solution)/shard_map/ppermute | solution.py:342
  67.5 1.4 %shard_map.114 = (bf16[1,128,1536]{2,1,0:T(8,128)(2,1)}, bf16[1,128,1536]{2,1,0:T(8,128)(2,1)}, bf16[1,128,1536]{2,1,0:T(8,128)(2,1)}, f32[31,384]{1,0:T(8,128)}, f32[384]{0:T(512)}) custom-call(s32[1]{0:T(128)} %bitcast.rank_ref, bf16[3,192,128]{2,1,0:T(8,128)(2,1)S(1)} %get-tuple-element.49.refs_0_, ...), custom_call_target="tpu_custom_call" | custom-call | bytes 2359296 | tf_op jit(solution)/shard_map/pallas_call | solution.py:128
  (25 shorter events, 0.3 us)
Async XLA Ops:
  2.1 10.9 %collective-permute-start = (bf16[4,192,128]{2,1,0:T(8,128)(2,1)S(1)}, bf16[4,192,128]{2,1,0:T(8,128)(2,1)S(1)}, u32[]{:S(2)}, u32[]{:S(2)}) collective-permute-start(bf16[4,192,128]{2,1,0:T(8,128)(2,1)S(1)} %get-tuple-element.43), channel_id=1, source_target_pairs={{0,3},{1,2},{2,1},{3,0},{4,7},{5,6},{6,5},{7,4},{8,11},{9,10},{10,... | collective-permute-start | bytes 589832 | tf_op jit(solution)/shard_map/ppermute | solution.py:342
  7.2 4.8 %copy-start = (f32[31,1536]{1,0:T(8,128)S(1)}, f32[31,1536]{1,0:T(8,128)}, u32[]{:S(2)}) copy-start(f32[31,1536]{1,0:T(8,128)} %param.11) | copy-start | bytes 571396
  7.2 16.8 %collective-permute-start.1 = (bf16[4,192,128]{2,1,0:T(8,128)(2,1)S(1)}, bf16[4,192,128]{2,1,0:T(8,128)(2,1)S(1)}, u32[]{:S(2)}, u32[]{:S(2)}) collective-permute-start(bf16[4,192,128]{2,1,0:T(8,128)(2,1)S(1)} %get-tuple-element.44), channel_id=1, source_target_pairs={{0,2},{1,3},{2,0},{3,1},{4,6},{5,7},{6,4},{7,5},{8,10},{9,11},{10,... | collective-permute-start | bytes 589832 | tf_op jit(solution)/shard_map/ppermute | solution.py:342
  9.2 2.8 %copy-start.1 = (f32[1536]{0:T(1024)S(1)}, f32[1536]{0:T(1024)}, u32[]{:S(2)}) copy-start(f32[1536]{0:T(1024)} %param.12) | copy-start | bytes 18436
  9.2 14.8 %collective-permute-start.2 = (bf16[4,192,128]{2,1,0:T(8,128)(2,1)S(1)}, bf16[4,192,128]{2,1,0:T(8,128)(2,1)S(1)}, u32[]{:S(2)}, u32[]{:S(2)}) collective-permute-start(bf16[4,192,128]{2,1,0:T(8,128)(2,1)S(1)} %get-tuple-element.45), channel_id=1, source_target_pairs={{0,1},{1,0},{2,3},{3,2},{4,5},{5,4},{6,7},{7,6},{8,9},{9,8},{10,11... | collective-permute-start | bytes 589832 | tf_op jit(solution)/shard_map/ppermute | solution.py:342
  9.9 28.8 %collective-permute-start.5 = (bf16[4,192,128]{2,1,0:T(8,128)(2,1)S(1)}, bf16[4,192,128]{2,1,0:T(8,128)(2,1)S(1)}, u32[]{:S(2)}, u32[]{:S(2)}) collective-permute-start(bf16[4,192,128]{2,1,0:T(8,128)(2,1)S(1)} %get-tuple-element.55), channel_id=1, source_target_pairs={{0,1},{1,0},{2,3},{3,2},{4,5},{5,4},{6,7},{7,6},{8,9},{9,8},{10,11... | collective-permute-start | bytes 589832 | tf_op jit(solution)/shard_map/ppermute | solution.py:342
  24.0 14.7 %collective-permute-start.3 = (bf16[4,192,128]{2,1,0:T(8,128)(2,1)S(1)}, bf16[4,192,128]{2,1,0:T(8,128)(2,1)S(1)}, u32[]{:S(2)}, u32[]{:S(2)}) collective-permute-start(bf16[4,192,128]{2,1,0:T(8,128)(2,1)S(1)} %get-tuple-element.53), channel_id=1, source_target_pairs={{0,3},{1,2},{2,1},{3,0},{4,7},{5,6},{6,5},{7,4},{8,11},{9,10},{10,... | collective-permute-start | bytes 589832 | tf_op jit(solution)/shard_map/ppermute | solution.py:342
  26.7 15.0 %collective-permute-start.4 = (bf16[4,192,128]{2,1,0:T(8,128)(2,1)S(1)}, bf16[4,192,128]{2,1,0:T(8,128)(2,1)S(1)}, u32[]{:S(2)}, u32[]{:S(2)}) collective-permute-start(bf16[4,192,128]{2,1,0:T(8,128)(2,1)S(1)} %get-tuple-element.54), channel_id=1, source_target_pairs={{0,2},{1,3},{2,0},{3,1},{4,6},{5,7},{6,4},{7,5},{8,10},{9,11},{10,... | collective-permute-start | bytes 589832 | tf_op jit(solution)/shard_map/ppermute | solution.py:342
  36.9 16.5 %collective-permute-start.8 = (bf16[3,192,128]{2,1,0:T(8,128)(2,1)S(1)}, bf16[3,192,128]{2,1,0:T(8,128)(2,1)S(1)}, u32[]{:S(2)}, u32[]{:S(2)}) collective-permute-start(bf16[3,192,128]{2,1,0:T(8,128)(2,1)S(1)} %get-tuple-element.68), channel_id=1, source_target_pairs={{0,1},{1,0},{2,3},{3,2},{4,5},{5,4},{6,7},{7,6},{8,9},{9,8},{10,11... | collective-permute-start | bytes 442376 | tf_op jit(solution)/shard_map/ppermute | solution.py:342
  41.7 13.8 %collective-permute-start.6 = (bf16[3,192,128]{2,1,0:T(8,128)(2,1)S(1)}, bf16[3,192,128]{2,1,0:T(8,128)(2,1)S(1)}, u32[]{:S(2)}, u32[]{:S(2)}) collective-permute-start(bf16[3,192,128]{2,1,0:T(8,128)(2,1)S(1)} %get-tuple-element.62), channel_id=1, source_target_pairs={{0,2},{1,3},{2,0},{3,1},{4,6},{5,7},{6,4},{7,5},{8,10},{9,11},{10,... | collective-permute-start | bytes 442376 | tf_op jit(solution)/shard_map/ppermute | solution.py:342
  41.7 14.6 %collective-permute-start.7 = (bf16[3,192,128]{2,1,0:T(8,128)(2,1)S(1)}, bf16[3,192,128]{2,1,0:T(8,128)(2,1)S(1)}, u32[]{:S(2)}, u32[]{:S(2)}) collective-permute-start(bf16[3,192,128]{2,1,0:T(8,128)(2,1)S(1)} %get-tuple-element.65), channel_id=1, source_target_pairs={{0,3},{1,2},{2,1},{3,0},{4,7},{5,6},{6,5},{7,4},{8,11},{9,10},{10,... | collective-permute-start | bytes 442376 | tf_op jit(solution)/shard_map/ppermute | solution.py:342
  53.4 10.6 %collective-permute-start.9 = (bf16[3,192,128]{2,1,0:T(8,128)(2,1)S(1)}, bf16[3,192,128]{2,1,0:T(8,128)(2,1)S(1)}, u32[]{:S(2)}, u32[]{:S(2)}) collective-permute-start(bf16[3,192,128]{2,1,0:T(8,128)(2,1)S(1)} %get-tuple-element.71), channel_id=1, source_target_pairs={{0,2},{1,3},{2,0},{3,1},{4,6},{5,7},{6,4},{7,5},{8,10},{9,11},{10,... | collective-permute-start | bytes 442376 | tf_op jit(solution)/shard_map/ppermute | solution.py:342
  55.5 2.5 %collective-permute-start.12 = (f32[4,32,96]{2,1,0:T(8,128)S(1)}, f32[4,32,96]{2,1,0:T(8,128)S(1)}, u32[]{:S(2)}, u32[]{:S(2)}) collective-permute-start(f32[4,32,96]{2,1,0:T(8,128)S(1)} %pad_maximum_fusion), channel_id=1, source_target_pairs={{0,4},{4,0},{8,12},{12,8},{16,20},{20,16},{24,28},{28,24},{1,5},{5... | collective-permute-start | bytes 147464 | tf_op jit(solution)/shard_map/ppermute | solution.py:352
  55.6 11.9 %collective-permute-start.11 = (bf16[3,192,128]{2,1,0:T(8,128)(2,1)S(1)}, bf16[3,192,128]{2,1,0:T(8,128)(2,1)S(1)}, u32[]{:S(2)}, u32[]{:S(2)}) collective-permute-start(bf16[3,192,128]{2,1,0:T(8,128)(2,1)S(1)} %get-tuple-element.73), channel_id=1, source_target_pairs={{0,1},{1,0},{2,3},{3,2},{4,5},{5,4},{6,7},{7,6},{8,9},{9,8},{10,11... | collective-permute-start | bytes 442376 | tf_op jit(solution)/shard_map/ppermute | solution.py:342
  56.3 11.2 %collective-permute-start.10 = (bf16[3,192,128]{2,1,0:T(8,128)(2,1)S(1)}, bf16[3,192,128]{2,1,0:T(8,128)(2,1)S(1)}, u32[]{:S(2)}, u32[]{:S(2)}) collective-permute-start(bf16[3,192,128]{2,1,0:T(8,128)(2,1)S(1)} %get-tuple-element.72), channel_id=1, source_target_pairs={{0,3},{1,2},{2,1},{3,0},{4,7},{5,6},{6,5},{7,4},{8,11},{9,10},{10,... | collective-permute-start | bytes 442376 | tf_op jit(solution)/shard_map/ppermute | solution.py:342
  58.0 4.3 %collective-permute-start.13 = (f32[4,32,96]{2,1,0:T(8,128)S(1)}, f32[4,32,96]{2,1,0:T(8,128)S(1)}, u32[]{:S(2)}, u32[]{:S(2)}) collective-permute-start(f32[4,32,96]{2,1,0:T(8,128)S(1)} %add.11), channel_id=1, source_target_pairs={{0,8},{4,12},{8,0},{12,4},{16,24},{20,28},{24,16},{28,20},{1,9},{5... | collective-permute-start | bytes 147464 | tf_op jit(solution)/shard_map/ppermute | solution.py:352
  62.4 5.1 %collective-permute-start.14 = (f32[4,32,96]{2,1,0:T(8,128)S(1)}, f32[4,32,96]{2,1,0:T(8,128)S(1)}, u32[]{:S(2)}, u32[]{:S(2)}) collective-permute-start(f32[4,32,96]{2,1,0:T(8,128)S(1)} %add.12.refs_8_), channel_id=1, source_target_pairs={{0,16},{4,20},{8,24},{12,28},{16,0},{20,4},{24,8},{28,12},{1,17},{... | collective-permute-start | bytes 147464 | tf_op jit(solution)/shard_map/ppermute | solution.py:352

commit v16 on v15

--- a/solution.py
+++ b/solution.py
@@ -379,9 +379,9 @@
             order.append(exchanged(grads, order[-1], False))
     before, grads, taps = order[-1], list(grads), jnp.concatenate(taps, axis=0)
     last = count - 1
-    grads[last - 1], before[1] = lax.optimization_barrier((grads[last - 1], before[1]))
+    grads[1], before[1] = lax.optimization_barrier((grads[1], before[1]))
     if last > 2:
-        (grads[1], taps), before[2] = lax.optimization_barrier(((grads[1], taps), before[2]))
+        (grads[2], taps), before[2] = lax.optimization_barrier(((grads[2], taps), before[2]))
         grads[last], before[last] = lax.optimization_barrier((grads[last], before[last]))
     order.append(exchanged(grads, None, False))
     return unpack(rank[None], doubled(taps, "dp"), order[chunks:], count, chunks)

time: 69.1 us -> 70.9 us (1.026)
  waiting for transfers between devices: 21.1 us -> 22.5 us
    ppermute x12, waiting for transfers between devices: 18.3 us -> 19.7 us  [exchanged(): moved[distance] = lax.ppermute(pieces[distance], 'seq', pairs)]
  transfers between devices with their start and end apart: 15 -> 15, of which waited for: 6 -> 5; matrix products, arithmetic and copies ran while one was open for 1% -> 0% of each run, Pallas kernels for 32% -> 31%
where the time goes in v16:
time: 70.9 us; the launch traced here: 70.3 us
  Pallas kernels  24.9 us (35%)
  waiting for transfers between devices  22.5 us (32%)
  starting transfers between devices  21.1 us (30%)
  between operations  1.43 us (2%)
    pallas_call x2, Pallas kernels, core(): pl.pallas_call(functools.partial(core_kernel, count, block), out_shape=(p...  20.1 us
    ppermute x12, waiting for transfers between devices, exchanged(): moved[distance] = lax.ppermute(pieces[distance], 'seq', pairs)  19.7 us
    ppermute x12, starting transfers between devices, exchanged(): moved[distance] = lax.ppermute(pieces[distance], 'seq', pairs)  17.9 us
    ppermute x3, starting transfers between devices, doubled(): pair = (total, lax.ppermute(total, axis, pairs))  3.22 us
    ppermute x3, waiting for transfers between devices, doubled(): pair = (total, lax.ppermute(total, axis, pairs))  2.77 us
    pallas_call x1, Pallas kernels, pack(): pl.pallas_call(functools.partial(pack_kernel, wanted, share), out_shape=(...  1.96 us
    pallas_call x1, Pallas kernels, pack(): pl.pallas_call(functools.partial(pack_first_kernel, far, share), out_shap...  1.49 us
  transfers between devices with their start and end apart: 15, of which 5 were waited for; matrix products, arithmetic and copies ran while one was open for 0% of the time, Pallas kernels for 31%

profile of v16, /device:TPU:0, one launch (start us, length us, event | category | flops | bytes accessed | tf_op | source)
XLA Modules:
  0.0 70.3 jit_solution(2354508614498117150)
XLA Ops:
  0.6 1.5 %shard_map.111 = (bf16[4,192,128]{2,1,0:T(8,128)(2,1)S(1)}, bf16[4,192,128]{2,1,0:T(8,128)(2,1)S(1)}) custom-call(s32[1]{0:T(128)} %bitcast.rank_ref, bf16[1,128,1536]{2,1,0:T(8,128)(2,1)} %refs_0_.3, bf16[1,128,1536]{2,1,0:T(8,128)(2,1)} %refs_1_.3, bf16[1,128,1536]{2,1,0:T(8,128)(2,1)} %refs_2_.3, bf16[1,128,1536]{2,1,0:T(8,128)(2,1)} %refs_3_.3), custom_call_target="tpu_custom_call" | custom-call | bytes 1048576 | tf_op jit(solution)/shard_map/pallas_call | solution.py:62
  2.1 5.1 %collective-permute-start = (bf16[4,192,128]{2,1,0:T(8,128)(2,1)S(1)}, bf16[4,192,128]{2,1,0:T(8,128)(2,1)S(1)}, u32[]{:S(2)}, u32[]{:S(2)}) collective-permute-start(bf16[4,192,128]{2,1,0:T(8,128)(2,1)S(1)} %get-tuple-element.43), channel_id=1, source_target_pairs={{0,3},{1,2},{2,1},{3,0},{4,7},{5,6},{6,5},{7,4},{8,11},{9,10},{10,... | collective-permute-start | bytes 589832 | tf_op jit(solution)/shard_map/ppermute | solution.py:342
  7.2 2.0 %shard_map.110 = (bf16[4,192,128]{2,1,0:T(8,128)(2,1)S(1)}, bf16[4,192,128]{2,1,0:T(8,128)(2,1)S(1)}, bf16[4,192,128]{2,1,0:T(8,128)(2,1)S(1)}, bf16[4,192,128]{...) custom-call(s32[1]{0:T(128)} %bitcast.rank_ref, ...), custom_call_target="tpu_custom_call" | custom-call | bytes 3145728 | tf_op jit(solution)/shard_map/pallas_call | solution.py:79
  9.2 0.7 collective-permute-start.2
  9.9 1.4 %collective-permute-start.5 = (bf16[4,192,128]{2,1,0:T(8,128)(2,1)S(1)}, bf16[4,192,128]{2,1,0:T(8,128)(2,1)S(1)}, u32[]{:S(2)}, u32[]{:S(2)}) collective-permute-start(bf16[4,192,128]{2,1,0:T(8,128)(2,1)S(1)} %get-tuple-element.55), channel_id=1, source_target_pairs={{0,1},{1,0},{2,3},{3,2},{4,5},{5,4},{6,7},{7,6},{8,9},{9,8},{10,11... | collective-permute-start | bytes 589832 | tf_op jit(solution)/shard_map/ppermute | solution.py:342
  12.0 0.1 reshape.17
  12.1 0.1 reshape.16
  12.3 0.8 %collective-permute-done.refs_1_ = bf16[4,192,128]{2,1,0:T(8,128)(2,1)S(1)} collective-permute-done((bf16[4,192,128]{2,1,0:T(8,128)(2,1)S(1)}, bf16[4,192,128]{2,1,0:T(8,128)(2,1)S(1)}, u32[]{:S(2)}, u32[]{:S(2)}) %collective-permute-start) | collective-permute-done | bytes 196640 | tf_op jit(solution)/shard_map/ppermute | solution.py:342
  13.1 11.0 %collective-permute-done.1.refs_2_ = bf16[4,192,128]{2,1,0:T(8,128)(2,1)S(1)} collective-permute-done((bf16[4,192,128]{2,1,0:T(8,128)(2,1)S(1)}, bf16[4,192,128]{2,1,0:T(8,128)(2,1)S(1)}, u32[]{:S(2)}, u32[]{:S(2)}) %collective-permute-start.1) | collective-permute-done | bytes 196640 | tf_op jit(solution)/shard_map/ppermute | solution.py:342
  24.0 2.6 %collective-permute-start.3 = (bf16[4,192,128]{2,1,0:T(8,128)(2,1)S(1)}, bf16[4,192,128]{2,1,0:T(8,128)(2,1)S(1)}, u32[]{:S(2)}, u32[]{:S(2)}) collective-permute-start(bf16[4,192,128]{2,1,0:T(8,128)(2,1)S(1)} %get-tuple-element.53), channel_id=1, source_target_pairs={{0,3},{1,2},{2,1},{3,0},{4,7},{5,6},{6,5},{7,4},{8,11},{9,10},{10,... | collective-permute-start | bytes 589832 | tf_op jit(solution)/shard_map/ppermute | solution.py:342
  26.7 0.1 pad_add_fusion.scalars
  26.8 10.1 %shard_map.112 = (bf16[3,192,128]{2,1,0:T(8,128)(2,1)S(1)}, bf16[3,192,128]{2,1,0:T(8,128)(2,1)S(1)}, bf16[3,192,128]{2,1,0:T(8,128)(2,1)S(1)}, bf16[3,192,128]{2,1,0:T(8,128)(2,1)S(1)}, f32[2,32,96]{2,1,0:T(8,128)S(1)}) custom-call(s32[2]{0:T(128)S(1)} %pad_add_fusion.scalars, f32[2,31,96]{2,1,0:T(8,128)S(1)} %get-tuple-element.76.weight_ref, ...), custom_call_target="tpu_custom_call" | custom-call | flops 1207959552 | bytes 1376256 | tf_op jit(solution)/shard_map/pallas_call | solution.py:310
  36.9 1.8 %collective-permute-start.8 = (bf16[3,192,128]{2,1,0:T(8,128)(2,1)S(1)}, bf16[3,192,128]{2,1,0:T(8,128)(2,1)S(1)}, u32[]{:S(2)}, u32[]{:S(2)}) collective-permute-start(bf16[3,192,128]{2,1,0:T(8,128)(2,1)S(1)} %get-tuple-element.68), channel_id=1, source_target_pairs={{0,1},{1,0},{2,3},{3,2},{4,5},{5,4},{6,7},{7,6},{8,9},{9,8},{10,11... | collective-permute-start | bytes 442376 | tf_op jit(solution)/shard_map/ppermute | solution.py:342
  38.7 3.0 %collective-permute-done.4.refs_2_ = bf16[4,192,128]{2,1,0:T(8,128)(2,1)S(1)} collective-permute-done((bf16[4,192,128]{2,1,0:T(8,128)(2,1)S(1)}, bf16[4,192,128]{2,1,0:T(8,128)(2,1)S(1)}, u32[]{:S(2)}, u32[]{:S(2)}) %collective-permute-start.4) | collective-permute-done | bytes 196640 | tf_op jit(solution)/shard_map/ppermute | solution.py:342
  41.7 1.7 %collective-permute-start.7 = (bf16[3,192,128]{2,1,0:T(8,128)(2,1)S(1)}, bf16[3,192,128]{2,1,0:T(8,128)(2,1)S(1)}, u32[]{:S(2)}, u32[]{:S(2)}) collective-permute-start(bf16[3,192,128]{2,1,0:T(8,128)(2,1)S(1)} %get-tuple-element.65), channel_id=1, source_target_pairs={{0,3},{1,2},{2,1},{3,0},{4,7},{5,6},{6,5},{7,4},{8,11},{9,10},{10,... | collective-permute-start | bytes 442376 | tf_op jit(solution)/shard_map/ppermute | solution.py:342
  43.4 9.9 %shard_map.113 = (bf16[3,192,128]{2,1,0:T(8,128)(2,1)S(1)}, bf16[3,192,128]{2,1,0:T(8,128)(2,1)S(1)}, bf16[3,192,128]{2,1,0:T(8,128)(2,1)S(1)}, bf16[3,192,128]{2,1,0:T(8,128)(2,1)S(1)}, f32[2,32,96]{2,1,0:T(8,128)S(1)}) custom-call(s32[2]{0:T(128)S(1)} %pad_add_fusion.scalars, f32[2,31,96]{2,1,0:T(8,128)S(1)} %get-tuple-element.75.weight_ref, ...), custom_call_target="tpu_custom_call" | custom-call | flops 1207959552 | bytes 1376256 | tf_op jit(solution)/shard_map/pallas_call | solution.py:310
  53.4 1.9 %collective-permute-start.11 = (bf16[3,192,128]{2,1,0:T(8,128)(2,1)S(1)}, bf16[3,192,128]{2,1,0:T(8,128)(2,1)S(1)}, u32[]{:S(2)}, u32[]{:S(2)}) collective-permute-start(bf16[3,192,128]{2,1,0:T(8,128)(2,1)S(1)} %get-tuple-element.73), channel_id=1, source_target_pairs={{0,1},{1,0},{2,3},{3,2},{4,5},{5,4},{6,7},{7,6},{8,9},{9,8},{10,11... | collective-permute-start | bytes 442376 | tf_op jit(solution)/shard_map/ppermute | solution.py:342
  55.3 1.0 %collective-permute-start.9 = (bf16[3,192,128]{2,1,0:T(8,128)(2,1)S(1)}, bf16[3,192,128]{2,1,0:T(8,128)(2,1)S(1)}, u32[]{:S(2)}, u32[]{:S(2)}) collective-permute-start(bf16[3,192,128]{2,1,0:T(8,128)(2,1)S(1)} %get-tuple-element.71), channel_id=1, source_target_pairs={{0,2},{1,3},{2,0},{3,1},{4,6},{5,7},{6,4},{7,5},{8,10},{9,11},{10,... | collective-permute-start | bytes 442376 | tf_op jit(solution)/shard_map/ppermute | solution.py:342
  56.3 1.7 %collective-permute-start.10 = (bf16[3,192,128]{2,1,0:T(8,128)(2,1)S(1)}, bf16[3,192,128]{2,1,0:T(8,128)(2,1)S(1)}, u32[]{:S(2)}, u32[]{:S(2)}) collective-permute-start(bf16[3,192,128]{2,1,0:T(8,128)(2,1)S(1)} %get-tuple-element.72), channel_id=1, source_target_pairs={{0,3},{1,2},{2,1},{3,0},{4,7},{5,6},{6,5},{7,4},{8,11},{9,10},{10,... | collective-permute-start | bytes 442376 | tf_op jit(solution)/shard_map/ppermute | solution.py:342
  58.0 1.6 %collective-permute-start.13 = (f32[4,32,96]{2,1,0:T(8,128)S(1)}, f32[4,32,96]{2,1,0:T(8,128)S(1)}, u32[]{:S(2)}, u32[]{:S(2)}) collective-permute-start(f32[4,32,96]{2,1,0:T(8,128)S(1)} %add.11), channel_id=1, source_target_pairs={{0,8},{4,12},{8,0},{12,4},{16,24},{20,28},{24,16},{28,20},{1,9},{5... | collective-permute-start | bytes 147464 | tf_op jit(solution)/shard_map/ppermute | solution.py:352
  59.6 2.8 %collective-permute-done.13 = f32[4,32,96]{2,1,0:T(8,128)S(1)} collective-permute-done((f32[4,32,96]{2,1,0:T(8,128)S(1)}, f32[4,32,96]{2,1,0:T(8,128)S(1)}, u32[]{:S(2)}, u32[]{:S(2)}) %collective-permute-start.13) | collective-permute-done | bytes 49184 | tf_op jit(solution)/shard_map/ppermute | solution.py:352
  62.4 1.6 %collective-permute-start.14 = (f32[4,32,96]{2,1,0:T(8,128)S(1)}, f32[4,32,96]{2,1,0:T(8,128)S(1)}, u32[]{:S(2)}, u32[]{:S(2)}) collective-permute-start(f32[4,32,96]{2,1,0:T(8,128)S(1)} %add.12.refs_8_), channel_id=1, source_target_pairs={{0,16},{4,20},{8,24},{12,28},{16,0},{20,4},{24,8},{28,12},{1,17},{... | collective-permute-start | bytes 147464 | tf_op jit(solution)/shard_map/ppermute | solution.py:352
  64.0 4.9 %collective-permute-done.9.refs_5_ = bf16[3,192,128]{2,1,0:T(8,128)(2,1)S(1)} collective-permute-done((bf16[3,192,128]{2,1,0:T(8,128)(2,1)S(1)}, bf16[3,192,128]{2,1,0:T(8,128)(2,1)S(1)}, u32[]{:S(2)}, u32[]{:S(2)}) %collective-permute-start.9) | collective-permute-done | bytes 147488 | tf_op jit(solution)/shard_map/ppermute | solution.py:342
  68.9 1.4 %shard_map.114 = (bf16[1,128,1536]{2,1,0:T(8,128)(2,1)}, bf16[1,128,1536]{2,1,0:T(8,128)(2,1)}, bf16[1,128,1536]{2,1,0:T(8,128)(2,1)}, f32[31,384]{1,0:T(8,128)}, f32[384]{0:T(512)}) custom-call(s32[1]{0:T(128)} %bitcast.rank_ref, bf16[3,192,128]{2,1,0:T(8,128)(2,1)S(1)} %get-tuple-element.49.refs_0_, ...), custom_call_target="tpu_custom_call" | custom-call | bytes 2359296 | tf_op jit(solution)/shard_map/pallas_call | solution.py:128
  (25 shorter events, 0.2 us)
Async XLA Ops:
  2.1 10.9 %collective-permute-start = (bf16[4,192,128]{2,1,0:T(8,128)(2,1)S(1)}, bf16[4,192,128]{2,1,0:T(8,128)(2,1)S(1)}, u32[]{:S(2)}, u32[]{:S(2)}) collective-permute-start(bf16[4,192,128]{2,1,0:T(8,128)(2,1)S(1)} %get-tuple-element.43), channel_id=1, source_target_pairs={{0,3},{1,2},{2,1},{3,0},{4,7},{5,6},{6,5},{7,4},{8,11},{9,10},{10,... | collective-permute-start | bytes 589832 | tf_op jit(solution)/shard_map/ppermute | solution.py:342
  7.2 4.8 %copy-start = (f32[31,1536]{1,0:T(8,128)S(1)}, f32[31,1536]{1,0:T(8,128)}, u32[]{:S(2)}) copy-start(f32[31,1536]{1,0:T(8,128)} %param.11) | copy-start | bytes 571396
  7.2 16.8 %collective-permute-start.1 = (bf16[4,192,128]{2,1,0:T(8,128)(2,1)S(1)}, bf16[4,192,128]{2,1,0:T(8,128)(2,1)S(1)}, u32[]{:S(2)}, u32[]{:S(2)}) collective-permute-start(bf16[4,192,128]{2,1,0:T(8,128)(2,1)S(1)} %get-tuple-element.44), channel_id=1, source_target_pairs={{0,2},{1,3},{2,0},{3,1},{4,6},{5,7},{6,4},{7,5},{8,10},{9,11},{10,... | collective-permute-start | bytes 589832 | tf_op jit(solution)/shard_map/ppermute | solution.py:342
  9.2 2.8 %copy-start.1 = (f32[1536]{0:T(1024)S(1)}, f32[1536]{0:T(1024)}, u32[]{:S(2)}) copy-start(f32[1536]{0:T(1024)} %param.12) | copy-start | bytes 18436
  9.2 14.8 %collective-permute-start.2 = (bf16[4,192,128]{2,1,0:T(8,128)(2,1)S(1)}, bf16[4,192,128]{2,1,0:T(8,128)(2,1)S(1)}, u32[]{:S(2)}, u32[]{:S(2)}) collective-permute-start(bf16[4,192,128]{2,1,0:T(8,128)(2,1)S(1)} %get-tuple-element.45), channel_id=1, source_target_pairs={{0,1},{1,0},{2,3},{3,2},{4,5},{5,4},{6,7},{7,6},{8,9},{9,8},{10,11... | collective-permute-start | bytes 589832 | tf_op jit(solution)/shard_map/ppermute | solution.py:342
  9.9 28.8 %collective-permute-start.5 = (bf16[4,192,128]{2,1,0:T(8,128)(2,1)S(1)}, bf16[4,192,128]{2,1,0:T(8,128)(2,1)S(1)}, u32[]{:S(2)}, u32[]{:S(2)}) collective-permute-start(bf16[4,192,128]{2,1,0:T(8,128)(2,1)S(1)} %get-tuple-element.55), channel_id=1, source_target_pairs={{0,1},{1,0},{2,3},{3,2},{4,5},{5,4},{6,7},{7,6},{8,9},{9,8},{10,11... | collective-permute-start | bytes 589832 | tf_op jit(solution)/shard_map/ppermute | solution.py:342
  24.0 14.7 %collective-permute-start.3 = (bf16[4,192,128]{2,1,0:T(8,128)(2,1)S(1)}, bf16[4,192,128]{2,1,0:T(8,128)(2,1)S(1)}, u32[]{:S(2)}, u32[]{:S(2)}) collective-permute-start(bf16[4,192,128]{2,1,0:T(8,128)(2,1)S(1)} %get-tuple-element.53), channel_id=1, source_target_pairs={{0,3},{1,2},{2,1},{3,0},{4,7},{5,6},{6,5},{7,4},{8,11},{9,10},{10,... | collective-permute-start | bytes 589832 | tf_op jit(solution)/shard_map/ppermute | solution.py:342
  26.7 15.0 %collective-permute-start.4 = (bf16[4,192,128]{2,1,0:T(8,128)(2,1)S(1)}, bf16[4,192,128]{2,1,0:T(8,128)(2,1)S(1)}, u32[]{:S(2)}, u32[]{:S(2)}) collective-permute-start(bf16[4,192,128]{2,1,0:T(8,128)(2,1)S(1)} %get-tuple-element.54), channel_id=1, source_target_pairs={{0,2},{1,3},{2,0},{3,1},{4,6},{5,7},{6,4},{7,5},{8,10},{9,11},{10,... | collective-permute-start | bytes 589832 | tf_op jit(solution)/shard_map/ppermute | solution.py:342
  36.9 16.5 %collective-permute-start.8 = (bf16[3,192,128]{2,1,0:T(8,128)(2,1)S(1)}, bf16[3,192,128]{2,1,0:T(8,128)(2,1)S(1)}, u32[]{:S(2)}, u32[]{:S(2)}) collective-permute-start(bf16[3,192,128]{2,1,0:T(8,128)(2,1)S(1)} %get-tuple-element.68), channel_id=1, source_target_pairs={{0,1},{1,0},{2,3},{3,2},{4,5},{5,4},{6,7},{7,6},{8,9},{9,8},{10,11... | collective-permute-start | bytes 442376 | tf_op jit(solution)/shard_map/ppermute | solution.py:342
  41.7 13.5 %collective-permute-start.6 = (bf16[3,192,128]{2,1,0:T(8,128)(2,1)S(1)}, bf16[3,192,128]{2,1,0:T(8,128)(2,1)S(1)}, u32[]{:S(2)}, u32[]{:S(2)}) collective-permute-start(bf16[3,192,128]{2,1,0:T(8,128)(2,1)S(1)} %get-tuple-element.62), channel_id=1, source_target_pairs={{0,2},{1,3},{2,0},{3,1},{4,6},{5,7},{6,4},{7,5},{8,10},{9,11},{10,... | collective-permute-start | bytes 442376 | tf_op jit(solution)/shard_map/ppermute | solution.py:342
  41.7 14.6 %collective-permute-start.7 = (bf16[3,192,128]{2,1,0:T(8,128)(2,1)S(1)}, bf16[3,192,128]{2,1,0:T(8,128)(2,1)S(1)}, u32[]{:S(2)}, u32[]{:S(2)}) collective-permute-start(bf16[3,192,128]{2,1,0:T(8,128)(2,1)S(1)} %get-tuple-element.65), channel_id=1, source_target_pairs={{0,3},{1,2},{2,1},{3,0},{4,7},{5,6},{6,5},{7,4},{8,11},{9,10},{10,... | collective-permute-start | bytes 442376 | tf_op jit(solution)/shard_map/ppermute | solution.py:342
  53.4 10.6 %collective-permute-start.11 = (bf16[3,192,128]{2,1,0:T(8,128)(2,1)S(1)}, bf16[3,192,128]{2,1,0:T(8,128)(2,1)S(1)}, u32[]{:S(2)}, u32[]{:S(2)}) collective-permute-start(bf16[3,192,128]{2,1,0:T(8,128)(2,1)S(1)} %get-tuple-element.73), channel_id=1, source_target_pairs={{0,1},{1,0},{2,3},{3,2},{4,5},{5,4},{6,7},{7,6},{8,9},{9,8},{10,11... | collective-permute-start | bytes 442376 | tf_op jit(solution)/shard_map/ppermute | solution.py:342
  55.3 2.7 %collective-permute-start.12 = (f32[4,32,96]{2,1,0:T(8,128)S(1)}, f32[4,32,96]{2,1,0:T(8,128)S(1)}, u32[]{:S(2)}, u32[]{:S(2)}) collective-permute-start(f32[4,32,96]{2,1,0:T(8,128)S(1)} %pad_maximum_fusion), channel_id=1, source_target_pairs={{0,4},{4,0},{8,12},{12,8},{16,20},{20,16},{24,28},{28,24},{1,5},{5... | collective-permute-start | bytes 147464 | tf_op jit(solution)/shard_map/ppermute | solution.py:352
  55.3 13.5 %collective-permute-start.9 = (bf16[3,192,128]{2,1,0:T(8,128)(2,1)S(1)}, bf16[3,192,128]{2,1,0:T(8,128)(2,1)S(1)}, u32[]{:S(2)}, u32[]{:S(2)}) collective-permute-start(bf16[3,192,128]{2,1,0:T(8,128)(2,1)S(1)} %get-tuple-element.71), channel_id=1, source_target_pairs={{0,2},{1,3},{2,0},{3,1},{4,6},{5,7},{6,4},{7,5},{8,10},{9,11},{10,... | collective-permute-start | bytes 442376 | tf_op jit(solution)/shard_map/ppermute | solution.py:342
  56.3 12.6 %collective-permute-start.10 = (bf16[3,192,128]{2,1,0:T(8,128)(2,1)S(1)}, bf16[3,192,128]{2,1,0:T(8,128)(2,1)S(1)}, u32[]{:S(2)}, u32[]{:S(2)}) collective-permute-start(bf16[3,192,128]{2,1,0:T(8,128)(2,1)S(1)} %get-tuple-element.72), channel_id=1, source_target_pairs={{0,3},{1,2},{2,1},{3,0},{4,7},{5,6},{6,5},{7,4},{8,11},{9,10},{10,... | collective-permute-start | bytes 442376 | tf_op jit(solution)/shard_map/ppermute | solution.py:342
  58.0 4.3 %collective-permute-start.13 = (f32[4,32,96]{2,1,0:T(8,128)S(1)}, f32[4,32,96]{2,1,0:T(8,128)S(1)}, u32[]{:S(2)}, u32[]{:S(2)}) collective-permute-start(f32[4,32,96]{2,1,0:T(8,128)S(1)} %add.11), channel_id=1, source_target_pairs={{0,8},{4,12},{8,0},{12,4},{16,24},{20,28},{24,16},{28,20},{1,9},{5... | collective-permute-start | bytes 147464 | tf_op jit(solution)/shard_map/ppermute | solution.py:352
  62.4 6.5 %collective-permute-start.14 = (f32[4,32,96]{2,1,0:T(8,128)S(1)}, f32[4,32,96]{2,1,0:T(8,128)S(1)}, u32[]{:S(2)}, u32[]{:S(2)}) collective-permute-start(f32[4,32,96]{2,1,0:T(8,128)S(1)} %add.12.refs_8_), channel_id=1, source_target_pairs={{0,16},{4,20},{8,24},{12,28},{16,0},{20,4},{24,8},{28,12},{1,17},{... | collective-permute-start | bytes 147464 | tf_op jit(solution)/shard_map/ppermute | solution.py:352

commit v17 on v15

--- a/solution.py
+++ b/solution.py
@@ -204,7 +204,7 @@
         for s in range(8):
             shifted[s] = padded[s : s + tall - 8, :].reshape(tall // 8 - 1, 8, depth)
 
-    step_tiles = 8
+    step_tiles = 4
     step_rows = 8 * step_tiles
 
     def window(index, offset):

time: 69.1 us -> 69.5 us (level)
  Pallas kernels: 24.9 us -> 26.4 us
  waiting for transfers between devices: 21.1 us -> 20 us
    pallas_call x2, Pallas kernels: 20.1 us -> 21.6 us  [core(): pl.pallas_call(functools.partial(core_kernel, count, block), out_shape=(p...]
    ppermute x12, waiting for transfers between devices: 18.3 us -> 17.2 us  [exchanged(): moved[distance] = lax.ppermute(pieces[distance], 'seq', pairs)]
  transfers between devices with their start and end apart: 15 -> 15, of which waited for: 6 -> 5; matrix products, arithmetic and copies ran while one was open for 1% -> 1% of each run, Pallas kernels for 32% -> 34%
where the time goes in v17:
time: 69.5 us; the launch traced here: 69.3 us
  Pallas kernels  26.4 us (38%)
  starting transfers between devices  21.1 us (30%)
  waiting for transfers between devices  20 us (29%)
  between operations  1.43 us (2%)
    pallas_call x2, Pallas kernels, core(): pl.pallas_call(functools.partial(core_kernel, count, block), out_shape=(p...  21.6 us
    ppermute x12, starting transfers between devices, exchanged(): moved[distance] = lax.ppermute(pieces[distance], 'seq', pairs)  17.9 us
    ppermute x12, waiting for transfers between devices, exchanged(): moved[distance] = lax.ppermute(pieces[distance], 'seq', pairs)  17.2 us
    ppermute x3, starting transfers between devices, doubled(): pair = (total, lax.ppermute(total, axis, pairs))  3.21 us
    ppermute x3, waiting for transfers between devices, doubled(): pair = (total, lax.ppermute(total, axis, pairs))  2.78 us
    pallas_call x1, Pallas kernels, pack(): pl.pallas_call(functools.partial(pack_kernel, wanted, share), out_shape=(...  1.96 us
    pallas_call x1, Pallas kernels, pack(): pl.pallas_call(functools.partial(pack_first_kernel, far, share), out_shap...  1.49 us
  transfers between devices with their start and end apart: 15, of which 5 were waited for; matrix products, arithmetic and copies ran while one was open for 1% of the time, Pallas kernels for 34%

profile of v17, /device:TPU:0, one launch (start us, length us, event | category | flops | bytes accessed | tf_op | source)
XLA Modules:
  0.0 69.3 jit_solution(8779302839430284241)
XLA Ops:
  0.6 1.5 %shard_map.111 = (bf16[4,192,128]{2,1,0:T(8,128)(2,1)S(1)}, bf16[4,192,128]{2,1,0:T(8,128)(2,1)S(1)}) custom-call(s32[1]{0:T(128)} %bitcast.rank_ref, bf16[1,128,1536]{2,1,0:T(8,128)(2,1)} %refs_0_.3, bf16[1,128,1536]{2,1,0:T(8,128)(2,1)} %refs_1_.3, bf16[1,128,1536]{2,1,0:T(8,128)(2,1)} %refs_2_.3, bf16[1,128,1536]{2,1,0:T(8,128)(2,1)} %refs_3_.3), custom_call_target="tpu_custom_call" | custom-call | bytes 1048576 | tf_op jit(solution)/shard_map/pallas_call | solution.py:62
  2.1 5.1 %collective-permute-start = (bf16[4,192,128]{2,1,0:T(8,128)(2,1)S(1)}, bf16[4,192,128]{2,1,0:T(8,128)(2,1)S(1)}, u32[]{:S(2)}, u32[]{:S(2)}) collective-permute-start(bf16[4,192,128]{2,1,0:T(8,128)(2,1)S(1)} %get-tuple-element.43), channel_id=1, source_target_pairs={{0,3},{1,2},{2,1},{3,0},{4,7},{5,6},{6,5},{7,4},{8,11},{9,10},{10,... | collective-permute-start | bytes 589832 | tf_op jit(solution)/shard_map/ppermute | solution.py:342
  7.2 2.0 %shard_map.110 = (bf16[4,192,128]{2,1,0:T(8,128)(2,1)S(1)}, bf16[4,192,128]{2,1,0:T(8,128)(2,1)S(1)}, bf16[4,192,128]{2,1,0:T(8,128)(2,1)S(1)}, bf16[4,192,128]{...) custom-call(s32[1]{0:T(128)} %bitcast.rank_ref, ...), custom_call_target="tpu_custom_call" | custom-call | bytes 3145728 | tf_op jit(solution)/shard_map/pallas_call | solution.py:79
  9.2 0.7 collective-permute-start.2
  9.9 1.4 %collective-permute-start.5 = (bf16[4,192,128]{2,1,0:T(8,128)(2,1)S(1)}, bf16[4,192,128]{2,1,0:T(8,128)(2,1)S(1)}, u32[]{:S(2)}, u32[]{:S(2)}) collective-permute-start(bf16[4,192,128]{2,1,0:T(8,128)(2,1)S(1)} %get-tuple-element.55), channel_id=1, source_target_pairs={{0,1},{1,0},{2,3},{3,2},{4,5},{5,4},{6,7},{7,6},{8,9},{9,8},{10,11... | collective-permute-start | bytes 589832 | tf_op jit(solution)/shard_map/ppermute | solution.py:342
  12.0 0.1 reshape.17
  12.1 0.1 reshape.16
  12.3 0.8 %collective-permute-done.refs_1_ = bf16[4,192,128]{2,1,0:T(8,128)(2,1)S(1)} collective-permute-done((bf16[4,192,128]{2,1,0:T(8,128)(2,1)S(1)}, bf16[4,192,128]{2,1,0:T(8,128)(2,1)S(1)}, u32[]{:S(2)}, u32[]{:S(2)}) %collective-permute-start) | collective-permute-done | bytes 196640 | tf_op jit(solution)/shard_map/ppermute | solution.py:342
  13.1 11.0 %collective-permute-done.1.refs_2_ = bf16[4,192,128]{2,1,0:T(8,128)(2,1)S(1)} collective-permute-done((bf16[4,192,128]{2,1,0:T(8,128)(2,1)S(1)}, bf16[4,192,128]{2,1,0:T(8,128)(2,1)S(1)}, u32[]{:S(2)}, u32[]{:S(2)}) %collective-permute-start.1) | collective-permute-done | bytes 196640 | tf_op jit(solution)/shard_map/ppermute | solution.py:342
  24.0 2.6 %collective-permute-start.3 = (bf16[4,192,128]{2,1,0:T(8,128)(2,1)S(1)}, bf16[4,192,128]{2,1,0:T(8,128)(2,1)S(1)}, u32[]{:S(2)}, u32[]{:S(2)}) collective-permute-start(bf16[4,192,128]{2,1,0:T(8,128)(2,1)S(1)} %get-tuple-element.53), channel_id=1, source_target_pairs={{0,3},{1,2},{2,1},{3,0},{4,7},{5,6},{6,5},{7,4},{8,11},{9,10},{10,... | collective-permute-start | bytes 589832 | tf_op jit(solution)/shard_map/ppermute | solution.py:342
  26.7 0.1 pad_add_fusion.scalars
  26.8 10.8 %shard_map.112 = (bf16[3,192,128]{2,1,0:T(8,128)(2,1)S(1)}, bf16[3,192,128]{2,1,0:T(8,128)(2,1)S(1)}, bf16[3,192,128]{2,1,0:T(8,128)(2,1)S(1)}, bf16[3,192,128]{2,1,0:T(8,128)(2,1)S(1)}, f32[2,32,96]{2,1,0:T(8,128)S(1)}) custom-call(s32[2]{0:T(128)S(1)} %pad_add_fusion.scalars, f32[2,31,96]{2,1,0:T(8,128)S(1)} %get-tuple-element.76.weight_ref, ...), custom_call_target="tpu_custom_call" | custom-call | flops 1207959552 | bytes 1376256 | tf_op jit(solution)/shard_map/pallas_call | solution.py:310
  37.5 1.8 %collective-permute-start.8 = (bf16[3,192,128]{2,1,0:T(8,128)(2,1)S(1)}, bf16[3,192,128]{2,1,0:T(8,128)(2,1)S(1)}, u32[]{:S(2)}, u32[]{:S(2)}) collective-permute-start(bf16[3,192,128]{2,1,0:T(8,128)(2,1)S(1)} %get-tuple-element.68), channel_id=1, source_target_pairs={{0,1},{1,0},{2,3},{3,2},{4,5},{5,4},{6,7},{7,6},{8,9},{9,8},{10,11... | collective-permute-start | bytes 442376 | tf_op jit(solution)/shard_map/ppermute | solution.py:342
  39.4 2.3 %collective-permute-done.4.refs_2_ = bf16[4,192,128]{2,1,0:T(8,128)(2,1)S(1)} collective-permute-done((bf16[4,192,128]{2,1,0:T(8,128)(2,1)S(1)}, bf16[4,192,128]{2,1,0:T(8,128)(2,1)S(1)}, u32[]{:S(2)}, u32[]{:S(2)}) %collective-permute-start.4) | collective-permute-done | bytes 196640 | tf_op jit(solution)/shard_map/ppermute | solution.py:342
  41.7 1.7 %collective-permute-start.7 = (bf16[3,192,128]{2,1,0:T(8,128)(2,1)S(1)}, bf16[3,192,128]{2,1,0:T(8,128)(2,1)S(1)}, u32[]{:S(2)}, u32[]{:S(2)}) collective-permute-start(bf16[3,192,128]{2,1,0:T(8,128)(2,1)S(1)} %get-tuple-element.65), channel_id=1, source_target_pairs={{0,3},{1,2},{2,1},{3,0},{4,7},{5,6},{6,5},{7,4},{8,11},{9,10},{10,... | collective-permute-start | bytes 442376 | tf_op jit(solution)/shard_map/ppermute | solution.py:342
  43.4 10.8 %shard_map.113 = (bf16[3,192,128]{2,1,0:T(8,128)(2,1)S(1)}, bf16[3,192,128]{2,1,0:T(8,128)(2,1)S(1)}, bf16[3,192,128]{2,1,0:T(8,128)(2,1)S(1)}, bf16[3,192,128]{2,1,0:T(8,128)(2,1)S(1)}, f32[2,32,96]{2,1,0:T(8,128)S(1)}) custom-call(s32[2]{0:T(128)S(1)} %pad_add_fusion.scalars, f32[2,31,96]{2,1,0:T(8,128)S(1)} %get-tuple-element.75.weight_ref, ...), custom_call_target="tpu_custom_call" | custom-call | flops 1207959552 | bytes 1376256 | tf_op jit(solution)/shard_map/pallas_call | solution.py:310
  54.2 2.1 %collective-permute-start.9 = (bf16[3,192,128]{2,1,0:T(8,128)(2,1)S(1)}, bf16[3,192,128]{2,1,0:T(8,128)(2,1)S(1)}, u32[]{:S(2)}, u32[]{:S(2)}) collective-permute-start(bf16[3,192,128]{2,1,0:T(8,128)(2,1)S(1)} %get-tuple-element.71), channel_id=1, source_target_pairs={{0,2},{1,3},{2,0},{3,1},{4,6},{5,7},{6,4},{7,5},{8,10},{9,11},{10,... | collective-permute-start | bytes 442376 | tf_op jit(solution)/shard_map/ppermute | solution.py:342
  56.4 0.7 %collective-permute-start.11 = (bf16[3,192,128]{2,1,0:T(8,128)(2,1)S(1)}, bf16[3,192,128]{2,1,0:T(8,128)(2,1)S(1)}, u32[]{:S(2)}, u32[]{:S(2)}) collective-permute-start(bf16[3,192,128]{2,1,0:T(8,128)(2,1)S(1)} %get-tuple-element.73), channel_id=1, source_target_pairs={{0,1},{1,0},{2,3},{3,2},{4,5},{5,4},{6,7},{7,6},{8,9},{9,8},{10,11... | collective-permute-start | bytes 442376 | tf_op jit(solution)/shard_map/ppermute | solution.py:342
  57.2 1.7 %collective-permute-start.10 = (bf16[3,192,128]{2,1,0:T(8,128)(2,1)S(1)}, bf16[3,192,128]{2,1,0:T(8,128)(2,1)S(1)}, u32[]{:S(2)}, u32[]{:S(2)}) collective-permute-start(bf16[3,192,128]{2,1,0:T(8,128)(2,1)S(1)} %get-tuple-element.72), channel_id=1, source_target_pairs={{0,3},{1,2},{2,1},{3,0},{4,7},{5,6},{6,5},{7,4},{8,11},{9,10},{10,... | collective-permute-start | bytes 442376 | tf_op jit(solution)/shard_map/ppermute | solution.py:342
  58.9 1.6 %collective-permute-start.13 = (f32[4,32,96]{2,1,0:T(8,128)S(1)}, f32[4,32,96]{2,1,0:T(8,128)S(1)}, u32[]{:S(2)}, u32[]{:S(2)}) collective-permute-start(f32[4,32,96]{2,1,0:T(8,128)S(1)} %add.11), channel_id=1, source_target_pairs={{0,8},{4,12},{8,0},{12,4},{16,24},{20,28},{24,16},{28,20},{1,9},{5... | collective-permute-start | bytes 147464 | tf_op jit(solution)/shard_map/ppermute | solution.py:352
  60.4 2.8 %collective-permute-done.13 = f32[4,32,96]{2,1,0:T(8,128)S(1)} collective-permute-done((f32[4,32,96]{2,1,0:T(8,128)S(1)}, f32[4,32,96]{2,1,0:T(8,128)S(1)}, u32[]{:S(2)}, u32[]{:S(2)}) %collective-permute-start.13) | collective-permute-done | bytes 49184 | tf_op jit(solution)/shard_map/ppermute | solution.py:352
  63.2 1.6 %collective-permute-start.14 = (f32[4,32,96]{2,1,0:T(8,128)S(1)}, f32[4,32,96]{2,1,0:T(8,128)S(1)}, u32[]{:S(2)}, u32[]{:S(2)}) collective-permute-start(f32[4,32,96]{2,1,0:T(8,128)S(1)} %add.12.refs_8_), channel_id=1, source_target_pairs={{0,16},{4,20},{8,24},{12,28},{16,0},{20,4},{24,8},{28,12},{1,17},{... | collective-permute-start | bytes 147464 | tf_op jit(solution)/shard_map/ppermute | solution.py:352
  64.8 3.1 %collective-permute-done.11.refs_7_ = bf16[3,192,128]{2,1,0:T(8,128)(2,1)S(1)} collective-permute-done((bf16[3,192,128]{2,1,0:T(8,128)(2,1)S(1)}, bf16[3,192,128]{2,1,0:T(8,128)(2,1)S(1)}, u32[]{:S(2)}, u32[]{:S(2)}) %collective-permute-start.11) | collective-permute-done | bytes 147488 | tf_op jit(solution)/shard_map/ppermute | solution.py:342
  67.9 1.4 %shard_map.114 = (bf16[1,128,1536]{2,1,0:T(8,128)(2,1)}, bf16[1,128,1536]{2,1,0:T(8,128)(2,1)}, bf16[1,128,1536]{2,1,0:T(8,128)(2,1)}, f32[31,384]{1,0:T(8,128)}, f32[384]{0:T(512)}) custom-call(s32[1]{0:T(128)} %bitcast.rank_ref, bf16[3,192,128]{2,1,0:T(8,128)(2,1)S(1)} %get-tuple-element.49.refs_0_, ...), custom_call_target="tpu_custom_call" | custom-call | bytes 2359296 | tf_op jit(solution)/shard_map/pallas_call | solution.py:128
  (25 shorter events, 0.2 us)
Async XLA Ops:
  2.1 10.9 %collective-permute-start = (bf16[4,192,128]{2,1,0:T(8,128)(2,1)S(1)}, bf16[4,192,128]{2,1,0:T(8,128)(2,1)S(1)}, u32[]{:S(2)}, u32[]{:S(2)}) collective-permute-start(bf16[4,192,128]{2,1,0:T(8,128)(2,1)S(1)} %get-tuple-element.43), channel_id=1, source_target_pairs={{0,3},{1,2},{2,1},{3,0},{4,7},{5,6},{6,5},{7,4},{8,11},{9,10},{10,... | collective-permute-start | bytes 589832 | tf_op jit(solution)/shard_map/ppermute | solution.py:342
  7.2 4.8 %copy-start = (f32[31,1536]{1,0:T(8,128)S(1)}, f32[31,1536]{1,0:T(8,128)}, u32[]{:S(2)}) copy-start(f32[31,1536]{1,0:T(8,128)} %param.11) | copy-start | bytes 571396
  7.2 16.8 %collective-permute-start.1 = (bf16[4,192,128]{2,1,0:T(8,128)(2,1)S(1)}, bf16[4,192,128]{2,1,0:T(8,128)(2,1)S(1)}, u32[]{:S(2)}, u32[]{:S(2)}) collective-permute-start(bf16[4,192,128]{2,1,0:T(8,128)(2,1)S(1)} %get-tuple-element.44), channel_id=1, source_target_pairs={{0,2},{1,3},{2,0},{3,1},{4,6},{5,7},{6,4},{7,5},{8,10},{9,11},{10,... | collective-permute-start | bytes 589832 | tf_op jit(solution)/shard_map/ppermute | solution.py:342
  9.2 2.8 %copy-start.1 = (f32[1536]{0:T(1024)S(1)}, f32[1536]{0:T(1024)}, u32[]{:S(2)}) copy-start(f32[1536]{0:T(1024)} %param.12) | copy-start | bytes 18436
  9.2 14.8 %collective-permute-start.2 = (bf16[4,192,128]{2,1,0:T(8,128)(2,1)S(1)}, bf16[4,192,128]{2,1,0:T(8,128)(2,1)S(1)}, u32[]{:S(2)}, u32[]{:S(2)}) collective-permute-start(bf16[4,192,128]{2,1,0:T(8,128)(2,1)S(1)} %get-tuple-element.45), channel_id=1, source_target_pairs={{0,1},{1,0},{2,3},{3,2},{4,5},{5,4},{6,7},{7,6},{8,9},{9,8},{10,11... | collective-permute-start | bytes 589832 | tf_op jit(solution)/shard_map/ppermute | solution.py:342
  9.9 29.4 %collective-permute-start.5 = (bf16[4,192,128]{2,1,0:T(8,128)(2,1)S(1)}, bf16[4,192,128]{2,1,0:T(8,128)(2,1)S(1)}, u32[]{:S(2)}, u32[]{:S(2)}) collective-permute-start(bf16[4,192,128]{2,1,0:T(8,128)(2,1)S(1)} %get-tuple-element.55), channel_id=1, source_target_pairs={{0,1},{1,0},{2,3},{3,2},{4,5},{5,4},{6,7},{7,6},{8,9},{9,8},{10,11... | collective-permute-start | bytes 589832 | tf_op jit(solution)/shard_map/ppermute | solution.py:342
  24.0 15.3 %collective-permute-start.3 = (bf16[4,192,128]{2,1,0:T(8,128)(2,1)S(1)}, bf16[4,192,128]{2,1,0:T(8,128)(2,1)S(1)}, u32[]{:S(2)}, u32[]{:S(2)}) collective-permute-start(bf16[4,192,128]{2,1,0:T(8,128)(2,1)S(1)} %get-tuple-element.53), channel_id=1, source_target_pairs={{0,3},{1,2},{2,1},{3,0},{4,7},{5,6},{6,5},{7,4},{8,11},{9,10},{10,... | collective-permute-start | bytes 589832 | tf_op jit(solution)/shard_map/ppermute | solution.py:342
  26.7 15.0 %collective-permute-start.4 = (bf16[4,192,128]{2,1,0:T(8,128)(2,1)S(1)}, bf16[4,192,128]{2,1,0:T(8,128)(2,1)S(1)}, u32[]{:S(2)}, u32[]{:S(2)}) collective-permute-start(bf16[4,192,128]{2,1,0:T(8,128)(2,1)S(1)} %get-tuple-element.54), channel_id=1, source_target_pairs={{0,2},{1,3},{2,0},{3,1},{4,6},{5,7},{6,4},{7,5},{8,10},{9,11},{10,... | collective-permute-start | bytes 589832 | tf_op jit(solution)/shard_map/ppermute | solution.py:342
  37.5 16.7 %collective-permute-start.8 = (bf16[3,192,128]{2,1,0:T(8,128)(2,1)S(1)}, bf16[3,192,128]{2,1,0:T(8,128)(2,1)S(1)}, u32[]{:S(2)}, u32[]{:S(2)}) collective-permute-start(bf16[3,192,128]{2,1,0:T(8,128)(2,1)S(1)} %get-tuple-element.68), channel_id=1, source_target_pairs={{0,1},{1,0},{2,3},{3,2},{4,5},{5,4},{6,7},{7,6},{8,9},{9,8},{10,11... | collective-permute-start | bytes 442376 | tf_op jit(solution)/shard_map/ppermute | solution.py:342
  41.7 14.6 %collective-permute-start.6 = (bf16[3,192,128]{2,1,0:T(8,128)(2,1)S(1)}, bf16[3,192,128]{2,1,0:T(8,128)(2,1)S(1)}, u32[]{:S(2)}, u32[]{:S(2)}) collective-permute-start(bf16[3,192,128]{2,1,0:T(8,128)(2,1)S(1)} %get-tuple-element.62), channel_id=1, source_target_pairs={{0,2},{1,3},{2,0},{3,1},{4,6},{5,7},{6,4},{7,5},{8,10},{9,11},{10,... | collective-permute-start | bytes 442376 | tf_op jit(solution)/shard_map/ppermute | solution.py:342
  41.7 15.5 %collective-permute-start.7 = (bf16[3,192,128]{2,1,0:T(8,128)(2,1)S(1)}, bf16[3,192,128]{2,1,0:T(8,128)(2,1)S(1)}, u32[]{:S(2)}, u32[]{:S(2)}) collective-permute-start(bf16[3,192,128]{2,1,0:T(8,128)(2,1)S(1)} %get-tuple-element.65), channel_id=1, source_target_pairs={{0,3},{1,2},{2,1},{3,0},{4,7},{5,6},{6,5},{7,4},{8,11},{9,10},{10,... | collective-permute-start | bytes 442376 | tf_op jit(solution)/shard_map/ppermute | solution.py:342
  54.2 10.6 %collective-permute-start.9 = (bf16[3,192,128]{2,1,0:T(8,128)(2,1)S(1)}, bf16[3,192,128]{2,1,0:T(8,128)(2,1)S(1)}, u32[]{:S(2)}, u32[]{:S(2)}) collective-permute-start(bf16[3,192,128]{2,1,0:T(8,128)(2,1)S(1)} %get-tuple-element.71), channel_id=1, source_target_pairs={{0,2},{1,3},{2,0},{3,1},{4,6},{5,7},{6,4},{7,5},{8,10},{9,11},{10,... | collective-permute-start | bytes 442376 | tf_op jit(solution)/shard_map/ppermute | solution.py:342
  56.4 2.5 %collective-permute-start.12 = (f32[4,32,96]{2,1,0:T(8,128)S(1)}, f32[4,32,96]{2,1,0:T(8,128)S(1)}, u32[]{:S(2)}, u32[]{:S(2)}) collective-permute-start(f32[4,32,96]{2,1,0:T(8,128)S(1)} %pad_maximum_fusion), channel_id=1, source_target_pairs={{0,4},{4,0},{8,12},{12,8},{16,20},{20,16},{24,28},{28,24},{1,5},{5... | collective-permute-start | bytes 147464 | tf_op jit(solution)/shard_map/ppermute | solution.py:352
  56.4 11.5 %collective-permute-start.11 = (bf16[3,192,128]{2,1,0:T(8,128)(2,1)S(1)}, bf16[3,192,128]{2,1,0:T(8,128)(2,1)S(1)}, u32[]{:S(2)}, u32[]{:S(2)}) collective-permute-start(bf16[3,192,128]{2,1,0:T(8,128)(2,1)S(1)} %get-tuple-element.73), channel_id=1, source_target_pairs={{0,1},{1,0},{2,3},{3,2},{4,5},{5,4},{6,7},{7,6},{8,9},{9,8},{10,11... | collective-permute-start | bytes 442376 | tf_op jit(solution)/shard_map/ppermute | solution.py:342
  57.2 10.8 %collective-permute-start.10 = (bf16[3,192,128]{2,1,0:T(8,128)(2,1)S(1)}, bf16[3,192,128]{2,1,0:T(8,128)(2,1)S(1)}, u32[]{:S(2)}, u32[]{:S(2)}) collective-permute-start(bf16[3,192,128]{2,1,0:T(8,128)(2,1)S(1)} %get-tuple-element.72), channel_id=1, source_target_pairs={{0,3},{1,2},{2,1},{3,0},{4,7},{5,6},{6,5},{7,4},{8,11},{9,10},{10,... | collective-permute-start | bytes 442376 | tf_op jit(solution)/shard_map/ppermute | solution.py:342
  58.9 4.3 %collective-permute-start.13 = (f32[4,32,96]{2,1,0:T(8,128)S(1)}, f32[4,32,96]{2,1,0:T(8,128)S(1)}, u32[]{:S(2)}, u32[]{:S(2)}) collective-permute-start(f32[4,32,96]{2,1,0:T(8,128)S(1)} %add.11), channel_id=1, source_target_pairs={{0,8},{4,12},{8,0},{12,4},{16,24},{20,28},{24,16},{28,20},{1,9},{5... | collective-permute-start | bytes 147464 | tf_op jit(solution)/shard_map/ppermute | solution.py:352
  63.2 4.7 %collective-permute-start.14 = (f32[4,32,96]{2,1,0:T(8,128)S(1)}, f32[4,32,96]{2,1,0:T(8,128)S(1)}, u32[]{:S(2)}, u32[]{:S(2)}) collective-permute-start(f32[4,32,96]{2,1,0:T(8,128)S(1)} %add.12.refs_8_), channel_id=1, source_target_pairs={{0,16},{4,20},{8,24},{12,28},{16,0},{20,4},{24,8},{28,12},{1,17},{... | collective-permute-start | bytes 147464 | tf_op jit(solution)/shard_map/ppermute | solution.py:352
